TPU v7x, 32 devices: a whole 2x2x4 slice. The times are simulated.
32 devices in a mesh: fsdp: 4 (over y, x), dp: 8 (over z, core).
Axes of the slice: x: 2, y: 2, z: 4, core: 2. Of those that a mesh axis runs over, the one named last changes fastest.
Arguments:
- tokens: bfloat16 [8, 1024, 2048], P('dp', 'fsdp'), may hold values from -6 to 6
- segments: int32 [8, 1024], P('dp'), may hold values from 0 to 4, as said below
- attn_gain: bfloat16 [2048], P('fsdp'), may hold values from 0.25 to 1.75
- w_query: bfloat16 [2048, 2048], P('fsdp'), may hold values from -0.125 to 0.125
- w_key: bfloat16 [2048, 1024], P('fsdp'), may hold values from -0.125 to 0.125
- w_value: bfloat16 [2048, 1024], P('fsdp'), may hold values from -0.125 to 0.125
- query_gain: bfloat16 [128], P('fsdp'), may hold values from 0.25 to 1.75
- key_gain: bfloat16 [128], P('fsdp'), may hold values from 0.25 to 1.75
- w_out: bfloat16 [2048, 2048], P(None, 'fsdp'), may hold values from -1.5 to 1.5
- mlp_gain: bfloat16 [2048], P('fsdp'), may hold values from 0.25 to 1.75
- w_gate: bfloat16 [2048, 6144], P('fsdp'), may hold values from -0.125 to 0.125
- w_up: bfloat16 [2048, 6144], P('fsdp'), may hold values from -0.125 to 0.125
- w_down: bfloat16 [6144, 2048], P(None, 'fsdp'), may hold values from -0.078125 to 0.078125
- cotangent: bfloat16 [8, 1024, 2048], P('dp', 'fsdp'), may hold values from -6 to 6
Outputs:
- output: bfloat16 [8, 1024, 2048], P('dp', 'fsdp')
- input_grad: float32 [8, 1024, 2048], P('dp', 'fsdp')
- grad_attn_gain: float32 [2048], P('fsdp')
- grad_query: float32 [2048, 2048], P('fsdp')
- grad_key: float32 [2048, 1024], P('fsdp')
- grad_value: float32 [2048, 1024], P('fsdp')
- grad_query_gain: float32 [128], P('fsdp')
- grad_key_gain: float32 [128], P('fsdp')
- grad_out: float32 [2048, 2048], P(None, 'fsdp')
- grad_mlp_gain: float32 [2048], P('fsdp')
- grad_gate: float32 [2048, 6144], P('fsdp')
- grad_up: float32 [2048, 6144], P('fsdp')
- grad_down: float32 [6144, 2048], P(None, 'fsdp')
Inputs may be any that keep to these rules, and one draw needn't show every extreme that they name: `segments`: document numbers start at 0 and never fall along a sequence; each sequence holds exactly 5 documents: 2 new ones begin within positions 1 to 128 and 2 within the last 128 positions.
All inputs are finite; a program needn't handle non-finite values.
Results may differ from a plain program's by a relative error of at most 0.02.
Values may be sent and summed in bfloat16 or wider, within the bound.
No kernel may reach another device: no remote copies, remote signals or barrier semaphores. Data moves between devices by JAX's collectives and lax.ppermute only.
A program may use at most 576 MiB of HBM per device.

v0:
```python
import math

import jax
import jax.numpy as jnp
from jax import lax
from jax.sharding import PartitionSpec as P

HEADS = 16
KV_HEADS = 8
HEAD = 128


epsilon = 1e-06
rope_base = 1000000.0
masked_score = -1e30


def rms_scale(vector):
    return lax.rsqrt(jnp.mean(vector * vector, axis=-1, keepdims=True) + epsilon)


def rotate(vector, cos_table, sin_table):
    half_size = vector.shape[-1] // 2
    turned = jnp.concatenate([-vector[..., half_size:], vector[..., :half_size]], axis=-1)
    return vector * cos_table + turned * sin_table


def rope_tables(positions, head_size):
    freq_index = jnp.arange(head_size // 2).astype(jnp.float32)
    inverse = rope_base ** (-2.0 * freq_index / head_size)
    angles = positions.astype(jnp.float32)[:, None] * inverse[None, :]
    angles = jnp.concatenate([angles, angles], axis=-1)
    return (jnp.cos(angles)[:, None, :], jnp.sin(angles)[:, None, :])


def norm_apply(vector, gain_values):
    return vector * rms_scale(vector) * gain_values


def swiglu(gate_act, upward):
    return gate_act / (1.0 + jnp.exp(-gate_act)) * upward


def matmul(first, second):
    return jnp.dot(first, second, preferred_element_type=jnp.float32)


def on_device(
    tokens,
    segments,
    attn_gain,
    w_query,
    w_key,
    w_value,
    query_gain,
    key_gain,
    w_out,
    mlp_gain,
    w_gate,
    w_up,
    w_down,
    cotangent,
):
    tok_rows = tokens.shape[1]
    doc_ids = segments[0]
    length = doc_ids.shape[0]
    group_size = HEADS // KV_HEADS
    key_width = KV_HEADS * HEAD
    score_scale = 1.0 / math.sqrt(HEAD)
    first_row = lax.axis_index("fsdp") * tok_rows
    token_index = first_row + jnp.arange(tok_rows, dtype=jnp.int32)
    key_index = jnp.arange(length, dtype=jnp.int32)
    doc_mine = lax.dynamic_slice_in_dim(doc_ids, first_row, tok_rows)
    earlier = jnp.sum((doc_ids[None, :] < doc_mine[:, None]).astype(jnp.int32), axis=1)
    cos_table, sin_table = rope_tables(token_index - earlier, HEAD)
    allowed = (doc_mine[:, None] == doc_ids[None, :]) & (key_index[None, :] <= token_index[:, None])
    gain_attn, gain_query, gain_key, gain_mlp, full_query, full_key, full_value, full_out = (
        lax.all_gather(attn_gain, "fsdp", axis=0, tiled=True),
        lax.all_gather(query_gain, "fsdp", axis=0, tiled=True),
        lax.all_gather(key_gain, "fsdp", axis=0, tiled=True),
        lax.all_gather(mlp_gain, "fsdp", axis=0, tiled=True),
        lax.all_gather(w_query, "fsdp", axis=0, tiled=True),
        lax.all_gather(w_key, "fsdp", axis=0, tiled=True),
        lax.all_gather(w_value, "fsdp", axis=0, tiled=True),
        lax.all_gather(w_out, "fsdp", axis=1, tiled=True),
    )
    stream = tokens[0].astype(jnp.float32)
    normed_exact, norm_pull = jax.vjp(norm_apply, stream, gain_attn.astype(jnp.float32))
    normed = normed_exact.astype(jnp.bfloat16)
    query_raw = matmul(normed, full_query)
    key_raw = matmul(normed, full_key)
    value_raw = matmul(normed, full_value)

    def head_apply(raw_rows, gain_values):
        shaped = raw_rows.reshape(tok_rows, -1, HEAD)
        return rotate(shaped * rms_scale(shaped) * gain_values, cos_table, sin_table)

    query_exact, query_pull = jax.vjp(head_apply, query_raw, gain_query.astype(jnp.float32))
    key_exact, key_pull = jax.vjp(head_apply, key_raw, gain_key.astype(jnp.float32))
    grouped = query_exact.astype(jnp.bfloat16).reshape(tok_rows, KV_HEADS, group_size, HEAD)
    key_local = key_exact.astype(jnp.bfloat16).reshape(tok_rows, key_width)
    value_local = value_raw.astype(jnp.bfloat16)
    key_all, value_all = (
        lax.all_gather(key_local, "fsdp", axis=0, tiled=True),
        lax.all_gather(value_local, "fsdp", axis=0, tiled=True),
    )
    key_heads = key_all.reshape(length, KV_HEADS, HEAD)
    value_heads = value_all.reshape(length, KV_HEADS, HEAD)
    scores = (
        jnp.einsum("qkgd,skd->kgqs", grouped, key_heads, preferred_element_type=jnp.float32)
        * score_scale
    )
    scores = jnp.where(allowed, scores, masked_score)
    top_score = jnp.max(scores, axis=-1, keepdims=True)
    shifted = jnp.exp(scores - top_score)
    denominator = jnp.sum(shifted, axis=-1, keepdims=True)
    log_total = top_score + jnp.log(denominator)
    attn_probs = (shifted / denominator).astype(jnp.bfloat16)
    attended = jnp.einsum(
        "kgqs,skd->qkgd", attn_probs, value_heads, preferred_element_type=jnp.float32
    )
    attended = attended.reshape(tok_rows, HEADS * HEAD).astype(jnp.bfloat16)
    middle = stream + matmul(attended, full_out)
    full_gate, full_up, full_down = (
        lax.all_gather(w_gate, "fsdp", axis=0, tiled=True),
        lax.all_gather(w_up, "fsdp", axis=0, tiled=True),
        lax.all_gather(w_down, "fsdp", axis=1, tiled=True),
    )
    normed_mlp_exact, mlp_norm_pull = jax.vjp(norm_apply, middle, gain_mlp.astype(jnp.float32))
    normed_mlp = normed_mlp_exact.astype(jnp.bfloat16)
    gate_act = matmul(normed_mlp, full_gate)
    upward = matmul(normed_mlp, full_up)
    hidden_exact, swiglu_pull = jax.vjp(swiglu, gate_act, upward)
    hidden = hidden_exact.astype(jnp.bfloat16)
    output = (middle + matmul(hidden, full_down)).astype(jnp.bfloat16)
    full_gate, full_up, full_down = (
        lax.all_gather(w_gate, "fsdp", axis=0, tiled=True),
        lax.all_gather(w_up, "fsdp", axis=0, tiled=True),
        lax.all_gather(w_down, "fsdp", axis=1, tiled=True),
    )
    out_grad = cotangent[0]
    grad_down_full = jnp.einsum("tf,td->fd", hidden, out_grad, preferred_element_type=jnp.float32)
    hidden_grad = jnp.einsum("td,fd->tf", out_grad, full_down, preferred_element_type=jnp.float32)
    gate_grad_exact, up_grad_exact = swiglu_pull(hidden_grad)
    gate_grad = gate_grad_exact.astype(jnp.bfloat16)
    up_grad = up_grad_exact.astype(jnp.bfloat16)
    grad_gate_full = jnp.einsum(
        "td,tf->df", normed_mlp, gate_grad, preferred_element_type=jnp.float32
    )
    grad_up_full = jnp.einsum("td,tf->df", normed_mlp, up_grad, preferred_element_type=jnp.float32)
    normed_mlp_grad = jnp.einsum(
        "tf,df->td", gate_grad, full_gate, preferred_element_type=jnp.float32
    )
    normed_mlp_grad = normed_mlp_grad + jnp.einsum(
        "tf,df->td", up_grad, full_up, preferred_element_type=jnp.float32
    )
    middle_norm_grad, gain_mlp_grad = mlp_norm_pull(normed_mlp_grad)
    middle_grad = out_grad.astype(jnp.float32) + middle_norm_grad
    mlp_shards = (
        lax.psum_scatter(
            grad_gate_full.astype(jnp.bfloat16), "fsdp", scatter_dimension=0, tiled=True
        ).astype(jnp.float32),
        lax.psum_scatter(
            grad_up_full.astype(jnp.bfloat16), "fsdp", scatter_dimension=0, tiled=True
        ).astype(jnp.float32),
        lax.psum_scatter(
            grad_down_full.astype(jnp.bfloat16), "fsdp", scatter_dimension=1, tiled=True
        ).astype(jnp.float32),
        lax.psum_scatter(
            gain_mlp_grad.astype(jnp.bfloat16), "fsdp", scatter_dimension=0, tiled=True
        ).astype(jnp.float32),
    )
    full_query, full_key, full_value, full_out = (
        lax.all_gather(w_query, "fsdp", axis=0, tiled=True),
        lax.all_gather(w_key, "fsdp", axis=0, tiled=True),
        lax.all_gather(w_value, "fsdp", axis=0, tiled=True),
        lax.all_gather(w_out, "fsdp", axis=1, tiled=True),
    )
    branch_grad = middle_grad.astype(jnp.bfloat16)
    grad_out_full = jnp.einsum(
        "tq,td->qd", attended, branch_grad, preferred_element_type=jnp.float32
    )
    attended_grad = jnp.einsum(
        "td,qd->tq", branch_grad, full_out, preferred_element_type=jnp.float32
    )
    attended_grad = attended_grad.astype(jnp.bfloat16).reshape(tok_rows, KV_HEADS, group_size, HEAD)
    scores = (
        jnp.einsum("qkgd,skd->kgqs", grouped, key_heads, preferred_element_type=jnp.float32)
        * score_scale
    )
    again_probs = jnp.where(
        allowed, jnp.exp(jnp.where(allowed, scores, masked_score) - log_total), 0.0
    )
    prob_grads = jnp.einsum(
        "qkgd,skd->kgqs", attended_grad, value_heads, preferred_element_type=jnp.float32
    )
    row_dots = jnp.sum(again_probs * prob_grads, axis=-1, keepdims=True)
    score_grads = (again_probs * (prob_grads - row_dots)).astype(jnp.bfloat16)
    probs_again = again_probs.astype(jnp.bfloat16)
    query_grad_exact = jnp.einsum(
        "kgqs,skd->qkgd", score_grads, key_heads, preferred_element_type=jnp.float32
    )
    query_grad_exact = query_grad_exact.reshape(tok_rows, HEADS, HEAD) * score_scale
    key_term = (
        jnp.einsum("kgqs,qkgd->skd", score_grads, grouped, preferred_element_type=jnp.float32)
        * score_scale
    )
    value_term = jnp.einsum(
        "kgqs,qkgd->skd", probs_again, attended_grad, preferred_element_type=jnp.float32
    )
    kv_grads = lax.psum_scatter(
        jnp.concatenate(
            [
                key_term.reshape(lax.axis_size("fsdp") * tok_rows, key_width),
                value_term.reshape(lax.axis_size("fsdp") * tok_rows, key_width),
            ],
            axis=1,
        ).astype(jnp.bfloat16),
        "fsdp",
        scatter_dimension=0,
        tiled=True,
    ).astype(jnp.float32)
    key_grad_exact, gain_key_grad = key_pull(
        kv_grads[:, :key_width].reshape(tok_rows, KV_HEADS, HEAD)
    )
    query_raw_grad, gain_query_grad = query_pull(query_grad_exact)
    query_grad = query_raw_grad.astype(jnp.bfloat16)
    key_grad = key_grad_exact.astype(jnp.bfloat16)
    value_grad = kv_grads[:, key_width:].astype(jnp.bfloat16)
    grad_query_full = jnp.einsum(
        "td,tq->dq", normed, query_grad, preferred_element_type=jnp.float32
    )
    grad_key_full = jnp.einsum("td,tq->dq", normed, key_grad, preferred_element_type=jnp.float32)
    grad_value_full = jnp.einsum(
        "td,tq->dq", normed, value_grad, preferred_element_type=jnp.float32
    )
    normed_grad = jnp.einsum(
        "tq,dq->td", query_grad, full_query, preferred_element_type=jnp.float32
    )
    normed_grad = normed_grad + jnp.einsum(
        "tq,dq->td", key_grad, full_key, preferred_element_type=jnp.float32
    )
    normed_grad = normed_grad + jnp.einsum(
        "tq,dq->td", value_grad, full_value, preferred_element_type=jnp.float32
    )
    stream_grad, gain_attn_grad = norm_pull(normed_grad)
    input_grad = (middle_grad + stream_grad)[None]
    attn_shards = (
        lax.psum_scatter(
            grad_query_full.astype(jnp.bfloat16), "fsdp", scatter_dimension=0, tiled=True
        ).astype(jnp.float32),
        lax.psum_scatter(
            grad_key_full.astype(jnp.bfloat16), "fsdp", scatter_dimension=0, tiled=True
        ).astype(jnp.float32),
        lax.psum_scatter(
            grad_value_full.astype(jnp.bfloat16), "fsdp", scatter_dimension=0, tiled=True
        ).astype(jnp.float32),
        lax.psum_scatter(
            grad_out_full.astype(jnp.bfloat16), "fsdp", scatter_dimension=1, tiled=True
        ).astype(jnp.float32),
        lax.psum_scatter(
            gain_attn_grad.astype(jnp.bfloat16), "fsdp", scatter_dimension=0, tiled=True
        ).astype(jnp.float32),
        lax.psum_scatter(
            gain_query_grad.astype(jnp.bfloat16), "fsdp", scatter_dimension=0, tiled=True
        ).astype(jnp.float32),
        lax.psum_scatter(
            gain_key_grad.astype(jnp.bfloat16), "fsdp", scatter_dimension=0, tiled=True
        ).astype(jnp.float32),
    )
    summed = (
        lax.psum(attn_shards[0].astype(jnp.bfloat16), "dp").astype(jnp.float32),
        lax.psum(attn_shards[1].astype(jnp.bfloat16), "dp").astype(jnp.float32),
        lax.psum(attn_shards[2].astype(jnp.bfloat16), "dp").astype(jnp.float32),
        lax.psum(attn_shards[3].astype(jnp.bfloat16), "dp").astype(jnp.float32),
        lax.psum(attn_shards[4].astype(jnp.bfloat16), "dp").astype(jnp.float32),
        lax.psum(attn_shards[5].astype(jnp.bfloat16), "dp").astype(jnp.float32),
        lax.psum(attn_shards[6].astype(jnp.bfloat16), "dp").astype(jnp.float32),
        lax.psum(mlp_shards[0].astype(jnp.bfloat16), "dp").astype(jnp.float32),
        lax.psum(mlp_shards[1].astype(jnp.bfloat16), "dp").astype(jnp.float32),
        lax.psum(mlp_shards[2].astype(jnp.bfloat16), "dp").astype(jnp.float32),
        lax.psum(mlp_shards[3].astype(jnp.bfloat16), "dp").astype(jnp.float32),
    )
    return (
        output[None],
        input_grad,
        summed[4],
        summed[0],
        summed[1],
        summed[2],
        summed[5],
        summed[6],
        summed[3],
        summed[10],
        summed[7],
        summed[8],
        summed[9],
    )


def solution(mesh):
    in_specs = (
        P("dp", "fsdp", None),
        P("dp", None),
        P("fsdp"),
        P("fsdp", None),
        P("fsdp", None),
        P("fsdp", None),
        P("fsdp"),
        P("fsdp"),
        P(None, "fsdp"),
        P("fsdp"),
        P("fsdp", None),
        P("fsdp", None),
        P(None, "fsdp"),
        P("dp", "fsdp", None),
    )
    out_specs = (
        P("dp", "fsdp", None),
        P("dp", "fsdp", None),
        P("fsdp"),
        P("fsdp", None),
        P("fsdp", None),
        P("fsdp", None),
        P("fsdp"),
        P("fsdp"),
        P(None, "fsdp"),
        P("fsdp"),
        P("fsdp", None),
        P("fsdp", None),
        P(None, "fsdp"),
    )
    return jax.shard_map(
        on_device, mesh=mesh, in_specs=in_specs, out_specs=out_specs, check_vma=False
    )
```

profile of v0, /device:TPU:0, one launch (start us, length us, event | category | flops | bytes accessed | tf_op | source)
XLA Modules:
  0.0 2722.7 jit_solution(17948594603156850667)
XLA Ops:
  9.4 9.5 all-gather
  20.6 44.7 %all-gather.12.cloned.1.call-done = bf16[2048,1024]{1,0:T(8,128)(2,1)} async-done(((bf16[512,1024]{1,0:T(8,128)(2,1)}), bf16[2048,1024]{1,0:T(8,128)(2,1)}) %all-gather.12.cloned.1.call-update) | async-done | bytes 4194320 | tf_op jit(solution)/shard_map/all_gather | solution.py:84
  72.1 9.0 all-reduce.13
  82.6 37.3 %all-gather.16.cloned.1.call-done = bf16[2048,1024]{1,0:T(8,128)(2,1)} async-done(((bf16[512,1024]{1,0:T(8,128)(2,1)}), bf16[2048,1024]{1,0:T(8,128)(2,1)}) %all-gather.16.cloned.1.call-update) | async-done | bytes 4194320 | tf_op jit(solution)/shard_map/all_gather | solution.py:83
  119.9 6.4 copy.51
  134.3 8.0 all-gather.1
  142.7 15.0 all-gather.14.cloned.1.call-done
  161.2 85.8 %all-gather.20.cloned.1.call-done = bf16[2048,2048]{1,0:T(8,128)(2,1)} async-done(((bf16[512,2048]{1,0:T(8,128)(2,1)}), bf16[2048,2048]{1,0:T(8,128)(2,1)}) %all-gather.20.cloned.1.call-update) | async-done | bytes 8388624 | tf_op jit(solution)/shard_map/all_gather | solution.py:82
  247.0 12.5 copy.52
  259.6 5.9 multiply_reduce_fusion.5
  267.4 17.1 all-gather.18.cloned.1.call-done
  284.5 9.5 fusion.79
  294.0 9.1 fusion.3
  303.2 8.5 fusion.40
  311.7 62.0 %all-gather.22.cloned.1.call-done = bf16[2048,2048]{1,0:T(8,128)(2,1)} async-done(((bf16[2048,512]{1,0:T(8,128)(2,1)}), bf16[2048,2048]{1,0:T(8,128)(2,1)}) %all-gather.22.cloned.1.call-update) | async-done | bytes 8388624 | tf_op jit(solution)/shard_map/all_gather | solution.py:85
  373.7 6.2 multiply_reduce_fusion.4
  380.1 223.2 %all-gather.26.cloned.1.call-done = bf16[2048,6144]{1,0:T(8,128)(2,1)} async-done(((bf16[512,6144]{1,0:T(8,128)(2,1)}), bf16[2048,6144]{1,0:T(8,128)(2,1)}) %all-gather.26.cloned.1.call-update) | async-done | bytes 25165840 | tf_op jit(solution)/shard_map/all_gather | solution.py:126
  603.3 16.0 fusion.81
  619.3 213.6 %all-gather.24.cloned.1.call-done = bf16[2048,6144]{1,0:T(8,128)(2,1)} async-done(((bf16[512,6144]{1,0:T(8,128)(2,1)}), bf16[2048,6144]{1,0:T(8,128)(2,1)}) %all-gather.24.cloned.1.call-update) | async-done | bytes 25165840 | tf_op jit(solution)/shard_map/all_gather | solution.py:125
  832.9 15.5 fusion.80
  848.4 214.0 %all-gather.28.cloned.1.call-done = bf16[6144,2048]{1,0:T(8,128)(2,1)} async-done(((bf16[6144,512]{1,0:T(8,128)(2,1)}), bf16[6144,2048]{1,0:T(8,128)(2,1)}) %all-gather.28.cloned.1.call-update) | async-done | bytes 25165840 | tf_op jit(solution)/shard_map/all_gather | solution.py:127
  1062.3 20.7 multiply_convert_fusion
  1083.0 13.5 fusion.82
  1096.5 15.0 multiply_reduce_fusion
  1122.2 10.6 bitcast_convert_fusion
  1132.8 13.9 fusion
  1146.7 11.1 fusion.2
  1157.8 6.4 fusion.11
  1174.4 45.1 %reduce-scatter.9.cloned.1.call-done = bf16[256,2048]{0,1:T(8,128)(2,1)} async-done(((bf16[1024,2048]{0,1:T(8,128)(2,1)}), bf16[256,2048]{0,1:T(8,128)(2,1)}) %reduce-scatter.9.cloned.1.call-update) | async-done | bytes 1048592 | tf_op jit(solution)/shard_map/reduce_scatter | solution.py:211
  1241.6 5.9 convolution_convert_fusion.4
  1247.5 14.1 convolution_convert_fusion
  1261.9 13.7 convolution_convert_fusion.1
  1275.7 13.9 convolution_convert_fusion.2
  1289.9 19.9 reduce-scatter.17.cloned.1.call-done
  1309.8 56.1 %reduce-scatter.15.cloned.1.call-done = bf16[512,1024]{1,0:T(8,128)(2,1)} async-done(((bf16[2048,1024]{1,0:T(8,128)(2,1)}), bf16[512,1024]{1,0:T(8,128)(2,1)}) %reduce-scatter.15.cloned.1.call-update) | async-done | bytes 1048592 | tf_op jit(solution)/shard_map/reduce_scatter | solution.py:255
  1365.9 56.5 %reduce-scatter.13.cloned.1.call-done = bf16[512,1024]{1,0:T(8,128)(2,1)} async-done(((bf16[2048,1024]{1,0:T(8,128)(2,1)}), bf16[512,1024]{1,0:T(8,128)(2,1)}) %reduce-scatter.13.cloned.1.call-update) | async-done | bytes 1048592 | tf_op jit(solution)/shard_map/reduce_scatter | solution.py:252
  1422.5 89.9 %reduce-scatter.11.cloned.1.call-done = bf16[512,2048]{1,0:T(8,128)(2,1)} async-done(((bf16[2048,2048]{1,0:T(8,128)(2,1)}), bf16[512,2048]{1,0:T(8,128)(2,1)}) %reduce-scatter.11.cloned.1.call-update) | async-done | bytes 2097168 | tf_op jit(solution)/shard_map/reduce_scatter | solution.py:249
  1512.4 225.1 %reduce-scatter.23.cloned.1.call-done = bf16[6144,512]{1,0:T(8,128)(2,1)} async-done(((bf16[6144,2048]{1,0:T(8,128)(2,1)}), bf16[6144,512]{1,0:T(8,128)(2,1)}) %reduce-scatter.23.cloned.1.call-update) | async-done | bytes 6291472 | tf_op jit(solution)/shard_map/reduce_scatter | solution.py:166
  1737.5 224.9 %reduce-scatter.21.cloned.1.call-done = bf16[512,6144]{1,0:T(8,128)(2,1)} async-done(((bf16[2048,6144]{1,0:T(8,128)(2,1)}), bf16[512,6144]{1,0:T(8,128)(2,1)}) %reduce-scatter.21.cloned.1.call-update) | async-done | bytes 6291472 | tf_op jit(solution)/shard_map/reduce_scatter | solution.py:163
  1962.4 225.2 %reduce-scatter.19.cloned.1.call-done = bf16[512,6144]{1,0:T(8,128)(2,1)} async-done(((bf16[2048,6144]{1,0:T(8,128)(2,1)}), bf16[512,6144]{1,0:T(8,128)(2,1)}) %reduce-scatter.19.cloned.1.call-update) | async-done | bytes 6291472 | tf_op jit(solution)/shard_map/reduce_scatter | solution.py:160
  2188.9 6.2 fusion.84
  2195.2 14.2 fusion.20
  2214.9 9.3 all-reduce.12
  2224.5 15.8 all-reduce.10
  2246.0 440.0 %all-reduce.16.cloned.1.call-done = (bf16[512,2048]{1,0:T(8,128)(2,1)}, bf16[512,1024]{1,0:T(8,128)(2,1)}, bf16[512,1024]{1,0:T(8,128)(2,1)}, bf16[2048,512]{1,0...) async-done(((bf16[512,2048]{1,0:T(8,128)(2,1)}, bf16[512,1024]{1,0:T(8,128)(2,1)}, bf16[512,1024]{1,0:T(8,128)(2,1)}, ...) | async-done | bytes 25165840 | tf_op jit(solution)/shard_map/psum | solution.py:272
  2696.1 6.4 convert_element_type.259
  2702.6 6.4 convert_element_type.261
  2709.0 6.6 convert_element_type.263
  (252 shorter events, 90.1 us)
Async XLA Ops:
  7.2 58.1 %copy-start = (bf16[1,256,2048]{2,1,0:T(8,128)(2,1)S(1)}, bf16[1,256,2048]{2,1,0:T(8,128)(2,1)}, u32[]{:S(2)}) copy-start(bf16[1,256,2048]{2,1,0:T(8,128)(2,1)} %param.14) | copy-start | bytes 3145732
  7.2 58.1 %all-gather.12.cloned.1.call-start = ((), (), s32[]{:S(2)}) async-start(), calls=%async_computation.8 | async-start | bytes 5242880 | tf_op jit(solution)/shard_map/all_gather | solution.py:84
  7.9 112.0 %all-gather.16.cloned.1.call-start = ((), (), s32[]{:S(2)}) async-start(), calls=%async_computation.10 | async-start | bytes 5242880 | tf_op jit(solution)/shard_map/all_gather | solution.py:83
  8.7 149.0 %all-gather.14.cloned.1.call-start = ((), (), s32[]{:S(2)}) async-start(), calls=%async_computation.9 | async-start | bytes 2621440 | tf_op jit(solution)/shard_map/all_gather | solution.py:105
  18.9 240.6 %copy-start.33 = (f32[4,1,512]{2,1,0:T(1,128)}, f32[4,1,512]{2,1,0:T(1,128)S(1)}, u32[]{:S(2)}) copy-start(f32[4,1,512]{2,1,0:T(1,128)S(1)} %convert_element_type.265) | copy-start | bytes 24580
  20.6 49.1 %copy-start.48 = (f32[256]{0:T(256)}, f32[256]{0:T(256)S(1)}, u32[]{:S(2)}) copy-start(f32[256]{0:T(256)S(1)} %fusion.25) | copy-start | bytes 3076
  20.6 239.0 %copy-start.43 = (f32[256]{0:T(256)}, f32[256]{0:T(256)S(1)}, u32[]{:S(2)}) copy-start(f32[256]{0:T(256)S(1)} %fusion.68) | copy-start | bytes 3076
  65.3 15.8 copy-start.47
  69.7 177.3 %all-gather.20.cloned.1.call-start = ((), (), s32[]{:S(2)}) async-start(), calls=%async_computation.12 | async-start | bytes 10485760 | tf_op jit(solution)/shard_map/all_gather | solution.py:82
  70.3 214.2 %all-gather.18.cloned.1.call-start = ((), (), s32[]{:S(2)}) async-start(), calls=%async_computation.11 | async-start | bytes 2621440 | tf_op jit(solution)/shard_map/all_gather | solution.py:104
  81.1 49.1 %copy-start.50 = (f32[128]{0:T(128)}, f32[128]{0:T(128)S(1)}, u32[]{:S(2)}) copy-start(f32[128]{0:T(128)S(1)} %convert_element_type.216) | copy-start | bytes 1540
  82.6 183.4 %copy-start.25 = (f32[256,128]{0,1:T(8,128)}, f32[256,128]{0,1:T(8,128)S(1)}, u32[]{:S(2)}) copy-start(f32[256,128]{0,1:T(8,128)S(1)} %get-tuple-element.53) | copy-start | bytes 393220
  82.6 183.4 %copy-start.28 = (f32[256,128]{0,1:T(8,128)}, f32[256,128]{0,1:T(8,128)S(1)}, u32[]{:S(2)}) copy-start(f32[256,128]{0,1:T(8,128)S(1)} %get-tuple-element.52) | copy-start | bytes 393220
  131.4 242.2 %all-gather.22.cloned.1.call-start = ((), (), s32[]{:S(2)}) async-start(), calls=%async_computation.13 | async-start | bytes 10485760 | tf_op jit(solution)/shard_map/all_gather | solution.py:85
  132.0 471.3 %all-gather.26.cloned.1.call-start = ((), (), s32[]{:S(2)}) async-start(), calls=%async_computation.15 | async-start | bytes 31457280 | tf_op jit(solution)/shard_map/all_gather | solution.py:126
  132.7 700.1 %all-gather.24.cloned.1.call-start = ((), (), s32[]{:S(2)}) async-start(), calls=%async_computation.14 | async-start | bytes 31457280 | tf_op jit(solution)/shard_map/all_gather | solution.py:125
  133.5 928.8 %all-gather.28.cloned.1.call-start = ((), (), s32[]{:S(2)}) async-start(), calls=%async_computation.16 | async-start | bytes 31457280 | tf_op jit(solution)/shard_map/all_gather | solution.py:127
  134.2 1085.2 %reduce-scatter.9.cloned.1.call-start = ((), (), s32[]{:S(2)}) async-start(), calls=%async_computation.17 | async-start | bytes 5242880 | tf_op jit(solution)/shard_map/reduce_scatter | solution.py:211
  134.3 131.8 %copy-start.52 = (f32[128]{0:T(128)}, f32[128]{0:T(128)S(1)}, u32[]{:S(2)}) copy-start(f32[128]{0:T(128)S(1)} %convert_element_type.221) | copy-start | bytes 1540
  142.6 141.8 %copy-start.15 = (pred[256,1024]{0,1:T(8,128)(4,1)}, pred[256,1024]{0,1:T(8,128)(4,1)S(1)}, u32[]{:S(2)}) copy-start(pred[256,1024]{0,1:T(8,128)(4,1)S(1)} %fusion.57) | copy-start | bytes 786436
  267.4 26.6 copy-start.4
  294.0 9.2 copy-start.14
  379.8 731.7 %copy-start.8 = (f32[256,2048]{1,0:T(8,128)}, f32[256,2048]{1,0:T(8,128)S(1)}, u32[]{:S(2)}) copy-start(f32[256,2048]{1,0:T(8,128)S(1)} %get-tuple-element.63) | copy-start | bytes 6291460
  380.1 452.8 %copy-start.13 = (bf16[256,2048]{1,0:T(8,128)(2,1)}, bf16[256,2048]{1,0:T(8,128)(2,1)S(1)}, u32[]{:S(2)}) copy-start(bf16[256,2048]{1,0:T(8,128)(2,1)S(1)} %multiply_convert_fusion.2) | copy-start | bytes 3145732
  1096.5 15.0 copy-start.23
  1115.1 7.1 copy-start.16
  1122.2 24.5 slice-start
  1122.2 24.5 slice-start.1
  1132.8 13.9 slice-start.2
  1132.8 13.9 slice-start.3
  1146.7 11.1 copy-start.5
  1166.7 143.2 %reduce-scatter.17.cloned.1.call-start = ((), (), s32[]{:S(2)}) async-start(), calls=%async_computation.21 | async-start | bytes 10485760 | tf_op jit(solution)/shard_map/reduce_scatter | solution.py:258
  1174.3 45.2 %copy-start.1 = (bf16[1,256,2048]{2,1,0:T(8,128)(2,1)S(1)}, bf16[1,256,2048]{2,1,0:T(8,128)(2,1)}, u32[]{:S(2)}) copy-start(bf16[1,256,2048]{2,1,0:T(8,128)(2,1)} %param.14) | copy-start | bytes 3145732
  1174.3 45.2 %copy-start.34 = (f32[4,1,512]{2,1,0:T(1,128)S(1)}, f32[4,1,512]{2,1,0:T(1,128)}, u32[]{:S(2)}) copy-start(f32[4,1,512]{2,1,0:T(1,128)} %copy-done.33) | copy-start | bytes 24580
  1174.3 45.2 %copy-start.44 = (f32[256]{0:T(256)S(1)}, f32[256]{0:T(256)}, u32[]{:S(2)}) copy-start(f32[256]{0:T(256)} %copy-done.43) | copy-start | bytes 3076
  1174.3 191.6 %reduce-scatter.15.cloned.1.call-start = ((), (), s32[]{:S(2)}) async-start(), calls=%async_computation.20 | async-start | bytes 5242880 | tf_op jit(solution)/shard_map/reduce_scatter | solution.py:255
  1224.0 198.4 %reduce-scatter.13.cloned.1.call-start = ((), (), s32[]{:S(2)}) async-start(), calls=%async_computation.19 | async-start | bytes 5242880 | tf_op jit(solution)/shard_map/reduce_scatter | solution.py:252
  1231.3 281.0 %reduce-scatter.11.cloned.1.call-start = ((), (), s32[]{:S(2)}) async-start(), calls=%async_computation.18 | async-start | bytes 10485760 | tf_op jit(solution)/shard_map/reduce_scatter | solution.py:249
  1247.5 490.0 %reduce-scatter.23.cloned.1.call-start = ((), (), s32[]{:S(2)}) async-start(), calls=%async_computation.24 | async-start | bytes 31457280 | tf_op jit(solution)/shard_map/reduce_scatter | solution.py:166
  1261.7 700.7 %reduce-scatter.21.cloned.1.call-start = ((), (), s32[]{:S(2)}) async-start(), calls=%async_computation.23 | async-start | bytes 31457280 | tf_op jit(solution)/shard_map/reduce_scatter | solution.py:163
  1275.7 911.9 %reduce-scatter.19.cloned.1.call-start = ((), (), s32[]{:S(2)}) async-start(), calls=%async_computation.22 | async-start | bytes 31457280 | tf_op jit(solution)/shard_map/reduce_scatter | solution.py:160
  1289.6 1396.3 %all-reduce.16.cloned.1.call-start = ((), (), s32[]{:S(2)}) async-start(), calls=%async_computation.25 | async-start | bytes 50331648 | tf_op jit(solution)/shard_map/psum | solution.py:272
  2195.2 14.2 copy-start.12
  2195.2 14.2 copy-start.21
  2211.9 30.6 %copy-start.49 = (f32[256]{0:T(256)S(1)}, f32[256]{0:T(256)}, u32[]{:S(2)}) copy-start(f32[256]{0:T(256)} %copy-done.48) | copy-start | bytes 3076
  2686.0 10.2 slice-start.9
  2693.4 9.2 slice-start.7
  2696.1 12.9 slice-start.5
  (41 other events, 113.4 us)
Sparse Core Ops, SparseCore 0:
  9.9 55.4 all-gather.11
  67.2 52.6 all-gather.15
  122.3 35.3 all-gather.13
  159.4 87.5 all-gather.19
  249.3 35.1 all-gather.17
  286.2 87.4 all-gather.21
  375.5 227.7 all-gather.25
  605.1 227.7 all-gather.23
  834.7 227.5 all-gather.27
  1166.8 52.6 reduce-scatter.8
  1223.4 86.3 reduce-scatter.16
  1313.2 52.6 reduce-scatter.14
  1369.8 52.6 reduce-scatter.12
  1426.0 86.3 reduce-scatter.10
  1515.6 221.8 reduce-scatter.22
  1740.5 221.8 reduce-scatter.20
  1965.6 221.8 reduce-scatter.18
  2190.8 495.0 all-reduce.15
where the time goes:
time: 2730 us; the launch traced here: 2720 us
  waiting for transfers between devices  2300 us (84%)
  matrix products  247 us (9%)
  other arithmetic  70.5 us (3%)
  blocking collectives  51.6 us (2%)
  local copies, waits for them, and re-layouts  35.1 us (1%)
    psum x1, waiting for transfers between devices, on_device(): lax.psum(attn_shards[0].astype(jnp.bfloat16), 'dp').astype(jnp.float32)  440 us
    reduce_scatter x1, waiting for transfers between devices, on_device(): lax.psum_scatter(grad_gate_full.astype(jnp.bfloat16), 'fsdp', scatter_dim...  225 us
    reduce_scatter x1, waiting for transfers between devices, on_device(): lax.psum_scatter(grad_down_full.astype(jnp.bfloat16), 'fsdp', scatter_dim...  225 us
    reduce_scatter x1, waiting for transfers between devices, on_device(): lax.psum_scatter(grad_up_full.astype(jnp.bfloat16), 'fsdp', scatter_dimen...  225 us
    all_gather x1, waiting for transfers between devices, on_device(): lax.all_gather(w_up, 'fsdp', axis=0, tiled=True)  223 us
    all_gather x1, waiting for transfers between devices, on_device(): lax.all_gather(w_down, 'fsdp', axis=1, tiled=True)  214 us
    all_gather x1, waiting for transfers between devices, on_device(): lax.all_gather(w_gate, 'fsdp', axis=0, tiled=True)  214 us
    reduce_scatter x1, waiting for transfers between devices, on_device(): lax.psum_scatter(grad_query_full.astype(jnp.bfloat16), 'fsdp', scatter_di...  89.9 us
  transfers between devices with their start and end apart: 18, of which 18 were waited for; matrix products, arithmetic and copies ran while one was open for 8% of the time, Pallas kernels for 0%

commit v1 on v0

v1 whole, which is shorter than its diff:
```python
import math

import jax
import jax.numpy as jnp
from jax import lax
from jax.sharding import Mesh
from jax.sharding import PartitionSpec as P

HEADS = 16
KV_HEADS = 8
HEAD = 128
GROUP = HEADS // KV_HEADS

epsilon = 1e-06
rope_base = 1000000.0
masked_score = -1e30
score_scale = 1.0 / math.sqrt(HEAD)

bf16 = jnp.bfloat16
f32 = jnp.float32


def matmul(first, second):
    return jnp.dot(first, second, preferred_element_type=f32)


def matmul_tn(first, second):
    return lax.dot_general(first, second, (((0,), (0,)), ((), ())), preferred_element_type=f32)


def matmul_nt(first, second):
    return lax.dot_general(first, second, (((1,), (1,)), ((), ())), preferred_element_type=f32)


def rms_scale(vector):
    return lax.rsqrt(jnp.mean(vector * vector, axis=-1, keepdims=True) + epsilon)


def norm_back(vector, scale, gain, incoming):
    scaled = gain * incoming
    d_vector = scale * scaled - vector * (scale**3) * jnp.mean(
        vector * scaled, axis=-1, keepdims=True
    )
    return d_vector, incoming * vector * scale


def swap(value, axis, k):
    return lax.ppermute(value, axis, [(j, j ^ k) for j in range(lax.axis_size(axis))])


def core_swap(value):
    return swap(value, "core", 1)


def rows_of(value, start, size):
    return lax.dynamic_slice_in_dim(value, start, size, axis=0)


def gather_rows(shard):
    n, me = lax.axis_size("fsdp"), lax.axis_index("fsdp")
    size = shard.shape[0]
    blocks = {0: shard}
    if n == 4 and size % 32 == 0:
        half = size // 2
        blocks[1] = swap(shard, "fsdp", 1)
        blocks[2] = swap(shard, "fsdp", 2)
        first = swap(blocks[1][:half], "fsdp", 2)
        second = swap(blocks[2][half:], "fsdp", 1)
        blocks[3] = jnp.concatenate([first, second], axis=0)
    else:
        for k in range(1, n):
            blocks[k] = swap(shard, "fsdp", k)
    out = jnp.zeros((n * size,) + shard.shape[1:], shard.dtype)
    for k, block in blocks.items():
        out = lax.dynamic_update_slice_in_dim(out, block, (me ^ k) * size, axis=0)
    return out


def scatter_rows(partial):
    n, me = lax.axis_size("fsdp"), lax.axis_index("fsdp")
    size = partial.shape[0] // n
    blocks = [rows_of(partial, (me ^ k) * size, size) for k in range(n)]
    total = blocks[0].astype(f32)
    if n == 4 and size % 32 == 0:
        half = size // 2
        first = swap(blocks[3][:half], "fsdp", 1)
        second = swap(blocks[3][half:], "fsdp", 2)
        top = blocks[2][:half].astype(f32) + first.astype(f32)
        low = blocks[1][half:].astype(f32) + second.astype(f32)
        to_x = jnp.concatenate([blocks[1][:half], low.astype(bf16)], axis=0)
        to_y = jnp.concatenate([top.astype(bf16), blocks[2][half:]], axis=0)
        total = total + swap(to_x, "fsdp", 1).astype(f32) + swap(to_y, "fsdp", 2).astype(f32)
    else:
        for k in range(1, n):
            total = total + swap(blocks[k], "fsdp", k).astype(f32)
    return total


def spread_rows(parts):
    n, me, core = lax.axis_size("fsdp"), lax.axis_index("fsdp"), lax.axis_index("core")
    rows = parts[0].shape[0]
    half = rows // 2
    widths = [part.shape[1] // n for part in parts]

    def piece(start, size, block):
        return jnp.concatenate(
            [
                lax.dynamic_slice(part, (start, block * width), (size, width))
                for part, width in zip(parts, widths)
            ],
            axis=1,
        )

    out = jnp.zeros((n * rows, sum(widths)), parts[0].dtype)
    out = lax.dynamic_update_slice(out, piece(0, rows, me), (me * rows, 0))
    for k in range(1, n):
        got = swap(piece(core * half, half, me ^ k), "fsdp", k)
        other = core_swap(got)
        base = (me ^ k) * rows
        out = lax.dynamic_update_slice(out, got, (base + core * half, 0))
        out = lax.dynamic_update_slice(out, other, (base + (1 - core) * half, 0))
    return out


def spread_columns(part):
    n, me, core = lax.axis_size("fsdp"), lax.axis_index("fsdp"), lax.axis_index("core")
    rows, width = part.shape[0] // n, part.shape[1]
    half = rows // 2
    out = jnp.zeros((rows, n * width), part.dtype)
    out = lax.dynamic_update_slice(out, rows_of(part, me * rows, rows), (0, me * width))
    for k in range(1, n):
        got = swap(rows_of(part, (me ^ k) * rows + core * half, half), "fsdp", k)
        other = core_swap(got)
        base = (me ^ k) * width
        out = lax.dynamic_update_slice(out, got, (core * half, base))
        out = lax.dynamic_update_slice(out, other, ((1 - core) * half, base))
    return out


def line_scatter(chunks):
    nz, z = lax.axis_size("z"), lax.axis_index("z")

    def chunk(index):
        return lax.dynamic_index_in_dim(
            chunks, jnp.clip(index, 0, nz - 1), 0, keepdims=False
        ).astype(f32)

    up = down = None
    for s in range(1, nz):
        up_send, down_send = chunk(z + nz - s), chunk(z - nz + s)
        if up is not None:
            up_send, down_send = up_send + up.astype(f32), down_send + down.astype(f32)
        up = lax.ppermute(up_send.astype(bf16), "z", [(j, j + 1) for j in range(s)])
        down = lax.ppermute(down_send.astype(bf16), "z", [(j, j - 1) for j in range(nz - s, nz)])
    total = chunk(z)
    if up is not None:
        total = total + up.astype(f32) + down.astype(f32)
    return total.astype(bf16)


def line_gather(chunk):
    nz, z = lax.axis_size("z"), lax.axis_index("z")
    ups, downs = [chunk], [chunk]
    for s in range(1, nz):
        ups.append(lax.ppermute(ups[-1], "z", [(j, j + 1) for j in range(s - 1, nz - 1)]))
        downs.append(lax.ppermute(downs[-1], "z", [(j, j - 1) for j in range(1, nz - s + 1)]))
    out = jnp.zeros((nz,) + chunk.shape, chunk.dtype)
    out = lax.dynamic_update_index_in_dim(out, chunk, z, 0)
    for s in range(1, nz):
        block = jnp.where(z >= s, ups[s], downs[nz - s])
        out = lax.dynamic_update_index_in_dim(out, block, (z - s) % nz, 0)
    return out


def core_halves(mine):
    core = lax.axis_index("core")
    other = core_swap(mine)
    first = jnp.where(core == 0, mine, other)
    second = jnp.where(core == 0, other, mine)
    return jnp.stack([first, second]).astype(f32)


def reduce_row_grads(grad):
    n, nz = lax.axis_size("fsdp"), lax.axis_size("z")
    me, core = lax.axis_index("fsdp"), lax.axis_index("core")
    width = grad.shape[1]
    piece = grad.shape[0] // (n * 2 * nz)
    split = grad.reshape(n, 2, nz, piece, width)
    keep = lax.dynamic_index_in_dim(split, core, 1, keepdims=False)
    send = lax.dynamic_index_in_dim(split, 1 - core, 1, keepdims=False)
    both = (keep.astype(f32) + core_swap(send).astype(f32)).astype(bf16)
    summed = line_scatter(jnp.swapaxes(both, 0, 1))
    out = jnp.zeros((piece, n, width), bf16)
    for k in range(n):
        block = lax.dynamic_index_in_dim(summed, me ^ k, 0, keepdims=False)
        if k:
            block = swap(block, "fsdp", k)
        out = lax.dynamic_update_index_in_dim(out, block, me ^ k, 1)
    full = core_halves(line_gather(out))
    return full.reshape(2 * nz * piece, n, width)


def reduce_column_grads(grad):
    n, nz = lax.axis_size("fsdp"), lax.axis_size("z")
    me, core = lax.axis_index("fsdp"), lax.axis_index("core")
    rows, wide = grad.shape
    width = wide // n
    piece = rows // (2 * nz)
    keep = rows_of(grad, core * (rows // 2), rows // 2)
    send = rows_of(grad, (1 - core) * (rows // 2), rows // 2)
    both = (keep.astype(f32) + core_swap(send).astype(f32)).astype(bf16)
    summed = line_scatter(both.reshape(nz, piece, wide))
    out = jnp.zeros((n, piece, width), bf16)
    for k in range(n):
        block = lax.dynamic_slice_in_dim(summed, (me ^ k) * width, width, axis=1)
        if k:
            block = swap(block, "fsdp", k)
        out = lax.dynamic_update_index_in_dim(out, block, me ^ k, 0)
    full = core_halves(line_gather(out))
    return jnp.moveaxis(full, 2, 0).reshape(n * rows, width)


def sum_all(value):
    for axis in ("core", "fsdp", "z"):
        size = lax.axis_size(axis)
        k = 1
        while k < size:
            value = value + swap(value, axis, k)
            k *= 2
    return value


def turn(value, cos_table, sin_table):
    half = HEAD // 2
    turned = jnp.concatenate([-value[..., half:], value[..., :half]], axis=-1)
    return value * cos_table + turned * sin_table


def turn_back(value, cos_table, sin_table):
    half = HEAD // 2
    turned = jnp.concatenate(
        [value[..., half:] * sin_table[..., half:], -value[..., :half] * sin_table[..., :half]],
        axis=-1,
    )
    return value * cos_table + turned


def on_device(
    tokens,
    segments,
    attn_gain,
    w_query,
    w_key,
    w_value,
    query_gain,
    key_gain,
    w_out,
    mlp_gain,
    w_gate,
    w_up,
    w_down,
    cotangent,
):
    n, me = lax.axis_size("fsdp"), lax.axis_index("fsdp")
    tok_rows, width = tokens.shape[1], tokens.shape[2]
    doc_ids = segments[0]
    length = doc_ids.shape[0]
    heads, kv_heads = HEADS // n, KV_HEADS // n
    q_width, kv_width = heads * HEAD, kv_heads * HEAD
    ff = w_gate.shape[1] // n

    index = jnp.arange(length, dtype=jnp.int32)
    earlier = jnp.sum((doc_ids[None, :] < doc_ids[:, None]).astype(jnp.int32), axis=1)
    position = index - earlier
    inverse = rope_base ** (-2.0 * jnp.arange(HEAD // 2).astype(f32) / HEAD)
    angles = position.astype(f32)[:, None] * inverse[None, :]
    angles = jnp.concatenate([angles, angles], axis=-1)
    cos_table, sin_table = jnp.cos(angles)[:, None, :], jnp.sin(angles)[:, None, :]
    allowed = (doc_ids[:, None] == doc_ids[None, :]) & (index[None, :] <= index[:, None])

    sizes = [attn_gain.shape[0], mlp_gain.shape[0], query_gain.shape[0], key_gain.shape[0]]
    packed = jnp.concatenate([attn_gain, mlp_gain, query_gain, key_gain])
    gains = gather_rows(packed[None]).astype(f32)
    ends = [sum(sizes[: j + 1]) for j in range(4)]
    gain_attn = gains[:, : ends[0]].reshape(-1)
    gain_mlp = gains[:, ends[0] : ends[1]].reshape(-1)
    gain_query = gains[:, ends[1] : ends[2]].reshape(-1)
    gain_key = gains[:, ends[2] : ends[3]].reshape(-1)

    full_qkv = spread_rows([w_query, w_key, w_value])
    tokens_all = gather_rows(tokens[0])
    full_out = spread_columns(w_out)
    full_gate_up = spread_rows([w_gate, w_up])
    full_down = spread_columns(w_down)
    cot_all = gather_rows(cotangent[0])

    stream_all = tokens_all.astype(f32)
    normed = (stream_all * rms_scale(stream_all) * gain_attn).astype(bf16)
    qkv = matmul(normed, full_qkv)
    query_raw = qkv[:, :q_width].reshape(length, heads, HEAD)
    key_raw = qkv[:, q_width : q_width + kv_width].reshape(length, kv_heads, HEAD)
    values = qkv[:, q_width + kv_width :].astype(bf16).reshape(length, kv_heads, HEAD)
    query_scale, key_scale = rms_scale(query_raw), rms_scale(key_raw)
    queries = turn(query_raw * query_scale * gain_query, cos_table, sin_table).astype(bf16)
    keys = turn(key_raw * key_scale * gain_key, cos_table, sin_table).astype(bf16)
    grouped = queries.reshape(length, kv_heads, GROUP, HEAD)
    scores = (
        jnp.einsum("qkgd,skd->kgqs", grouped, keys, preferred_element_type=f32) * score_scale
    )
    scores = jnp.where(allowed, scores, masked_score)
    top = jnp.max(scores, axis=-1, keepdims=True)
    shifted = jnp.exp(scores - top)
    denominator = jnp.sum(shifted, axis=-1, keepdims=True)
    log_total = top + jnp.log(denominator)
    probs = (shifted / denominator).astype(bf16)
    attended = jnp.einsum("kgqs,skd->qkgd", probs, values, preferred_element_type=f32)
    attended = attended.reshape(length, q_width).astype(bf16)
    stream = tokens[0].astype(f32)
    middle = stream + scatter_rows(matmul(attended, full_out).astype(bf16))

    mlp_scale = rms_scale(middle)
    normed_mlp = gather_rows((middle * mlp_scale * gain_mlp).astype(bf16))
    gate_up = matmul(normed_mlp, full_gate_up)
    gate, up = gate_up[:, :ff], gate_up[:, ff:]
    sg = 1.0 / (1.0 + jnp.exp(-gate))
    hidden = (gate * sg * up).astype(bf16)
    d_hidden = matmul_nt(cot_all, full_down)
    d_gate = d_hidden * up * sg * (1.0 + gate * (1.0 - sg))
    d_up = d_hidden * gate * sg
    d_gate_up = jnp.concatenate([d_gate.astype(bf16), d_up.astype(bf16)], axis=1)
    d_normed_mlp = scatter_rows(matmul_nt(d_gate_up, full_gate_up).astype(bf16))
    output = (middle + scatter_rows(matmul(hidden, full_down).astype(bf16))).astype(bf16)
    grad_down = reduce_column_grads(matmul_tn(hidden, cot_all).astype(bf16))
    grad_gate_up = reduce_row_grads(matmul_tn(normed_mlp, d_gate_up).astype(bf16))
    d_middle, mlp_gain_rows = norm_back(middle, mlp_scale, gain_mlp, d_normed_mlp)
    d_middle = cotangent[0].astype(f32) + d_middle

    d_branch = gather_rows(d_middle.astype(bf16))
    grad_out = reduce_column_grads(matmul_tn(attended, d_branch).astype(bf16))
    d_attended = matmul_nt(d_branch, full_out).astype(bf16).reshape(length, kv_heads, GROUP, HEAD)
    scores = (
        jnp.einsum("qkgd,skd->kgqs", grouped, keys, preferred_element_type=f32) * score_scale
    )
    again = jnp.where(
        allowed, jnp.exp(jnp.where(allowed, scores, masked_score) - log_total), 0.0
    )
    d_probs = jnp.einsum("qkgd,skd->kgqs", d_attended, values, preferred_element_type=f32)
    row_dots = jnp.sum(again * d_probs, axis=-1, keepdims=True)
    d_scores = (again * (d_probs - row_dots)).astype(bf16)
    probs_again = again.astype(bf16)
    d_queries = (
        jnp.einsum("kgqs,skd->qkgd", d_scores, keys, preferred_element_type=f32) * score_scale
    ).reshape(length, heads, HEAD)
    d_keys = (
        jnp.einsum("kgqs,qkgd->skd", d_scores, grouped, preferred_element_type=f32) * score_scale
    )
    d_values = jnp.einsum("kgqs,qkgd->skd", probs_again, d_attended, preferred_element_type=f32)
    d_query_raw, query_gain_rows = norm_back(
        query_raw, query_scale, gain_query, turn_back(d_queries, cos_table, sin_table)
    )
    d_key_raw, key_gain_rows = norm_back(
        key_raw, key_scale, gain_key, turn_back(d_keys, cos_table, sin_table)
    )
    d_qkv = jnp.concatenate(
        [
            d_query_raw.astype(bf16).reshape(length, q_width),
            d_key_raw.astype(bf16).reshape(length, kv_width),
            d_values.astype(bf16).reshape(length, kv_width),
        ],
        axis=1,
    )
    d_normed = scatter_rows(matmul_nt(d_qkv, full_qkv).astype(bf16))
    grad_qkv = reduce_row_grads(matmul_tn(normed, d_qkv).astype(bf16))
    d_stream, attn_gain_rows = norm_back(stream, rms_scale(stream), gain_attn, d_normed)
    input_grad = d_middle + d_stream

    gain_grads = sum_all(
        jnp.concatenate(
            [
                jnp.sum(attn_gain_rows, axis=0),
                jnp.sum(mlp_gain_rows, axis=0),
                jnp.sum(query_gain_rows, axis=(0, 1)),
                jnp.sum(key_gain_rows, axis=(0, 1)),
            ]
        )
    )
    shares, start = [], 0
    for size in sizes:
        shares.append(rows_of(gain_grads, start + me * size, size))
        start += n * size

    rows = width // n
    return (
        output[None],
        input_grad[None],
        shares[0],
        grad_qkv[:, :, :q_width].reshape(rows, n * q_width),
        grad_qkv[:, :, q_width : q_width + kv_width].reshape(rows, n * kv_width),
        grad_qkv[:, :, q_width + kv_width :].reshape(rows, n * kv_width),
        shares[2],
        shares[3],
        grad_out,
        shares[1],
        grad_gate_up[:, :, :ff].reshape(rows, n * ff),
        grad_gate_up[:, :, ff:].reshape(rows, n * ff),
        grad_down,
    )


def solution(mesh):
    n, replicas = mesh.shape["fsdp"], mesh.shape["dp"]
    split = Mesh(mesh.devices.reshape(n, replicas // 2, 2), ("fsdp", "z", "core"))
    dp = ("z", "core")
    in_specs = (
        P(dp, "fsdp", None),
        P(dp, None),
        P("fsdp"),
        P("fsdp", None),
        P("fsdp", None),
        P("fsdp", None),
        P("fsdp"),
        P("fsdp"),
        P(None, "fsdp"),
        P("fsdp"),
        P("fsdp", None),
        P("fsdp", None),
        P(None, "fsdp"),
        P(dp, "fsdp", None),
    )
    out_specs = (
        P(dp, "fsdp", None),
        P(dp, "fsdp", None),
        P("fsdp"),
        P("fsdp", None),
        P("fsdp", None),
        P("fsdp", None),
        P("fsdp"),
        P("fsdp"),
        P(None, "fsdp"),
        P("fsdp"),
        P("fsdp", None),
        P("fsdp", None),
        P(None, "fsdp"),
    )
    return jax.shard_map(
        on_device, mesh=split, in_specs=in_specs, out_specs=out_specs, check_vma=False
    )
```

time: 2730 us -> 1360 us (0.50)
  waiting for transfers between devices: 2300 us -> 478 us
  local copies, waits for them, and re-layouts: 35.1 us -> 310 us
  starting transfers between devices: 1.51 us -> 269 us
  matrix products: 247 us -> 165 us
  other arithmetic: 70.5 us -> 124 us
  blocking collectives: 51.6 us -> 0 us
    reduce_scatter x8 -> x0, waiting for transfers between devices: 943 us -> none  [the longest x1 225 us: on_device(): lax.psum_scatter(grad_gate_full.astype(jnp.bfloat16), 'fsdp', scatter_dim...]
    all_gather x9 -> x0, waiting for transfers between devices: 913 us -> none  [the longest x1 223 us: on_device(): lax.all_gather(w_up, 'fsdp', axis=0, tiled=True)]
    ppermute x0 -> x132, waiting for transfers between devices: none -> 478 us  [the longest x84 227 us: swap(): lax.ppermute(value, axis, [(j, j ^ k) for j in range(lax.axis_size(axis))])]
    psum x1 -> x0, waiting for transfers between devices: 440 us -> none  [on_device(): lax.psum(attn_shards[0].astype(jnp.bfloat16), 'dp').astype(jnp.float32)]
    ppermute x0 -> x132, starting transfers between devices: none -> 269 us  [the longest x84 142 us: swap(): lax.ppermute(value, axis, [(j, j ^ k) for j in range(lax.axis_size(axis))])]
    dynamic_update_slice x0 -> x60, local copies, waits for them, and re-layouts: none -> 104 us  [the longest x6 41.1 us: spread_columns(): out = lax.dynamic_update_slice(out, got, (core * half, base))]
    dot_general x27 -> x18, matrix products: 247 us -> 165 us  [the longest x4 47 us: matmul_nt(): lax.dot_general(first, second, (((1,), (1,)), ((), ())), preferred_elemen...]
    slice x2 -> x26, local copies, waits for them, and re-layouts: 0.01 us -> 73 us  [the longest x2 31 us: on_device(): grad_gate_up[:, :, ff:].reshape(rows, n * ff)]
  transfers between devices with their start and end apart: 18 -> 132, of which waited for: 18 -> 43; matrix products, arithmetic and copies ran while one was open for 8% -> 33% of each run, Pallas kernels for 0% -> 0%
where the time goes in v1:
time: 1360 us; the launch traced here: 1350 us
  waiting for transfers between devices  478 us (35%)
  local copies, waits for them, and re-layouts  310 us (23%)
  starting transfers between devices  269 us (20%)
  matrix products  165 us (12%)
  other arithmetic  124 us (9%)
    ppermute x84, waiting for transfers between devices, swap(): lax.ppermute(value, axis, [(j, j ^ k) for j in range(lax.axis_size(axis))])  227 us
    ppermute x84, starting transfers between devices, swap(): lax.ppermute(value, axis, [(j, j ^ k) for j in range(lax.axis_size(axis))])  142 us
    ppermute x12, waiting for transfers between devices, line_scatter(): up = lax.ppermute(up_send.astype(bf16), 'z', [(j, j + 1) for j in range(s)])  125 us
    ppermute x12, waiting for transfers between devices, line_gather(): lax.ppermute(downs[-1], 'z', [(j, j - 1) for j in range(1, nz - s + 1)])  121 us
    ppermute x12, starting transfers between devices, line_scatter(): up = lax.ppermute(up_send.astype(bf16), 'z', [(j, j + 1) for j in range(s)])  69.1 us
    unnamed x198, local copies, waits for them, and re-layouts  54.2 us
    dot_general x4, matrix products, matmul_nt(): lax.dot_general(first, second, (((1,), (1,)), ((), ())), preferred_elemen...  47 us
    dynamic_update_slice x6, local copies, waits for them, and re-layouts, spread_columns(): out = lax.dynamic_update_slice(out, got, (core * half, base))  41.1 us
  transfers between devices with their start and end apart: 132, of which 43 were waited for; matrix products, arithmetic and copies ran while one was open for 33% of the time, Pallas kernels for 0%

profile of v1, /device:TPU:0, one launch (start us, length us, event | category | flops | bytes accessed | tf_op | source)
XLA Modules:
  0.0 1348.7 jit_solution(1980170724905475832)
XLA Ops:
  70.5 37.5 %collective-permute-done.17 = bf16[256,512]{1,0:T(8,128)(2,1)S(1)} collective-permute-done((bf16[256,512]{1,0:T(8,128)(2,1)}, bf16[256,512]{1,0:T(8,128)(2,1)S(1)}, u32[]{:S(2)}, u32[]{:S(2)}) %collective-permute-start.17) | collective-permute-done | bytes 262176 | tf_op jit(solution)/shard_map/ppermute | solution.py:48
  126.2 7.9 collective-permute-done.1
  175.6 31.5 %collective-permute-done.3 = bf16[128,2048]{1,0:T(8,128)(2,1)S(1)} collective-permute-done((bf16[128,2048]{1,0:T(8,128)(2,1)S(1)}, bf16[128,2048]{1,0:T(8,128)(2,1)S(1)}, u32[]{:S(2)}, u32[]{:S(2)}) %collective-permute-start.3) | collective-permute-done | bytes 524320 | tf_op jit(solution)/shard_map/ppermute | solution.py:48
  232.5 7.8 fusion.90
  240.4 8.1 fusion.3
  267.5 10.0 dynamic_update_slice.282
  283.1 40.5 %collective-permute-done.19 = bf16[128,2048]{1,0:T(8,128)(2,1)} collective-permute-done((bf16[128,2048]{1,0:T(8,128)(2,1)}, bf16[128,2048]{1,0:T(8,128)(2,1)}, u32[]{:S(2)}, u32[]{:S(2)}) %collective-permute-start.19) | collective-permute-done | bytes 524320 | tf_op jit(solution)/shard_map/ppermute | solution.py:48
  331.5 8.0 dynamic_update_slice.283
  339.5 9.3 dynamic_update_slice.284
  348.8 8.0 dynamic_update_slice.285
  356.8 8.6 dynamic_update_slice.286
  366.6 7.8 dynamic_update_slice.287
  384.1 23.0 %collective-permute-done.24 = bf16[256,2048]{1,0:T(8,128)(2,1)S(1)} collective-permute-done((bf16[256,2048]{1,0:T(8,128)(2,1)S(1)}, bf16[256,2048]{1,0:T(8,128)(2,1)S(1)}, u32[]{:S(2)}, u32[]{:S(2)}) %collective-permute-start.24) | collective-permute-done | bytes 1048608 | tf_op jit(solution)/shard_map/ppermute | solution.py:48
  409.6 10.8 collective-permute-done.26
  423.2 15.5 %fusion.91 = f32[1024,3072]{1,0:T(8,128)} fusion(bf16[1024,2048]{1,0:T(8,128)(2,1)S(1)} %maximum_dynamic-update-slice_fusion.3, bf16[2048,3072]{1,0:T(8,128)(2,1)S(1)} %constant_dynamic-update-slice_fusion.6), kind=kOutput, calls=%fused_computation.354 | convolution fusion | flops 12884901888 | bytes 29360128 | tf_op jit(solution)/shard_map/dot_general | solution.py:24
  438.7 16.4 %multiply_convert_fusion.1 = (bf16[1024,1536]{1,0:T(8,128)(2,1)S(1)}, bf16[1024,1536]{1,0:T(8,128)(2,1)}, bf16[1024,1536]{1,0:T(8,128)(2,1)}) fusion(f32[1024,3072]{1,0:T(8,128)} %fusion.91, bf16[1024,2048]{1,0:T(8,128)(2,1)} %maximum_dynamic-update-slice_fusion.4, bf16[1536,2048]{1,0:T(8,128)(2,1)} %dynamic_update_slice.287), kind=kOutput, calls=%fused_computation.32 | convolution fusion | flops 6467616768 | bytes 32505856 | tf_op jit(solution)/shard_map/dot_general | solution.py:32
  456.8 18.6 %fusion.16 = bf16[1024,2048]{1,0:T(8,128)(2,1)} fusion(bf16[2048,3072]{1,0:T(8,128)(2,1)} %copy-done.12, bf16[1024,1536]{1,0:T(8,128)(2,1)} %get-tuple-element.56, bf16[1024,1536]{1,0:T(8,128)(2,1)S(1)} %get-tuple-element.55), kind=kOutput, calls=%fused_computation.48 | convolution fusion | flops 12899581952 | bytes 23068672 | tf_op jit(solution)/shard_map/dot_general | solution.py:32
  480.8 8.8 convolution_convert_fusion.2
  509.6 18.9 %convolution_convert_fusion = bf16[2048,3072]{1,0:T(8,128)(2,1)} fusion(bf16[1024,2048]{1,0:T(8,128)(2,1)S(1)} %copy-done.28, bf16[1024,1536]{1,0:T(8,128)(2,1)} %get-tuple-element.56, bf16[1024,1536]{1,0:T(8,128)(2,1)} %copy-done.89), kind=kOutput, calls=%fused_computation.13 | convolution fusion | flops 12903776256 | bytes 23068672 | tf_op jit(solution)/shard_map/dot_general | solution.py:28
  528.4 11.4 constant_dynamic-slice_fusion.12
  559.3 9.7 convolution_convert_fusion.1
  569.1 13.4 collective-permute-done.52
  585.6 8.4 collective-permute-done.54
  600.0 12.2 fusion
  612.1 12.3 fusion.2
  635.0 10.3 fusion.47
  660.1 9.1 convolution_convert_fusion.4
  697.5 25.9 %collective-permute-done.99 = bf16[4,64,3072]{2,1,0:T(8,128)(2,1)S(1)} collective-permute-done((bf16[4,64,3072]{2,1,0:T(8,128)(2,1)S(1)}, bf16[4,64,3072]{2,1,0:T(8,128)(2,1)S(1)}, u32[]{:S(2)}, u32[]{:S(2)}) %collective-permute-start.99) | collective-permute-done | bytes 1572896 | tf_op jit(solution)/shard_map/ppermute | solution.py:153
  728.7 11.6 collective-permute-done.116
  745.0 34.1 %collective-permute-done.82 = bf16[64,2048]{1,0:T(8,128)(2,1)S(1)} collective-permute-done((bf16[64,2048]{1,0:T(8,128)(2,1)S(1)}, bf16[64,2048]{1,0:T(8,128)(2,1)S(1)}, u32[]{:S(2)}, u32[]{:S(2)}) %collective-permute-start.82) | collective-permute-done | bytes 262176 | tf_op jit(solution)/shard_map/ppermute | solution.py:153
  791.1 15.2 %collective-permute-done.83 = bf16[64,2048]{1,0:T(8,128)(2,1)S(1)} collective-permute-done((bf16[64,2048]{1,0:T(8,128)(2,1)S(1)}, bf16[64,2048]{1,0:T(8,128)(2,1)S(1)}, u32[]{:S(2)}, u32[]{:S(2)}) %collective-permute-start.83) | collective-permute-done | bytes 262176 | tf_op jit(solution)/shard_map/ppermute | solution.py:153
  821.8 16.7 %collective-permute-start.101 = (bf16[4,64,3072]{2,1,0:T(8,128)(2,1)S(1)}, bf16[4,64,3072]{2,1,0:T(8,128)(2,1)S(1)}, u32[]{:S(2)}, u32[]{:S(2)}) collective-permute-start(bf16[4,64,3072]{2,1,0:T(8,128)(2,1)S(1)} %get-tuple-element.68), channel_id=1, source_target_pairs={{0,2},{2,4},{4,6},{1,3},{3,5},{5,7},{8,10},{10,12},{12,14},{9,11},... | collective-permute-start | bytes 4718600 | tf_op jit(solution)/shard_map/ppermute | solution.py:153
  846.1 12.7 collective-permute-start.65
  860.2 13.0 collective-permute-done.101
  878.0 21.6 %collective-permute-done.65 = bf16[4,64,1024]{2,1,0:T(8,128)(2,1)S(1)} collective-permute-done((bf16[4,64,1024]{2,1,0:T(8,128)(2,1)S(1)}, bf16[4,64,1024]{2,1,0:T(8,128)(2,1)S(1)}, u32[]{:S(2)}, u32[]{:S(2)}) %collective-permute-start.65) | collective-permute-done | bytes 524320 | tf_op jit(solution)/shard_map/ppermute | solution.py:153
  953.1 22.4 %collective-permute-done.109 = bf16[64,4,3072]{2,0,1:T(8,128)(2,1)S(1)} collective-permute-done((bf16[64,4,3072]{2,0,1:T(8,128)(2,1)S(1)}, bf16[64,4,3072]{2,0,1:T(8,128)(2,1)S(1)}, u32[]{:S(2)}, u32[]{:S(2)}) %collective-permute-start.109) | collective-permute-done | bytes 1572896 | tf_op jit(solution)/shard_map/ppermute | solution.py:166
  991.2 29.3 %collective-permute-done.93 = bf16[4,64,512]{2,1,0:T(8,128)(2,1)S(1)} collective-permute-done((bf16[4,64,512]{2,1,0:T(8,128)(2,1)S(1)}, bf16[4,64,512]{2,1,0:T(8,128)(2,1)S(1)}, u32[]{:S(2)}, u32[]{:S(2)}) %collective-permute-start.93) | collective-permute-done | bytes 262176 | tf_op jit(solution)/shard_map/ppermute | solution.py:166
  1020.4 15.2 %collective-permute-start.125 = (bf16[4,192,512]{2,1,0:T(8,128)(2,1)S(1)}, bf16[4,192,512]{2,1,0:T(8,128)(2,1)S(1)}, u32[]{:S(2)}, u32[]{:S(2)}) collective-permute-start(bf16[4,192,512]{2,1,0:T(8,128)(2,1)S(1)} %bitcast_dynamic-update-slice_fusion.20), channel_id=1, source_target_pairs={{0,2},{2,4},{4,6},{1,3},{3,5},{5,7},{8,10},{10,12},{12,14},{9,11},... | collective-permute-start | bytes 2359304 | tf_op jit(solution)/shard_map/ppermute | solution.py:165
  1038.7 19.0 %collective-permute-done.94 = bf16[4,64,512]{2,1,0:T(8,128)(2,1)S(1)} collective-permute-done((bf16[4,64,512]{2,1,0:T(8,128)(2,1)S(1)}, bf16[4,64,512]{2,1,0:T(8,128)(2,1)S(1)}, u32[]{:S(2)}, u32[]{:S(2)}) %collective-permute-start.94) | collective-permute-done | bytes 262176 | tf_op jit(solution)/shard_map/ppermute | solution.py:166
  1079.7 40.4 %collective-permute-done.75 = bf16[64,4,1024]{2,0,1:T(8,128)(2,1)S(1)} collective-permute-done((bf16[64,4,1024]{2,0,1:T(8,128)(2,1)S(1)}, bf16[64,4,1024]{2,0,1:T(8,128)(2,1)S(1)}, u32[]{:S(2)}, u32[]{:S(2)}) %collective-permute-start.75) | collective-permute-done | bytes 524320 | tf_op jit(solution)/shard_map/ppermute | solution.py:166
  1144.8 35.0 %collective-permute-start.62 = (f32[4352]{0:T(1024)S(1)}, f32[4352]{0:T(1024)S(1)}, u32[]{:S(2)}, u32[]{:S(2)}) collective-permute-start(f32[4352]{0:T(1024)S(1)} %add.742), channel_id=1, source_target_pairs={{0,2},{2,0},{4,6},{6,4},{1,3},{3,1},{5,7},{7,5},{8,10},{10,8},{12,... | collective-permute-start | bytes 52232 | tf_op jit(solution)/shard_map/ppermute | solution.py:48
  1183.4 29.3 %collective-permute-start.63 = (f32[4352]{0:T(1024)S(1)}, f32[4352]{0:T(1024)S(1)}, u32[]{:S(2)}, u32[]{:S(2)}) collective-permute-start(f32[4352]{0:T(1024)S(1)} %add.743), channel_id=1, source_target_pairs={{0,4},{2,6},{4,0},{6,2},{1,5},{3,7},{5,1},{7,3},{8,12},{10,14},{12... | collective-permute-start | bytes 52232 | tf_op jit(solution)/shard_map/ppermute | solution.py:48
  1270.9 8.8 copy.167
  1279.7 18.4 %fusion.80 = (f32[512,4,1536]{2,0,1:T(8,128)}, f32[512,4,1536]{2,0,1:T(8,128)}) fusion(f32[512,4,3072]{2,0,1:T(8,128)} %bitcast.380), kind=kLoop, calls=%fused_computation.343 | loop fusion | bytes 50331648 | tf_op jit(solution)/shard_map/slice | solution.py:405
  1298.1 12.6 copy.168
  1310.7 12.6 copy.177
  1323.3 12.6 copy.169
  1335.9 12.6 copy.178
  (682 shorter events, 542.3 us)
Async XLA Ops:
  3.5 52.6 %collective-permute-start.4 = (bf16[1,1088]{1,0:T(2,128)(2,1)S(1)}, bf16[1,1088]{1,0:T(2,128)(2,1)S(1)}, u32[]{:S(2)}, u32[]{:S(2)}) collective-permute-start(bf16[1,1088]{1,0:T(2,128)(2,1)S(1)} %broadcast_in_dim.185), channel_id=1, source_target_pairs={{0,8},{8,0},{16,24},{24,16},{1,9},{9,1},{17,25},{25,17},{2,10},{10... | collective-permute-start | bytes 6536 | tf_op jit(solution)/shard_map/ppermute | solution.py:48
  6.4 50.3 %collective-permute-start.5 = (bf16[1,1088]{1,0:T(2,128)(2,1)S(1)}, bf16[1,1088]{1,0:T(2,128)(2,1)}, u32[]{:S(2)}, u32[]{:S(2)}) collective-permute-start(bf16[1,1088]{1,0:T(2,128)(2,1)S(1)} %broadcast_in_dim.185), channel_id=1, source_target_pairs={{0,16},{8,24},{16,0},{24,8},{1,17},{9,25},{17,1},{25,9},{2,18},{10... | collective-permute-start | bytes 6536 | tf_op jit(solution)/shard_map/ppermute | solution.py:48
  7.9 48.8 %collective-permute-start.6 = (bf16[1,1088]{1,0:T(2,128)(2,1)S(1)}, bf16[1,1088]{1,0:T(2,128)(2,1)}, u32[]{:S(2)}, u32[]{:S(2)}) collective-permute-start(bf16[1,1088]{1,0:T(2,128)(2,1)S(1)} %broadcast_in_dim.185), channel_id=1, source_target_pairs={{0,24},{8,16},{16,8},{24,0},{1,25},{9,17},{17,9},{25,1},{2,26},{10... | collective-permute-start | bytes 6536 | tf_op jit(solution)/shard_map/ppermute | solution.py:48
  10.0 49.7 %collective-permute-start.13 = (bf16[256,512]{1,0:T(8,128)(2,1)}, bf16[256,512]{1,0:T(8,128)(2,1)}, u32[]{:S(2)}, u32[]{:S(2)}) collective-permute-start(bf16[256,512]{1,0:T(8,128)(2,1)} %get-tuple-element.125), channel_id=1, source_target_pairs={{0,8},{8,0},{16,24},{24,16},{1,9},{9,1},{17,25},{25,17},{2,10},{10... | collective-permute-start | bytes 786440 | tf_op jit(solution)/shard_map/ppermute | solution.py:48
  11.9 48.3 %collective-permute-start.15 = (bf16[256,512]{1,0:T(8,128)(2,1)}, bf16[256,512]{1,0:T(8,128)(2,1)}, u32[]{:S(2)}, u32[]{:S(2)}) collective-permute-start(bf16[256,512]{1,0:T(8,128)(2,1)} %get-tuple-element.126), channel_id=1, source_target_pairs={{0,16},{8,24},{16,0},{24,8},{1,17},{9,25},{17,1},{25,9},{2,18},{10... | collective-permute-start | bytes 786440 | tf_op jit(solution)/shard_map/ppermute | solution.py:48
  56.1 54.9 %collective-permute-start.7 = (bf16[256,1024]{1,0:T(8,128)(2,1)}, bf16[256,1024]{1,0:T(8,128)(2,1)}, u32[]{:S(2)}, u32[]{:S(2)}) collective-permute-start(bf16[256,1024]{1,0:T(8,128)(2,1)} %pad_maximum_fusion.20), channel_id=1, source_target_pairs={{0,8},{8,0},{16,24},{24,16},{1,9},{9,1},{17,25},{25,17},{2,10},{10... | collective-permute-start | bytes 1572872 | tf_op jit(solution)/shard_map/ppermute | solution.py:48
  56.7 54.3 %collective-permute-start.9 = (bf16[256,1024]{1,0:T(8,128)(2,1)}, bf16[256,1024]{1,0:T(8,128)(2,1)}, u32[]{:S(2)}, u32[]{:S(2)}) collective-permute-start(bf16[256,1024]{1,0:T(8,128)(2,1)} %pad_maximum_fusion.21), channel_id=1, source_target_pairs={{0,16},{8,24},{16,0},{24,8},{1,17},{9,25},{17,1},{25,9},{2,18},{10... | collective-permute-start | bytes 1572872 | tf_op jit(solution)/shard_map/ppermute | solution.py:48
  56.8 54.8 %collective-permute-start.11 = (bf16[256,1024]{1,0:T(8,128)(2,1)S(1)}, bf16[256,1024]{1,0:T(8,128)(2,1)}, u32[]{:S(2)}, u32[]{:S(2)}) collective-permute-start(bf16[256,1024]{1,0:T(8,128)(2,1)S(1)} %pad_maximum_fusion.22), channel_id=1, source_target_pairs={{0,24},{8,16},{16,8},{24,0},{1,25},{9,17},{17,9},{25,1},{2,26},{10... | collective-permute-start | bytes 1572872 | tf_op jit(solution)/shard_map/ppermute | solution.py:48
  59.7 61.2 %collective-permute-start = (bf16[256,2048]{1,0:T(8,128)(2,1)S(1)}, bf16[256,2048]{1,0:T(8,128)(2,1)}, u32[]{:S(2)}, u32[]{:S(2)}) collective-permute-start(bf16[256,2048]{1,0:T(8,128)(2,1)S(1)} %bitcast.394), channel_id=1, source_target_pairs={{0,8},{8,0},{16,24},{24,16},{1,9},{9,1},{17,25},{25,17},{2,10},{10... | collective-permute-start | bytes 3145736 | tf_op jit(solution)/shard_map/ppermute | solution.py:48
  60.2 47.7 %collective-permute-start.17 = (bf16[256,512]{1,0:T(8,128)(2,1)}, bf16[256,512]{1,0:T(8,128)(2,1)S(1)}, u32[]{:S(2)}, u32[]{:S(2)}) collective-permute-start(bf16[256,512]{1,0:T(8,128)(2,1)} %get-tuple-element.124), channel_id=1, source_target_pairs={{0,24},{8,16},{16,8},{24,0},{1,25},{9,17},{17,9},{25,1},{2,26},{10... | collective-permute-start | bytes 786440 | tf_op jit(solution)/shard_map/ppermute | solution.py:48
  119.5 49.6 %collective-permute-start.43 = (bf16[256,2048]{1,0:T(8,128)(2,1)S(1)}, bf16[256,2048]{1,0:T(8,128)(2,1)}, u32[]{:S(2)}, u32[]{:S(2)}) collective-permute-start(bf16[256,2048]{1,0:T(8,128)(2,1)S(1)} %bitcast.414), channel_id=1, source_target_pairs={{0,8},{8,0},{16,24},{24,16},{1,9},{9,1},{17,25},{25,17},{2,10},{10... | collective-permute-start | bytes 3145736 | tf_op jit(solution)/shard_map/ppermute | solution.py:48
  158.3 167.8 %collective-permute-start.27 = (bf16[256,3072]{1,0:T(8,128)(2,1)}, bf16[256,3072]{1,0:T(8,128)(2,1)}, u32[]{:S(2)}, u32[]{:S(2)}) collective-permute-start(bf16[256,3072]{1,0:T(8,128)(2,1)} %pad_maximum_fusion.7), channel_id=1, source_target_pairs={{0,8},{8,0},{16,24},{24,16},{1,9},{9,1},{17,25},{25,17},{2,10},{10... | collective-permute-start | bytes 4718600 | tf_op jit(solution)/shard_map/ppermute | solution.py:48
  167.0 96.6 %collective-permute-start.33 = (bf16[768,512]{1,0:T(8,128)(2,1)}, bf16[768,512]{1,0:T(8,128)(2,1)}, u32[]{:S(2)}, u32[]{:S(2)}) collective-permute-start(bf16[768,512]{1,0:T(8,128)(2,1)} %get-tuple-element.73), channel_id=1, source_target_pairs={{0,8},{8,0},{16,24},{24,16},{1,9},{9,1},{17,25},{25,17},{2,10},{10... | collective-permute-start | bytes 2359304 | tf_op jit(solution)/shard_map/ppermute | solution.py:48
  169.1 94.6 %collective-permute-start.35 = (bf16[768,512]{1,0:T(8,128)(2,1)}, bf16[768,512]{1,0:T(8,128)(2,1)}, u32[]{:S(2)}, u32[]{:S(2)}) collective-permute-start(bf16[768,512]{1,0:T(8,128)(2,1)} %get-tuple-element.74), channel_id=1, source_target_pairs={{0,16},{8,24},{16,0},{24,8},{1,17},{9,25},{17,1},{25,9},{2,18},{10... | collective-permute-start | bytes 2359304 | tf_op jit(solution)/shard_map/ppermute | solution.py:48
  207.1 58.6 %collective-permute-start.37 = (bf16[768,512]{1,0:T(8,128)(2,1)}, bf16[768,512]{1,0:T(8,128)(2,1)}, u32[]{:S(2)}, u32[]{:S(2)}) collective-permute-start(bf16[768,512]{1,0:T(8,128)(2,1)} %get-tuple-element.72), channel_id=1, source_target_pairs={{0,24},{8,16},{16,8},{24,0},{1,25},{9,17},{17,9},{25,1},{2,26},{10... | collective-permute-start | bytes 2359304 | tf_op jit(solution)/shard_map/ppermute | solution.py:48
  209.0 70.9 %collective-permute-start.46 = (bf16[128,2048]{1,0:T(8,128)(2,1)}, bf16[128,2048]{1,0:T(8,128)(2,1)}, u32[]{:S(2)}, u32[]{:S(2)}) collective-permute-start(bf16[128,2048]{1,0:T(8,128)(2,1)} %slice.245), channel_id=1, source_target_pairs={{0,8},{8,0},{16,24},{24,16},{1,9},{9,1},{17,25},{25,17},{2,10},{10... | collective-permute-start | bytes 1572872 | tf_op jit(solution)/shard_map/ppermute | solution.py:48
  263.7 59.9 %collective-permute-start.19 = (bf16[128,2048]{1,0:T(8,128)(2,1)}, bf16[128,2048]{1,0:T(8,128)(2,1)}, u32[]{:S(2)}, u32[]{:S(2)}) collective-permute-start(bf16[128,2048]{1,0:T(8,128)(2,1)} %get-tuple-element.104), channel_id=1, source_target_pairs={{0,16},{8,24},{16,0},{24,8},{1,17},{9,25},{17,1},{25,9},{2,18},{10... | collective-permute-start | bytes 1572872 | tf_op jit(solution)/shard_map/ppermute | solution.py:48
  265.7 57.9 %collective-permute-start.21 = (bf16[128,2048]{1,0:T(8,128)(2,1)}, bf16[128,2048]{1,0:T(8,128)(2,1)}, u32[]{:S(2)}, u32[]{:S(2)}) collective-permute-start(bf16[128,2048]{1,0:T(8,128)(2,1)} %get-tuple-element.106), channel_id=1, source_target_pairs={{0,8},{8,0},{16,24},{24,16},{1,9},{9,1},{17,25},{25,17},{2,10},{10... | collective-permute-start | bytes 1572872 | tf_op jit(solution)/shard_map/ppermute | solution.py:48
  279.8 85.6 %collective-permute-start.29 = (bf16[256,3072]{1,0:T(8,128)(2,1)S(1)}, bf16[256,3072]{1,0:T(8,128)(2,1)S(1)}, u32[]{:S(2)}, u32[]{:S(2)}) collective-permute-start(bf16[256,3072]{1,0:T(8,128)(2,1)S(1)} %copy-done.53), channel_id=1, source_target_pairs={{0,16},{8,24},{16,0},{24,8},{1,17},{9,25},{17,1},{25,9},{2,18},{10... | collective-permute-start | bytes 4718600 | tf_op jit(solution)/shard_map/ppermute | solution.py:48
  279.9 86.2 %collective-permute-start.31 = (bf16[256,3072]{1,0:T(8,128)(2,1)S(1)}, bf16[256,3072]{1,0:T(8,128)(2,1)S(1)}, u32[]{:S(2)}, u32[]{:S(2)}) collective-permute-start(bf16[256,3072]{1,0:T(8,128)(2,1)S(1)} %copy-done.52), channel_id=1, source_target_pairs={{0,24},{8,16},{16,8},{24,0},{1,25},{9,17},{17,9},{25,1},{2,26},{10... | collective-permute-start | bytes 4718600 | tf_op jit(solution)/shard_map/ppermute | solution.py:48
  326.3 51.3 %collective-permute-start.22 = (bf16[256,2048]{1,0:T(8,128)(2,1)S(1)}, bf16[256,2048]{1,0:T(8,128)(2,1)S(1)}, u32[]{:S(2)}, u32[]{:S(2)}) collective-permute-start(bf16[256,2048]{1,0:T(8,128)(2,1)S(1)} %pad_maximum_fusion.11), channel_id=1, source_target_pairs={{0,16},{8,24},{16,0},{24,8},{1,17},{9,25},{17,1},{25,9},{2,18},{10... | collective-permute-start | bytes 3145736 | tf_op jit(solution)/shard_map/ppermute | solution.py:48
  327.2 50.4 %collective-permute-start.20 = (bf16[256,2048]{1,0:T(8,128)(2,1)S(1)}, bf16[256,2048]{1,0:T(8,128)(2,1)S(1)}, u32[]{:S(2)}, u32[]{:S(2)}) collective-permute-start(bf16[256,2048]{1,0:T(8,128)(2,1)S(1)} %pad_maximum_fusion.10), channel_id=1, source_target_pairs={{0,8},{8,0},{16,24},{24,16},{1,9},{9,1},{17,25},{25,17},{2,10},{10... | collective-permute-start | bytes 3145736 | tf_op jit(solution)/shard_map/ppermute | solution.py:48
  495.1 48.4 %collective-permute-start.50 = (bf16[256,2048]{1,0:T(8,128)(2,1)}, bf16[256,2048]{1,0:T(8,128)(2,1)S(1)}, u32[]{:S(2)}, u32[]{:S(2)}) collective-permute-start(bf16[256,2048]{1,0:T(8,128)(2,1)} %pad_maximum_fusion.15), channel_id=1, source_target_pairs={{0,16},{8,24},{16,0},{24,8},{1,17},{9,25},{17,1},{25,9},{2,18},{10... | collective-permute-start | bytes 3145736 | tf_op jit(solution)/shard_map/ppermute | solution.py:48
  496.4 47.1 %collective-permute-start.48 = (bf16[256,2048]{1,0:T(8,128)(2,1)}, bf16[256,2048]{1,0:T(8,128)(2,1)}, u32[]{:S(2)}, u32[]{:S(2)}) collective-permute-start(bf16[256,2048]{1,0:T(8,128)(2,1)} %pad_maximum_fusion.14), channel_id=1, source_target_pairs={{0,8},{8,0},{16,24},{24,16},{1,9},{9,1},{17,25},{25,17},{2,10},{10... | collective-permute-start | bytes 3145736 | tf_op jit(solution)/shard_map/ppermute | solution.py:48
  543.4 133.0 %collective-permute-start.98 = (bf16[4,4,64,3072]{3,2,0,1:T(8,128)(2,1)S(1)}, bf16[4,4,64,3072]{3,2,0,1:T(8,128)(2,1)}, u32[]{:S(2)}, u32[]{:S(2)}) collective-permute-start(bf16[4,4,64,3072]{3,2,0,1:T(8,128)(2,1)S(1)} %bitcast.407), channel_id=1, source_target_pairs={{0,1},{1,0},{2,3},{3,2},{4,5},{5,4},{6,7},{7,6},{8,9},{9,8},{10,11... | collective-permute-start | bytes 18874376 | tf_op jit(solution)/shard_map/ppermute | solution.py:48
  585.3 86.4 %collective-permute-start.115 = (bf16[768,2048]{1,0:T(8,128)(2,1)}, bf16[768,2048]{1,0:T(8,128)(2,1)}, u32[]{:S(2)}, u32[]{:S(2)}) collective-permute-start(bf16[768,2048]{1,0:T(8,128)(2,1)} %constant_dynamic-slice_fusion.9), channel_id=1, source_target_pairs={{0,1},{1,0},{2,3},{3,2},{4,5},{5,4},{6,7},{7,6},{8,9},{9,8},{10,11... | collective-permute-start | bytes 9437192 | tf_op jit(solution)/shard_map/ppermute | solution.py:48
  689.1 51.2 %collective-permute-start.116 = (bf16[192,2048]{1,0:T(8,128)(2,1)S(1)}, bf16[192,2048]{1,0:T(8,128)(2,1)S(1)}, u32[]{:S(2)}, u32[]{:S(2)}) collective-permute-start(bf16[192,2048]{1,0:T(8,128)(2,1)S(1)} %copy-done.58), channel_id=1, source_target_pairs={{0,2},{1,3},{8,10},{9,11},{16,18},{17,19},{24,26},{25,27}} | collective-permute-start | bytes 2359304 | tf_op jit(solution)/shard_map/ppermute | solution.py:153
  692.7 87.1 %collective-permute-start.58 = (bf16[256,2048]{1,0:T(8,128)(2,1)S(1)}, bf16[256,2048]{1,0:T(8,128)(2,1)S(1)}, u32[]{:S(2)}, u32[]{:S(2)}) collective-permute-start(bf16[256,2048]{1,0:T(8,128)(2,1)S(1)} %pad_maximum_fusion.17), channel_id=1, source_target_pairs={{0,16},{8,24},{16,0},{24,8},{1,17},{9,25},{17,1},{25,9},{2,18},{10... | collective-permute-start | bytes 3145736 | tf_op jit(solution)/shard_map/ppermute | solution.py:48
  693.7 90.6 %collective-permute-start.56 = (bf16[256,2048]{1,0:T(8,128)(2,1)S(1)}, bf16[256,2048]{1,0:T(8,128)(2,1)S(1)}, u32[]{:S(2)}, u32[]{:S(2)}) collective-permute-start(bf16[256,2048]{1,0:T(8,128)(2,1)S(1)} %pad_maximum_fusion.16), channel_id=1, source_target_pairs={{0,8},{8,0},{16,24},{24,16},{1,9},{9,1},{17,25},{25,17},{2,10},{10... | collective-permute-start | bytes 3145736 | tf_op jit(solution)/shard_map/ppermute | solution.py:48
  696.6 89.9 %collective-permute-start.102 = (bf16[4,64,3072]{2,1,0:T(8,128)(2,1)S(1)}, bf16[4,64,3072]{2,1,0:T(8,128)(2,1)S(1)}, u32[]{:S(2)}, u32[]{:S(2)}) collective-permute-start(bf16[4,64,3072]{2,1,0:T(8,128)(2,1)S(1)} %get-tuple-element.71), channel_id=1, source_target_pairs={{6,4},{7,5},{14,12},{15,13},{22,20},{23,21},{30,28},{31,29}} | collective-permute-start | bytes 4718600 | tf_op jit(solution)/shard_map/ppermute | solution.py:154
  724.1 64.3 %collective-permute-start.100 = (bf16[4,64,3072]{2,1,0:T(8,128)(2,1)S(1)}, bf16[4,64,3072]{2,1,0:T(8,128)(2,1)S(1)}, u32[]{:S(2)}, u32[]{:S(2)}) collective-permute-start(bf16[4,64,3072]{2,1,0:T(8,128)(2,1)S(1)} %fusion.19), channel_id=1, source_target_pairs={{0,2},{2,4},{1,3},{3,5},{8,10},{10,12},{9,11},{11,13},{16,18},{18,... | collective-permute-start | bytes 4718600 | tf_op jit(solution)/shard_map/ppermute | solution.py:153
  790.6 48.5 %collective-permute-start.64 = (bf16[4,4,64,1024]{3,2,0,1:T(8,128)(2,1)S(1)}, bf16[4,4,64,1024]{3,2,0,1:T(8,128)(2,1)S(1)}, u32[]{:S(2)}, u32[]{:S(2)}) collective-permute-start(bf16[4,4,64,1024]{3,2,0,1:T(8,128)(2,1)S(1)} %bitcast.418), channel_id=1, source_target_pairs={{0,1},{1,0},{2,3},{3,2},{4,5},{5,4},{6,7},{7,6},{8,9},{9,8},{10,11... | collective-permute-start | bytes 6291464 | tf_op jit(solution)/shard_map/ppermute | solution.py:48
  821.8 51.4 %collective-permute-start.101 = (bf16[4,64,3072]{2,1,0:T(8,128)(2,1)S(1)}, bf16[4,64,3072]{2,1,0:T(8,128)(2,1)S(1)}, u32[]{:S(2)}, u32[]{:S(2)}) collective-permute-start(bf16[4,64,3072]{2,1,0:T(8,128)(2,1)S(1)} %get-tuple-element.68), channel_id=1, source_target_pairs={{0,2},{2,4},{4,6},{1,3},{3,5},{5,7},{8,10},{10,12},{12,14},{9,11},... | collective-permute-start | bytes 4718600 | tf_op jit(solution)/shard_map/ppermute | solution.py:153
  841.5 96.8 %collective-permute-start.118 = (bf16[192,2048]{1,0:T(8,128)(2,1)S(1)}, bf16[192,2048]{1,0:T(8,128)(2,1)S(1)}, u32[]{:S(2)}, u32[]{:S(2)}) collective-permute-start(bf16[192,2048]{1,0:T(8,128)(2,1)S(1)} %get-tuple-element.109), channel_id=1, source_target_pairs={{0,2},{2,4},{4,6},{1,3},{3,5},{5,7},{8,10},{10,12},{12,14},{9,11},... | collective-permute-start | bytes 2359304 | tf_op jit(solution)/shard_map/ppermute | solution.py:153
  846.1 53.5 %collective-permute-start.65 = (bf16[4,64,1024]{2,1,0:T(8,128)(2,1)S(1)}, bf16[4,64,1024]{2,1,0:T(8,128)(2,1)S(1)}, u32[]{:S(2)}, u32[]{:S(2)}) collective-permute-start(bf16[4,64,1024]{2,1,0:T(8,128)(2,1)S(1)} %get-tuple-element.117), channel_id=1, source_target_pairs={{0,2},{1,3},{8,10},{9,11},{16,18},{17,19},{24,26},{25,27}} | collective-permute-start | bytes 1572872 | tf_op jit(solution)/shard_map/ppermute | solution.py:153
  859.1 72.9 %collective-permute-start.68 = (bf16[4,64,1024]{2,1,0:T(8,128)(2,1)S(1)}, bf16[4,64,1024]{2,1,0:T(8,128)(2,1)S(1)}, u32[]{:S(2)}, u32[]{:S(2)}) collective-permute-start(bf16[4,64,1024]{2,1,0:T(8,128)(2,1)S(1)} %get-tuple-element.118), channel_id=1, source_target_pairs={{6,4},{7,5},{14,12},{15,13},{22,20},{23,21},{30,28},{31,29}} | collective-permute-start | bytes 1572872 | tf_op jit(solution)/shard_map/ppermute | solution.py:154
  876.3 54.3 %collective-permute-start.89 = (bf16[64,512]{1,0:T(8,128)(2,1)S(1)}, bf16[64,512]{1,0:T(8,128)(2,1)S(1)}, u32[]{:S(2)}, u32[]{:S(2)}) collective-permute-start(bf16[64,512]{1,0:T(8,128)(2,1)S(1)} %get-tuple-element.159), channel_id=1, source_target_pairs={{0,16},{8,24},{16,0},{24,8},{1,17},{9,25},{17,1},{25,9},{2,18},{10... | collective-permute-start | bytes 196616 | tf_op jit(solution)/shard_map/ppermute | solution.py:48
  948.5 109.6 %collective-permute-start.108 = (bf16[64,4,3072]{2,0,1:T(8,128)(2,1)S(1)}, bf16[64,4,3072]{2,0,1:T(8,128)(2,1)S(1)}, u32[]{:S(2)}, u32[]{:S(2)}) collective-permute-start(bf16[64,4,3072]{2,0,1:T(8,128)(2,1)S(1)} %bitcast_dynamic-update-slice_fusion.12), channel_id=1, source_target_pairs={{0,2},{2,4},{4,6},{1,3},{3,5},{5,7},{8,10},{10,12},{12,14},{9,11},... | collective-permute-start | bytes 4718600 | tf_op jit(solution)/shard_map/ppermute | solution.py:165
  975.5 83.3 %collective-permute-start.110 = (bf16[64,4,3072]{2,0,1:T(8,128)(2,1)S(1)}, bf16[64,4,3072]{2,0,1:T(8,128)(2,1)S(1)}, u32[]{:S(2)}, u32[]{:S(2)}) collective-permute-start(bf16[64,4,3072]{2,0,1:T(8,128)(2,1)S(1)} %collective-permute-done.109), channel_id=1, source_target_pairs={{2,0},{4,2},{3,1},{5,3},{10,8},{12,10},{11,9},{13,11},{18,16},{20,... | collective-permute-start | bytes 4718600 | tf_op jit(solution)/shard_map/ppermute | solution.py:166
  976.8 58.8 %collective-permute-start.67 = (bf16[4,64,1024]{2,1,0:T(8,128)(2,1)S(1)}, bf16[4,64,1024]{2,1,0:T(8,128)(2,1)S(1)}, u32[]{:S(2)}, u32[]{:S(2)}) collective-permute-start(bf16[4,64,1024]{2,1,0:T(8,128)(2,1)S(1)} %get-tuple-element.115), channel_id=1, source_target_pairs={{0,2},{2,4},{4,6},{1,3},{3,5},{5,7},{8,10},{10,12},{12,14},{9,11},... | collective-permute-start | bytes 1572872 | tf_op jit(solution)/shard_map/ppermute | solution.py:153
  989.8 47.3 %collective-permute-start.70 = (bf16[4,64,1024]{2,1,0:T(8,128)(2,1)S(1)}, bf16[4,64,1024]{2,1,0:T(8,128)(2,1)S(1)}, u32[]{:S(2)}, u32[]{:S(2)}) collective-permute-start(bf16[4,64,1024]{2,1,0:T(8,128)(2,1)S(1)} %fusion.58), channel_id=1, source_target_pairs={{2,0},{4,2},{6,4},{3,1},{5,3},{7,5},{10,8},{12,10},{14,12},{11,9},... | collective-permute-start | bytes 1572872 | tf_op jit(solution)/shard_map/ppermute | solution.py:154
  1058.0 64.9 %collective-permute-start.112 = (bf16[64,4,3072]{2,0,1:T(8,128)(2,1)S(1)}, bf16[64,4,3072]{2,0,1:T(8,128)(2,1)S(1)}, u32[]{:S(2)}, u32[]{:S(2)}) collective-permute-start(bf16[64,4,3072]{2,0,1:T(8,128)(2,1)S(1)} %collective-permute-done.108), channel_id=1, source_target_pairs={{2,4},{4,6},{3,5},{5,7},{10,12},{12,14},{11,13},{13,15},{18,20},{2... | collective-permute-start | bytes 4718600 | tf_op jit(solution)/shard_map/ppermute | solution.py:165
  1058.8 65.4 %collective-permute-start.111 = (bf16[64,4,3072]{2,0,1:T(8,128)(2,1)S(1)}, bf16[64,4,3072]{2,0,1:T(8,128)(2,1)S(1)}, u32[]{:S(2)}, u32[]{:S(2)}) collective-permute-start(bf16[64,4,3072]{2,0,1:T(8,128)(2,1)S(1)} %collective-permute-done.110), channel_id=1, source_target_pairs={{2,0},{3,1},{10,8},{11,9},{18,16},{19,17},{26,24},{27,25}} | collective-permute-start | bytes 4718600 | tf_op jit(solution)/shard_map/ppermute | solution.py:166
  1060.2 61.4 %collective-permute-start.127 = (bf16[4,192,512]{2,1,0:T(8,128)(2,1)S(1)}, bf16[4,192,512]{2,1,0:T(8,128)(2,1)S(1)}, u32[]{:S(2)}, u32[]{:S(2)}) collective-permute-start(bf16[4,192,512]{2,1,0:T(8,128)(2,1)S(1)} %collective-permute-done.126), channel_id=1, source_target_pairs={{2,0},{4,2},{3,1},{5,3},{10,8},{12,10},{11,9},{13,11},{18,16},{20,... | collective-permute-start | bytes 2359304 | tf_op jit(solution)/shard_map/ppermute | solution.py:166
  1061.5 69.1 %collective-permute-start.129 = (bf16[4,192,512]{2,1,0:T(8,128)(2,1)S(1)}, bf16[4,192,512]{2,1,0:T(8,128)(2,1)S(1)}, u32[]{:S(2)}, u32[]{:S(2)}) collective-permute-start(bf16[4,192,512]{2,1,0:T(8,128)(2,1)S(1)} %collective-permute-done.125), channel_id=1, source_target_pairs={{2,4},{4,6},{3,5},{5,7},{10,12},{12,14},{11,13},{13,15},{18,20},{2... | collective-permute-start | bytes 2359304 | tf_op jit(solution)/shard_map/ppermute | solution.py:165
  1130.2 133.7 %collective-permute-start.114 = (bf16[4,64,4,3072]{3,1,2,0:T(8,128)(2,1)}, bf16[4,64,4,3072]{3,1,2,0:T(8,128)(2,1)}, u32[]{:S(2)}, u32[]{:S(2)}) collective-permute-start(bf16[4,64,4,3072]{3,1,2,0:T(8,128)(2,1)} %bitcast_dynamic-update-slice_fusion), channel_id=1, source_target_pairs={{0,1},{1,0},{2,3},{3,2},{4,5},{5,4},{6,7},{7,6},{8,9},{9,8},{10,11... | collective-permute-start | bytes 18874376 | tf_op jit(solution)/shard_map/ppermute | solution.py:48
  1130.6 49.8 %collective-permute-start.130 = (bf16[4,192,512]{2,1,0:T(8,128)(2,1)S(1)}, bf16[4,192,512]{2,1,0:T(8,128)(2,1)S(1)}, u32[]{:S(2)}, u32[]{:S(2)}) collective-permute-start(bf16[4,192,512]{2,1,0:T(8,128)(2,1)S(1)} %collective-permute-done.129), channel_id=1, source_target_pairs={{4,6},{5,7},{12,14},{13,15},{20,22},{21,23},{28,30},{29,31}} | collective-permute-start | bytes 2359304 | tf_op jit(solution)/shard_map/ppermute | solution.py:165
  1181.5 74.6 %collective-permute-start.131 = (bf16[4,4,192,512]{3,2,0,1:T(8,128)(2,1)S(1)}, bf16[4,4,192,512]{3,2,0,1:T(8,128)(2,1)}, u32[]{:S(2)}, u32[]{:S(2)}) collective-permute-start(bf16[4,4,192,512]{3,2,0,1:T(8,128)(2,1)S(1)} %bitcast_dynamic-update-slice_fusion.7), channel_id=1, source_target_pairs={{0,1},{1,0},{2,3},{3,2},{4,5},{5,4},{6,7},{7,6},{8,9},{9,8},{10,11... | collective-permute-start | bytes 9437192 | tf_op jit(solution)/shard_map/ppermute | solution.py:48
  (181 other events, 3461.3 us)

commit v2 on v1

v2 whole, which is shorter than its diff:
```python
import math

import jax
import jax.numpy as jnp
from jax import lax
from jax.experimental import pallas as pl
from jax.experimental.pallas import tpu as pltpu
from jax.sharding import Mesh
from jax.sharding import PartitionSpec as P

HEADS = 16
KV_HEADS = 8
HEAD = 128
GROUP = HEADS // KV_HEADS

epsilon = 1e-06
rope_base = 1000000.0
masked_score = -1e30
score_scale = 1.0 / math.sqrt(HEAD)

bf16 = jnp.bfloat16
f32 = jnp.float32


def matmul(first, second):
    return jnp.dot(first, second, preferred_element_type=f32)


def matmul_tn(first, second):
    return lax.dot_general(first, second, (((0,), (0,)), ((), ())), preferred_element_type=f32)


def matmul_nt(first, second):
    return lax.dot_general(first, second, (((1,), (1,)), ((), ())), preferred_element_type=f32)


def rms_scale(vector):
    return lax.rsqrt(jnp.mean(vector * vector, axis=-1, keepdims=True) + epsilon)


def norm_back(vector, scale, gain, incoming):
    scaled = gain * incoming
    d_vector = scale * scaled - vector * (scale**3) * jnp.mean(
        vector * scaled, axis=-1, keepdims=True
    )
    return d_vector, incoming * vector * scale


def swap(value, axis, k):
    return lax.ppermute(value, axis, [(j, j ^ k) for j in range(lax.axis_size(axis))])


def core_swap(value):
    return swap(value, "core", 1)


def rows_of(value, start, size):
    return lax.dynamic_slice_in_dim(value, start, size, axis=0)


def fence(*trees):
    leaves, shape = jax.tree.flatten(trees)
    return jax.tree.unflatten(shape, lax.optimization_barrier(leaves))


def gather_begin(shard):
    n = lax.axis_size("fsdp")
    if n == 4:
        return [swap(shard, "fsdp", 1), swap(shard, "fsdp", 2)]
    return [swap(shard, "fsdp", k) for k in range(1, n)]


def gather_end(shard, begun):
    if lax.axis_size("fsdp") != 4:
        return [shard] + begun
    half = shard.shape[0] // 2
    first = swap(begun[0][:half], "fsdp", 2)
    second = swap(begun[1][half:], "fsdp", 1)
    return [shard] + begun + [jnp.concatenate([first, second], axis=0)]


def scatter_begin(far):
    n = lax.axis_size("fsdp")
    if n == 4:
        half = far.shape[0] // 2
        return [swap(far[:half], "fsdp", 1), swap(far[half:], "fsdp", 2)]
    return [swap(far, "fsdp", n - 1)]


def scatter_middle(near, begun):
    n = lax.axis_size("fsdp")
    if n != 4:
        return begun + [swap(block, "fsdp", k + 1) for k, block in enumerate(near)]
    near_x, near_y = near
    first, second = begun
    half = first.shape[0]
    low = (near_x[half:].astype(f32) + second.astype(f32)).astype(bf16)
    top = (near_y[:half].astype(f32) + first.astype(f32)).astype(bf16)
    return [
        swap(jnp.concatenate([near_x[:half], low], axis=0), "fsdp", 1),
        swap(jnp.concatenate([top, near_y[half:]], axis=0), "fsdp", 2),
    ]


def scatter_end(own, got):
    total = own.astype(f32)
    for block in got:
        total = total + block.astype(f32)
    return total


def assemble(shape, pieces, places):
    count = len(pieces)

    def kernel(place_ref, *refs):
        ins, out, hold = refs[:count], refs[count], refs[count + 1]
        sem_in, sem_out = refs[count + 2], refs[count + 3]

        def window(ref, k):
            row = pl.multiple_of(place_ref[2 * k], 16)
            column = pl.multiple_of(place_ref[2 * k + 1], 128)
            rows, columns = ins[k].shape
            return ref.at[pl.ds(row, rows), pl.ds(column, columns)]

        loads = [
            pltpu.make_async_copy(ins[k], window(hold, k), sem_in.at[k]) for k in range(count)
        ]
        stores = [
            pltpu.make_async_copy(window(hold, k), window(out, k), sem_out.at[k])
            for k in range(count)
        ]
        for load in loads:
            load.start()
        for load, store in zip(loads, stores):
            load.wait()
            store.start()
        for store in stores:
            store.wait()

    size = 2 * math.prod(shape)
    return pl.pallas_call(
        kernel,
        out_shape=jax.ShapeDtypeStruct(shape, bf16),
        in_specs=[pl.BlockSpec(memory_space=pltpu.SMEM)]
        + [pl.BlockSpec(memory_space=pl.ANY)] * count,
        out_specs=pl.BlockSpec(memory_space=pl.ANY),
        scratch_shapes=[
            pltpu.VMEM(shape, bf16),
            pltpu.SemaphoreType.DMA((count,)),
            pltpu.SemaphoreType.DMA((count,)),
        ],
        compiler_params=pltpu.CompilerParams(vmem_limit_bytes=size + (4 << 20)),
        cost_estimate=pl.CostEstimate(flops=0, bytes_accessed=2 * size, transcendentals=0),
        name="assemble",
    )(jnp.stack([jnp.int32(v) for place in places for v in place]), *pieces)


def spread_begin(quarter_of):
    n, me = lax.axis_size("fsdp"), lax.axis_index("fsdp")
    mine = 2 * (lax.axis_index("z") % 2) + lax.axis_index("core")
    return [swap(quarter_of(me ^ k, mine), "fsdp", k) for k in range(1, n)]


def spread_pieces(got, along, across, across_along):
    n, me = lax.axis_size("fsdp"), lax.axis_index("fsdp")
    side, core = lax.axis_index("z") % 2, lax.axis_index("core")
    pieces = []
    for k in range(1, n):
        for block, quarter in (
            (got, 2 * side + core),
            (along, 2 * (1 - side) + core),
            (across, 2 * side + 1 - core),
            (across_along, 2 * (1 - side) + 1 - core),
        ):
            pieces.append((me ^ k, quarter, block[k - 1]))
    return pieces


class RowKind:
    def __init__(self, *parts):
        self.parts = parts

    def cut(self, start, size, block):
        n = lax.axis_size("fsdp")
        widths = [part.shape[1] // n for part in self.parts]
        return jnp.concatenate(
            [
                lax.dynamic_slice(part, (start, block * width), (size, width))
                for part, width in zip(self.parts, widths)
            ],
            axis=1,
        )

    def quarter(self, j, q):
        size = self.parts[0].shape[0] // 4
        return self.cut(q * size, size, j)

    def join(self, pieces):
        n, me = lax.axis_size("fsdp"), lax.axis_index("fsdp")
        rows = self.parts[0].shape[0]
        width = sum(part.shape[1] for part in self.parts) // n
        return assemble(
            (n * rows, width),
            [self.cut(0, rows, me)] + [block for _, _, block in pieces],
            [(me * rows, 0)] + [(j * rows + q * (rows // 4), 0) for j, q, _ in pieces],
        )


class ColumnKind:
    def __init__(self, part):
        self.part = part

    def quarter(self, j, q):
        rows = self.part.shape[0] // lax.axis_size("fsdp")
        return rows_of(self.part, j * rows + q * (rows // 4), rows // 4)

    def join(self, pieces):
        n, me = lax.axis_size("fsdp"), lax.axis_index("fsdp")
        rows, width = self.part.shape[0] // n, self.part.shape[1]
        return assemble(
            (rows, n * width),
            [rows_of(self.part, me * rows, rows)] + [block for _, _, block in pieces],
            [(0, me * width)] + [(q * (rows // 4), j * width) for j, q, _ in pieces],
        )


def stack_along(got):
    return swap(got, "z", 1)


class Reduction:
    def __init__(self, grad):
        self.grad = grad
        self.other = None

    def take(self, c):
        n, me = lax.axis_size("fsdp"), lax.axis_index("fsdp")
        rows, width = self.grad.shape[1:]
        return jnp.concatenate(
            [
                lax.dynamic_slice(
                    self.grad, (me ^ k, c * (rows // 2), 0), (1, rows // 2, width)
                )
                for k in range(n)
            ]
        )

    def begin(self):
        core = lax.axis_index("core")
        both = self.take(core).astype(f32) + core_swap(self.take(1 - core)).astype(f32)
        self.half = both.astype(bf16)

    def exchange(self):
        n = lax.axis_size("fsdp")
        self.half = jnp.stack(
            [self.half[0]] + [swap(self.half[k], "fsdp", k) for k in range(1, n)]
        )

    def finish(self, by_rows, start=0, size=None):
        n, me = lax.axis_size("fsdp"), lax.axis_index("fsdp")
        core = lax.axis_index("core")
        if self.other is None:
            self.other = core_swap(self.half)
        rows, width = self.half.shape[1:]
        size = width if size is None else size
        column = start // size

        def kernel(place, mine, other, out):
            @pl.when(pl.program_id(0) == 0)
            def _():
                out[...] = mine[0].astype(f32)

            @pl.when(pl.program_id(0) == 1)
            def _():
                out[...] = other[0].astype(f32)

        def mine_at(w, k, place):
            return (jnp.where(w == 0, k, n - 1), 0, column)

        def other_at(w, k, place):
            return (jnp.where(w == 0, 0, k), 0, column)

        def out_at(w, k, place):
            source = place[0] ^ k
            side = jnp.where(w == 0, place[1], 1 - place[1])
            return (side, source) if by_rows else (source * 2 + side, 0)

        return pl.pallas_call(
            kernel,
            out_shape=jax.ShapeDtypeStruct(
                (2 * rows, n * size) if by_rows else (2 * n * rows, size), f32
            ),
            grid_spec=pltpu.PrefetchScalarGridSpec(
                num_scalar_prefetch=1,
                grid=(2, n),
                in_specs=[
                    pl.BlockSpec((1, rows, size), mine_at),
                    pl.BlockSpec((1, rows, size), other_at),
                ],
                out_specs=pl.BlockSpec((rows, size), out_at),
            ),
            compiler_params=pltpu.CompilerParams(vmem_limit_bytes=32 << 20),
            cost_estimate=pl.CostEstimate(
                flops=0, bytes_accessed=2 * n * rows * size * 40, transcendentals=0
            ),
            name="place",
        )(jnp.stack([me, core]).astype(jnp.int32), self.half, self.other)


def turn(value, cos_table, sin_table):
    half = HEAD // 2
    turned = jnp.concatenate([-value[..., half:], value[..., :half]], axis=-1)
    return value * cos_table + turned * sin_table


def turn_back(value, cos_table, sin_table):
    half = HEAD // 2
    turned = jnp.concatenate(
        [value[..., half:] * sin_table[..., half:], -value[..., :half] * sin_table[..., :half]],
        axis=-1,
    )
    return value * cos_table + turned


def attention_forward(queries, keys, values, allowed):
    length, heads = queries.shape[:2]
    grouped = queries.reshape(length, heads // GROUP, GROUP, HEAD)
    scores = (
        jnp.einsum("qkgd,skd->kgqs", grouped, keys, preferred_element_type=f32) * score_scale
    )
    scores = jnp.where(allowed, scores, masked_score)
    top = jnp.max(scores, axis=-1, keepdims=True)
    shifted = jnp.exp(scores - top)
    denominator = jnp.sum(shifted, axis=-1, keepdims=True)
    log_total = top + jnp.log(denominator)
    probs = (shifted / denominator).astype(bf16)
    attended = jnp.einsum("kgqs,skd->qkgd", probs, values, preferred_element_type=f32)
    return attended.reshape(length, heads * HEAD).astype(bf16), log_total


def attention_backward(queries, keys, values, allowed, log_total, d_attended):
    length, heads = queries.shape[:2]
    grouped = queries.reshape(length, heads // GROUP, GROUP, HEAD)
    d_attended = d_attended.reshape(length, heads // GROUP, GROUP, HEAD)
    scores = (
        jnp.einsum("qkgd,skd->kgqs", grouped, keys, preferred_element_type=f32) * score_scale
    )
    again = jnp.where(
        allowed, jnp.exp(jnp.where(allowed, scores, masked_score) - log_total), 0.0
    )
    d_probs = jnp.einsum("qkgd,skd->kgqs", d_attended, values, preferred_element_type=f32)
    row_dots = jnp.sum(again * d_probs, axis=-1, keepdims=True)
    d_scores = (again * (d_probs - row_dots)).astype(bf16)
    probs_again = again.astype(bf16)
    d_queries = (
        jnp.einsum("kgqs,skd->qkgd", d_scores, keys, preferred_element_type=f32) * score_scale
    ).reshape(length, heads, HEAD)
    d_keys = (
        jnp.einsum("kgqs,qkgd->skd", d_scores, grouped, preferred_element_type=f32) * score_scale
    )
    d_values = jnp.einsum("kgqs,qkgd->skd", probs_again, d_attended, preferred_element_type=f32)
    return d_queries, d_keys, d_values


def on_device(
    tokens,
    segments,
    attn_gain,
    w_query,
    w_key,
    w_value,
    query_gain,
    key_gain,
    w_out,
    mlp_gain,
    w_gate,
    w_up,
    w_down,
    cotangent,
):
    n, me = lax.axis_size("fsdp"), lax.axis_index("fsdp")
    tok_rows, width = tokens.shape[1], tokens.shape[2]
    length = segments.shape[1]
    heads, kv_heads = HEADS // n, KV_HEADS // n
    q_width, kv_width = heads * HEAD, kv_heads * HEAD
    ff = w_gate.shape[1] // n
    rows = width // n

    def block(value, k):
        return value[k * tok_rows : (k + 1) * tok_rows]

    def by_columns(first, second):
        columns = second.shape[1] // n
        return jnp.stack(
            [
                matmul_tn(first, second[:, j * columns : (j + 1) * columns]).astype(bf16)
                for j in range(n)
            ]
        )

    def by_rows(first, second):
        return matmul_tn(first, second).astype(bf16).reshape(n, rows, second.shape[1])

    qkv_kind, out_kind = RowKind(w_query, w_key, w_value), ColumnKind(w_out)
    gu_kind, down_kind = RowKind(w_gate, w_up), ColumnKind(w_down)

    sizes = [attn_gain.shape[0], mlp_gain.shape[0], query_gain.shape[0], key_gain.shape[0]]
    packed = jnp.concatenate([attn_gain, mlp_gain, query_gain, key_gain])[None]
    gains = [packed] + [swap(packed, "fsdp", k) for k in range(1, n)]
    tok = gather_begin(tokens[0])
    qkv_got = spread_begin(qkv_kind.quarter)
    index = jnp.concatenate(
        [(me ^ k) * tok_rows + jnp.arange(tok_rows, dtype=jnp.int32) for k in range(n)]
    )
    doc_ids = jnp.concatenate(
        [rows_of(segments[0], (me ^ k) * tok_rows, tok_rows) for k in range(n)]
    )
    earlier = jnp.sum((doc_ids[None, :] < doc_ids[:, None]).astype(jnp.int32), axis=1)
    position = index - earlier
    inverse = rope_base ** (-2.0 * jnp.arange(HEAD // 2).astype(f32) / HEAD)
    angles = position.astype(f32)[:, None] * inverse[None, :]
    angles = jnp.concatenate([angles, angles], axis=-1)
    cos_table, sin_table = jnp.cos(angles)[:, None, :], jnp.sin(angles)[:, None, :]
    allowed = (doc_ids[:, None] == doc_ids[None, :]) & (index[None, :] <= index[:, None])
    gains = jnp.concatenate(gains, axis=0)
    gains = jnp.concatenate(
        [lax.dynamic_slice_in_dim(gains, me ^ j, 1, axis=0) for j in range(n)], axis=0
    ).astype(f32)
    ends = [sum(sizes[: j + 1]) for j in range(4)]
    gain_attn = gains[:, : ends[0]].reshape(-1)
    gain_mlp = gains[:, ends[0] : ends[1]].reshape(-1)
    gain_query = gains[:, ends[1] : ends[2]].reshape(-1)
    gain_key = gains[:, ends[2] : ends[3]].reshape(-1)
    qkv_got = jnp.stack(qkv_got)
    tok, qkv_got, (cos_table, sin_table, allowed), (w_out, w_gate, w_up, w_down, cotangent) = fence(
        tok,
        qkv_got,
        (cos_table, sin_table, allowed),
        (w_out, w_gate, w_up, w_down, cotangent),
    )
    out_kind = ColumnKind(w_out)
    gu_kind, down_kind = RowKind(w_gate, w_up), ColumnKind(w_down)

    tok = gather_end(tokens[0], tok)
    qkv_along, qkv_across = stack_along(qkv_got), core_swap(qkv_got)
    out_got = spread_begin(out_kind.quarter)
    tok, qkv_along, qkv_across, w_gate, w_up = fence(tok, qkv_along, qkv_across, w_gate, w_up)
    gu_kind = RowKind(w_gate, w_up)

    qkv_across_along = core_swap(qkv_along)
    gu_got = spread_begin(gu_kind.quarter)
    tokens_all = jnp.concatenate(tok, axis=0)
    stream_all = tokens_all.astype(f32)
    normed = (stream_all * rms_scale(stream_all) * gain_attn).astype(bf16)
    out_got = jnp.stack(out_got)
    out_along, out_across = stack_along(out_got), core_swap(out_got)
    full_qkv = qkv_kind.join(spread_pieces(qkv_got, qkv_along, qkv_across, qkv_across_along))
    qkv = matmul(normed, full_qkv)
    query_raw = qkv[:, :q_width].reshape(length, heads, HEAD)
    key_raw = qkv[:, q_width : q_width + kv_width].reshape(length, kv_heads, HEAD)
    values = qkv[:, q_width + kv_width :].astype(bf16).reshape(length, kv_heads, HEAD)
    query_scale, key_scale = rms_scale(query_raw), rms_scale(key_raw)
    queries = turn(query_raw * query_scale * gain_query, cos_table, sin_table).astype(bf16)
    keys = turn(key_raw * key_scale * gain_key, cos_table, sin_table).astype(bf16)
    attended, log_total = attention_forward(queries, keys, values, allowed)
    out_across_along = core_swap(out_along)
    full_out = out_kind.join(spread_pieces(out_got, out_along, out_across, out_across_along))
    gu_got = jnp.stack(gu_got)
    attended, full_out, gu_got, w_down = fence(attended, full_out, gu_got, w_down)
    down_kind = ColumnKind(w_down)

    gu_along, gu_across = stack_along(gu_got), core_swap(gu_got)
    parts = [matmul(block(attended, n - 1), full_out).astype(bf16)]
    begun = scatter_begin(parts[0])
    parts = [matmul(block(attended, k), full_out).astype(bf16) for k in range(n - 1)] + parts
    begun, parts, gu_across = fence(begun, parts, gu_across)

    stream = tokens[0].astype(f32)
    middle = stream + scatter_end(parts[0], scatter_middle(parts[1 : n - 1], begun))
    mlp_scale = rms_scale(middle)
    normed_mine = (middle * mlp_scale * gain_mlp).astype(bf16)
    middle, mlp_scale, normed_mine, gu_along, w_down = fence(
        middle, mlp_scale, normed_mine, gu_along, w_down
    )
    down_kind = ColumnKind(w_down)

    begun = gather_begin(normed_mine)
    gu_across_along = core_swap(gu_along)
    full_gu = gu_kind.join(spread_pieces(gu_got, gu_along, gu_across, gu_across_along))
    begun, full_gu, w_down, cotangent = fence(begun, full_gu, w_down, cotangent)
    down_kind = ColumnKind(w_down)

    normed_parts = gather_end(normed_mine, begun)
    gate_up_parts = [matmul(part, full_gu) for part in normed_parts[: n - 1]]
    normed_parts, gate_up_parts, w_down, cotangent = fence(
        normed_parts, gate_up_parts, w_down, cotangent
    )
    down_kind = ColumnKind(w_down)

    cot = cotangent[0]
    down_got = spread_begin(down_kind.quarter)
    cot_begun = gather_begin(cot)
    gate_up = jnp.concatenate(gate_up_parts + [matmul(normed_parts[n - 1], full_gu)], axis=0)
    normed_mlp = jnp.concatenate(normed_parts, axis=0)
    gate, up = gate_up[:, :ff], gate_up[:, ff:]
    sg = 1.0 / (1.0 + jnp.exp(-gate))
    hidden = (gate * sg * up).astype(bf16)
    down_got = jnp.stack(down_got)
    down_got, cot_begun, gate_up, hidden, normed_mlp = fence(
        down_got, cot_begun, gate_up, hidden, normed_mlp
    )

    cot_all = jnp.concatenate(gather_end(cot, cot_begun), axis=0)
    down_along, down_across = stack_along(down_got), core_swap(down_got)
    down_across_along = core_swap(down_along)
    full_down = down_kind.join(
        spread_pieces(down_got, down_along, down_across, down_across_along)
    )
    cot_all, full_down, hidden, gate_up = fence(cot_all, full_down, hidden, gate_up)

    gate, up = gate_up[:, :ff], gate_up[:, ff:]
    sg = 1.0 / (1.0 + jnp.exp(-gate))
    d_hidden = matmul_nt(cot_all, full_down)
    d_gate = (d_hidden * up * sg * (1.0 + gate * (1.0 - sg))).astype(bf16)
    d_up = (d_hidden * gate * sg).astype(bf16)
    d_gate_up = jnp.concatenate([d_gate, d_up], axis=1)
    down = Reduction(by_columns(hidden, cot_all))
    down.begin()
    down.half, d_gate_up, hidden = fence(down.half, d_gate_up, hidden)

    down.half = lax.psum(down.half, "z")
    begun = scatter_begin(matmul_nt(block(d_gate_up, n - 1), full_gu).astype(bf16))
    parts = [matmul_nt(block(d_gate_up, k), full_gu).astype(bf16) for k in range(n - 1)]
    d_normed_mlp = scatter_end(parts[0], scatter_middle(parts[1:], begun))
    d_middle, mlp_gain_rows = norm_back(middle, mlp_scale, gain_mlp, d_normed_mlp)
    mlp_gain_grad = jnp.sum(mlp_gain_rows, axis=0)
    d_middle = cot.astype(f32) + d_middle
    d_mine = d_middle.astype(bf16)
    gate_sum = Reduction(by_rows(normed_mlp, d_gate_up[:, :ff]))
    gate_sum.begin()
    up_sum = Reduction(by_rows(normed_mlp, d_gate_up[:, ff:]))
    out_parts = [matmul(block(hidden, k), full_down).astype(bf16) for k in range(n)]
    down.half, d_middle, d_mine, mlp_gain_grad, gate_sum.half, up_sum.grad, out_parts = fence(
        down.half, d_middle, d_mine, mlp_gain_grad, gate_sum.half, up_sum.grad, out_parts
    )

    gate_sum.half = lax.psum(gate_sum.half, "z")
    d_branch = jnp.concatenate(gather_end(d_mine, gather_begin(d_mine)), axis=0)
    d_attended = matmul_nt(d_branch, full_out).astype(bf16)
    up_sum.begin()
    down.exchange()
    down_full = down.finish(False)
    gate_sum.half, d_branch, d_attended, up_sum.half, down_full, out_parts = fence(
        gate_sum.half, d_branch, d_attended, up_sum.half, down_full, out_parts
    )

    up_sum.half = lax.psum(up_sum.half, "z")
    d_queries, d_keys, d_values = attention_backward(
        queries, keys, values, allowed, log_total, d_attended
    )
    d_query_raw, query_gain_rows = norm_back(
        query_raw, query_scale, gain_query, turn_back(d_queries, cos_table, sin_table)
    )
    d_key_raw, key_gain_rows = norm_back(
        key_raw, key_scale, gain_key, turn_back(d_keys, cos_table, sin_table)
    )
    head_gain_grads = [
        jnp.sum(query_gain_rows, axis=(0, 1)),
        jnp.sum(key_gain_rows, axis=(0, 1)),
    ]
    d_qkv = jnp.concatenate(
        [
            d_query_raw.astype(bf16).reshape(length, q_width),
            d_key_raw.astype(bf16).reshape(length, kv_width),
            d_values.astype(bf16).reshape(length, kv_width),
        ],
        axis=1,
    )
    out_got = scatter_middle(out_parts[1 : n - 1], scatter_begin(out_parts[n - 1]))
    output = (middle + scatter_end(out_parts[0], out_got)).astype(bf16)
    gate_sum.exchange()
    gate_full = gate_sum.finish(True)
    out_sum = Reduction(by_columns(attended, d_branch))
    out_sum.begin()
    out_sum.exchange()
    qkv_sum = Reduction(by_rows(normed, d_qkv))
    qkv_sum.begin()
    qkv_sum.exchange()
    up_sum.half, d_qkv, head_gain_grads, out_sum.half, qkv_sum.half, output, gate_full = fence(
        up_sum.half, d_qkv, head_gain_grads, out_sum.half, qkv_sum.half, output, gate_full
    )

    qkv_sum.half, out_sum.half = lax.psum((qkv_sum.half, out_sum.half), "z")
    begun = scatter_begin(matmul_nt(block(d_qkv, n - 1), full_qkv).astype(bf16))
    parts = [matmul_nt(block(d_qkv, k), full_qkv).astype(bf16) for k in range(n - 1)]
    d_normed = scatter_end(parts[0], scatter_middle(parts[1:], begun))
    d_stream, attn_gain_rows = norm_back(stream, rms_scale(stream), gain_attn, d_normed)
    input_grad = d_middle + d_stream
    gain_grads = jnp.concatenate(
        [jnp.sum(attn_gain_rows, axis=0), mlp_gain_grad] + head_gain_grads
    )
    for axis in ("core", "fsdp", "z"):
        k = 1
        while k < lax.axis_size(axis):
            gain_grads = gain_grads + swap(gain_grads, axis, k)
            k *= 2
    shares, start = [], 0
    for size in sizes:
        shares.append(rows_of(gain_grads, start + me * size, size))
        start += n * size
    up_sum.exchange()
    shares, input_grad, up_full, qkv_sum.half, out_sum.half = fence(
        shares, input_grad, up_sum.finish(True), qkv_sum.half, out_sum.half
    )
    return (
        output[None],
        input_grad[None],
        shares[0],
        qkv_sum.finish(True, 0, q_width),
        qkv_sum.finish(True, q_width, kv_width),
        qkv_sum.finish(True, q_width + kv_width, kv_width),
        shares[2],
        shares[3],
        out_sum.finish(False),
        shares[1],
        gate_full,
        up_full,
        down_full,
    )


def solution(mesh):
    n, replicas = mesh.shape["fsdp"], mesh.shape["dp"]
    split = Mesh(mesh.devices.reshape(n, replicas // 2, 2), ("fsdp", "z", "core"))
    dp = ("z", "core")
    in_specs = (
        P(dp, "fsdp", None),
        P(dp, None),
        P("fsdp"),
        P("fsdp", None),
        P("fsdp", None),
        P("fsdp", None),
        P("fsdp"),
        P("fsdp"),
        P(None, "fsdp"),
        P("fsdp"),
        P("fsdp", None),
        P("fsdp", None),
        P(None, "fsdp"),
        P(dp, "fsdp", None),
    )
    out_specs = (
        P(dp, "fsdp", None),
        P(dp, "fsdp", None),
        P("fsdp"),
        P("fsdp", None),
        P("fsdp", None),
        P("fsdp", None),
        P("fsdp"),
        P("fsdp"),
        P(None, "fsdp"),
        P("fsdp"),
        P("fsdp", None),
        P("fsdp", None),
        P(None, "fsdp"),
    )
    return jax.shard_map(
        on_device, mesh=split, in_specs=in_specs, out_specs=out_specs, check_vma=False
    )
```

time: 1360 us -> 1020 us (0.75)
  local copies, waits for them, and re-layouts: 310 us -> 70.1 us
  starting transfers between devices: 269 us -> 85.7 us
  Pallas kernels: 0 us -> 50.5 us
  matrix products: 165 us -> 189 us
  other arithmetic: 124 us -> 109 us
    ppermute x48 -> x0, waiting for transfers between devices: 251 us -> none  [the longest x12 125 us: line_scatter(): up = lax.ppermute(up_send.astype(bf16), 'z', [(j, j + 1) for j in range(s)])]
    ppermute x84 -> x89, waiting for transfers between devices: 227 us -> 376 us  [swap(): lax.ppermute(value, axis, [(j, j ^ k) for j in range(lax.axis_size(axis))])]
    ppermute x48 -> x0, starting transfers between devices: 127 us -> none  [the longest x12 69.1 us: line_scatter(): up = lax.ppermute(up_send.astype(bf16), 'z', [(j, j + 1) for j in range(s)])]
    psum x0 -> x4, waiting for transfers between devices: none -> 111 us  [the longest x1 55.9 us: on_device(): down.half = lax.psum(down.half, 'z')]
    dynamic_update_slice x60 -> x0, local copies, waits for them, and re-layouts: 104 us -> none  [the longest x6 41.1 us: spread_columns(): out = lax.dynamic_update_slice(out, got, (core * half, base))]
    slice x21 -> x30, local copies, waits for them, and re-layouts: 71.7 us -> 10.8 us  [the longest x5 6.01 us: exchange(): self.half[0]]
    ppermute x84 -> x89, starting transfers between devices: 142 us -> 85.6 us  [swap(): lax.ppermute(value, axis, [(j, j ^ k) for j in range(lax.axis_size(axis))])]
    pallas_call x0 -> x11, Pallas kernels: none -> 50.5 us  [the longest x7 42.2 us: finish(): pl.pallas_call(kernel, out_shape=jax.ShapeDtypeStruct((2 * rows, n * size...]
  transfers between devices with their start and end apart: 132 -> 93, of which waited for: 43 -> 52; matrix products, arithmetic and copies ran while one was open for 33% -> 22% of each run, Pallas kernels for 0% -> 4%
where the time goes in v2:
time: 1020 us; the launch traced here: 1010 us
  waiting for transfers between devices  488 us (48%)
  matrix products  189 us (19%)
  other arithmetic  109 us (11%)
  starting transfers between devices  85.7 us (8%)
  local copies, waits for them, and re-layouts  70.1 us (7%)
  Pallas kernels  50.5 us (5%)
  between operations  16.4 us (2%)
    ppermute x89, waiting for transfers between devices, swap(): lax.ppermute(value, axis, [(j, j ^ k) for j in range(lax.axis_size(axis))])  376 us
    ppermute x89, starting transfers between devices, swap(): lax.ppermute(value, axis, [(j, j ^ k) for j in range(lax.axis_size(axis))])  85.6 us
    dot_general x10, matrix products, matmul_nt(): lax.dot_general(first, second, (((1,), (1,)), ((), ())), preferred_elemen...  64.2 us
    psum x1, waiting for transfers between devices, on_device(): down.half = lax.psum(down.half, 'z')  55.9 us
    dot_general x11, matrix products, matmul_tn(): lax.dot_general(first, second, (((0,), (0,)), ((), ())), preferred_elemen...  44.1 us
    pallas_call x7, Pallas kernels, finish(): pl.pallas_call(kernel, out_shape=jax.ShapeDtypeStruct((2 * rows, n * size...  42.2 us
    dot_general x13, matrix products, matmul(): return jnp.dot(first, second, preferred_element_type=f32)  39.3 us
    psum x1, waiting for transfers between devices, on_device(): gate_sum.half = lax.psum(gate_sum.half, 'z')  39.1 us
  transfers between devices with their start and end apart: 93, of which 52 were waited for; matrix products, arithmetic and copies ran while one was open for 22% of the time, Pallas kernels for 4%

profile of v2, /device:TPU:0, one launch (start us, length us, event | category | flops | bytes accessed | tf_op | source)
XLA Modules:
  0.0 1007.8 jit_solution(76395509562005369)
XLA Ops:
  37.9 10.7 %collective-permute-done.4 = bf16[128,1024]{1,0:T(8,128)(2,1)} collective-permute-done((bf16[128,1024]{1,0:T(8,128)(2,1)S(1)}, bf16[128,1024]{1,0:T(8,128)(2,1)}, u32[]{:S(2)}, u32[]{:S(2)}) %collective-permute-start.4) | collective-permute-done | bytes 262176 | tf_op jit(solution)/shard_map/ppermute | solution.py:50
  67.6 6.6 collective-permute-done.16
  115.8 7.6 fusion.102
  123.4 8.1 fusion.3
  131.5 8.2 fusion.42
  151.1 8.9 collective-permute-done.23
  167.7 18.6 %collective-permute-done.26 = bf16[256,2048]{1,0:T(8,128)(2,1)S(1)} collective-permute-done((bf16[256,2048]{1,0:T(8,128)(2,1)S(1)}, bf16[256,2048]{1,0:T(8,128)(2,1)S(1)}, u32[]{:S(2)}, u32[]{:S(2)}) %collective-permute-start.26) | collective-permute-done | bytes 1048608 | tf_op jit(solution)/shard_map/ppermute | solution.py:50
  190.6 6.7 collective-permute-done.27
  206.7 18.3 %collective-permute-done.29 = bf16[256,2048]{1,0:T(8,128)(2,1)S(1)} collective-permute-done((bf16[256,2048]{1,0:T(8,128)(2,1)S(1)}, bf16[256,2048]{1,0:T(8,128)(2,1)S(1)}, u32[]{:S(2)}, u32[]{:S(2)}) %collective-permute-start.29) | collective-permute-done | bytes 1048608 | tf_op jit(solution)/shard_map/ppermute | solution.py:50
  239.7 6.9 collective-permute-done.32
  271.8 12.0 %collective-permute-done.33 = bf16[384,512]{1,0:T(8,128)(2,1)S(1)} collective-permute-done((bf16[384,512]{1,0:T(8,128)(2,1)}, bf16[384,512]{1,0:T(8,128)(2,1)S(1)}, u32[]{:S(2)}, u32[]{:S(2)}) %collective-permute-start.33) | collective-permute-done | bytes 393248 | tf_op jit(solution)/shard_map/ppermute | solution.py:50
  283.8 5.5 collective-permute-done.35
  298.6 17.0 %collective-permute-done.40 = bf16[3,384,512]{2,1,0:T(8,128)(2,1)S(1)} collective-permute-done((bf16[3,384,512]{2,1,0:T(8,128)(2,1)S(1)}, bf16[3,384,512]{2,1,0:T(8,128)(2,1)S(1)}, u32[]{:S(2)}, u32[]{:S(2)}) %collective-permute-start.40) | collective-permute-done | bytes 1179680 | tf_op jit(solution)/shard_map/ppermute | solution.py:50
  331.5 13.9 %multiply_convert_fusion.1 = (bf16[1024,1536]{1,0:T(8,128)(2,1)S(1)}, bf16[1024,1536]{1,0:T(8,128)(2,1)}) fusion(f32[1024,3072]{1,0:T(8,128)} %copy-done.12, bf16[1024,2048]{1,0:T(8,128)(2,1)} %copy-done.88, bf16[1536,2048]{1,0:T(8,128)(2,1)S(1)} %assemble.7), kind=kOutput, calls=%fused_computation.29 | convolution fusion | flops 6462898176 | bytes 29360128 | tf_op jit(solution)/shard_map/dot_general | solution.py:34
  345.3 5.4 pad_maximum_fusion.2
  353.9 9.6 convolution_convert_fusion.19
  363.5 9.6 convolution_convert_fusion.21
  373.1 5.8 convolution_convert_fusion.20
  379.0 12.1 %convolution_convert_fusion = bf16[2048,1536]{1,0:T(8,128)(2,1)} fusion(bf16[1024,2048]{1,0:T(8,128)(2,1)} %pad_maximum_fusion.4, bf16[1024,3072]{1,0:T(8,128)(2,1)} %pad_maximum_fusion.2), kind=kOutput, calls=%fused_computation.20 | convolution fusion | flops 6445596672 | bytes 13631488 | tf_op jit(solution)/shard_map/dot_general | solution.py:30
  391.0 10.5 %convolution_convert_fusion.1 = bf16[2048,1536]{1,0:T(8,128)(2,1)} fusion(bf16[1024,2048]{1,0:T(8,128)(2,1)S(1)} %copy-done.29, bf16[1024,3072]{1,0:T(8,128)(2,1)} %pad_maximum_fusion.2), kind=kOutput, calls=%fused_computation.21 | convolution fusion | flops 6445596672 | bytes 13631488 | tf_op jit(solution)/shard_map/dot_general | solution.py:30
  401.7 6.0 convolution_convert_fusion.15
  416.6 6.6 collective-permute-done.46
  430.8 17.1 %collective-permute-done.47 = bf16[256,2048]{1,0:T(8,128)(2,1)S(1)} collective-permute-done((bf16[256,2048]{1,0:T(8,128)(2,1)S(1)}, bf16[256,2048]{1,0:T(8,128)(2,1)S(1)}, u32[]{:S(2)}, u32[]{:S(2)}) %collective-permute-start.47) | collective-permute-done | bytes 1048608 | tf_op jit(solution)/shard_map/ppermute | solution.py:50
  449.9 11.1 %multiply_reduce_fusion.1 = (f32[2048]{0:T(1024)S(1)}, f32[256]{0:T(256)S(1)}, f32[256,2048]{1,0:T(8,128)}) fusion(f32[256,2048]{1,0:T(8,128)S(1)} %copy-done.14, f32[256]{0:T(256)S(1)} %copy-done.104, f32[2048]{0:T(1024)S(1)} %bitcast.442, bf16[256,2048]{1,0:T(8,128)(2,1)} %copy-done.113, bf16[256,2048]{1,0:T(8,128)(2,1)} %copy-done.114, ...), kind=kOutput, calls=%fused_computation.110 | convolution fusion | flops 3227514624 | bytes 20465664 | tf_op jit(solution)/shard_map/dot_general | solution.py:34
  467.3 55.9 %all-reduce.6.cloned.1.call-done = bf16[4,768,512]{2,1,0:T(8,128)(2,1)} async-done(((bf16[4,768,512]{2,1,0:T(8,128)(2,1)}), bf16[4,768,512]{2,1,0:T(8,128)(2,1)}) %all-reduce.6.cloned.1.call-update) | async-done | bytes 3145744 | tf_op jit(solution)/shard_map/psum | solution.py:531
  538.0 10.0 collective-permute-done.56
  549.4 14.2 %collective-permute-done.55 = bf16[768,512]{1,0:T(8,128)(2,1)S(1)} collective-permute-done((bf16[768,512]{1,0:T(8,128)(2,1)S(1)}, bf16[768,512]{1,0:T(8,128)(2,1)S(1)}, u32[]{:S(2)}, u32[]{:S(2)}) %collective-permute-start.55) | collective-permute-done | bytes 786464 | tf_op jit(solution)/shard_map/ppermute | solution.py:50
  569.0 17.2 %collective-permute-done.49 = bf16[256,2048]{1,0:T(8,128)(2,1)} collective-permute-done((bf16[256,2048]{1,0:T(8,128)(2,1)}, bf16[256,2048]{1,0:T(8,128)(2,1)}, u32[]{:S(2)}, u32[]{:S(2)}) %collective-permute-start.49) | collective-permute-done | bytes 1048608 | tf_op jit(solution)/shard_map/ppermute | solution.py:50
  592.3 7.8 collective-permute-done.51
  609.3 8.8 place.7
  618.1 39.1 %all-reduce.8.cloned.1.call-done = bf16[4,256,1536]{2,1,0:T(8,128)(2,1)} async-done(((bf16[4,256,1536]{2,1,0:T(8,128)(2,1)}), bf16[4,256,1536]{2,1,0:T(8,128)(2,1)}) %all-reduce.8.cloned.1.call-update) | async-done | bytes 3145744 | tf_op jit(solution)/shard_map/psum | solution.py:547
  666.9 8.4 fusion.46
  675.3 11.9 %fusion = (f32[2,2,1024]{2,1,0:T(2,128)S(1)}, f32[2,1024,1024,2]{2,1,3,0:T(8,128)}) fusion(f32[2,2,1024,1024]{2,3,1,0:T(8,128)} %get-tuple-element.394, f32[2,2,1024]{2,1,0:T(2,128)S(1)} %log_add_fusion, pred[1024,1024]{0,1:T(8,128)(4,1)S(1)} %copy-done.20, bf16[1024,2,128,1]{0,2,3,1:T(8,128)(2,1)S(1)} %bitcast.415, bf16[1024,2,2,128]{0,3,2,1:T(8,128)(2,1)S(1)} %bitcast.413), kind=kOutput, calls=%fused_computation.2 | convolution fusion | flops 1090514944 | bytes 36208640 | tf_op jit(solution)/shard_map/qkgd,skd->kgqs/dot_general | solution.py:351
  687.2 12.3 %fusion.2 = bf16[2,2,1024,1024]{2,3,1,0:T(8,128)(2,1)S(1)} fusion(f32[2,1024,1024,2]{2,1,3,0:T(8,128)} %get-tuple-element.397, f32[2,2,1024,1024]{2,3,1,0:T(8,128)} %get-tuple-element.394, f32[2,2,1024]{2,1,0:T(2,128)S(1)} %get-tuple-element.396, f32[2,2,1024]{2,1,0:T(2,128)S(1)} %log_add_fusion, pred[1024,1024]{0,1:T(8,128)(4,1)S(1)} %copy-done.20), kind=kLoop, calls=%fused_computation.4 | loop fusion | flops 20971520 | bytes 43024384 | tf_op jit(solution)/shard_map/convert_element_type | solution.py:353
  729.6 12.7 %collective-permute-done.72 = bf16[256,1536]{1,0:T(8,128)(2,1)S(1)} collective-permute-done((bf16[256,1536]{1,0:T(8,128)(2,1)}, bf16[256,1536]{1,0:T(8,128)(2,1)S(1)}, u32[]{:S(2)}, u32[]{:S(2)}) %collective-permute-start.72) | collective-permute-done | bytes 786464 | tf_op jit(solution)/shard_map/ppermute | solution.py:50
  742.3 14.0 %collective-permute-done.71 = bf16[256,1536]{1,0:T(8,128)(2,1)S(1)} collective-permute-done((bf16[256,1536]{1,0:T(8,128)(2,1)S(1)}, bf16[256,1536]{1,0:T(8,128)(2,1)S(1)}, u32[]{:S(2)}, u32[]{:S(2)}) %collective-permute-start.71) | collective-permute-done | bytes 786464 | tf_op jit(solution)/shard_map/ppermute | solution.py:50
  771.8 24.9 %collective-permute-done.60 = bf16[256,512]{1,0:T(8,128)(2,1)S(1)} collective-permute-done((bf16[256,512]{1,0:T(8,128)(2,1)S(1)}, bf16[256,512]{1,0:T(8,128)(2,1)S(1)}, u32[]{:S(2)}, u32[]{:S(2)}) %collective-permute-start.60) | collective-permute-done | bytes 262176 | tf_op jit(solution)/shard_map/ppermute | solution.py:50
  812.2 10.6 %collective-permute-done.65 = bf16[256,1024]{1,0:T(8,128)(2,1)S(1)} collective-permute-done((bf16[256,1024]{1,0:T(8,128)(2,1)S(1)}, bf16[256,1024]{1,0:T(8,128)(2,1)S(1)}, u32[]{:S(2)}, u32[]{:S(2)}) %collective-permute-start.65) | collective-permute-done | bytes 524320 | tf_op jit(solution)/shard_map/ppermute | solution.py:50
  822.8 9.2 collective-permute-done.64
  833.6 8.7 place.8
  857.5 6.6 collective-permute-done.76
  866.0 17.3 %collective-permute-done.74 = bf16[128,2048]{1,0:T(8,128)(2,1)} collective-permute-done((bf16[128,2048]{1,0:T(8,128)(2,1)}, bf16[128,2048]{1,0:T(8,128)(2,1)}, u32[]{:S(2)}, u32[]{:S(2)}) %collective-permute-start.74) | collective-permute-done | bytes 524320 | tf_op jit(solution)/shard_map/ppermute | solution.py:50
  884.5 15.7 %collective-permute-done.84 = bf16[256,1536]{1,0:T(8,128)(2,1)} collective-permute-done((bf16[256,1536]{1,0:T(8,128)(2,1)}, bf16[256,1536]{1,0:T(8,128)(2,1)}, u32[]{:S(2)}, u32[]{:S(2)}) %collective-permute-start.84) | collective-permute-done | bytes 786464 | tf_op jit(solution)/shard_map/ppermute | solution.py:50
  903.8 16.9 %collective-permute-done.77 = bf16[256,2048]{1,0:T(8,128)(2,1)S(1)} collective-permute-done((bf16[256,2048]{1,0:T(8,128)(2,1)S(1)}, bf16[256,2048]{1,0:T(8,128)(2,1)S(1)}, u32[]{:S(2)}, u32[]{:S(2)}) %collective-permute-start.77) | collective-permute-done | bytes 1048608 | tf_op jit(solution)/shard_map/ppermute | solution.py:50
  920.7 7.5 collective-permute-done.75
  953.0 8.8 place.9
  961.8 16.3 %all-reduce.12.cloned.1.call-done = (bf16[4,256,1024]{2,1,0:T(8,128)(2,1)}, bf16[4,256,512]{2,1,0:T(8,128)(2,1)}) async-done(((bf16[4,256,1024]{2,1,0:T(8,128)(2,1)}, bf16[4,256,512]{2,1,0:T(8,128)(2,1)}), (bf16[4,256,1024]{2,1,0:T(8,128)(2,1)}, bf16[4,256,512]{2,1,0:T(8,128)(2,1)})) %all-reduce.12.cloned.1.call-update) | async-done | bytes 3145744 | tf_op jit(solution)/shard_map/psum | solution.py:593
  978.6 5.4 collective-permute-done.88.other
  (642 shorter events, 388.7 us)
Async XLA Ops:
  7.2 516.0 %all-reduce.6.cloned.1.call-start = ((), (), s32[]{:S(2)}) async-start(), calls=%async_computation | async-start | bytes 6291456 | tf_op jit(solution)/shard_map/psum | solution.py:531
  10.6 22.7 %collective-permute-start.11 = (bf16[1,1088]{1,0:T(2,128)(2,1)}, bf16[1,1088]{1,0:T(2,128)(2,1)}, u32[]{:S(2)}, u32[]{:S(2)}) collective-permute-start(bf16[1,1088]{1,0:T(2,128)(2,1)} %broadcast_in_dim.20), channel_id=1, source_target_pairs={{0,24},{8,16},{16,8},{24,0},{1,25},{9,17},{17,9},{25,1},{2,26},{10... | collective-permute-start | bytes 6536 | tf_op jit(solution)/shard_map/ppermute | solution.py:50
  15.1 38.6 %collective-permute-start.1 = (bf16[256,2048]{1,0:T(8,128)(2,1)}, bf16[256,2048]{1,0:T(8,128)(2,1)S(1)}, u32[]{:S(2)}, u32[]{:S(2)}) collective-permute-start(bf16[256,2048]{1,0:T(8,128)(2,1)} %bitcast.396), channel_id=1, source_target_pairs={{0,16},{8,24},{16,0},{24,8},{1,17},{9,25},{17,1},{25,9},{2,18},{10... | collective-permute-start | bytes 3145736 | tf_op jit(solution)/shard_map/ppermute | solution.py:50
  17.1 36.6 %collective-permute-start = (bf16[256,2048]{1,0:T(8,128)(2,1)}, bf16[256,2048]{1,0:T(8,128)(2,1)S(1)}, u32[]{:S(2)}, u32[]{:S(2)}) collective-permute-start(bf16[256,2048]{1,0:T(8,128)(2,1)} %bitcast.397), channel_id=1, source_target_pairs={{0,8},{8,0},{16,24},{24,16},{1,9},{9,1},{17,25},{25,17},{2,10},{10... | collective-permute-start | bytes 3145736 | tf_op jit(solution)/shard_map/ppermute | solution.py:50
  90.8 48.9 %collective-permute-start.20 = (bf16[128,3072]{1,0:T(8,128)(2,1)}, bf16[128,3072]{1,0:T(8,128)(2,1)}, u32[]{:S(2)}, u32[]{:S(2)}) collective-permute-start(bf16[128,3072]{1,0:T(8,128)(2,1)} %pad_maximum_fusion.34), channel_id=1, source_target_pairs={{0,16},{8,24},{16,0},{24,8},{1,17},{9,25},{17,1},{25,9},{2,18},{10... | collective-permute-start | bytes 2359304 | tf_op jit(solution)/shard_map/ppermute | solution.py:50
  92.3 47.4 %collective-permute-start.21 = (bf16[128,3072]{1,0:T(8,128)(2,1)}, bf16[128,3072]{1,0:T(8,128)(2,1)}, u32[]{:S(2)}, u32[]{:S(2)}) collective-permute-start(bf16[128,3072]{1,0:T(8,128)(2,1)} %pad_maximum_fusion.35), channel_id=1, source_target_pairs={{0,24},{8,16},{16,8},{24,0},{1,25},{9,17},{17,9},{25,1},{2,26},{10... | collective-permute-start | bytes 2359304 | tf_op jit(solution)/shard_map/ppermute | solution.py:50
  95.6 44.2 %collective-permute-start.19 = (bf16[128,3072]{1,0:T(8,128)(2,1)}, bf16[128,3072]{1,0:T(8,128)(2,1)}, u32[]{:S(2)}, u32[]{:S(2)}) collective-permute-start(bf16[128,3072]{1,0:T(8,128)(2,1)} %pad_maximum_fusion.33), channel_id=1, source_target_pairs={{0,8},{8,0},{16,24},{24,16},{1,9},{9,1},{17,25},{25,17},{2,10},{10... | collective-permute-start | bytes 2359304 | tf_op jit(solution)/shard_map/ppermute | solution.py:50
  143.4 54.0 %collective-permute-start.27 = (bf16[3,128,3072]{2,1,0:T(8,128)(2,1)}, bf16[3,128,3072]{2,1,0:T(8,128)(2,1)}, u32[]{:S(2)}, u32[]{:S(2)}) collective-permute-start(bf16[3,128,3072]{2,1,0:T(8,128)(2,1)} %pad_maximum_fusion.12), channel_id=1, source_target_pairs={{0,2},{2,0},{4,6},{6,4},{1,3},{3,1},{5,7},{7,5},{8,10},{10,8},{12,... | collective-permute-start | bytes 7077896 | tf_op jit(solution)/shard_map/ppermute | solution.py:50
  161.9 24.4 %collective-permute-start.26 = (bf16[256,2048]{1,0:T(8,128)(2,1)S(1)}, bf16[256,2048]{1,0:T(8,128)(2,1)S(1)}, u32[]{:S(2)}, u32[]{:S(2)}) collective-permute-start(bf16[256,2048]{1,0:T(8,128)(2,1)S(1)} %pad_maximum_fusion.22), channel_id=1, source_target_pairs={{0,16},{8,24},{16,0},{24,8},{1,17},{9,25},{17,1},{25,9},{2,18},{10... | collective-permute-start | bytes 3145736 | tf_op jit(solution)/shard_map/ppermute | solution.py:50
  163.5 24.1 %collective-permute-start.25 = (bf16[256,2048]{1,0:T(8,128)(2,1)S(1)}, bf16[256,2048]{1,0:T(8,128)(2,1)}, u32[]{:S(2)}, u32[]{:S(2)}) collective-permute-start(bf16[256,2048]{1,0:T(8,128)(2,1)S(1)} %pad_maximum_fusion.21), channel_id=1, source_target_pairs={{0,8},{8,0},{16,24},{24,16},{1,9},{9,1},{17,25},{25,17},{2,10},{10... | collective-permute-start | bytes 3145736 | tf_op jit(solution)/shard_map/ppermute | solution.py:50
  199.3 25.6 %collective-permute-start.29 = (bf16[256,2048]{1,0:T(8,128)(2,1)S(1)}, bf16[256,2048]{1,0:T(8,128)(2,1)S(1)}, u32[]{:S(2)}, u32[]{:S(2)}) collective-permute-start(bf16[256,2048]{1,0:T(8,128)(2,1)S(1)} %multiply_convert_fusion.2), channel_id=1, source_target_pairs={{0,16},{8,24},{16,0},{24,8},{1,17},{9,25},{17,1},{25,9},{2,18},{10... | collective-permute-start | bytes 3145736 | tf_op jit(solution)/shard_map/ppermute | solution.py:50
  199.9 25.3 %collective-permute-start.28 = (bf16[256,2048]{1,0:T(8,128)(2,1)S(1)}, bf16[256,2048]{1,0:T(8,128)(2,1)S(1)}, u32[]{:S(2)}, u32[]{:S(2)}) collective-permute-start(bf16[256,2048]{1,0:T(8,128)(2,1)S(1)} %multiply_convert_fusion.2), channel_id=1, source_target_pairs={{0,8},{8,0},{16,24},{24,16},{1,9},{9,1},{17,25},{25,17},{2,10},{10... | collective-permute-start | bytes 3145736 | tf_op jit(solution)/shard_map/ppermute | solution.py:50
  247.8 42.7 %collective-permute-start.37 = (bf16[256,2048]{1,0:T(8,128)(2,1)S(1)}, bf16[256,2048]{1,0:T(8,128)(2,1)S(1)}, u32[]{:S(2)}, u32[]{:S(2)}) collective-permute-start(bf16[256,2048]{1,0:T(8,128)(2,1)S(1)} %bitcast.410), channel_id=1, source_target_pairs={{0,16},{8,24},{16,0},{24,8},{1,17},{9,25},{17,1},{25,9},{2,18},{10... | collective-permute-start | bytes 3145736 | tf_op jit(solution)/shard_map/ppermute | solution.py:50
  249.3 41.3 %collective-permute-start.36 = (bf16[256,2048]{1,0:T(8,128)(2,1)S(1)}, bf16[256,2048]{1,0:T(8,128)(2,1)}, u32[]{:S(2)}, u32[]{:S(2)}) collective-permute-start(bf16[256,2048]{1,0:T(8,128)(2,1)S(1)} %bitcast.411), channel_id=1, source_target_pairs={{0,8},{8,0},{16,24},{24,16},{1,9},{9,1},{17,25},{25,17},{2,10},{10... | collective-permute-start | bytes 3145736 | tf_op jit(solution)/shard_map/ppermute | solution.py:50
  252.1 31.7 %collective-permute-start.33 = (bf16[384,512]{1,0:T(8,128)(2,1)}, bf16[384,512]{1,0:T(8,128)(2,1)S(1)}, u32[]{:S(2)}, u32[]{:S(2)}) collective-permute-start(bf16[384,512]{1,0:T(8,128)(2,1)} %get-tuple-element.246), channel_id=1, source_target_pairs={{0,8},{8,0},{16,24},{24,16},{1,9},{9,1},{17,25},{25,17},{2,10},{10... | collective-permute-start | bytes 1179656 | tf_op jit(solution)/shard_map/ppermute | solution.py:50
  253.5 35.8 %collective-permute-start.35 = (bf16[384,512]{1,0:T(8,128)(2,1)}, bf16[384,512]{1,0:T(8,128)(2,1)}, u32[]{:S(2)}, u32[]{:S(2)}) collective-permute-start(bf16[384,512]{1,0:T(8,128)(2,1)} %get-tuple-element.247), channel_id=1, source_target_pairs={{0,24},{8,16},{16,8},{24,0},{1,25},{9,17},{17,9},{25,1},{2,26},{10... | collective-permute-start | bytes 1179656 | tf_op jit(solution)/shard_map/ppermute | solution.py:50
  254.2 35.1 %collective-permute-start.34 = (bf16[384,512]{1,0:T(8,128)(2,1)S(1)}, bf16[384,512]{1,0:T(8,128)(2,1)}, u32[]{:S(2)}, u32[]{:S(2)}) collective-permute-start(bf16[384,512]{1,0:T(8,128)(2,1)S(1)} %get-tuple-element.248), channel_id=1, source_target_pairs={{0,16},{8,24},{16,0},{24,8},{1,17},{9,25},{17,1},{25,9},{2,18},{10... | collective-permute-start | bytes 1179656 | tf_op jit(solution)/shard_map/ppermute | solution.py:50
  290.6 24.9 %collective-permute-start.40 = (bf16[3,384,512]{2,1,0:T(8,128)(2,1)S(1)}, bf16[3,384,512]{2,1,0:T(8,128)(2,1)S(1)}, u32[]{:S(2)}, u32[]{:S(2)}) collective-permute-start(bf16[3,384,512]{2,1,0:T(8,128)(2,1)S(1)} %pad_maximum_fusion.18), channel_id=1, source_target_pairs={{0,2},{2,0},{4,6},{6,4},{1,3},{3,1},{5,7},{7,5},{8,10},{10,8},{12,... | collective-permute-start | bytes 3538952 | tf_op jit(solution)/shard_map/ppermute | solution.py:50
  401.6 255.7 %all-reduce.8.cloned.1.call-start = ((), (), s32[]{:S(2)}) async-start(), calls=%async_computation.1 | async-start | bytes 6291456 | tf_op jit(solution)/shard_map/psum | solution.py:547
  412.7 52.5 %collective-permute-start.48 = (bf16[4,256,1536]{2,1,0:T(8,128)(2,1)S(1)}, bf16[4,256,1536]{2,1,0:T(8,128)(2,1)S(1)}, u32[]{:S(2)}, u32[]{:S(2)}) collective-permute-start(bf16[4,256,1536]{2,1,0:T(8,128)(2,1)S(1)} %pad_maximum_fusion.7), channel_id=1, source_target_pairs={{0,1},{1,0},{2,3},{3,2},{4,5},{5,4},{6,7},{7,6},{8,9},{9,8},{10,11... | collective-permute-start | bytes 9437192 | tf_op jit(solution)/shard_map/ppermute | solution.py:50
  423.4 24.5 %collective-permute-start.47 = (bf16[256,2048]{1,0:T(8,128)(2,1)S(1)}, bf16[256,2048]{1,0:T(8,128)(2,1)S(1)}, u32[]{:S(2)}, u32[]{:S(2)}) collective-permute-start(bf16[256,2048]{1,0:T(8,128)(2,1)S(1)} %pad_maximum_fusion.25), channel_id=1, source_target_pairs={{0,16},{8,24},{16,0},{24,8},{1,17},{9,25},{17,1},{25,9},{2,18},{10... | collective-permute-start | bytes 3145736 | tf_op jit(solution)/shard_map/ppermute | solution.py:50
  424.4 24.2 %collective-permute-start.45 = (bf16[256,2048]{1,0:T(8,128)(2,1)S(1)}, bf16[256,2048]{1,0:T(8,128)(2,1)S(1)}, u32[]{:S(2)}, u32[]{:S(2)}) collective-permute-start(bf16[256,2048]{1,0:T(8,128)(2,1)S(1)} %pad_maximum_fusion.24), channel_id=1, source_target_pairs={{0,8},{8,0},{16,24},{24,16},{1,9},{9,1},{17,25},{25,17},{2,10},{10... | collective-permute-start | bytes 3145736 | tf_op jit(solution)/shard_map/ppermute | solution.py:50
  528.7 34.9 %collective-permute-start.55 = (bf16[768,512]{1,0:T(8,128)(2,1)S(1)}, bf16[768,512]{1,0:T(8,128)(2,1)S(1)}, u32[]{:S(2)}, u32[]{:S(2)}) collective-permute-start(bf16[768,512]{1,0:T(8,128)(2,1)S(1)} %get-tuple-element.273), channel_id=1, source_target_pairs={{0,16},{8,24},{16,0},{24,8},{1,17},{9,25},{17,1},{25,9},{2,18},{10... | collective-permute-start | bytes 2359304 | tf_op jit(solution)/shard_map/ppermute | solution.py:50
  529.3 35.6 %collective-permute-start.54 = (bf16[768,512]{1,0:T(8,128)(2,1)S(1)}, bf16[768,512]{1,0:T(8,128)(2,1)}, u32[]{:S(2)}, u32[]{:S(2)}) collective-permute-start(bf16[768,512]{1,0:T(8,128)(2,1)S(1)} %get-tuple-element.274), channel_id=1, source_target_pairs={{0,8},{8,0},{16,24},{24,16},{1,9},{9,1},{17,25},{25,17},{2,10},{10... | collective-permute-start | bytes 2359304 | tf_op jit(solution)/shard_map/ppermute | solution.py:50
  536.4 68.9 %collective-permute-start.53 = (bf16[4,256,1536]{2,1,0:T(8,128)(2,1)}, bf16[4,256,1536]{2,1,0:T(8,128)(2,1)}, u32[]{:S(2)}, u32[]{:S(2)}) collective-permute-start(bf16[4,256,1536]{2,1,0:T(8,128)(2,1)} %pad_maximum_fusion.8), channel_id=1, source_target_pairs={{0,1},{1,0},{2,3},{3,2},{4,5},{5,4},{6,7},{7,6},{8,9},{9,8},{10,11... | collective-permute-start | bytes 9437192 | tf_op jit(solution)/shard_map/ppermute | solution.py:50
  536.4 49.8 %collective-permute-start.49 = (bf16[256,2048]{1,0:T(8,128)(2,1)}, bf16[256,2048]{1,0:T(8,128)(2,1)}, u32[]{:S(2)}, u32[]{:S(2)}) collective-permute-start(bf16[256,2048]{1,0:T(8,128)(2,1)} %get-tuple-element.171), channel_id=1, source_target_pairs={{0,8},{8,0},{16,24},{24,16},{1,9},{9,1},{17,25},{25,17},{2,10},{10... | collective-permute-start | bytes 3145736 | tf_op jit(solution)/shard_map/ppermute | solution.py:50
  537.9 304.4 %all-reduce.10.cloned.1.call-start = ((), (), s32[]{:S(2)}) async-start(), calls=%async_computation.2 | async-start | bytes 6291456 | tf_op jit(solution)/shard_map/psum | solution.py:557
  548.0 41.3 %collective-permute-start.50 = (bf16[256,2048]{1,0:T(8,128)(2,1)}, bf16[256,2048]{1,0:T(8,128)(2,1)S(1)}, u32[]{:S(2)}, u32[]{:S(2)}) collective-permute-start(bf16[256,2048]{1,0:T(8,128)(2,1)} %get-tuple-element.171), channel_id=1, source_target_pairs={{0,16},{8,24},{16,0},{24,8},{1,17},{9,25},{17,1},{25,9},{2,18},{10... | collective-permute-start | bytes 3145736 | tf_op jit(solution)/shard_map/ppermute | solution.py:50
  567.3 42.1 %collective-permute-start.57 = (bf16[4,768,512]{2,1,0:T(8,128)(2,1)S(1)}, bf16[4,768,512]{2,1,0:T(8,128)(2,1)}, u32[]{:S(2)}, u32[]{:S(2)}) collective-permute-start(bf16[4,768,512]{2,1,0:T(8,128)(2,1)S(1)} %pad_maximum_fusion.9.mine), channel_id=1, source_target_pairs={{0,1},{1,0},{2,3},{3,2},{4,5},{5,4},{6,7},{7,6},{8,9},{9,8},{10,11... | collective-permute-start | bytes 9437192 | tf_op jit(solution)/shard_map/ppermute | solution.py:50
  704.7 273.4 %all-reduce.12.cloned.1.call-start = ((), (), s32[]{:S(2)}) async-start(), calls=%async_computation.3 | async-start | bytes 6291456 | tf_op jit(solution)/shard_map/psum | solution.py:593
  708.8 54.5 %collective-permute-start.66 = (bf16[128,2048]{1,0:T(8,128)(2,1)}, bf16[128,2048]{1,0:T(8,128)(2,1)}, u32[]{:S(2)}, u32[]{:S(2)}) collective-permute-start(bf16[128,2048]{1,0:T(8,128)(2,1)} %get-tuple-element.326), channel_id=1, source_target_pairs={{0,16},{8,24},{16,0},{24,8},{1,17},{9,25},{17,1},{25,9},{2,18},{10... | collective-permute-start | bytes 1572872 | tf_op jit(solution)/shard_map/ppermute | solution.py:50
  712.9 29.4 %collective-permute-start.72 = (bf16[256,1536]{1,0:T(8,128)(2,1)}, bf16[256,1536]{1,0:T(8,128)(2,1)S(1)}, u32[]{:S(2)}, u32[]{:S(2)}) collective-permute-start(bf16[256,1536]{1,0:T(8,128)(2,1)} %get-tuple-element.268), channel_id=1, source_target_pairs={{0,24},{8,16},{16,8},{24,0},{1,25},{9,17},{17,9},{25,1},{2,26},{10... | collective-permute-start | bytes 2359304 | tf_op jit(solution)/shard_map/ppermute | solution.py:50
  713.4 42.9 %collective-permute-start.71 = (bf16[256,1536]{1,0:T(8,128)(2,1)S(1)}, bf16[256,1536]{1,0:T(8,128)(2,1)S(1)}, u32[]{:S(2)}, u32[]{:S(2)}) collective-permute-start(bf16[256,1536]{1,0:T(8,128)(2,1)S(1)} %get-tuple-element.269), channel_id=1, source_target_pairs={{0,16},{8,24},{16,0},{24,8},{1,17},{9,25},{17,1},{25,9},{2,18},{10... | collective-permute-start | bytes 2359304 | tf_op jit(solution)/shard_map/ppermute | solution.py:50
  714.9 42.8 %collective-permute-start.70 = (bf16[256,1536]{1,0:T(8,128)(2,1)S(1)}, bf16[256,1536]{1,0:T(8,128)(2,1)}, u32[]{:S(2)}, u32[]{:S(2)}) collective-permute-start(bf16[256,1536]{1,0:T(8,128)(2,1)S(1)} %get-tuple-element.270), channel_id=1, source_target_pairs={{0,8},{8,0},{16,24},{24,16},{1,9},{9,1},{17,25},{25,17},{2,10},{10... | collective-permute-start | bytes 2359304 | tf_op jit(solution)/shard_map/ppermute | solution.py:50
  727.7 32.7 %collective-permute-start.58 = (bf16[4,256,512]{2,1,0:T(8,128)(2,1)S(1)}, bf16[4,256,512]{2,1,0:T(8,128)(2,1)S(1)}, u32[]{:S(2)}, u32[]{:S(2)}) collective-permute-start(bf16[4,256,512]{2,1,0:T(8,128)(2,1)S(1)} %pad_maximum_fusion.26), channel_id=1, source_target_pairs={{0,1},{1,0},{2,3},{3,2},{4,5},{5,4},{6,7},{7,6},{8,9},{9,8},{10,11... | collective-permute-start | bytes 3145736 | tf_op jit(solution)/shard_map/ppermute | solution.py:50
  742.3 63.5 %collective-permute-start.62 = (bf16[4,256,1024]{2,1,0:T(8,128)(2,1)S(1)}, bf16[4,256,1024]{2,1,0:T(8,128)(2,1)S(1)}, u32[]{:S(2)}, u32[]{:S(2)}) collective-permute-start(bf16[4,256,1024]{2,1,0:T(8,128)(2,1)S(1)} %pad_maximum_fusion.16), channel_id=1, source_target_pairs={{0,1},{1,0},{2,3},{3,2},{4,5},{5,4},{6,7},{7,6},{8,9},{9,8},{10,11... | collective-permute-start | bytes 6291464 | tf_op jit(solution)/shard_map/ppermute | solution.py:50
  759.6 74.0 %collective-permute-start.73 = (bf16[4,256,1536]{2,1,0:T(8,128)(2,1)S(1)}, bf16[4,256,1536]{2,1,0:T(8,128)(2,1)}, u32[]{:S(2)}, u32[]{:S(2)}) collective-permute-start(bf16[4,256,1536]{2,1,0:T(8,128)(2,1)S(1)} %pad_maximum_fusion.10.mine), channel_id=1, source_target_pairs={{0,1},{1,0},{2,3},{3,2},{4,5},{5,4},{6,7},{7,6},{8,9},{9,8},{10,11... | collective-permute-start | bytes 9437192 | tf_op jit(solution)/shard_map/ppermute | solution.py:50
  759.8 50.2 %collective-permute-start.69 = (bf16[256,2048]{1,0:T(8,128)(2,1)S(1)}, bf16[256,2048]{1,0:T(8,128)(2,1)S(1)}, u32[]{:S(2)}, u32[]{:S(2)}) collective-permute-start(bf16[256,2048]{1,0:T(8,128)(2,1)S(1)} %pad_maximum_fusion.29), channel_id=1, source_target_pairs={{0,16},{8,24},{16,0},{24,8},{1,17},{9,25},{17,1},{25,9},{2,18},{10... | collective-permute-start | bytes 3145736 | tf_op jit(solution)/shard_map/ppermute | solution.py:50
  763.2 33.4 %collective-permute-start.60 = (bf16[256,512]{1,0:T(8,128)(2,1)S(1)}, bf16[256,512]{1,0:T(8,128)(2,1)S(1)}, u32[]{:S(2)}, u32[]{:S(2)}) collective-permute-start(bf16[256,512]{1,0:T(8,128)(2,1)S(1)} %get-tuple-element.330), channel_id=1, source_target_pairs={{0,16},{8,24},{16,0},{24,8},{1,17},{9,25},{17,1},{25,9},{2,18},{10... | collective-permute-start | bytes 786440 | tf_op jit(solution)/shard_map/ppermute | solution.py:50
  770.3 40.2 %collective-permute-start.67 = (bf16[256,2048]{1,0:T(8,128)(2,1)S(1)}, bf16[256,2048]{1,0:T(8,128)(2,1)S(1)}, u32[]{:S(2)}, u32[]{:S(2)}) collective-permute-start(bf16[256,2048]{1,0:T(8,128)(2,1)S(1)} %pad_maximum_fusion.28), channel_id=1, source_target_pairs={{0,8},{8,0},{16,24},{24,16},{1,9},{9,1},{17,25},{25,17},{2,10},{10... | collective-permute-start | bytes 3145736 | tf_op jit(solution)/shard_map/ppermute | solution.py:50
  808.5 23.5 %collective-permute-start.64 = (bf16[256,1024]{1,0:T(8,128)(2,1)S(1)}, bf16[256,1024]{1,0:T(8,128)(2,1)S(1)}, u32[]{:S(2)}, u32[]{:S(2)}) collective-permute-start(bf16[256,1024]{1,0:T(8,128)(2,1)S(1)} %get-tuple-element.289), channel_id=1, source_target_pairs={{0,16},{8,24},{16,0},{24,8},{1,17},{9,25},{17,1},{25,9},{2,18},{10... | collective-permute-start | bytes 1572872 | tf_op jit(solution)/shard_map/ppermute | solution.py:50
  851.2 32.1 %collective-permute-start.74 = (bf16[128,2048]{1,0:T(8,128)(2,1)}, bf16[128,2048]{1,0:T(8,128)(2,1)}, u32[]{:S(2)}, u32[]{:S(2)}) collective-permute-start(bf16[128,2048]{1,0:T(8,128)(2,1)} %get-tuple-element.324), channel_id=1, source_target_pairs={{0,16},{8,24},{16,0},{24,8},{1,17},{9,25},{17,1},{25,9},{2,18},{10... | collective-permute-start | bytes 1572872 | tf_op jit(solution)/shard_map/ppermute | solution.py:50
  854.0 30.5 %collective-permute-start.85 = (bf16[256,1536]{1,0:T(8,128)(2,1)}, bf16[256,1536]{1,0:T(8,128)(2,1)}, u32[]{:S(2)}, u32[]{:S(2)}) collective-permute-start(bf16[256,1536]{1,0:T(8,128)(2,1)} %get-tuple-element.264), channel_id=1, source_target_pairs={{0,24},{8,16},{16,8},{24,0},{1,25},{9,17},{17,9},{25,1},{2,26},{10... | collective-permute-start | bytes 2359304 | tf_op jit(solution)/shard_map/ppermute | solution.py:50
  855.4 44.8 %collective-permute-start.84 = (bf16[256,1536]{1,0:T(8,128)(2,1)}, bf16[256,1536]{1,0:T(8,128)(2,1)}, u32[]{:S(2)}, u32[]{:S(2)}) collective-permute-start(bf16[256,1536]{1,0:T(8,128)(2,1)} %get-tuple-element.265), channel_id=1, source_target_pairs={{0,16},{8,24},{16,0},{24,8},{1,17},{9,25},{17,1},{25,9},{2,18},{10... | collective-permute-start | bytes 2359304 | tf_op jit(solution)/shard_map/ppermute | solution.py:50
  856.0 44.2 %collective-permute-start.83 = (bf16[256,1536]{1,0:T(8,128)(2,1)S(1)}, bf16[256,1536]{1,0:T(8,128)(2,1)}, u32[]{:S(2)}, u32[]{:S(2)}) collective-permute-start(bf16[256,1536]{1,0:T(8,128)(2,1)S(1)} %get-tuple-element.266), channel_id=1, source_target_pairs={{0,8},{8,0},{16,24},{24,16},{1,9},{9,1},{17,25},{25,17},{2,10},{10... | collective-permute-start | bytes 2359304 | tf_op jit(solution)/shard_map/ppermute | solution.py:50
  865.4 55.3 %collective-permute-start.77 = (bf16[256,2048]{1,0:T(8,128)(2,1)S(1)}, bf16[256,2048]{1,0:T(8,128)(2,1)S(1)}, u32[]{:S(2)}, u32[]{:S(2)}) collective-permute-start(bf16[256,2048]{1,0:T(8,128)(2,1)S(1)} %pad_maximum_fusion.31), channel_id=1, source_target_pairs={{0,16},{8,24},{16,0},{24,8},{1,17},{9,25},{17,1},{25,9},{2,18},{10... | collective-permute-start | bytes 3145736 | tf_op jit(solution)/shard_map/ppermute | solution.py:50
  902.4 50.6 %collective-permute-start.86 = (bf16[4,256,1536]{2,1,0:T(8,128)(2,1)S(1)}, bf16[4,256,1536]{2,1,0:T(8,128)(2,1)}, u32[]{:S(2)}, u32[]{:S(2)}) collective-permute-start(bf16[4,256,1536]{2,1,0:T(8,128)(2,1)S(1)} %pad_maximum_fusion.11.mine), channel_id=1, source_target_pairs={{0,1},{1,0},{2,3},{3,2},{4,5},{5,4},{6,7},{7,6},{8,9},{9,8},{10,11... | collective-permute-start | bytes 9437192 | tf_op jit(solution)/shard_map/ppermute | solution.py:50
  902.5 25.6 %collective-permute-start.75 = (bf16[256,2048]{1,0:T(8,128)(2,1)S(1)}, bf16[256,2048]{1,0:T(8,128)(2,1)S(1)}, u32[]{:S(2)}, u32[]{:S(2)}) collective-permute-start(bf16[256,2048]{1,0:T(8,128)(2,1)S(1)} %pad_maximum_fusion.30), channel_id=1, source_target_pairs={{0,8},{8,0},{16,24},{24,16},{1,9},{9,1},{17,25},{25,17},{2,10},{10... | collective-permute-start | bytes 3145736 | tf_op jit(solution)/shard_map/ppermute | solution.py:50
  (174 other events, 1948.7 us)
Sparse Core Ops, SparseCore 0:
  401.7 121.3 all-reduce.5
  538.1 119.1 all-reduce.7
  704.8 120.0 all-reduce.9
  857.6 120.4 all-reduce.11

commit v3 on v2

v3 whole, which is shorter than its diff:
```python
import math

import jax
import jax.numpy as jnp
from jax import lax
from jax.experimental import pallas as pl
from jax.experimental.layout import Layout, with_layout_constraint
from jax.experimental.pallas import tpu as pltpu
from jax.sharding import Mesh
from jax.sharding import PartitionSpec as P

HEADS = 16
KV_HEADS = 8
HEAD = 128
GROUP = HEADS // KV_HEADS

epsilon = 1e-06
rope_base = 1000000.0
masked_score = -1e30
score_scale = 1.0 / math.sqrt(HEAD)

bf16 = jnp.bfloat16
f32 = jnp.float32


def matmul(first, second):
    return jnp.dot(first, second, preferred_element_type=f32)


def matmul_tn(first, second):
    return lax.dot_general(first, second, (((0,), (0,)), ((), ())), preferred_element_type=f32)


def matmul_nt(first, second):
    return lax.dot_general(first, second, (((1,), (1,)), ((), ())), preferred_element_type=f32)


def rms_scale(vector):
    return lax.rsqrt(jnp.mean(vector * vector, axis=-1, keepdims=True) + epsilon)


def norm_back(vector, scale, gain, incoming):
    scaled = gain * incoming
    d_vector = scale * scaled - vector * (scale**3) * jnp.mean(
        vector * scaled, axis=-1, keepdims=True
    )
    return d_vector, incoming * vector * scale


def swap(value, axis, k):
    return lax.ppermute(value, axis, [(j, j ^ k) for j in range(lax.axis_size(axis))])


def core_swap(value):
    return swap(value, "core", 1)


def rows_of(value, start, size):
    return lax.dynamic_slice_in_dim(value, start, size, axis=0)


def fence(*trees):
    leaves, shape = jax.tree.flatten(trees)
    return jax.tree.unflatten(shape, lax.optimization_barrier(leaves))


def block_of_work(whole, body):
    shapes = jax.eval_shape(body)
    return lax.cond(
        whole,
        body,
        lambda: jax.tree.map(lambda leaf: jnp.zeros(leaf.shape, leaf.dtype), shapes),
    )


def gather_begin(shard):
    n = lax.axis_size("fsdp")
    if n == 4:
        return [swap(shard, "fsdp", 1), swap(shard, "fsdp", 2)]
    return [swap(shard, "fsdp", k) for k in range(1, n)]


def gather_end(shard, begun):
    if lax.axis_size("fsdp") != 4:
        return [shard] + begun
    half = shard.shape[0] // 2
    first = swap(begun[0][:half], "fsdp", 2)
    second = swap(begun[1][half:], "fsdp", 1)
    return [shard] + begun + [jnp.concatenate([first, second], axis=0)]


def scatter_begin(far):
    n = lax.axis_size("fsdp")
    if n == 4:
        half = far.shape[0] // 2
        return [swap(far[:half], "fsdp", 1), swap(far[half:], "fsdp", 2)]
    return [swap(far, "fsdp", n - 1)]


def scatter_middle(near, begun):
    n = lax.axis_size("fsdp")
    if n != 4:
        return begun + [swap(block, "fsdp", k + 1) for k, block in enumerate(near)]
    near_x, near_y = near
    first, second = begun
    half = first.shape[0]
    low = (near_x[half:].astype(f32) + second.astype(f32)).astype(bf16)
    top = (near_y[:half].astype(f32) + first.astype(f32)).astype(bf16)
    return [
        swap(jnp.concatenate([near_x[:half], low], axis=0), "fsdp", 1),
        swap(jnp.concatenate([top, near_y[half:]], axis=0), "fsdp", 2),
    ]


def scatter_end(own, got):
    total = own.astype(f32)
    for block in got:
        total = total + block.astype(f32)
    return total


def gather_direct(shard):
    n = lax.axis_size("fsdp")
    return [shard] + [swap(shard, "fsdp", k) for k in range(1, n)]


def scatter_direct(block_of):
    n = lax.axis_size("fsdp")
    got = {k: swap(block_of(k), "fsdp", k) for k in range(n - 1, 0, -1)}
    return [block_of(0)] + [got[k] for k in range(1, n)]


def add_up(blocks):
    return scatter_end(blocks[0], blocks[1:])


def assemble(shape, sources, pieces):
    count, held = len(pieces), len(sources)

    def kernel(place_ref, *refs):
        ins, out, hold = refs[:held], refs[held], refs[held + 1]
        sem_in, sem_out = refs[held + 2], refs[held + 3]

        def window(ref, k, first):
            size = pieces[k][2]
            row = pl.multiple_of(place_ref[4 * k + first], 16)
            column = pl.multiple_of(place_ref[4 * k + first + 1], 128)
            return ref.at[pl.ds(row, size[0]), pl.ds(column, size[1])]

        def source(k):
            ref, lead = ins[pieces[k][0]], pieces[k][1]
            return window(ref if lead is None else ref.at[lead], k, 0)

        loads = [
            pltpu.make_async_copy(source(k), window(hold, k, 2), sem_in.at[k])
            for k in range(count)
        ]
        stores = [
            pltpu.make_async_copy(window(hold, k, 2), window(out, k, 2), sem_out.at[k])
            for k in range(count)
        ]
        for load in loads:
            load.start()
        for load, store in zip(loads, stores):
            load.wait()
            store.start()
        for store in stores:
            store.wait()

    size = 2 * math.prod(shape)
    places = [jnp.int32(v) for piece in pieces for at in piece[3:] for v in at]
    return pl.pallas_call(
        kernel,
        out_shape=jax.ShapeDtypeStruct(shape, bf16),
        in_specs=[pl.BlockSpec(memory_space=pltpu.SMEM)]
        + [
            pl.BlockSpec(memory_space=pl.ANY if source.ndim == 3 else pltpu.HBM)
            for source in sources
        ],
        out_specs=pl.BlockSpec(memory_space=pl.ANY),
        scratch_shapes=[
            pltpu.VMEM(shape, bf16),
            pltpu.SemaphoreType.DMA((count,)),
            pltpu.SemaphoreType.DMA((count,)),
        ],
        compiler_params=pltpu.CompilerParams(vmem_limit_bytes=size + (4 << 20)),
        cost_estimate=pl.CostEstimate(flops=0, bytes_accessed=2 * size, transcendentals=0),
        name="assemble",
    )(jnp.stack(places), *sources)


class Spread:
    def __init__(self, by_rows, by_columns, along_z=True):
        self.by_rows, self.by_columns, self.along_z = by_rows, by_columns, along_z
        self.shares = 4 if along_z else 2

    def share(self, j, q):
        n = lax.axis_size("fsdp")
        cuts = []
        for part in self.by_rows:
            size, width = part.shape[0] // self.shares, part.shape[1] // n
            cuts.append(lax.dynamic_slice(part, (q * size, j * width), (size, width)))
        for part in self.by_columns:
            rows = part.shape[0] // n
            size = rows // self.shares
            cuts.append(rows_of(part, j * rows + q * size, size))
        return cuts[0] if len(cuts) == 1 else jnp.concatenate(cuts, axis=1)

    def begin(self):
        n, me = lax.axis_size("fsdp"), lax.axis_index("fsdp")
        mine = lax.axis_index("core")
        if self.along_z:
            mine = 2 * (lax.axis_index("z") % 2) + mine
        return [swap(self.share(me ^ k, mine), "fsdp", k) for k in range(1, n)]

    def pieces(self, sources):
        n, me = lax.axis_size("fsdp"), lax.axis_index("fsdp")
        side, core = lax.axis_index("z") % 2, lax.axis_index("core")
        shares = [core, 1 - core]
        if self.along_z:
            shares = [
                2 * side + core,
                2 * (1 - side) + core,
                2 * side + 1 - core,
                2 * (1 - side) + 1 - core,
            ]
        return [
            (source, k, me ^ k, shares[source])
            for k in range(1, n)
            for source in range(len(sources))
        ]

    def join_rows(self, sources):
        n, me = lax.axis_size("fsdp"), lax.axis_index("fsdp")
        rows = self.by_rows[0].shape[0]
        widths = [part.shape[1] // n for part in self.by_rows]
        total, size = sum(widths), rows // self.shares
        pieces = [
            (source, k - 1, (size, total), (0, 0), (j * rows + q * size, 0))
            for source, k, j, q in self.pieces(sources)
        ]
        start = 0
        for index, width in enumerate(widths):
            pieces.append(
                (len(sources) + index, None, (rows, width), (0, me * width), (me * rows, start))
            )
            start += width
        return assemble((n * rows, total), [*sources, *self.by_rows], pieces)

    def join_columns(self, sources):
        n, me = lax.axis_size("fsdp"), lax.axis_index("fsdp")
        start = sum(part.shape[1] // n for part in self.by_rows)
        (part,) = self.by_columns
        rows, width = part.shape[0] // n, part.shape[1]
        size = rows // self.shares
        pieces = [
            (source, k - 1, (size, width), (0, start), (q * size, j * width))
            for source, k, j, q in self.pieces(sources)
        ]
        pieces.append((len(sources), None, (rows, width), (me * rows, 0), (0, me * width)))
        return assemble((rows, n * width), [*sources, part], pieces)


class Reduction:
    def __init__(self, grad):
        self.grad = grad
        self.other = None

    def take(self, c):
        n, me = lax.axis_size("fsdp"), lax.axis_index("fsdp")
        rows, width = self.grad.shape[1:]
        return jnp.concatenate(
            [
                lax.dynamic_slice(
                    self.grad, (me ^ k, c * (rows // 2), 0), (1, rows // 2, width)
                )
                for k in range(n)
            ]
        )

    def begin(self):
        core = lax.axis_index("core")
        both = self.take(core).astype(f32) + core_swap(self.take(1 - core)).astype(f32)
        self.half = both.astype(bf16)

    def exchange(self):
        n = lax.axis_size("fsdp")
        self.half = jnp.stack(
            [self.half[0]] + [swap(self.half[k], "fsdp", k) for k in range(1, n)]
        )

    def finish(self, by_rows, start=0, size=None):
        n, me = lax.axis_size("fsdp"), lax.axis_index("fsdp")
        core = lax.axis_index("core")
        if self.other is None:
            self.other = core_swap(self.half)
        rows, width = self.half.shape[1:]
        size = width if size is None else size
        column = start // size

        def kernel(place, mine, other, out):
            @pl.when(pl.program_id(0) == 0)
            def _():
                out[...] = mine[0].astype(f32)

            @pl.when(pl.program_id(0) == 1)
            def _():
                out[...] = other[0].astype(f32)

        def mine_at(w, k, place):
            return (jnp.where(w == 0, k, n - 1), 0, column)

        def other_at(w, k, place):
            return (jnp.where(w == 0, 0, k), 0, column)

        def out_at(w, k, place):
            source = place[0] ^ k
            side = jnp.where(w == 0, place[1], 1 - place[1])
            return (side, source) if by_rows else (source * 2 + side, 0)

        return pl.pallas_call(
            kernel,
            out_shape=jax.ShapeDtypeStruct(
                (2 * rows, n * size) if by_rows else (2 * n * rows, size), f32
            ),
            grid_spec=pltpu.PrefetchScalarGridSpec(
                num_scalar_prefetch=1,
                grid=(2, n),
                in_specs=[
                    pl.BlockSpec((1, rows, size), mine_at),
                    pl.BlockSpec((1, rows, size), other_at),
                ],
                out_specs=pl.BlockSpec((rows, size), out_at),
            ),
            compiler_params=pltpu.CompilerParams(vmem_limit_bytes=32 << 20),
            cost_estimate=pl.CostEstimate(
                flops=0, bytes_accessed=2 * n * rows * size * 40, transcendentals=0
            ),
            name="place",
        )(jnp.stack([me, core]).astype(jnp.int32), self.half, self.other)


def roll_half(value):
    return pltpu.roll(value, HEAD // 2, axis=1)


def attention_specs(length, heads, kv_heads):
    wide, tall = GROUP * HEAD, heads
    return dict(
        queries=pl.BlockSpec((length, wide), lambda g, me: (0, g)),
        head=pl.BlockSpec((length, HEAD), lambda g, me: (0, g)),
        keys_in=pl.BlockSpec((length, HEAD), lambda g, me: (0, tall + g)),
        values_in=pl.BlockSpec((length, HEAD), lambda g, me: (0, tall + kv_heads + g)),
        table=pl.BlockSpec((length, HEAD), lambda g, me: (0, 0)),
        gain=pl.BlockSpec((1, HEAD), lambda g, me: (0, 0)),
        gain_out=pl.BlockSpec((1, 1, HEAD), lambda g, me: (g, 0, 0)),
    )


def attention_forward(qkv, cos_table, sin_table, gain_query, gain_key, first, heads, kv_heads):
    length = qkv.shape[0]
    n, _, size = first.shape

    def kernel(
        me_ref, q_ref, k_ref, v_ref, cos_ref, sin_ref, qg_ref, kg_ref, first_ref,
        queries_ref, keys_ref, values_ref, attended_ref, lse_ref, vt_ref,
    ):
        me = me_ref[0]

        def rows(block):
            return pl.ds(pl.multiple_of((block ^ me) * size, size), size)

        def prepare(raw, gain):
            normed = raw * rms_scale(raw) * gain
            return (normed * cos_ref[...] + roll_half(normed) * sin_ref[...]).astype(bf16)

        keys_ref[...] = prepare(k_ref[...], kg_ref[...])
        values_ref[...] = v_ref[...].astype(bf16)
        for k in range(n):
            vt_ref[k] = v_ref[k * size : (k + 1) * size, :].T.astype(bf16)
        for h in range(GROUP):
            columns = slice(h * HEAD, (h + 1) * HEAD)
            queries_ref[:, columns] = prepare(q_ref[:, columns], qg_ref[...])
        inside = lax.broadcasted_iota(jnp.int32, (size, size), 0) <= lax.broadcasted_iota(
            jnp.int32, (size, size), 1
        )
        place = lax.broadcasted_iota(jnp.int32, (size, size), 0)
        for h in range(GROUP):
            columns = slice(h * HEAD, (h + 1) * HEAD)
            for i in range(n):
                query = queries_ref[rows(i), columns]
                begin = first_ref[i ^ me]
                total = jnp.zeros((1, size), f32)
                out = jnp.zeros((HEAD, size), f32)
                for j in range(i + 1):
                    scores = matmul_nt(keys_ref[rows(j), :], query) * score_scale
                    allowed = place >= begin - j * size
                    if i == j:
                        allowed = allowed & inside
                    weight = jnp.where(allowed, jnp.exp(scores), 0.0)
                    total = total + jnp.sum(weight, axis=0, keepdims=True)
                    out = out + matmul(vt_ref[j ^ me], weight.astype(bf16))
                attended_ref[rows(i), columns] = (out / total).T.astype(bf16)
                lse_ref[0, h, i ^ me] = jnp.log(total)

    spec = attention_specs(length, heads, kv_heads)
    me = lax.axis_index("fsdp").reshape(1).astype(jnp.int32)
    return pl.pallas_call(
        kernel,
        out_shape=[
            jax.ShapeDtypeStruct((length, heads * HEAD), bf16),
            jax.ShapeDtypeStruct((length, kv_heads * HEAD), bf16),
            jax.ShapeDtypeStruct((length, kv_heads * HEAD), bf16),
            jax.ShapeDtypeStruct((length, heads * HEAD), bf16),
            jax.ShapeDtypeStruct((kv_heads, GROUP, n, 1, size), f32),
        ],
        grid_spec=pltpu.PrefetchScalarGridSpec(
            num_scalar_prefetch=1,
            grid=(kv_heads,),
            in_specs=[
                spec["queries"],
                spec["keys_in"],
                spec["values_in"],
                spec["table"],
                spec["table"],
                spec["gain"],
                spec["gain"],
                pl.BlockSpec((n, 1, size), lambda g, me: (0, 0, 0)),
            ],
            out_specs=[
                spec["queries"],
                spec["head"],
                spec["head"],
                spec["queries"],
                pl.BlockSpec((1, GROUP, n, 1, size), lambda g, me: (g, 0, 0, 0, 0)),
            ],
            scratch_shapes=[pltpu.VMEM((n, HEAD, size), bf16)],
        ),
        compiler_params=pltpu.CompilerParams(vmem_limit_bytes=48 << 20),
        cost_estimate=pl.CostEstimate(
            flops=4 * heads * length * length * HEAD,
            bytes_accessed=12 * length * heads * HEAD,
            transcendentals=heads * length * length,
        ),
        name="attention_forward",
    )(me, qkv, qkv, qkv, cos_table, sin_table, gain_query[None], gain_key[None], first)


def attention_backward(
    qkv, queries, keys, values, lse, d_attended, cos_table, sin_table, gain_query, gain_key, first
):
    length = qkv.shape[0]
    n, _, size = first.shape
    heads, kv_heads = queries.shape[1] // HEAD, keys.shape[1] // HEAD

    def kernel(
        me_ref, qr_ref, kr_ref, q_ref, k_ref, v_ref, lse_ref, da_ref, cos_ref, sin_ref,
        qg_ref, kg_ref, first_ref, dq_ref, dk_ref, dv_ref, dqg_ref, dkg_ref,
        kt_ref, probs_ref, dp_ref, dq_acc, dk_acc, dv_acc,
    ):
        me = me_ref[0]

        def rows(block):
            return pl.ds(pl.multiple_of((block ^ me) * size, size), size)

        def finish(raw, gain, incoming):
            turned = incoming * cos_ref[...] - roll_half(incoming) * sin_ref[...]
            d_raw, d_gain = norm_back(raw, rms_scale(raw), gain, turned)
            return d_raw.astype(bf16), jnp.sum(d_gain, axis=0, keepdims=True)

        for k in range(n):
            part = k_ref[k * size : (k + 1) * size, :].astype(f32)
            kt_ref[k] = part.T.astype(bf16)
        dk_acc[...] = jnp.zeros_like(dk_acc)
        dv_acc[...] = jnp.zeros_like(dv_acc)
        inside = lax.broadcasted_iota(jnp.int32, (size, size), 0) <= lax.broadcasted_iota(
            jnp.int32, (size, size), 1
        )
        place = lax.broadcasted_iota(jnp.int32, (size, size), 0)
        gain_total = jnp.zeros((1, HEAD), f32)
        for h in range(GROUP):
            columns = slice(h * HEAD, (h + 1) * HEAD)
            for i in range(n):
                query, d_out = q_ref[rows(i), columns], da_ref[rows(i), columns]
                begin, shift = first_ref[i ^ me], lse_ref[0, h, i ^ me]
                dots = jnp.zeros((1, size), f32)
                for j in range(i + 1):
                    scores = matmul_nt(k_ref[rows(j), :], query) * score_scale
                    allowed = place >= begin - j * size
                    if i == j:
                        allowed = allowed & inside
                    probs = jnp.where(allowed, jnp.exp(scores - shift), 0.0)
                    d_probs = matmul_nt(v_ref[rows(j), :], d_out)
                    dots = dots + jnp.sum(probs * d_probs, axis=0, keepdims=True)
                    probs_ref[j] = probs
                    dp_ref[j] = d_probs
                d_query = jnp.zeros((HEAD, size), f32)
                for j in range(i + 1):
                    probs = probs_ref[j]
                    d_scores = (probs * (dp_ref[j] - dots)).astype(bf16)
                    d_query = d_query + matmul(kt_ref[j ^ me], d_scores)
                    dk_acc[rows(j), :] += matmul(d_scores, query)
                    dv_acc[rows(j), :] += matmul(probs.astype(bf16), d_out)
                dq_acc[rows(i), :] = d_query.T * score_scale
            d_raw, d_gain = finish(qr_ref[:, columns], qg_ref[...], dq_acc[...])
            dq_ref[:, columns] = d_raw
            gain_total = gain_total + d_gain
        dqg_ref[0] = gain_total
        d_raw, d_gain = finish(kr_ref[...], kg_ref[...], dk_acc[...] * score_scale)
        dk_ref[...] = d_raw
        dkg_ref[0] = d_gain
        dv_ref[...] = dv_acc[...].astype(bf16)

    spec = attention_specs(length, heads, kv_heads)
    me = lax.axis_index("fsdp").reshape(1).astype(jnp.int32)
    d_query, d_key, d_value, d_query_gain, d_key_gain = pl.pallas_call(
        kernel,
        out_shape=[
            jax.ShapeDtypeStruct((length, heads * HEAD), bf16),
            jax.ShapeDtypeStruct((length, kv_heads * HEAD), bf16),
            jax.ShapeDtypeStruct((length, kv_heads * HEAD), bf16),
            jax.ShapeDtypeStruct((kv_heads, 1, HEAD), f32),
            jax.ShapeDtypeStruct((kv_heads, 1, HEAD), f32),
        ],
        grid_spec=pltpu.PrefetchScalarGridSpec(
            num_scalar_prefetch=1,
            grid=(kv_heads,),
            in_specs=[
                spec["queries"],
                spec["keys_in"],
                spec["queries"],
                spec["head"],
                spec["head"],
                pl.BlockSpec((1, GROUP, n, 1, size), lambda g, me: (g, 0, 0, 0, 0)),
                spec["queries"],
                spec["table"],
                spec["table"],
                spec["gain"],
                spec["gain"],
                pl.BlockSpec((n, 1, size), lambda g, me: (0, 0, 0)),
            ],
            out_specs=[
                spec["queries"],
                spec["head"],
                spec["head"],
                spec["gain_out"],
                spec["gain_out"],
            ],
            scratch_shapes=[
                pltpu.VMEM((n, HEAD, size), bf16),
                pltpu.VMEM((n, size, size), f32),
                pltpu.VMEM((n, size, size), f32),
                pltpu.VMEM((length, HEAD), f32),
                pltpu.VMEM((length, HEAD), f32),
                pltpu.VMEM((length, HEAD), f32),
            ],
        ),
        compiler_params=pltpu.CompilerParams(vmem_limit_bytes=48 << 20),
        cost_estimate=pl.CostEstimate(
            flops=10 * heads * length * length * HEAD,
            bytes_accessed=20 * length * heads * HEAD,
            transcendentals=heads * length * length,
        ),
        name="attention_backward",
    )(
        me, qkv, qkv, queries, keys, values, lse, d_attended, cos_table, sin_table,
        gain_query[None], gain_key[None], first,
    )
    return (
        jnp.concatenate([d_query, d_key, d_value], axis=1),
        jnp.sum(d_query_gain, axis=(0, 1)),
        jnp.sum(d_key_gain, axis=(0, 1)),
    )


def feed_forward_backward(cot, gate_up_parts, full_down, full_gu):
    n = len(gate_up_parts)
    length, width = cot.shape
    size = length // n
    ff = full_down.shape[0]
    step = 512 if ff % 512 == 0 else 256
    steps = ff // step

    def kernel(cot_ref, *refs):
        gates, ups = refs[:n], refs[n : 2 * n]
        down, wg, wu, d_gate_ref, d_up_ref, out_ref, total, d_hidden_ref = refs[2 * n :]
        f = pl.program_id(0)
        d_hidden_ref[...] = matmul_nt(cot_ref[...], down[...])
        for k in range(n):
            rows = slice(k * size, (k + 1) * size)
            d_hidden = d_hidden_ref[rows, :]
            gate, up = gates[k][...], ups[k][...]
            sg = 1.0 / (1.0 + jnp.exp(-gate))
            d_gate_ref[rows, :] = (d_hidden * up * sg * (1.0 + gate * (1.0 - sg))).astype(bf16)
            d_up_ref[rows, :] = (d_hidden * gate * sg).astype(bf16)

        @pl.when(f == 0)
        def _():
            total[...] = matmul_nt(d_gate_ref[...], wg[...])

        @pl.when(f > 0)
        def _():
            total[...] += matmul_nt(d_gate_ref[...], wg[...])

        @pl.when(f < steps - 1)
        def _():
            total[...] += matmul_nt(d_up_ref[...], wu[...])

        @pl.when(f == steps - 1)
        def _():
            out_ref[...] = (total[...] + matmul_nt(d_up_ref[...], wu[...])).astype(bf16)

    once = pl.Buffered(1)
    return pl.pallas_call(
        kernel,
        out_shape=[
            jax.ShapeDtypeStruct((length, ff), bf16),
            jax.ShapeDtypeStruct((length, ff), bf16),
            jax.ShapeDtypeStruct((length, width), bf16),
        ],
        grid=(steps,),
        in_specs=[pl.BlockSpec((length, width), lambda f: (0, 0), pipeline_mode=once)]
        + [pl.BlockSpec((size, step), lambda f: (0, f))] * n
        + [pl.BlockSpec((size, step), lambda f: (0, steps + f))] * n
        + [
            pl.BlockSpec((step, width), lambda f: (f, 0)),
            pl.BlockSpec((width, step), lambda f: (0, f)),
            pl.BlockSpec((width, step), lambda f: (0, steps + f)),
        ],
        out_specs=[
            pl.BlockSpec((length, step), lambda f: (0, f)),
            pl.BlockSpec((length, step), lambda f: (0, f)),
            pl.BlockSpec((length, width), lambda f: (0, 0), pipeline_mode=once),
        ],
        scratch_shapes=[pltpu.VMEM((length, width), f32), pltpu.VMEM((length, step), f32)],
        compiler_params=pltpu.CompilerParams(vmem_limit_bytes=60 << 20),
        cost_estimate=pl.CostEstimate(
            flops=6 * length * ff * width,
            bytes_accessed=6 * ff * width,
            transcendentals=length * ff,
        ),
        name="feed_forward_backward",
    )(cot, *gate_up_parts, *gate_up_parts, full_down, full_gu, full_gu)


def on_device(
    tokens,
    segments,
    attn_gain,
    w_query,
    w_key,
    w_value,
    query_gain,
    key_gain,
    w_out,
    mlp_gain,
    w_gate,
    w_up,
    w_down,
    cotangent,
):
    n, me = lax.axis_size("fsdp"), lax.axis_index("fsdp")
    tok_rows, width = tokens.shape[1], tokens.shape[2]
    length = segments.shape[1]
    heads, kv_heads = HEADS // n, KV_HEADS // n
    q_width, kv_width = heads * HEAD, kv_heads * HEAD
    ff = w_gate.shape[1] // n
    rows = width // n

    def block(value, k):
        return value[k * tok_rows : (k + 1) * tok_rows]

    def by_columns(first, second):
        columns = second.shape[1] // n
        return jnp.stack(
            [
                matmul_tn(first, second[:, j * columns : (j + 1) * columns]).astype(bf16)
                for j in range(n)
            ]
        )

    def by_rows(first, second):
        grad = with_layout_constraint(
            matmul_tn(first, second).astype(bf16), Layout(major_to_minor=(0, 1))
        )
        return grad.reshape(n, rows, second.shape[1])

    sizes = [attn_gain.shape[0], mlp_gain.shape[0], query_gain.shape[0], key_gain.shape[0]]
    packed = jnp.concatenate([attn_gain, mlp_gain, query_gain, key_gain])[None]
    tok = gather_begin(tokens[0])
    gains = [packed] + [swap(packed, "fsdp", k) for k in range(1, n)]
    attn_spread = Spread([w_query, w_key, w_value], [w_out])
    attn_got = attn_spread.begin()
    index = jnp.concatenate(
        [(me ^ k) * tok_rows + jnp.arange(tok_rows, dtype=jnp.int32) for k in range(n)]
    )
    doc_ids = jnp.concatenate(
        [rows_of(segments[0], (me ^ k) * tok_rows, tok_rows) for k in range(n)]
    )
    earlier = jnp.sum((doc_ids[None, :] < doc_ids[:, None]).astype(jnp.int32), axis=1)
    position = index - earlier
    inverse = rope_base ** (-2.0 * jnp.arange(HEAD // 2).astype(f32) / HEAD)
    angles = position.astype(f32)[:, None] * inverse[None, :]
    cosine, sine = jnp.cos(angles), jnp.sin(angles)
    cos_table = jnp.concatenate([cosine, cosine], axis=1)
    sin_table = jnp.concatenate([-sine, sine], axis=1)
    first = earlier.reshape(n, 1, tok_rows)
    gains = jnp.concatenate(gains, axis=0)
    gains = jnp.concatenate(
        [lax.dynamic_slice_in_dim(gains, me ^ j, 1, axis=0) for j in range(n)], axis=0
    ).astype(f32)
    ends = [sum(sizes[: j + 1]) for j in range(4)]
    gain_attn = gains[:, : ends[0]].reshape(-1)
    gain_mlp = gains[:, ends[0] : ends[1]].reshape(-1)
    gain_query = gains[:, ends[1] : ends[2]].reshape(-1)
    gain_key = gains[:, ends[2] : ends[3]].reshape(-1)
    attn_got = jnp.stack(attn_got)
    tok, attn_got, cos_table, sin_table, first, w_gate, w_up = fence(
        tok, attn_got, cos_table, sin_table, first, w_gate, w_up
    )

    tok = gather_end(tokens[0], tok)
    attn_along, attn_across = swap(attn_got, "z", 1), core_swap(attn_got)
    gu_spread = Spread([w_gate, w_up], [])
    gu_got = gu_spread.begin()
    tok, attn_along, attn_across = fence(tok, attn_along, attn_across)

    attn_sources = [attn_got, attn_along, attn_across, core_swap(attn_along)]
    stream_all = jnp.concatenate(tok, axis=0).astype(f32)
    normed = (stream_all * rms_scale(stream_all) * gain_attn).astype(bf16)
    full_qkv = attn_spread.join_rows(attn_sources)
    qkv = matmul(normed, full_qkv)
    queries, keys, values, attended, lse = attention_forward(
        qkv, cos_table, sin_table, gain_query, gain_key, first, heads, kv_heads
    )
    full_out = attn_spread.join_columns(attn_sources)
    attended, full_out, gu_got, cotangent = fence(attended, full_out, gu_got, cotangent)
    cot = cotangent[0]

    gu_got = jnp.stack(gu_got)
    gu_along, gu_across = swap(gu_got, "z", 1), core_swap(gu_got)
    begun = scatter_begin(matmul(block(attended, n - 1), full_out).astype(bf16))
    parts = [matmul(block(attended, k), full_out).astype(bf16) for k in range(n - 1)]
    stream = tokens[0].astype(f32)
    middle = stream + scatter_end(parts[0], scatter_middle(parts[1:], begun))
    mlp_scale = rms_scale(middle)
    normed_mine = (middle * mlp_scale * gain_mlp).astype(bf16)
    middle, mlp_scale, normed_mine = fence(middle, mlp_scale, normed_mine)

    begun = gather_begin(normed_mine)
    begun, gu_along, gu_across = fence(begun, gu_along, gu_across)

    def gate_and_up(part):
        both = matmul(part, full_gu)
        gate, up = both[:, :ff], both[:, ff:]
        return both, (gate / (1.0 + jnp.exp(-gate)) * up).astype(bf16)

    normed_parts = gather_end(normed_mine, begun)
    full_gu = gu_spread.join_rows([gu_got, gu_along, gu_across, core_swap(gu_along)])
    normed_parts, full_gu, cot, w_down = fence(normed_parts, full_gu, cot, w_down)

    cot_begun = gather_begin(cot)
    acts = [gate_and_up(part) for part in normed_parts]
    normed_mlp = jnp.concatenate(normed_parts, axis=0)
    hidden = jnp.concatenate([act[1] for act in acts], axis=0)
    cot_begun, acts, normed_mlp, hidden, w_down = fence(
        cot_begun, acts, normed_mlp, hidden, w_down
    )

    cot_parts = gather_end(cot, cot_begun)
    cot_all = jnp.concatenate(cot_parts, axis=0)
    cot_all, w_down = fence(cot_all, w_down)
    down = Reduction(by_columns(hidden, cot_all))
    down.begin()
    down.half, cot_all, w_down = fence(down.half, cot_all, w_down)

    whole = segments[0, 0] == 0

    def feed_forward_part():
        down_spread = Spread([], [w_down], along_z=False)
        got = jnp.stack(down_spread.begin())
        full_down = down_spread.join_columns([got, core_swap(got)])
        d_gate, d_up, d_normed_mlp = feed_forward_backward(
            cot_all, [act[0] for act in acts], full_down, full_gu
        )
        gate = Reduction(by_rows(normed_mlp, d_gate))
        gate.begin()
        gate.exchange()
        up = Reduction(by_rows(normed_mlp, d_up))
        up.begin()
        return full_down, d_normed_mlp, gate.half, up.half

    down.half = lax.psum(down.half, "z")
    full_down, d_normed_mlp, gate_half, up_half = block_of_work(whole, feed_forward_part)
    down.half, full_down, d_normed_mlp, gate_half, up_half = fence(
        down.half, full_down, d_normed_mlp, gate_half, up_half
    )

    def attention_part():
        begun = scatter_begin(block(d_normed_mlp, n - 1))
        got = scatter_middle([block(d_normed_mlp, k) for k in range(1, n - 1)], begun)
        d_normed_mine = scatter_end(block(d_normed_mlp, 0), got)
        d_middle, mlp_gain_rows = norm_back(middle, mlp_scale, gain_mlp, d_normed_mine)
        mlp_gain_grad = jnp.sum(mlp_gain_rows, axis=0)
        d_middle = cot.astype(f32) + d_middle
        d_mine = d_middle.astype(bf16)
        out_parts = [matmul(block(hidden, k), full_down).astype(bf16) for k in range(n)]
        d_branch = jnp.concatenate(gather_end(d_mine, gather_begin(d_mine)), axis=0)
        d_attended = matmul_nt(d_branch, full_out).astype(bf16)
        d_attended, down_half, out_parts = fence(d_attended, down.half, out_parts)
        d_qkv, *head_gain_grads = attention_backward(
            qkv,
            queries,
            keys,
            values,
            lse,
            d_attended,
            cos_table,
            sin_table,
            gain_query,
            gain_key,
            first,
        )
        out_sum = Reduction(by_columns(attended, d_branch))
        out_sum.begin()
        out_sum.exchange()
        qkv_sum = Reduction(by_rows(normed, d_qkv))
        qkv_sum.begin()
        qkv_sum.exchange()
        out_got = scatter_middle(out_parts[1 : n - 1], scatter_begin(out_parts[n - 1]))
        output = (middle + scatter_end(out_parts[0], out_got)).astype(bf16)
        down_sum = Reduction(None)
        down_sum.half = down_half
        down_sum.exchange()
        return (
            d_middle,
            mlp_gain_grad,
            d_qkv,
            head_gain_grads,
            out_sum.half,
            qkv_sum.half,
            output,
            down_sum.finish(False),
        )

    gate_half, up_half = lax.psum((gate_half, up_half), "z")
    gate_half, up_half, done = fence(gate_half, up_half, block_of_work(whole, attention_part))
    d_middle, mlp_gain_grad, d_qkv, head_gain_grads, out_half, qkv_half, output, down_full = done

    def input_part():
        begun = scatter_begin(matmul_nt(block(d_qkv, n - 1), full_qkv).astype(bf16))
        parts = [matmul_nt(block(d_qkv, k), full_qkv).astype(bf16) for k in range(n - 1)]
        d_normed = scatter_end(parts[0], scatter_middle(parts[1:], begun))
        d_stream, attn_gain_rows = norm_back(stream, rms_scale(stream), gain_attn, d_normed)
        gain_grads = jnp.concatenate(
            [jnp.sum(attn_gain_rows, axis=0), mlp_gain_grad] + head_gain_grads
        )
        for axis in ("core", "fsdp", "z"):
            k = 1
            while k < lax.axis_size(axis):
                gain_grads = gain_grads + swap(gain_grads, axis, k)
                k *= 2
        shares, start = [], 0
        for size in sizes:
            shares.append(rows_of(gain_grads, start + me * size, size))
            start += n * size
        gate, up = Reduction(None), Reduction(None)
        gate.half, up.half = gate_half, up_half
        up.exchange()
        return shares, d_middle + d_stream, gate.finish(True), up.finish(True)

    qkv_sum, out_sum = Reduction(None), Reduction(None)
    qkv_sum.half, out_sum.half = lax.psum((qkv_half, out_half), "z")
    qkv_sum.half, out_sum.half, done = fence(
        qkv_sum.half, out_sum.half, block_of_work(whole, input_part)
    )
    shares, input_grad, gate_full, up_full = done
    return (
        output[None],
        input_grad[None],
        shares[0],
        qkv_sum.finish(True, 0, q_width),
        qkv_sum.finish(True, q_width, kv_width),
        qkv_sum.finish(True, q_width + kv_width, kv_width),
        shares[2],
        shares[3],
        out_sum.finish(False),
        shares[1],
        gate_full,
        up_full,
        down_full,
    )


def solution(mesh):
    n, replicas = mesh.shape["fsdp"], mesh.shape["dp"]
    split = Mesh(mesh.devices.reshape(n, replicas // 2, 2), ("fsdp", "z", "core"))
    dp = ("z", "core")
    in_specs = (
        P(dp, "fsdp", None),
        P(dp, None),
        P("fsdp"),
        P("fsdp", None),
        P("fsdp", None),
        P("fsdp", None),
        P("fsdp"),
        P("fsdp"),
        P(None, "fsdp"),
        P("fsdp"),
        P("fsdp", None),
        P("fsdp", None),
        P(None, "fsdp"),
        P(dp, "fsdp", None),
    )
    out_specs = (
        P(dp, "fsdp", None),
        P(dp, "fsdp", None),
        P("fsdp"),
        P("fsdp", None),
        P("fsdp", None),
        P("fsdp", None),
        P("fsdp"),
        P("fsdp"),
        P(None, "fsdp"),
        P("fsdp"),
        P("fsdp", None),
        P("fsdp", None),
        P(None, "fsdp"),
    )
    return jax.shard_map(
        on_device, mesh=split, in_specs=in_specs, out_specs=out_specs, check_vma=False
    )
```

time: 1020 us -> 848 us (0.83)
  matrix products: 189 us -> 97 us
  waiting for transfers between devices: 488 us -> 402 us
  Pallas kernels: 50.5 us -> 111 us
  other arithmetic: 109 us -> 76.5 us
  local copies, waits for them, and re-layouts: 70.1 us -> 54.1 us
    psum x1, waiting for transfers between devices: 55.9 us -> 0.02 us  [on_device(): down.half = lax.psum(down.half, 'z')]
    pallas_call x0 -> x3, Pallas kernels: none -> 54.9 us  [the longest x1 33 us: feed_forward_backward(): pl.pallas_call(kernel, out_shape=[jax.ShapeDtypeStruct((length, ff), bf16...]
    psum x3 -> x2, waiting for transfers between devices: 55.4 us -> 2.11 us  [the longest x1 2.09 us: on_device(): qkv_sum.half, out_sum.half = lax.psum((qkv_half, out_half), 'z')]
    dot_general x10 -> x5, matrix products: 64.2 us -> 16.6 us  [matmul_nt(): lax.dot_general(first, second, (((1,), (1,)), ((), ())), preferred_elemen...]
    dot_general x6 -> x0, matrix products: 41.3 us -> none  [the longest x1 11.9 us: attention_backward(): jnp.einsum('qkgd,skd->kgqs', d_attended, values, preferred_element_type=f32)]
    ppermute x89 -> x81, waiting for transfers between devices: 376 us -> 400 us  [swap(): lax.ppermute(value, axis, [(j, j ^ k) for j in range(lax.axis_size(axis))])]
    convert_element_type x7 -> x8, other arithmetic: 21.8 us -> 12.8 us  [the longest x1 6.76 us: on_device(): normed = (stream_all * rms_scale(stream_all) * gain_attn).astype(bf16)]
    ppermute x89 -> x81, starting transfers between devices: 85.6 us -> 80.4 us  [swap(): lax.ppermute(value, axis, [(j, j ^ k) for j in range(lax.axis_size(axis))])]
  transfers between devices with their start and end apart: 93 -> 84, of which waited for: 52 -> 46; matrix products, arithmetic and copies ran while one was open for 22% -> 23% of each run, Pallas kernels for 4% -> 11%
where the time goes in v3:
time: 848 us; the launch traced here: 838 us
  waiting for transfers between devices  402 us (47%)
  Pallas kernels  111 us (13%)
  matrix products  97 us (11%)
  starting transfers between devices  80.5 us (9%)
  other arithmetic  76.5 us (9%)
  local copies, waits for them, and re-layouts  54.1 us (6%)
  between operations  15.7 us (2%)
    ppermute x81, waiting for transfers between devices, swap(): lax.ppermute(value, axis, [(j, j ^ k) for j in range(lax.axis_size(axis))])  400 us
    ppermute x81, starting transfers between devices, swap(): lax.ppermute(value, axis, [(j, j ^ k) for j in range(lax.axis_size(axis))])  80.4 us
    pallas_call x7, Pallas kernels, finish(): pl.pallas_call(kernel, out_shape=jax.ShapeDtypeStruct((2 * rows, n * size...  43.3 us
    dot_general x13, matrix products, matmul(): return jnp.dot(first, second, preferred_element_type=f32)  43.3 us
    dot_general x11, matrix products, matmul_tn(): lax.dot_general(first, second, (((0,), (0,)), ((), ())), preferred_elemen...  37.1 us
    pallas_call x1, Pallas kernels, feed_forward_backward(): pl.pallas_call(kernel, out_shape=[jax.ShapeDtypeStruct((length, ff), bf16...  33 us
    unnamed x124, local copies, waits for them, and re-layouts  19.1 us
  transfers between devices with their start and end apart: 84, of which 46 were waited for; matrix products, arithmetic and copies ran while one was open for 23% of the time, Pallas kernels for 11%

profile of v3, /device:TPU:0, one launch (start us, length us, event | category | flops | bytes accessed | tf_op | source)
XLA Modules:
  0.0 838.1 jit_solution(17641988057727415376)
XLA Ops:
  41.3 9.7 %collective-permute-done.51 = bf16[128,1536]{1,0:T(8,128)(2,1)} collective-permute-done((bf16[128,1536]{1,0:T(8,128)(2,1)}, bf16[128,1536]{1,0:T(8,128)(2,1)}, u32[]{:S(2)}, u32[]{:S(2)}) %collective-permute-start.51) | collective-permute-done | bytes 393248 | tf_op jit(solution)/shard_map/ppermute | solution.py:51
  51.0 6.6 collective-permute-done.50
  70.2 6.3 collective-permute-done.53
  79.0 5.7 collective-permute-done.54.refs_1_
  87.7 6.8 fusion.20
  104.3 8.2 attention_forward.1
  117.2 10.5 %collective-permute-done.65 = bf16[128,2048]{1,0:T(8,128)(2,1)S(1)} collective-permute-done((bf16[128,2048]{1,0:T(8,128)(2,1)S(1)}, bf16[128,2048]{1,0:T(8,128)(2,1)S(1)}, u32[]{:S(2)}, u32[]{:S(2)}) %collective-permute-start.65) | collective-permute-done | bytes 524320 | tf_op jit(solution)/shard_map/ppermute | solution.py:51
  134.2 18.6 %collective-permute-done.66 = bf16[256,2048]{1,0:T(8,128)(2,1)S(1)} collective-permute-done((bf16[256,2048]{1,0:T(8,128)(2,1)S(1)}, bf16[256,2048]{1,0:T(8,128)(2,1)S(1)}, u32[]{:S(2)}, u32[]{:S(2)}) %collective-permute-start.66) | collective-permute-done | bytes 1048608 | tf_op jit(solution)/shard_map/ppermute | solution.py:51
  158.0 26.9 %collective-permute-done.69.refs_1_ = bf16[3,128,3072]{2,1,0:T(8,128)(2,1)} collective-permute-done((bf16[3,128,3072]{2,1,0:T(8,128)(2,1)S(1)}, bf16[3,128,3072]{2,1,0:T(8,128)(2,1)}, u32[]{:S(2)}, u32[]{:S(2)}) %collective-permute-start.69) | collective-permute-done | bytes 2359328 | tf_op jit(solution)/shard_map/ppermute | solution.py:51
  189.2 11.7 %collective-permute-done.72 = bf16[128,2048]{1,0:T(8,128)(2,1)} collective-permute-done((bf16[128,2048]{1,0:T(8,128)(2,1)S(1)}, bf16[128,2048]{1,0:T(8,128)(2,1)}, u32[]{:S(2)}, u32[]{:S(2)}) %collective-permute-start.72) | collective-permute-done | bytes 524320 | tf_op jit(solution)/shard_map/ppermute | solution.py:51
  242.3 9.8 %collective-permute-done.76 = bf16[128,2048]{1,0:T(8,128)(2,1)S(1)} collective-permute-done((bf16[128,2048]{1,0:T(8,128)(2,1)S(1)}, bf16[128,2048]{1,0:T(8,128)(2,1)S(1)}, u32[]{:S(2)}, u32[]{:S(2)}) %collective-permute-start.76) | collective-permute-done | bytes 524320 | tf_op jit(solution)/shard_map/ppermute | solution.py:51
  262.8 5.6 collective-permute-done.78
  272.5 148.3 %conditional.3 = (bf16[1536,2048]{1,0:T(8,128)(2,1)}, bf16[1024,2048]{1,0:T(8,128)(2,1)}, bf16[4,256,1536]{2,1,0:T(8,128)(2,1)}, bf16[4,256,1536]{2,1,0:T(8,128)(2,1)}) conditional(s32[]{:T(128)} %bitcast.104, () %tuple.54, (bf16[6144,512]{1,0:T(8,128)(2,1)}, bf16[1024,2048]{1,0:T(8,128)(2,1)}, f32[256,3072]{1,0:T(8,128)}, f32[256,3072]{1,0:T(8,128)}, ...), branch_computations={%region_4.5_spmd, %region_5.6_spmd} | conditional | flops 32257081344 | bytes 220202240 | solution.py:69
  277.9 17.8 %collective-permute-done.2 = bf16[768,512]{1,0:T(8,128)(2,1)S(1)} collective-permute-done((bf16[768,512]{1,0:T(8,128)(2,1)S(1)}, bf16[768,512]{1,0:T(8,128)(2,1)S(1)}, u32[]{:S(2)}, u32[]{:S(2)}) %collective-permute-start.2) | collective-permute-done | bytes 786464 | tf_op jit(solution)/shard_map/cond/branch_1_fun/ppermute | solution.py:51
  295.7 16.0 %collective-permute-done.1 = bf16[768,512]{1,0:T(8,128)(2,1)S(1)} collective-permute-done((bf16[768,512]{1,0:T(8,128)(2,1)S(1)}, bf16[768,512]{1,0:T(8,128)(2,1)S(1)}, u32[]{:S(2)}, u32[]{:S(2)}) %collective-permute-start.1) | collective-permute-done | bytes 786464 | tf_op jit(solution)/shard_map/cond/branch_1_fun/ppermute | solution.py:51
  316.7 5.6 assemble.4.refs_8_
  322.3 33.0 %feed_forward_backward.1 = (bf16[1024,1536]{1,0:T(8,128)(2,1)}, bf16[1024,1536]{1,0:T(8,128)(2,1)}, bf16[1024,2048]{1,0:T(8,128)(2,1)}) custom-call(bf16[1024,2048]{1,0:T(8,128)(2,1)} %get-tuple-element.81.cot_ref, f32[256,3072]{1,0:T(8,128)} %get-tuple-element.82.refs_0_.refs_4_, f32[256,3072]{1,0:T(8,128)} %get-tuple-element.83.refs_1_.refs_5_, ...), custom_call_target="tpu_custom_call" | custom-call | flops 19327352832 | bytes 18874368 | tf_op jit(solution)/shard_map/cond/branch_1_fun/feed_forward_backward/pallas_call | solution.py:614
  355.3 10.3 %convolution_convert_fusion = bf16[1536,2048]{0,1:T(8,128)(2,1)S(1)} fusion(bf16[1024,1536]{1,0:T(8,128)(2,1)} %get-tuple-element.90, bf16[1024,2048]{1,0:T(8,128)(2,1)} %get-tuple-element.89), kind=kOutput, calls=%fused_computation | convolution fusion | flops 6445596672 | bytes 13631488 | tf_op jit(solution)/shard_map/cond/branch_1_fun/dot_general | solution.py:31
  365.7 7.2 convolution_convert_fusion.1
  387.1 15.8 %collective-permute-done.7 = bf16[256,1536]{1,0:T(8,128)(2,1)S(1)} collective-permute-done((bf16[256,1536]{1,0:T(8,128)(2,1)S(1)}, bf16[256,1536]{1,0:T(8,128)(2,1)S(1)}, u32[]{:S(2)}, u32[]{:S(2)}) %collective-permute-start.7) | collective-permute-done | bytes 786464 | tf_op jit(solution)/shard_map/cond/branch_1_fun/ppermute | solution.py:51
  402.8 16.0 %collective-permute-done.6 = bf16[256,1536]{1,0:T(8,128)(2,1)S(1)} collective-permute-done((bf16[256,1536]{1,0:T(8,128)(2,1)S(1)}, bf16[256,1536]{1,0:T(8,128)(2,1)S(1)}, u32[]{:S(2)}, u32[]{:S(2)}) %collective-permute-start.6) | collective-permute-done | bytes 786464 | tf_op jit(solution)/shard_map/cond/branch_1_fun/ppermute | solution.py:51
  422.5 260.8 %conditional.4 = (f32[256,2048]{1,0:T(8,128)}, f32[2048]{0:T(1024)S(1)}, bf16[1024,1024]{1,0:T(8,128)(2,1)}, f32[128]{0:T(128)S(1)}, f32[128]{0:T(128)S(1)}, /*i...) conditional(s32[]{:T(128)} %bitcast.104, () %tuple.57, ...), branch_computations={%region_8.9_spmd, %region_9.14_spmd} | conditional | flops 20464007168 | bytes 535879712 | solution.py:69
  426.8 12.1 %collective-permute-done.9 = bf16[128,2048]{1,0:T(8,128)(2,1)S(1)} collective-permute-done((bf16[128,2048]{1,0:T(8,128)(2,1)S(1)}, bf16[128,2048]{1,0:T(8,128)(2,1)S(1)}, u32[]{:S(2)}, u32[]{:S(2)}) %collective-permute-start.9) | collective-permute-done | bytes 524320 | tf_op jit(solution)/shard_map/cond/branch_1_fun/ppermute | solution.py:51
  443.1 5.7 convolution_convert_fusion.6
  448.8 16.3 %collective-permute-done.12 = bf16[256,2048]{1,0:T(8,128)(2,1)S(1)} collective-permute-done((bf16[256,2048]{1,0:T(8,128)(2,1)S(1)}, bf16[256,2048]{1,0:T(8,128)(2,1)S(1)}, u32[]{:S(2)}, u32[]{:S(2)}) %collective-permute-start.12) | collective-permute-done | bytes 1048608 | tf_op jit(solution)/shard_map/cond/branch_1_fun/ppermute | solution.py:51
  479.2 5.7 convolution_convert_fusion.4
  484.8 10.8 %collective-permute-done.13 = bf16[256,2048]{1,0:T(8,128)(2,1)S(1)} collective-permute-done((bf16[256,2048]{1,0:T(8,128)(2,1)}, bf16[256,2048]{1,0:T(8,128)(2,1)S(1)}, u32[]{:S(2)}, u32[]{:S(2)}) %collective-permute-start.13) | collective-permute-done | bytes 1048608 | tf_op jit(solution)/shard_map/cond/branch_1_fun/ppermute | solution.py:51
  497.3 5.7 convolution_convert_fusion.3
  523.7 13.7 %attention_backward.1 = (bf16[1024,512]{1,0:T(8,128)(2,1)S(1)}, bf16[1024,256]{1,0:T(8,128)(2,1)S(1)}, bf16[1024,256]{1,0:T(8,128)(2,1)S(1)}, f32[2,1,128]{2,1,0:T(1,128)S(1)}, f32[2,1,128]{2,1,0:T(1,128)S(1)}) custom-call(s32[1]{0:T(128)} %bitcast.24.me_ref, f32[1024,1024]{1,0:T(8,128)S(1)} %copy-done.17, f32[1024,1024]{1,0:T(8,128)S(1)} %copy-done.17, ...), custom_call_target="tpu_custom_call" | custom-call | flops 5368709120 | bytes 10485760 | tf_op jit(solution)/shard_map/cond/branch_1_fun/attention_backward/pallas_call | solution.py:516
  547.1 6.5 convolution_convert_fusion.2
  556.9 15.6 %collective-permute-done.31 = bf16[768,512]{1,0:T(8,128)(2,1)S(1)} collective-permute-done((bf16[768,512]{1,0:T(8,128)(2,1)S(1)}, bf16[768,512]{1,0:T(8,128)(2,1)S(1)}, u32[]{:S(2)}, u32[]{:S(2)}) %collective-permute-start.31) | collective-permute-done | bytes 786464 | tf_op jit(solution)/shard_map/cond/branch_1_fun/ppermute | solution.py:51
  573.4 7.2 collective-permute-done.30
  580.6 6.7 collective-permute-done.29
  594.2 6.3 collective-permute-done.20
  602.6 23.4 %collective-permute-done.19 = bf16[256,512]{0,1:T(8,128)(2,1)S(1)} collective-permute-done((bf16[256,512]{0,1:T(8,128)(2,1)S(1)}, bf16[256,512]{0,1:T(8,128)(2,1)S(1)}, u32[]{:S(2)}, u32[]{:S(2)}) %collective-permute-start.19) | collective-permute-done | bytes 262176 | tf_op jit(solution)/shard_map/cond/branch_1_fun/ppermute | solution.py:51
  636.5 15.8 %collective-permute-done.26 = bf16[256,2048]{1,0:T(8,128)(2,1)} collective-permute-done((bf16[256,2048]{1,0:T(8,128)(2,1)}, bf16[256,2048]{1,0:T(8,128)(2,1)}, u32[]{:S(2)}, u32[]{:S(2)}) %collective-permute-start.26) | collective-permute-done | bytes 1048608 | tf_op jit(solution)/shard_map/cond/branch_1_fun/ppermute | solution.py:51
  655.5 8.5 %collective-permute-done.24 = bf16[256,1024]{1,0:T(8,128)(2,1)S(1)} collective-permute-done((bf16[256,1024]{1,0:T(8,128)(2,1)S(1)}, bf16[256,1024]{1,0:T(8,128)(2,1)S(1)}, u32[]{:S(2)}, u32[]{:S(2)}) %collective-permute-start.24) | collective-permute-done | bytes 524320 | tf_op jit(solution)/shard_map/cond/branch_1_fun/ppermute | solution.py:51
  664.0 8.9 %collective-permute-done.22 = bf16[256,1024]{1,0:T(8,128)(2,1)S(1)} collective-permute-done((bf16[256,1024]{1,0:T(8,128)(2,1)S(1)}, bf16[256,1024]{1,0:T(8,128)(2,1)S(1)}, u32[]{:S(2)}, u32[]{:S(2)}) %collective-permute-start.22) | collective-permute-done | bytes 524320 | tf_op jit(solution)/shard_map/cond/branch_1_fun/ppermute | solution.py:51
  674.5 8.7 %place.7 = f32[6144,512]{1,0:T(8,128)} custom-call(s32[2]{0:T(128)S(1)} %pad_add_fusion.place, bf16[4,768,512]{2,1,0:T(8,128)(2,1)S(1)} %pad_maximum_fusion.4.mine, bf16[4,768,512]{2,1,0:T(8,128)(2,1)} %collective-permute-done.32.other), custom_call_target="tpu_custom_call" | custom-call | bytes 125829120 | tf_op jit(solution)/shard_map/cond/branch_1_fun/place/pallas_call | solution.py:321
  687.7 118.6 %conditional.5 = (f32[512]{0:T(512)S(1)}, f32[512]{0:T(512)S(1)}, f32[32]{0:T(128)S(1)}, f32[32]{0:T(128)S(1)}, f32[256,2048]{1,0:T(8,128)}, /*index=5*/f32[512,6144]{1,0:T(8,128)}, f32[512,6144]{1,0:T(8,128)}) conditional(s32[]{:T(128)} %bitcast.104, () %tuple.60, (bf16[1024,1024]{1,0:T(8,128)(2,1)}, bf16[2048,1024]{1,0:T(8,128)(2,1)}, ...), branch_computations={%region_16.17_spmd, %region_17.21_spmd} | conditional | flops 4320178176 | bytes 398116320 | solution.py:69
  701.9 5.1 collective-permute-done.35
  708.7 16.6 %collective-permute-done.33 = bf16[128,2048]{1,0:T(8,128)(2,1)S(1)} collective-permute-done((bf16[128,2048]{1,0:T(8,128)(2,1)S(1)}, bf16[128,2048]{1,0:T(8,128)(2,1)S(1)}, u32[]{:S(2)}, u32[]{:S(2)}) %collective-permute-start.33) | collective-permute-done | bytes 524320 | tf_op jit(solution)/shard_map/cond/branch_1_fun/ppermute | solution.py:51
  727.4 14.8 %collective-permute-done.44 = bf16[256,1536]{1,0:T(8,128)(2,1)S(1)} collective-permute-done((bf16[256,1536]{1,0:T(8,128)(2,1)S(1)}, bf16[256,1536]{1,0:T(8,128)(2,1)S(1)}, u32[]{:S(2)}, u32[]{:S(2)}) %collective-permute-start.44) | collective-permute-done | bytes 786464 | tf_op jit(solution)/shard_map/cond/branch_1_fun/ppermute | solution.py:51
  742.9 18.7 %collective-permute-done.36 = bf16[256,2048]{1,0:T(8,128)(2,1)S(1)} collective-permute-done((bf16[256,2048]{1,0:T(8,128)(2,1)S(1)}, bf16[256,2048]{1,0:T(8,128)(2,1)S(1)}, u32[]{:S(2)}, u32[]{:S(2)}) %collective-permute-start.36) | collective-permute-done | bytes 1048608 | tf_op jit(solution)/shard_map/cond/branch_1_fun/ppermute | solution.py:51
  781.9 5.5 subtract_add_fusion.1
  787.6 10.0 %place.8 = f32[512,6144]{1,0:T(8,128)} custom-call(s32[2]{0:T(128)S(1)} %pad_add_fusion.1.place, bf16[4,256,1536]{2,1,0:T(8,128)(2,1)} %get-tuple-element.132.mine, bf16[4,256,1536]{2,1,0:T(8,128)(2,1)} %collective-permute-done.42.other), custom_call_target="tpu_custom_call" | custom-call | bytes 125829120 | tf_op jit(solution)/shard_map/cond/branch_1_fun/place/pallas_call | solution.py:321
  797.5 8.7 %place.9 = f32[512,6144]{1,0:T(8,128)} custom-call(s32[2]{0:T(128)S(1)} %pad_add_fusion.1.place, bf16[4,256,1536]{2,1,0:T(8,128)(2,1)S(1)} %pad_maximum_fusion.14.mine, bf16[4,256,1536]{2,1,0:T(8,128)(2,1)} %collective-permute-done.46.other), custom_call_target="tpu_custom_call" | custom-call | bytes 125829120 | tf_op jit(solution)/shard_map/cond/branch_1_fun/place/pallas_call | solution.py:321
  809.0 5.3 collective-permute-done.80.other
  (502 shorter events, 311.3 us)
Async XLA Ops:
  7.2 413.7 %all-reduce.6.cloned.1.call-start = ((), (), s32[]{:S(2)}) async-start(), calls=%async_computation | async-start | bytes 6291456 | tf_op jit(solution)/shard_map/psum | solution.py:793
  10.2 25.3 %collective-permute-start.58 = (bf16[1,1088]{1,0:T(2,128)(2,1)S(1)}, bf16[1,1088]{1,0:T(2,128)(2,1)}, u32[]{:S(2)}, u32[]{:S(2)}) collective-permute-start(bf16[1,1088]{1,0:T(2,128)(2,1)S(1)} %broadcast_in_dim.6), channel_id=1, source_target_pairs={{0,24},{8,16},{16,8},{24,0},{1,25},{9,17},{17,9},{25,1},{2,26},{10... | collective-permute-start | bytes 6536 | tf_op jit(solution)/shard_map/ppermute | solution.py:51
  14.7 44.2 %collective-permute-start.47 = (bf16[256,2048]{1,0:T(8,128)(2,1)}, bf16[256,2048]{1,0:T(8,128)(2,1)S(1)}, u32[]{:S(2)}, u32[]{:S(2)}) collective-permute-start(bf16[256,2048]{1,0:T(8,128)(2,1)} %bitcast.185), channel_id=1, source_target_pairs={{0,8},{8,0},{16,24},{24,16},{1,9},{9,1},{17,25},{25,17},{2,10},{10... | collective-permute-start | bytes 3145736 | tf_op jit(solution)/shard_map/ppermute | solution.py:51
  16.6 42.3 %collective-permute-start.48 = (bf16[256,2048]{1,0:T(8,128)(2,1)}, bf16[256,2048]{1,0:T(8,128)(2,1)}, u32[]{:S(2)}, u32[]{:S(2)}) collective-permute-start(bf16[256,2048]{1,0:T(8,128)(2,1)} %bitcast.186), channel_id=1, source_target_pairs={{0,16},{8,24},{16,0},{24,8},{1,17},{9,25},{17,1},{25,9},{2,18},{10... | collective-permute-start | bytes 3145736 | tf_op jit(solution)/shard_map/ppermute | solution.py:51
  59.0 25.7 %collective-permute-start.54 = (bf16[3,128,1536]{2,1,0:T(8,128)(2,1)S(1)}, bf16[3,128,1536]{2,1,0:T(8,128)(2,1)S(1)}, u32[]{:S(2)}, u32[]{:S(2)}) collective-permute-start(bf16[3,128,1536]{2,1,0:T(8,128)(2,1)S(1)} %pad_maximum_fusion.24.refs_0_), channel_id=1, source_target_pairs={{0,2},{2,0},{4,6},{6,4},{1,3},{3,1},{5,7},{7,5},{8,10},{10,8},{12,... | collective-permute-start | bytes 3538952 | tf_op jit(solution)/shard_map/ppermute | solution.py:51
  60.6 24.1 %collective-permute-start.55 = (bf16[3,128,1536]{2,1,0:T(8,128)(2,1)S(1)}, bf16[3,128,1536]{2,1,0:T(8,128)(2,1)S(1)}, u32[]{:S(2)}, u32[]{:S(2)}) collective-permute-start(bf16[3,128,1536]{2,1,0:T(8,128)(2,1)S(1)} %pad_maximum_fusion.24.refs_0_), channel_id=1, source_target_pairs={{0,1},{1,0},{2,3},{3,2},{4,5},{5,4},{6,7},{7,6},{8,9},{9,8},{10,11... | collective-permute-start | bytes 3538952 | tf_op jit(solution)/shard_map/ppermute | solution.py:51
  66.8 45.7 %collective-permute-start.60 = (bf16[128,3072]{1,0:T(8,128)(2,1)}, bf16[128,3072]{1,0:T(8,128)(2,1)}, u32[]{:S(2)}, u32[]{:S(2)}) collective-permute-start(bf16[128,3072]{1,0:T(8,128)(2,1)} %pad_maximum_fusion.29), channel_id=1, source_target_pairs={{0,8},{8,0},{16,24},{24,16},{1,9},{9,1},{17,25},{25,17},{2,10},{10... | collective-permute-start | bytes 2359304 | tf_op jit(solution)/shard_map/ppermute | solution.py:51
  76.5 36.0 %collective-permute-start.61 = (bf16[128,3072]{1,0:T(8,128)(2,1)}, bf16[128,3072]{1,0:T(8,128)(2,1)}, u32[]{:S(2)}, u32[]{:S(2)}) collective-permute-start(bf16[128,3072]{1,0:T(8,128)(2,1)} %pad_maximum_fusion.30), channel_id=1, source_target_pairs={{0,16},{8,24},{16,0},{24,8},{1,17},{9,25},{17,1},{25,9},{2,18},{10... | collective-permute-start | bytes 2359304 | tf_op jit(solution)/shard_map/ppermute | solution.py:51
  78.0 34.5 %collective-permute-start.62 = (bf16[128,3072]{1,0:T(8,128)(2,1)}, bf16[128,3072]{1,0:T(8,128)(2,1)}, u32[]{:S(2)}, u32[]{:S(2)}) collective-permute-start(bf16[128,3072]{1,0:T(8,128)(2,1)} %pad_maximum_fusion.31), channel_id=1, source_target_pairs={{0,24},{8,16},{16,8},{24,0},{1,25},{9,17},{17,9},{25,1},{2,26},{10... | collective-permute-start | bytes 2359304 | tf_op jit(solution)/shard_map/ppermute | solution.py:51
  127.9 24.8 %collective-permute-start.66 = (bf16[256,2048]{1,0:T(8,128)(2,1)S(1)}, bf16[256,2048]{1,0:T(8,128)(2,1)S(1)}, u32[]{:S(2)}, u32[]{:S(2)}) collective-permute-start(bf16[256,2048]{1,0:T(8,128)(2,1)S(1)} %pad_maximum_fusion.27), channel_id=1, source_target_pairs={{0,16},{8,24},{16,0},{24,8},{1,17},{9,25},{17,1},{25,9},{2,18},{10... | collective-permute-start | bytes 3145736 | tf_op jit(solution)/shard_map/ppermute | solution.py:51
  129.8 24.5 %collective-permute-start.64 = (bf16[256,2048]{1,0:T(8,128)(2,1)S(1)}, bf16[256,2048]{1,0:T(8,128)(2,1)S(1)}, u32[]{:S(2)}, u32[]{:S(2)}) collective-permute-start(bf16[256,2048]{1,0:T(8,128)(2,1)S(1)} %pad_maximum_fusion.26), channel_id=1, source_target_pairs={{0,8},{8,0},{16,24},{24,16},{1,9},{9,1},{17,25},{25,17},{2,10},{10... | collective-permute-start | bytes 3145736 | tf_op jit(solution)/shard_map/ppermute | solution.py:51
  132.5 52.4 %collective-permute-start.69 = (bf16[3,128,3072]{2,1,0:T(8,128)(2,1)S(1)}, bf16[3,128,3072]{2,1,0:T(8,128)(2,1)}, u32[]{:S(2)}, u32[]{:S(2)}) collective-permute-start(bf16[3,128,3072]{2,1,0:T(8,128)(2,1)S(1)} %pad_maximum_fusion.23.refs_0_), channel_id=1, source_target_pairs={{0,2},{2,0},{4,6},{6,4},{1,3},{3,1},{5,7},{7,5},{8,10},{10,8},{12,... | collective-permute-start | bytes 7077896 | tf_op jit(solution)/shard_map/ppermute | solution.py:51
  134.1 50.8 %collective-permute-start.70 = (bf16[3,128,3072]{2,1,0:T(8,128)(2,1)S(1)}, bf16[3,128,3072]{2,1,0:T(8,128)(2,1)S(1)}, u32[]{:S(2)}, u32[]{:S(2)}) collective-permute-start(bf16[3,128,3072]{2,1,0:T(8,128)(2,1)S(1)} %pad_maximum_fusion.23.refs_0_), channel_id=1, source_target_pairs={{0,1},{1,0},{2,3},{3,2},{4,5},{5,4},{6,7},{7,6},{8,9},{9,8},{10,11... | collective-permute-start | bytes 7077896 | tf_op jit(solution)/shard_map/ppermute | solution.py:51
  155.7 30.6 %collective-permute-start.67 = (bf16[256,2048]{1,0:T(8,128)(2,1)S(1)}, bf16[256,2048]{1,0:T(8,128)(2,1)S(1)}, u32[]{:S(2)}, u32[]{:S(2)}) collective-permute-start(bf16[256,2048]{1,0:T(8,128)(2,1)S(1)} %multiply_convert_fusion), channel_id=1, source_target_pairs={{0,8},{8,0},{16,24},{24,16},{1,9},{9,1},{17,25},{25,17},{2,10},{10... | collective-permute-start | bytes 3145736 | tf_op jit(solution)/shard_map/ppermute | solution.py:51
  156.5 29.8 %collective-permute-start.68 = (bf16[256,2048]{1,0:T(8,128)(2,1)S(1)}, bf16[256,2048]{1,0:T(8,128)(2,1)S(1)}, u32[]{:S(2)}, u32[]{:S(2)}) collective-permute-start(bf16[256,2048]{1,0:T(8,128)(2,1)S(1)} %multiply_convert_fusion), channel_id=1, source_target_pairs={{0,16},{8,24},{16,0},{24,8},{1,17},{9,25},{17,1},{25,9},{2,18},{10... | collective-permute-start | bytes 3145736 | tf_op jit(solution)/shard_map/ppermute | solution.py:51
  214.9 24.5 %collective-permute-start.74 = (bf16[256,2048]{1,0:T(8,128)(2,1)S(1)}, bf16[256,2048]{1,0:T(8,128)(2,1)S(1)}, u32[]{:S(2)}, u32[]{:S(2)}) collective-permute-start(bf16[256,2048]{1,0:T(8,128)(2,1)S(1)} %bitcast.192), channel_id=1, source_target_pairs={{0,8},{8,0},{16,24},{24,16},{1,9},{9,1},{17,25},{25,17},{2,10},{10... | collective-permute-start | bytes 3145736 | tf_op jit(solution)/shard_map/ppermute | solution.py:51
  215.6 23.9 %collective-permute-start.75 = (bf16[256,2048]{1,0:T(8,128)(2,1)S(1)}, bf16[256,2048]{1,0:T(8,128)(2,1)S(1)}, u32[]{:S(2)}, u32[]{:S(2)}) collective-permute-start(bf16[256,2048]{1,0:T(8,128)(2,1)S(1)} %bitcast.193), channel_id=1, source_target_pairs={{0,16},{8,24},{16,0},{24,8},{1,17},{9,25},{17,1},{25,9},{2,18},{10... | collective-permute-start | bytes 3145736 | tf_op jit(solution)/shard_map/ppermute | solution.py:51
  270.6 412.8 %all-reduce.10.cloned.1.call-start = ((), (), s32[]{:S(2)}) async-start(), calls=%async_computation.2 | async-start | bytes 12582912 | tf_op jit(solution)/shard_map/psum | solution.py:846
  275.6 36.1 %collective-permute-start.1 = (bf16[768,512]{1,0:T(8,128)(2,1)S(1)}, bf16[768,512]{1,0:T(8,128)(2,1)S(1)}, u32[]{:S(2)}, u32[]{:S(2)}) collective-permute-start(bf16[768,512]{1,0:T(8,128)(2,1)S(1)} %get-tuple-element.372), channel_id=1, source_target_pairs={{0,16},{8,24},{16,0},{24,8},{1,17},{9,25},{17,1},{25,9},{2,18},{10... | collective-permute-start | bytes 2359304 | tf_op jit(solution)/shard_map/cond/branch_1_fun/ppermute | solution.py:51
  276.4 35.3 %collective-permute-start = (bf16[768,512]{1,0:T(8,128)(2,1)S(1)}, bf16[768,512]{1,0:T(8,128)(2,1)S(1)}, u32[]{:S(2)}, u32[]{:S(2)}) collective-permute-start(bf16[768,512]{1,0:T(8,128)(2,1)S(1)} %get-tuple-element.370), channel_id=1, source_target_pairs={{0,8},{8,0},{16,24},{24,16},{1,9},{9,1},{17,25},{25,17},{2,10},{10... | collective-permute-start | bytes 2359304 | tf_op jit(solution)/shard_map/cond/branch_1_fun/ppermute | solution.py:51
  382.6 36.2 %collective-permute-start.6 = (bf16[256,1536]{1,0:T(8,128)(2,1)S(1)}, bf16[256,1536]{1,0:T(8,128)(2,1)S(1)}, u32[]{:S(2)}, u32[]{:S(2)}) collective-permute-start(bf16[256,1536]{1,0:T(8,128)(2,1)S(1)} %get-tuple-element.375), channel_id=1, source_target_pairs={{0,16},{8,24},{16,0},{24,8},{1,17},{9,25},{17,1},{25,9},{2,18},{10... | collective-permute-start | bytes 2359304 | tf_op jit(solution)/shard_map/cond/branch_1_fun/ppermute | solution.py:51
  383.4 35.4 %collective-permute-start.5 = (bf16[256,1536]{1,0:T(8,128)(2,1)S(1)}, bf16[256,1536]{1,0:T(8,128)(2,1)S(1)}, u32[]{:S(2)}, u32[]{:S(2)}) collective-permute-start(bf16[256,1536]{1,0:T(8,128)(2,1)S(1)} %get-tuple-element.376), channel_id=1, source_target_pairs={{0,8},{8,0},{16,24},{24,16},{1,9},{9,1},{17,25},{25,17},{2,10},{10... | collective-permute-start | bytes 2359304 | tf_op jit(solution)/shard_map/cond/branch_1_fun/ppermute | solution.py:51
  421.0 387.4 %all-reduce.8.cloned.1.call-start = ((), (), s32[]{:S(2)}) async-start(), calls=%async_computation.1 | async-start | bytes 6291456 | tf_op jit(solution)/shard_map/psum | solution.py:873
  441.0 24.1 %collective-permute-start.12 = (bf16[256,2048]{1,0:T(8,128)(2,1)S(1)}, bf16[256,2048]{1,0:T(8,128)(2,1)S(1)}, u32[]{:S(2)}, u32[]{:S(2)}) collective-permute-start(bf16[256,2048]{1,0:T(8,128)(2,1)S(1)} %pad_maximum_fusion.9), channel_id=1, source_target_pairs={{0,16},{8,24},{16,0},{24,8},{1,17},{9,25},{17,1},{25,9},{2,18},{10... | collective-permute-start | bytes 3145736 | tf_op jit(solution)/shard_map/cond/branch_1_fun/ppermute | solution.py:51
  442.5 23.7 %collective-permute-start.10 = (bf16[256,2048]{1,0:T(8,128)(2,1)S(1)}, bf16[256,2048]{1,0:T(8,128)(2,1)S(1)}, u32[]{:S(2)}, u32[]{:S(2)}) collective-permute-start(bf16[256,2048]{1,0:T(8,128)(2,1)S(1)} %pad_maximum_fusion.8), channel_id=1, source_target_pairs={{0,8},{8,0},{16,24},{24,16},{1,9},{9,1},{17,25},{25,17},{2,10},{10... | collective-permute-start | bytes 3145736 | tf_op jit(solution)/shard_map/cond/branch_1_fun/ppermute | solution.py:51
  472.6 23.0 %collective-permute-start.13 = (bf16[256,2048]{1,0:T(8,128)(2,1)}, bf16[256,2048]{1,0:T(8,128)(2,1)S(1)}, u32[]{:S(2)}, u32[]{:S(2)}) collective-permute-start(bf16[256,2048]{1,0:T(8,128)(2,1)} %get-tuple-element.352), channel_id=1, source_target_pairs={{0,8},{8,0},{16,24},{24,16},{1,9},{9,1},{17,25},{25,17},{2,10},{10... | collective-permute-start | bytes 3145736 | tf_op jit(solution)/shard_map/cond/branch_1_fun/ppermute | solution.py:51
  477.9 26.4 %collective-permute-start.14 = (bf16[256,2048]{1,0:T(8,128)(2,1)}, bf16[256,2048]{1,0:T(8,128)(2,1)S(1)}, u32[]{:S(2)}, u32[]{:S(2)}) collective-permute-start(bf16[256,2048]{1,0:T(8,128)(2,1)} %get-tuple-element.352), channel_id=1, source_target_pairs={{0,16},{8,24},{16,0},{24,8},{1,17},{9,25},{17,1},{25,9},{2,18},{10... | collective-permute-start | bytes 3145736 | tf_op jit(solution)/shard_map/cond/branch_1_fun/ppermute | solution.py:51
  539.0 51.5 %collective-permute-start.17 = (bf16[4,256,512]{1,2,0:T(8,128)(2,1)S(1)}, bf16[4,256,512]{1,2,0:T(8,128)(2,1)S(1)}, u32[]{:S(2)}, u32[]{:S(2)}) collective-permute-start(bf16[4,256,512]{1,2,0:T(8,128)(2,1)S(1)} %pad_maximum_fusion.10), channel_id=1, source_target_pairs={{0,1},{1,0},{2,3},{3,2},{4,5},{5,4},{6,7},{7,6},{8,9},{9,8},{10,11... | collective-permute-start | bytes 3145736 | tf_op jit(solution)/shard_map/cond/branch_1_fun/ppermute | solution.py:51
  541.8 30.7 %collective-permute-start.31 = (bf16[768,512]{1,0:T(8,128)(2,1)S(1)}, bf16[768,512]{1,0:T(8,128)(2,1)S(1)}, u32[]{:S(2)}, u32[]{:S(2)}) collective-permute-start(bf16[768,512]{1,0:T(8,128)(2,1)S(1)} %get-tuple-element.413), channel_id=1, source_target_pairs={{0,24},{8,16},{16,8},{24,0},{1,25},{9,17},{17,9},{25,1},{2,26},{10... | collective-permute-start | bytes 2359304 | tf_op jit(solution)/shard_map/cond/branch_1_fun/ppermute | solution.py:51
  543.3 37.3 %collective-permute-start.30 = (bf16[768,512]{1,0:T(8,128)(2,1)S(1)}, bf16[768,512]{1,0:T(8,128)(2,1)S(1)}, u32[]{:S(2)}, u32[]{:S(2)}) collective-permute-start(bf16[768,512]{1,0:T(8,128)(2,1)S(1)} %get-tuple-element.414), channel_id=1, source_target_pairs={{0,16},{8,24},{16,0},{24,8},{1,17},{9,25},{17,1},{25,9},{2,18},{10... | collective-permute-start | bytes 2359304 | tf_op jit(solution)/shard_map/cond/branch_1_fun/ppermute | solution.py:51
  544.7 42.6 %collective-permute-start.29 = (bf16[768,512]{1,0:T(8,128)(2,1)S(1)}, bf16[768,512]{1,0:T(8,128)(2,1)S(1)}, u32[]{:S(2)}, u32[]{:S(2)}) collective-permute-start(bf16[768,512]{1,0:T(8,128)(2,1)S(1)} %get-tuple-element.415), channel_id=1, source_target_pairs={{0,8},{8,0},{16,24},{24,16},{1,9},{9,1},{17,25},{25,17},{2,10},{10... | collective-permute-start | bytes 2359304 | tf_op jit(solution)/shard_map/cond/branch_1_fun/ppermute | solution.py:51
  556.8 72.9 %collective-permute-start.21 = (bf16[4,256,1024]{2,1,0:T(8,128)(2,1)}, bf16[4,256,1024]{2,1,0:T(8,128)(2,1)}, u32[]{:S(2)}, u32[]{:S(2)}) collective-permute-start(bf16[4,256,1024]{2,1,0:T(8,128)(2,1)} %pad_maximum_fusion.6), channel_id=1, source_target_pairs={{0,1},{1,0},{2,3},{3,2},{4,5},{5,4},{6,7},{7,6},{8,9},{9,8},{10,11... | collective-permute-start | bytes 6291464 | tf_op jit(solution)/shard_map/cond/branch_1_fun/ppermute | solution.py:51
  587.8 86.7 %collective-permute-start.32 = (bf16[4,768,512]{2,1,0:T(8,128)(2,1)S(1)}, bf16[4,768,512]{2,1,0:T(8,128)(2,1)}, u32[]{:S(2)}, u32[]{:S(2)}) collective-permute-start(bf16[4,768,512]{2,1,0:T(8,128)(2,1)S(1)} %pad_maximum_fusion.4.mine), channel_id=1, source_target_pairs={{0,1},{1,0},{2,3},{3,2},{4,5},{5,4},{6,7},{7,6},{8,9},{9,8},{10,11... | collective-permute-start | bytes 9437192 | tf_op jit(solution)/shard_map/cond/branch_1_fun/ppermute | solution.py:51
  589.4 45.7 %collective-permute-start.28 = (bf16[256,2048]{1,0:T(8,128)(2,1)}, bf16[256,2048]{1,0:T(8,128)(2,1)}, u32[]{:S(2)}, u32[]{:S(2)}) collective-permute-start(bf16[256,2048]{1,0:T(8,128)(2,1)} %pad_maximum_fusion.13), channel_id=1, source_target_pairs={{0,16},{8,24},{16,0},{24,8},{1,17},{9,25},{17,1},{25,9},{2,18},{10... | collective-permute-start | bytes 3145736 | tf_op jit(solution)/shard_map/cond/branch_1_fun/ppermute | solution.py:51
  593.3 32.6 %collective-permute-start.19 = (bf16[256,512]{0,1:T(8,128)(2,1)S(1)}, bf16[256,512]{0,1:T(8,128)(2,1)S(1)}, u32[]{:S(2)}, u32[]{:S(2)}) collective-permute-start(bf16[256,512]{0,1:T(8,128)(2,1)S(1)} %get-tuple-element.432), channel_id=1, source_target_pairs={{0,16},{8,24},{16,0},{24,8},{1,17},{9,25},{17,1},{25,9},{2,18},{10... | collective-permute-start | bytes 786440 | tf_op jit(solution)/shard_map/cond/branch_1_fun/ppermute | solution.py:51
  600.5 26.9 %collective-permute-start.18 = (bf16[256,512]{0,1:T(8,128)(2,1)}, bf16[256,512]{0,1:T(8,128)(2,1)}, u32[]{:S(2)}, u32[]{:S(2)}) collective-permute-start(bf16[256,512]{0,1:T(8,128)(2,1)} %get-tuple-element.433), channel_id=1, source_target_pairs={{0,8},{8,0},{16,24},{24,16},{1,9},{9,1},{17,25},{25,17},{2,10},{10... | collective-permute-start | bytes 786440 | tf_op jit(solution)/shard_map/cond/branch_1_fun/ppermute | solution.py:51
  625.9 26.4 %collective-permute-start.26 = (bf16[256,2048]{1,0:T(8,128)(2,1)}, bf16[256,2048]{1,0:T(8,128)(2,1)}, u32[]{:S(2)}, u32[]{:S(2)}) collective-permute-start(bf16[256,2048]{1,0:T(8,128)(2,1)} %pad_maximum_fusion.12), channel_id=1, source_target_pairs={{0,8},{8,0},{16,24},{24,16},{1,9},{9,1},{17,25},{25,17},{2,10},{10... | collective-permute-start | bytes 3145736 | tf_op jit(solution)/shard_map/cond/branch_1_fun/ppermute | solution.py:51
  633.0 31.0 %collective-permute-start.24 = (bf16[256,1024]{1,0:T(8,128)(2,1)S(1)}, bf16[256,1024]{1,0:T(8,128)(2,1)S(1)}, u32[]{:S(2)}, u32[]{:S(2)}) collective-permute-start(bf16[256,1024]{1,0:T(8,128)(2,1)S(1)} %get-tuple-element.417), channel_id=1, source_target_pairs={{0,24},{8,16},{16,8},{24,0},{1,25},{9,17},{17,9},{25,1},{2,26},{10... | collective-permute-start | bytes 1572872 | tf_op jit(solution)/shard_map/cond/branch_1_fun/ppermute | solution.py:51
  634.2 29.8 %collective-permute-start.23 = (bf16[256,1024]{1,0:T(8,128)(2,1)S(1)}, bf16[256,1024]{1,0:T(8,128)(2,1)S(1)}, u32[]{:S(2)}, u32[]{:S(2)}) collective-permute-start(bf16[256,1024]{1,0:T(8,128)(2,1)S(1)} %get-tuple-element.418), channel_id=1, source_target_pairs={{0,16},{8,24},{16,0},{24,8},{1,17},{9,25},{17,1},{25,9},{2,18},{10... | collective-permute-start | bytes 1572872 | tf_op jit(solution)/shard_map/cond/branch_1_fun/ppermute | solution.py:51
  635.2 37.7 %collective-permute-start.22 = (bf16[256,1024]{1,0:T(8,128)(2,1)S(1)}, bf16[256,1024]{1,0:T(8,128)(2,1)S(1)}, u32[]{:S(2)}, u32[]{:S(2)}) collective-permute-start(bf16[256,1024]{1,0:T(8,128)(2,1)S(1)} %get-tuple-element.419), channel_id=1, source_target_pairs={{0,8},{8,0},{16,24},{24,16},{1,9},{9,1},{17,25},{25,17},{2,10},{10... | collective-permute-start | bytes 1572872 | tf_op jit(solution)/shard_map/cond/branch_1_fun/ppermute | solution.py:51
  693.6 31.7 %collective-permute-start.33 = (bf16[128,2048]{1,0:T(8,128)(2,1)S(1)}, bf16[128,2048]{1,0:T(8,128)(2,1)S(1)}, u32[]{:S(2)}, u32[]{:S(2)}) collective-permute-start(bf16[128,2048]{1,0:T(8,128)(2,1)S(1)} %get-tuple-element.389), channel_id=1, source_target_pairs={{0,16},{8,24},{16,0},{24,8},{1,17},{9,25},{17,1},{25,9},{2,18},{10... | collective-permute-start | bytes 1572872 | tf_op jit(solution)/shard_map/cond/branch_1_fun/ppermute | solution.py:51
  694.3 93.3 %collective-permute-start.42 = (bf16[4,256,1536]{2,1,0:T(8,128)(2,1)}, bf16[4,256,1536]{2,1,0:T(8,128)(2,1)}, u32[]{:S(2)}, u32[]{:S(2)}) collective-permute-start(bf16[4,256,1536]{2,1,0:T(8,128)(2,1)} %get-tuple-element.132.mine), channel_id=1, source_target_pairs={{0,1},{1,0},{2,3},{3,2},{4,5},{5,4},{6,7},{7,6},{8,9},{9,8},{10,11... | collective-permute-start | bytes 9437192 | tf_op jit(solution)/shard_map/cond/branch_1_fun/ppermute | solution.py:51
  694.5 31.7 %collective-permute-start.45 = (bf16[256,1536]{1,0:T(8,128)(2,1)S(1)}, bf16[256,1536]{1,0:T(8,128)(2,1)S(1)}, u32[]{:S(2)}, u32[]{:S(2)}) collective-permute-start(bf16[256,1536]{1,0:T(8,128)(2,1)S(1)} %get-tuple-element.386), channel_id=1, source_target_pairs={{0,24},{8,16},{16,8},{24,0},{1,25},{9,17},{17,9},{25,1},{2,26},{10... | collective-permute-start | bytes 2359304 | tf_op jit(solution)/shard_map/cond/branch_1_fun/ppermute | solution.py:51
  696.0 46.2 %collective-permute-start.44 = (bf16[256,1536]{1,0:T(8,128)(2,1)S(1)}, bf16[256,1536]{1,0:T(8,128)(2,1)S(1)}, u32[]{:S(2)}, u32[]{:S(2)}) collective-permute-start(bf16[256,1536]{1,0:T(8,128)(2,1)S(1)} %get-tuple-element.387), channel_id=1, source_target_pairs={{0,16},{8,24},{16,0},{24,8},{1,17},{9,25},{17,1},{25,9},{2,18},{10... | collective-permute-start | bytes 2359304 | tf_op jit(solution)/shard_map/cond/branch_1_fun/ppermute | solution.py:51
  707.1 35.1 %collective-permute-start.43 = (bf16[256,1536]{1,0:T(8,128)(2,1)S(1)}, bf16[256,1536]{1,0:T(8,128)(2,1)S(1)}, u32[]{:S(2)}, u32[]{:S(2)}) collective-permute-start(bf16[256,1536]{1,0:T(8,128)(2,1)S(1)} %get-tuple-element.388), channel_id=1, source_target_pairs={{0,8},{8,0},{16,24},{24,16},{1,9},{9,1},{17,25},{25,17},{2,10},{10... | collective-permute-start | bytes 2359304 | tf_op jit(solution)/shard_map/cond/branch_1_fun/ppermute | solution.py:51
  725.3 36.3 %collective-permute-start.36 = (bf16[256,2048]{1,0:T(8,128)(2,1)S(1)}, bf16[256,2048]{1,0:T(8,128)(2,1)S(1)}, u32[]{:S(2)}, u32[]{:S(2)}) collective-permute-start(bf16[256,2048]{1,0:T(8,128)(2,1)S(1)} %pad_maximum_fusion.16), channel_id=1, source_target_pairs={{0,16},{8,24},{16,0},{24,8},{1,17},{9,25},{17,1},{25,9},{2,18},{10... | collective-permute-start | bytes 3145736 | tf_op jit(solution)/shard_map/cond/branch_1_fun/ppermute | solution.py:51
  726.2 35.4 %collective-permute-start.34 = (bf16[256,2048]{1,0:T(8,128)(2,1)S(1)}, bf16[256,2048]{1,0:T(8,128)(2,1)S(1)}, u32[]{:S(2)}, u32[]{:S(2)}) collective-permute-start(bf16[256,2048]{1,0:T(8,128)(2,1)S(1)} %pad_maximum_fusion.15), channel_id=1, source_target_pairs={{0,8},{8,0},{16,24},{24,16},{1,9},{9,1},{17,25},{25,17},{2,10},{10... | collective-permute-start | bytes 3145736 | tf_op jit(solution)/shard_map/cond/branch_1_fun/ppermute | solution.py:51
  742.6 55.0 %collective-permute-start.46 = (bf16[4,256,1536]{2,1,0:T(8,128)(2,1)S(1)}, bf16[4,256,1536]{2,1,0:T(8,128)(2,1)}, u32[]{:S(2)}, u32[]{:S(2)}) collective-permute-start(bf16[4,256,1536]{2,1,0:T(8,128)(2,1)S(1)} %pad_maximum_fusion.14.mine), channel_id=1, source_target_pairs={{0,1},{1,0},{2,3},{3,2},{4,5},{5,4},{6,7},{7,6},{8,9},{9,8},{10,11... | collective-permute-start | bytes 9437192 | tf_op jit(solution)/shard_map/cond/branch_1_fun/ppermute | solution.py:51
  (124 other events, 1702.0 us)
Sparse Core Ops, SparseCore 0:
  270.7 121.1 all-reduce.5
  421.1 223.0 all-reduce.9
  685.9 122.4 all-reduce.7

commit v4 on v3

--- a/solution.py
+++ b/solution.py
@@ -73,55 +73,47 @@
     )
 
 
-def gather_begin(shard):
-    n = lax.axis_size("fsdp")
-    if n == 4:
-        return [swap(shard, "fsdp", 1), swap(shard, "fsdp", 2)]
-    return [swap(shard, "fsdp", k) for k in range(1, n)]
-
-
-def gather_end(shard, begun):
-    if lax.axis_size("fsdp") != 4:
-        return [shard] + begun
-    half = shard.shape[0] // 2
-    first = swap(begun[0][:half], "fsdp", 2)
-    second = swap(begun[1][half:], "fsdp", 1)
-    return [shard] + begun + [jnp.concatenate([first, second], axis=0)]
-
-
-def scatter_begin(far):
-    n = lax.axis_size("fsdp")
-    if n == 4:
-        half = far.shape[0] // 2
-        return [swap(far[:half], "fsdp", 1), swap(far[half:], "fsdp", 2)]
-    return [swap(far, "fsdp", n - 1)]
-
-
-def scatter_middle(near, begun):
+def gather(shard, beside=None):
     n = lax.axis_size("fsdp")
     if n != 4:
-        return begun + [swap(block, "fsdp", k + 1) for k, block in enumerate(near)]
-    near_x, near_y = near
-    first, second = begun
-    half = first.shape[0]
-    low = (near_x[half:].astype(f32) + second.astype(f32)).astype(bf16)
-    top = (near_y[:half].astype(f32) + first.astype(f32)).astype(bf16)
-    return [
-        swap(jnp.concatenate([near_x[:half], low], axis=0), "fsdp", 1),
-        swap(jnp.concatenate([top, near_y[half:]], axis=0), "fsdp", 2),
+        return fence([shard] + [swap(shard, "fsdp", k) for k in range(1, n)], beside)
+    half = shard.shape[0] // 2
+    top, low = shard[:half], shard[half:]
+    x_top, y_low = swap(top, "fsdp", 1), swap(low, "fsdp", 2)
+    x_low, y_top = swap(low, "fsdp", 1), swap(top, "fsdp", 2)
+    x_top, y_low, beside = fence(x_top, y_low, beside)
+    far = [swap(x_top, "fsdp", 2), swap(y_low, "fsdp", 1)]
+    blocks = [
+        shard,
+        jnp.concatenate([x_top, x_low], axis=0),
+        jnp.concatenate([y_top, y_low], axis=0),
+        jnp.concatenate(far, axis=0),
     ]
-
-
-def scatter_end(own, got):
-    total = own.astype(f32)
-    for block in got:
-        total = total + block.astype(f32)
-    return total
-
-
-def gather_direct(shard):
+    return blocks, beside
+
+
+def scatter(part_of):
     n = lax.axis_size("fsdp")
-    return [shard] + [swap(shard, "fsdp", k) for k in range(1, n)]
+    if n != 4:
+        halves = []
+        for h in range(2):
+            total = part_of(0, h).astype(f32)
+            for k in range(1, n):
+                total = total + swap(part_of(k, h), "fsdp", k).astype(f32)
+            halves.append(total)
+        return jnp.concatenate(halves, axis=0)
+    from_x, from_y = swap(part_of(3, 0), "fsdp", 1), swap(part_of(3, 1), "fsdp", 2)
+    x_top, y_low = swap(part_of(1, 0), "fsdp", 1), swap(part_of(2, 1), "fsdp", 2)
+    low = (part_of(1, 1).astype(f32) + from_y.astype(f32)).astype(bf16)
+    top = (part_of(2, 0).astype(f32) + from_x.astype(f32)).astype(bf16)
+    x_low, y_top = swap(low, "fsdp", 1), swap(top, "fsdp", 2)
+    return jnp.concatenate(
+        [
+            part_of(0, 0).astype(f32) + x_top.astype(f32) + y_top.astype(f32),
+            part_of(0, 1).astype(f32) + x_low.astype(f32) + y_low.astype(f32),
+        ],
+        axis=0,
+    )
 
 
 def scatter_direct(block_of):
@@ -131,7 +123,10 @@
 
 
 def add_up(blocks):
-    return scatter_end(blocks[0], blocks[1:])
+    total = blocks[0].astype(f32)
+    for block in blocks[1:]:
+        total = total + block.astype(f32)
+    return total
 
 
 def assemble(shape, sources, pieces):
@@ -264,80 +259,81 @@
 class Reduction:
     def __init__(self, grad):
         self.grad = grad
-        self.other = None
-
-    def take(self, c):
-        n, me = lax.axis_size("fsdp"), lax.axis_index("fsdp")
-        rows, width = self.grad.shape[1:]
-        return jnp.concatenate(
-            [
-                lax.dynamic_slice(
-                    self.grad, (me ^ k, c * (rows // 2), 0), (1, rows // 2, width)
-                )
-                for k in range(n)
-            ]
-        )
 
     def begin(self):
         core = lax.axis_index("core")
-        both = self.take(core).astype(f32) + core_swap(self.take(1 - core)).astype(f32)
+        rows = self.grad.shape[1] // 2
+
+        def take(c):
+            return lax.dynamic_slice_in_dim(self.grad, c * rows, rows, axis=1)
+
+        both = take(core).astype(f32) + core_swap(take(1 - core)).astype(f32)
         self.half = both.astype(bf16)
 
     def exchange(self):
-        n = lax.axis_size("fsdp")
-        self.half = jnp.stack(
-            [self.half[0]] + [swap(self.half[k], "fsdp", k) for k in range(1, n)]
-        )
-
-    def finish(self, by_rows, start=0, size=None):
+        n, me = lax.axis_size("fsdp"), lax.axis_index("fsdp")
+        parts = [
+            lax.dynamic_index_in_dim(self.half, me ^ k, 0, keepdims=False) for k in range(n)
+        ]
+        self.half = jnp.stack([parts[0]] + [swap(parts[k], "fsdp", k) for k in range(1, n)])
+
+    def finish(self, by_rows, sizes=None):
         n, me = lax.axis_size("fsdp"), lax.axis_index("fsdp")
         core = lax.axis_index("core")
-        if self.other is None:
-            self.other = core_swap(self.half)
+        other = core_swap(self.half)
         rows, width = self.half.shape[1:]
-        size = width if size is None else size
-        column = start // size
-
-        def kernel(place, mine, other, out):
+        sizes = [width] if sizes is None else sizes
+
+        def kernel(place, mine, other, *outs):
+            def write(ref):
+                start = 0
+                for out, size in zip(outs, sizes):
+                    out[...] = ref[0, :, start : start + size].astype(f32)
+                    start += size
+
             @pl.when(pl.program_id(0) == 0)
             def _():
-                out[...] = mine[0].astype(f32)
+                write(mine)
 
             @pl.when(pl.program_id(0) == 1)
             def _():
-                out[...] = other[0].astype(f32)
+                write(other)
 
         def mine_at(w, k, place):
-            return (jnp.where(w == 0, k, n - 1), 0, column)
+            return (jnp.where(w == 0, k, n - 1), 0, 0)
 
         def other_at(w, k, place):
-            return (jnp.where(w == 0, 0, k), 0, column)
+            return (jnp.where(w == 0, 0, k), 0, 0)
 
         def out_at(w, k, place):
             source = place[0] ^ k
             side = jnp.where(w == 0, place[1], 1 - place[1])
             return (side, source) if by_rows else (source * 2 + side, 0)
 
-        return pl.pallas_call(
+        result = pl.pallas_call(
             kernel,
-            out_shape=jax.ShapeDtypeStruct(
-                (2 * rows, n * size) if by_rows else (2 * n * rows, size), f32
-            ),
+            out_shape=[
+                jax.ShapeDtypeStruct(
+                    (2 * rows, n * size) if by_rows else (2 * n * rows, size), f32
+                )
+                for size in sizes
+            ],
             grid_spec=pltpu.PrefetchScalarGridSpec(
                 num_scalar_prefetch=1,
                 grid=(2, n),
                 in_specs=[
-                    pl.BlockSpec((1, rows, size), mine_at),
-                    pl.BlockSpec((1, rows, size), other_at),
+                    pl.BlockSpec((1, rows, width), mine_at),
+                    pl.BlockSpec((1, rows, width), other_at),
                 ],
-                out_specs=pl.BlockSpec((rows, size), out_at),
+                out_specs=[pl.BlockSpec((rows, size), out_at) for size in sizes],
             ),
             compiler_params=pltpu.CompilerParams(vmem_limit_bytes=32 << 20),
             cost_estimate=pl.CostEstimate(
-                flops=0, bytes_accessed=2 * n * rows * size * 40, transcendentals=0
+                flops=0, bytes_accessed=2 * n * rows * width * 6, transcendentals=0
             ),
             name="place",
-        )(jnp.stack([me, core]).astype(jnp.int32), self.half, self.other)
+        )(jnp.stack([me, core]).astype(jnp.int32), self.half, other)
+        return result if len(sizes) > 1 else result[0]
 
 
 def roll_half(value):
@@ -579,38 +575,42 @@
     size = length // n
     ff = full_down.shape[0]
     step = 512 if ff % 512 == 0 else 256
-    steps = ff // step
+    first = ff // step
+    tile = 256
 
     def kernel(cot_ref, *refs):
         gates, ups = refs[:n], refs[n : 2 * n]
-        down, wg, wu, d_gate_ref, d_up_ref, out_ref, total, d_hidden_ref = refs[2 * n :]
+        down, wgu, d_gate_ref, d_up_ref, out_ref, both, d_hidden_ref = refs[2 * n :]
         f = pl.program_id(0)
-        d_hidden_ref[...] = matmul_nt(cot_ref[...], down[...])
-        for k in range(n):
-            rows = slice(k * size, (k + 1) * size)
-            d_hidden = d_hidden_ref[rows, :]
-            gate, up = gates[k][...], ups[k][...]
-            sg = 1.0 / (1.0 + jnp.exp(-gate))
-            d_gate_ref[rows, :] = (d_hidden * up * sg * (1.0 + gate * (1.0 - sg))).astype(bf16)
-            d_up_ref[rows, :] = (d_hidden * gate * sg).astype(bf16)
-
-        @pl.when(f == 0)
+
+        @pl.when(f < first)
         def _():
-            total[...] = matmul_nt(d_gate_ref[...], wg[...])
-
-        @pl.when(f > 0)
+            d_hidden_ref[...] = matmul_nt(cot_ref[...], down[...])
+            for k in range(n):
+                rows = slice(k * size, (k + 1) * size)
+                d_hidden = d_hidden_ref[rows, :]
+                gate, up = gates[k][...].astype(f32), ups[k][...].astype(f32)
+                sg = 1.0 / (1.0 + jnp.exp(-gate))
+                d_gate = (d_hidden * up * sg * (1.0 + gate * (1.0 - sg))).astype(bf16)
+                d_up = (d_hidden * gate * sg).astype(bf16)
+                d_gate_ref[rows, :] = d_gate
+                d_up_ref[rows, :] = d_up
+                at = pl.multiple_of(f * step, step)
+                both[rows, pl.ds(at, step)] = d_gate
+                both[rows, pl.ds(ff + at, step)] = d_up
+
+        @pl.when(f >= first)
         def _():
-            total[...] += matmul_nt(d_gate_ref[...], wg[...])
-
-        @pl.when(f < steps - 1)
-        def _():
-            total[...] += matmul_nt(d_up_ref[...], wu[...])
-
-        @pl.when(f == steps - 1)
-        def _():
-            out_ref[...] = (total[...] + matmul_nt(d_up_ref[...], wu[...])).astype(bf16)
+            out_ref[...] = matmul_nt(both[...], wgu[...]).astype(bf16)
 
     once = pl.Buffered(1)
+
+    def early(f):
+        return jnp.minimum(f, first - 1)
+
+    def late(f):
+        return jnp.maximum(f - first, 0)
+
     return pl.pallas_call(
         kernel,
         out_shape=[
@@ -618,21 +618,20 @@
             jax.ShapeDtypeStruct((length, ff), bf16),
             jax.ShapeDtypeStruct((length, width), bf16),
         ],
-        grid=(steps,),
+        grid=(first + width // tile,),
         in_specs=[pl.BlockSpec((length, width), lambda f: (0, 0), pipeline_mode=once)]
-        + [pl.BlockSpec((size, step), lambda f: (0, f))] * n
-        + [pl.BlockSpec((size, step), lambda f: (0, steps + f))] * n
+        + [pl.BlockSpec((size, step), lambda f: (0, early(f)))] * n
+        + [pl.BlockSpec((size, step), lambda f: (0, first + early(f)))] * n
         + [
-            pl.BlockSpec((step, width), lambda f: (f, 0)),
-            pl.BlockSpec((width, step), lambda f: (0, f)),
-            pl.BlockSpec((width, step), lambda f: (0, steps + f)),
+            pl.BlockSpec((step, width), lambda f: (early(f), 0)),
+            pl.BlockSpec((tile, 2 * ff), lambda f: (late(f), 0)),
         ],
         out_specs=[
-            pl.BlockSpec((length, step), lambda f: (0, f)),
-            pl.BlockSpec((length, step), lambda f: (0, f)),
-            pl.BlockSpec((length, width), lambda f: (0, 0), pipeline_mode=once),
+            pl.BlockSpec((length, step), lambda f: (0, early(f))),
+            pl.BlockSpec((length, step), lambda f: (0, early(f))),
+            pl.BlockSpec((length, tile), lambda f: (0, late(f))),
         ],
-        scratch_shapes=[pltpu.VMEM((length, width), f32), pltpu.VMEM((length, step), f32)],
+        scratch_shapes=[pltpu.VMEM((length, 2 * ff), bf16), pltpu.VMEM((length, step), f32)],
         compiler_params=pltpu.CompilerParams(vmem_limit_bytes=60 << 20),
         cost_estimate=pl.CostEstimate(
             flops=6 * length * ff * width,
@@ -640,7 +639,7 @@
             transcendentals=length * ff,
         ),
         name="feed_forward_backward",
-    )(cot, *gate_up_parts, *gate_up_parts, full_down, full_gu, full_gu)
+    )(cot, *gate_up_parts, *gate_up_parts, full_down, full_gu)
 
 
 def on_device(
@@ -670,14 +669,19 @@
     def block(value, k):
         return value[k * tok_rows : (k + 1) * tok_rows]
 
+    def half_block(value, k, h):
+        start = k * tok_rows + h * (tok_rows // 2)
+        return value[start : start + tok_rows // 2]
+
     def by_columns(first, second):
         columns = second.shape[1] // n
-        return jnp.stack(
+        grad = jnp.stack(
             [
                 matmul_tn(first, second[:, j * columns : (j + 1) * columns]).astype(bf16)
                 for j in range(n)
             ]
         )
+        return with_layout_constraint(grad, Layout(major_to_minor=(0, 1, 2)))
 
     def by_rows(first, second):
         grad = with_layout_constraint(
@@ -687,8 +691,9 @@
 
     sizes = [attn_gain.shape[0], mlp_gain.shape[0], query_gain.shape[0], key_gain.shape[0]]
     packed = jnp.concatenate([attn_gain, mlp_gain, query_gain, key_gain])[None]
-    tok = gather_begin(tokens[0])
+    tok, _ = gather(tokens[0])
     gains = [packed] + [swap(packed, "fsdp", k) for k in range(1, n)]
+    gains, w_query, w_key, w_value, w_out = fence(gains, w_query, w_key, w_value, w_out)
     attn_spread = Spread([w_query, w_key, w_value], [w_out])
     attn_got = attn_spread.begin()
     index = jnp.concatenate(
@@ -715,19 +720,21 @@
     gain_query = gains[:, ends[1] : ends[2]].reshape(-1)
     gain_key = gains[:, ends[2] : ends[3]].reshape(-1)
     attn_got = jnp.stack(attn_got)
-    tok, attn_got, cos_table, sin_table, first, w_gate, w_up = fence(
-        tok, attn_got, cos_table, sin_table, first, w_gate, w_up
-    )
-
-    tok = gather_end(tokens[0], tok)
     attn_along, attn_across = swap(attn_got, "z", 1), core_swap(attn_got)
+    whole = segments[0, 0] == 0
+    tok, cos_table, sin_table, first, w_gate, w_up, whole = fence(
+        tok, cos_table, sin_table, first, w_gate, w_up, whole
+    )
+
     gu_spread = Spread([w_gate, w_up], [])
     gu_got = gu_spread.begin()
-    tok, attn_along, attn_across = fence(tok, attn_along, attn_across)
-
     attn_sources = [attn_got, attn_along, attn_across, core_swap(attn_along)]
-    stream_all = jnp.concatenate(tok, axis=0).astype(f32)
-    normed = (stream_all * rms_scale(stream_all) * gain_attn).astype(bf16)
+
+    def normed_block(part):
+        part = part.astype(f32)
+        return (part * rms_scale(part) * gain_attn).astype(bf16)
+
+    normed = jnp.concatenate([normed_block(part) for part in tok], axis=0)
     full_qkv = attn_spread.join_rows(attn_sources)
     qkv = matmul(normed, full_qkv)
     queries, keys, values, attended, lse = attention_forward(
@@ -739,75 +746,85 @@
 
     gu_got = jnp.stack(gu_got)
     gu_along, gu_across = swap(gu_got, "z", 1), core_swap(gu_got)
-    begun = scatter_begin(matmul(block(attended, n - 1), full_out).astype(bf16))
-    parts = [matmul(block(attended, k), full_out).astype(bf16) for k in range(n - 1)]
+    def out_part(k, h):
+        return matmul(half_block(attended, k, h), full_out).astype(bf16)
+
     stream = tokens[0].astype(f32)
-    middle = stream + scatter_end(parts[0], scatter_middle(parts[1:], begun))
+    middle = stream + scatter(out_part)
     mlp_scale = rms_scale(middle)
     normed_mine = (middle * mlp_scale * gain_mlp).astype(bf16)
-    middle, mlp_scale, normed_mine = fence(middle, mlp_scale, normed_mine)
-
-    begun = gather_begin(normed_mine)
-    begun, gu_along, gu_across = fence(begun, gu_along, gu_across)
+    middle, mlp_scale, normed_mine, w_down = fence(middle, mlp_scale, normed_mine, w_down)
+
+    normed_parts, _ = gather(normed_mine)
+    down_spread = Spread([], [w_down])
+    down_got = jnp.stack(down_spread.begin())
+    normed_parts, gu_along, gu_across, cot, down_got = fence(
+        normed_parts, gu_along, gu_across, cot, down_got
+    )
 
     def gate_and_up(part):
         both = matmul(part, full_gu)
         gate, up = both[:, :ff], both[:, ff:]
         return both, (gate / (1.0 + jnp.exp(-gate)) * up).astype(bf16)
 
-    normed_parts = gather_end(normed_mine, begun)
     full_gu = gu_spread.join_rows([gu_got, gu_along, gu_across, core_swap(gu_along)])
-    normed_parts, full_gu, cot, w_down = fence(normed_parts, full_gu, cot, w_down)
-
-    cot_begun = gather_begin(cot)
-    acts = [gate_and_up(part) for part in normed_parts]
+
+    down_along, down_across = swap(down_got, "z", 1), core_swap(down_got)
+    own_act = gate_and_up(normed_parts[0])
+    cot_parts, (own_act, full_gu) = gather(cot, beside=(own_act, full_gu))
+    acts = [own_act] + [gate_and_up(part) for part in normed_parts[1:]]
+    acts, down_along, down_across = fence(acts, down_along, down_across)
     normed_mlp = jnp.concatenate(normed_parts, axis=0)
     hidden = jnp.concatenate([act[1] for act in acts], axis=0)
-    cot_begun, acts, normed_mlp, hidden, w_down = fence(
-        cot_begun, acts, normed_mlp, hidden, w_down
-    )
-
-    cot_parts = gather_end(cot, cot_begun)
     cot_all = jnp.concatenate(cot_parts, axis=0)
-    cot_all, w_down = fence(cot_all, w_down)
-    down = Reduction(by_columns(hidden, cot_all))
-    down.begin()
-    down.half, cot_all, w_down = fence(down.half, cot_all, w_down)
-
-    whole = segments[0, 0] == 0
+    full_down = down_spread.join_columns(
+        [down_got, down_along, down_across, core_swap(down_along)]
+    )
+    cot_all, full_down, hidden, normed_mlp, acts = fence(
+        cot_all, full_down, hidden, normed_mlp, acts
+    )
+
+    core = lax.axis_index("core")
+
+    def down_grad(c):
+        part = lax.dynamic_slice_in_dim(hidden, c * (ff // 2), ff // 2, axis=1)
+        return by_columns(part, cot_all)
+
+    down = Reduction(None)
+    other = core_swap(down_grad(1 - core))
+    down.half = (down_grad(core).astype(f32) + other.astype(f32)).astype(bf16)
+    down.half, cot_all, full_down = fence(down.half, cot_all, full_down)
 
     def feed_forward_part():
-        down_spread = Spread([], [w_down], along_z=False)
-        got = jnp.stack(down_spread.begin())
-        full_down = down_spread.join_columns([got, core_swap(got)])
+        out_partial, cots = fence(matmul(hidden, full_down).astype(bf16), cot_all)
+        out_got = scatter_direct(lambda k: block(out_partial, k))
         d_gate, d_up, d_normed_mlp = feed_forward_backward(
-            cot_all, [act[0] for act in acts], full_down, full_gu
+            cots, [act[0] for act in acts], full_down, full_gu
         )
-        gate = Reduction(by_rows(normed_mlp, d_gate))
+        grad_gate, d_up, out_got = fence(by_rows(normed_mlp, d_gate), d_up, out_got)
+        output = (middle + add_up(out_got)).astype(bf16)
+        gate = Reduction(grad_gate)
         gate.begin()
         gate.exchange()
         up = Reduction(by_rows(normed_mlp, d_up))
         up.begin()
-        return full_down, d_normed_mlp, gate.half, up.half
+        return output, d_normed_mlp, gate.half, up.half
 
     down.half = lax.psum(down.half, "z")
-    full_down, d_normed_mlp, gate_half, up_half = block_of_work(whole, feed_forward_part)
-    down.half, full_down, d_normed_mlp, gate_half, up_half = fence(
-        down.half, full_down, d_normed_mlp, gate_half, up_half
+    output, d_normed_mlp, gate_half, up_half = block_of_work(whole, feed_forward_part)
+    down.half, output, d_normed_mlp, gate_half, up_half = fence(
+        down.half, output, d_normed_mlp, gate_half, up_half
     )
 
     def attention_part():
-        begun = scatter_begin(block(d_normed_mlp, n - 1))
-        got = scatter_middle([block(d_normed_mlp, k) for k in range(1, n - 1)], begun)
-        d_normed_mine = scatter_end(block(d_normed_mlp, 0), got)
+        d_normed_mine = scatter(lambda k, h: half_block(d_normed_mlp, k, h))
         d_middle, mlp_gain_rows = norm_back(middle, mlp_scale, gain_mlp, d_normed_mine)
         mlp_gain_grad = jnp.sum(mlp_gain_rows, axis=0)
         d_middle = cot.astype(f32) + d_middle
         d_mine = d_middle.astype(bf16)
-        out_parts = [matmul(block(hidden, k), full_down).astype(bf16) for k in range(n)]
-        d_branch = jnp.concatenate(gather_end(d_mine, gather_begin(d_mine)), axis=0)
+        d_branch = jnp.concatenate(gather(d_mine)[0], axis=0)
         d_attended = matmul_nt(d_branch, full_out).astype(bf16)
-        d_attended, down_half, out_parts = fence(d_attended, down.half, out_parts)
+        d_attended, down_half = fence(d_attended, down.half)
         d_qkv, *head_gain_grads = attention_backward(
             qkv,
             queries,
@@ -827,30 +844,30 @@
         qkv_sum = Reduction(by_rows(normed, d_qkv))
         qkv_sum.begin()
         qkv_sum.exchange()
-        out_got = scatter_middle(out_parts[1 : n - 1], scatter_begin(out_parts[n - 1]))
-        output = (middle + scatter_end(out_parts[0], out_got)).astype(bf16)
         down_sum = Reduction(None)
         down_sum.half = down_half
         down_sum.exchange()
         return (
             d_middle,
             mlp_gain_grad,
-            d_qkv,
+            matmul_nt(d_qkv, full_qkv).astype(bf16),
             head_gain_grads,
             out_sum.half,
             qkv_sum.half,
-            output,
             down_sum.finish(False),
         )
 
     gate_half, up_half = lax.psum((gate_half, up_half), "z")
     gate_half, up_half, done = fence(gate_half, up_half, block_of_work(whole, attention_part))
-    d_middle, mlp_gain_grad, d_qkv, head_gain_grads, out_half, qkv_half, output, down_full = done
+    d_middle, mlp_gain_grad, partial, head_gain_grads, out_half, qkv_half, down_full = done
 
     def input_part():
-        begun = scatter_begin(matmul_nt(block(d_qkv, n - 1), full_qkv).astype(bf16))
-        parts = [matmul_nt(block(d_qkv, k), full_qkv).astype(bf16) for k in range(n - 1)]
-        d_normed = scatter_end(parts[0], scatter_middle(parts[1:], begun))
+        d_normed = scatter(lambda k, h: half_block(partial, k, h))
+        gate, up = Reduction(None), Reduction(None)
+        gate.half, up.half = gate_half, up_half
+        up.exchange()
+        d_normed, gate_full = fence(d_normed, gate.finish(True))
+        stream = tokens[0].astype(f32)
         d_stream, attn_gain_rows = norm_back(stream, rms_scale(stream), gain_attn, d_normed)
         gain_grads = jnp.concatenate(
             [jnp.sum(attn_gain_rows, axis=0), mlp_gain_grad] + head_gain_grads
@@ -864,10 +881,7 @@
         for size in sizes:
             shares.append(rows_of(gain_grads, start + me * size, size))
             start += n * size
-        gate, up = Reduction(None), Reduction(None)
-        gate.half, up.half = gate_half, up_half
-        up.exchange()
-        return shares, d_middle + d_stream, gate.finish(True), up.finish(True)
+        return shares, d_middle + d_stream, gate_full, up.finish(True)
 
     qkv_sum, out_sum = Reduction(None), Reduction(None)
     qkv_sum.half, out_sum.half = lax.psum((qkv_half, out_half), "z")
@@ -875,13 +889,14 @@
         qkv_sum.half, out_sum.half, block_of_work(whole, input_part)
     )
     shares, input_grad, gate_full, up_full = done
+    query_full, key_full, value_full = qkv_sum.finish(True, [q_width, kv_width, kv_width])
     return (
         output[None],
         input_grad[None],
         shares[0],
-        qkv_sum.finish(True, 0, q_width),
-        qkv_sum.finish(True, q_width, kv_width),
-        qkv_sum.finish(True, q_width + kv_width, kv_width),
+        query_full,
+        key_full,
+        value_full,
         shares[2],
         shares[3],
         out_sum.finish(False),

time: 848 us -> 789 us (0.930)
  waiting for transfers between devices: 402 us -> 332 us
  matrix products: 97 us -> 78.5 us
  local copies, waits for them, and re-layouts: 54.1 us -> 72.3 us
  starting transfers between devices: 80.5 us -> 90 us
    ppermute x81 -> x96, waiting for transfers between devices: 400 us -> 319 us  [swap(): lax.ppermute(value, axis, [(j, j ^ k) for j in range(lax.axis_size(axis))])]
    psum x1, waiting for transfers between devices: 0.02 us -> 12.9 us  [on_device(): gate_half, up_half = lax.psum((gate_half, up_half), 'z')]
    dot_general x13 -> x14, matrix products: 43.3 us -> 32.5 us  [matmul(): return jnp.dot(first, second, preferred_element_type=f32)]
    cond x61 -> x69, local copies, waits for them, and re-layouts: 7.19 us -> 17 us
    ppermute x81 -> x96, starting transfers between devices: 80.4 us -> 89.9 us  [swap(): lax.ppermute(value, axis, [(j, j ^ k) for j in range(lax.axis_size(axis))])]
    pallas_call x7 -> x5, Pallas kernels: 43.3 us -> 37.1 us  [finish(): pl.pallas_call(kernel, out_shape=[jax.ShapeDtypeStruct((2 * rows, n * siz...]
    unnamed x124 -> x162, local copies, waits for them, and re-layouts: 19.1 us -> 19.9 us
    dot_general x11 -> x15, matrix products: 37.1 us -> 37.5 us  [matmul_tn(): lax.dot_general(first, second, (((0,), (0,)), ((), ())), preferred_elemen...]
  transfers between devices with their start and end apart: 84 -> 99, of which waited for: 46 -> 56; matrix products, arithmetic and copies ran while one was open for 23% -> 25% of each run, Pallas kernels for 11% -> 12%
where the time goes in v4:
time: 789 us; the launch traced here: 779 us
  waiting for transfers between devices  332 us (42%)
  Pallas kernels  103 us (13%)
  starting transfers between devices  90 us (11%)
  other arithmetic  84.9 us (11%)
  matrix products  78.5 us (10%)
  local copies, waits for them, and re-layouts  72.3 us (9%)
  between operations  16.3 us (2%)
    ppermute x96, waiting for transfers between devices, swap(): lax.ppermute(value, axis, [(j, j ^ k) for j in range(lax.axis_size(axis))])  319 us
    ppermute x96, starting transfers between devices, swap(): lax.ppermute(value, axis, [(j, j ^ k) for j in range(lax.axis_size(axis))])  89.9 us
    dot_general x15, matrix products, matmul_tn(): lax.dot_general(first, second, (((0,), (0,)), ((), ())), preferred_elemen...  37.5 us
    pallas_call x5, Pallas kernels, finish(): pl.pallas_call(kernel, out_shape=[jax.ShapeDtypeStruct((2 * rows, n * siz...  37.1 us
    dot_general x14, matrix products, matmul(): return jnp.dot(first, second, preferred_element_type=f32)  32.5 us
    pallas_call x1, Pallas kernels, feed_forward_backward(): pl.pallas_call(kernel, out_shape=[jax.ShapeDtypeStruct((length, ff), bf16...  32.1 us
    unnamed x162, local copies, waits for them, and re-layouts  19.9 us
    cond x69, local copies, waits for them, and re-layouts  17 us
  transfers between devices with their start and end apart: 99, of which 56 were waited for; matrix products, arithmetic and copies ran while one was open for 25% of the time, Pallas kernels for 12%

profile of v4, /device:TPU:0, one launch (start us, length us, event | category | flops | bytes accessed | tf_op | source)
XLA Modules:
  0.0 778.8 jit_solution(8985958823050812983)
XLA Ops:
  39.6 5.8 collective-permute-done.48
  47.0 6.9 collective-permute-done.59
  70.9 6.2 collective-permute-done.52
  93.3 4.5 fusion.86.q_ref.k_ref.v_ref
  97.8 8.4 %attention_forward.1 = (bf16[1024,512]{1,0:T(8,128)(2,1)}, bf16[1024,256]{1,0:T(8,128)(2,1)}, bf16[1024,256]{1,0:T(8,128)(2,1)}, bf16[1024,512]{1,0:T(8,128)(2,1)S(1)}, f32[2,2,4,1,256]{4,3,2,1,0:T(1,128)}) custom-call(s32[1]{0:T(128)} %bitcast.55.me_ref, f32[1024,1024]{1,0:T(8,128)S(1)} %fusion.86.q_ref.k_ref.v_ref, ...), custom_call_target="tpu_custom_call" | custom-call | flops 2147483648 | bytes 6291456 | tf_op jit(solution)/shard_map/attention_forward/pallas_call | solution.py:404
  106.2 9.5 %collective-permute-done.64 = bf16[128,3072]{1,0:T(8,128)(2,1)} collective-permute-done((bf16[128,3072]{1,0:T(8,128)(2,1)}, bf16[128,3072]{1,0:T(8,128)(2,1)}, u32[]{:S(2)}, u32[]{:S(2)}) %collective-permute-start.64) | collective-permute-done | bytes 786464 | tf_op jit(solution)/shard_map/ppermute | solution.py:51
  121.9 16.9 %collective-permute-done.69 = bf16[128,2048]{1,0:T(8,128)(2,1)S(1)} collective-permute-done((bf16[128,2048]{1,0:T(8,128)(2,1)S(1)}, bf16[128,2048]{1,0:T(8,128)(2,1)S(1)}, u32[]{:S(2)}, u32[]{:S(2)}) %collective-permute-start.69) | collective-permute-done | bytes 524320 | tf_op jit(solution)/shard_map/ppermute | solution.py:51
  158.2 9.3 %collective-permute-done.82 = bf16[384,512]{1,0:T(8,128)(2,1)S(1)} collective-permute-done((bf16[384,512]{1,0:T(8,128)(2,1)S(1)}, bf16[384,512]{1,0:T(8,128)(2,1)S(1)}, u32[]{:S(2)}, u32[]{:S(2)}) %collective-permute-start.82) | collective-permute-done | bytes 393248 | tf_op jit(solution)/shard_map/ppermute | solution.py:51
  174.8 8.0 %collective-permute-done.73 = bf16[128,2048]{1,0:T(8,128)(2,1)S(1)} collective-permute-done((bf16[128,2048]{1,0:T(8,128)(2,1)S(1)}, bf16[128,2048]{1,0:T(8,128)(2,1)S(1)}, u32[]{:S(2)}, u32[]{:S(2)}) %collective-permute-start.73) | collective-permute-done | bytes 524320 | tf_op jit(solution)/shard_map/ppermute | solution.py:51
  182.9 10.3 %collective-permute-done.80 = bf16[384,512]{1,0:T(8,128)(2,1)S(1)} collective-permute-done((bf16[384,512]{1,0:T(8,128)(2,1)S(1)}, bf16[384,512]{1,0:T(8,128)(2,1)S(1)}, u32[]{:S(2)}, u32[]{:S(2)}) %collective-permute-start.80) | collective-permute-done | bytes 393248 | tf_op jit(solution)/shard_map/ppermute | solution.py:51
  198.6 5.5 collective-permute-done.77
  254.0 9.0 %collective-permute-done.88 = bf16[128,2048]{1,0:T(8,128)(2,1)S(1)} collective-permute-done((bf16[128,2048]{1,0:T(8,128)(2,1)S(1)}, bf16[128,2048]{1,0:T(8,128)(2,1)S(1)}, u32[]{:S(2)}, u32[]{:S(2)}) %collective-permute-start.88) | collective-permute-done | bytes 524320 | tf_op jit(solution)/shard_map/ppermute | solution.py:51
  288.4 118.5 %conditional.3 = (bf16[256,2048]{1,0:T(8,128)(2,1)}, bf16[1024,2048]{1,0:T(8,128)(2,1)}, bf16[4,256,1536]{2,1,0:T(8,128)(2,1)}, bf16[4,256,1536]{2,1,0:T(8,128)(2,1)}) conditional(s32[]{:T(128)} %convert_element_type.395, () %tuple.62, (bf16[1024,1536]{1,0:T(8,128)(2,1)}, bf16[1536,2048]{1,0:T(8,128)(2,1)}, bf16[1024,2048]{1,0:T(8,128)(2,1)}, ...), branch_computations={%region_7.8_spmd, %region_8.9_spmd} | conditional | flops 38685114368 | bytes 265290592 | solution.py:69
  288.4 10.4 %convolution_convert_fusion.2 = bf16[1024,2048]{1,0:T(8,128)(2,1)S(1)} fusion(bf16[1024,1536]{1,0:T(8,128)(2,1)} %get-tuple-element.81, bf16[1536,2048]{1,0:T(8,128)(2,1)} %get-tuple-element.82.refs_8_), kind=kOutput, calls=%fused_computation.4 | convolution fusion | flops 6444548096 | bytes 13631488 | tf_op jit(solution)/shard_map/cond/branch_1_fun/dot_general | solution.py:27
  304.0 32.1 %feed_forward_backward.1 = (bf16[1024,1536]{1,0:T(8,128)(2,1)}, bf16[1024,1536]{1,0:T(8,128)(2,1)}, bf16[1024,2048]{1,0:T(8,128)(2,1)}) custom-call(bf16[1024,2048]{1,0:T(8,128)(2,1)} %get-tuple-element.84.cot_ref, f32[256,3072]{1,0:T(8,128)} %get-tuple-element.85.refs_0_.refs_4_, f32[256,3072]{1,0:T(8,128)} %get-tuple-element.86.refs_1_.refs_5_, ...), custom_call_target="tpu_custom_call" | custom-call | flops 19327352832 | bytes 18874368 | tf_op jit(solution)/shard_map/cond/branch_1_fun/feed_forward_backward/pallas_call | solution.py:614
  336.2 9.9 %convolution_convert_fusion.1 = bf16[1536,2048]{0,1:T(8,128)(2,1)S(1)} fusion(bf16[1024,1536]{1,0:T(8,128)(2,1)} %get-tuple-element.90, bf16[1024,2048]{1,0:T(8,128)(2,1)} %get-tuple-element.91), kind=kOutput, calls=%fused_computation.1 | convolution fusion | flops 6445596672 | bytes 13631488 | tf_op jit(solution)/shard_map/cond/branch_1_fun/dot_general | solution.py:31
  351.6 7.4 convolution_convert_fusion
  374.0 4.4 add_convert_fusion
  378.4 9.7 %collective-permute-done.22 = bf16[256,1536]{1,0:T(8,128)(2,1)S(1)} collective-permute-done((bf16[256,1536]{1,0:T(8,128)(2,1)S(1)}, bf16[256,1536]{1,0:T(8,128)(2,1)S(1)}, u32[]{:S(2)}, u32[]{:S(2)}) %collective-permute-start.22) | collective-permute-done | bytes 786464 | tf_op jit(solution)/shard_map/cond/branch_1_fun/ppermute | solution.py:51
  388.1 16.3 %collective-permute-done.21 = bf16[256,1536]{1,0:T(8,128)(2,1)S(1)} collective-permute-done((bf16[256,1536]{1,0:T(8,128)(2,1)S(1)}, bf16[256,1536]{1,0:T(8,128)(2,1)S(1)}, u32[]{:S(2)}, u32[]{:S(2)}) %collective-permute-start.21) | collective-permute-done | bytes 786464 | tf_op jit(solution)/shard_map/cond/branch_1_fun/ppermute | solution.py:51
  413.2 205.2 %conditional.4 = (f32[256,2048]{1,0:T(8,128)}, f32[2048]{0:T(1024)S(1)}, bf16[1024,2048]{1,0:T(8,128)(2,1)}, f32[128]{0:T(128)S(1)}, f32[128]{0:T(128)S(1)}, /*i...) conditional(s32[]{:T(128)} %convert_element_type.395, () %tuple.65, ...), branch_computations={%region_11.12_spmd, %region_12.17_spmd} | conditional | flops 18291357696 | bytes 395370496 | solution.py:69
  418.7 11.5 %collective-permute-done.25 = bf16[128,2048]{1,0:T(8,128)(2,1)S(1)} collective-permute-done((bf16[128,2048]{1,0:T(8,128)(2,1)S(1)}, bf16[128,2048]{1,0:T(8,128)(2,1)S(1)}, u32[]{:S(2)}, u32[]{:S(2)}) %collective-permute-start.25) | collective-permute-done | bytes 524320 | tf_op jit(solution)/shard_map/cond/branch_1_fun/ppermute | solution.py:51
  433.5 7.1 collective-permute-done.24
  440.6 5.7 collective-permute-done.26
  449.3 5.7 collective-permute-done.29
  466.8 10.9 %collective-permute-done.30 = bf16[128,2048]{1,0:T(8,128)(2,1)S(1)} collective-permute-done((bf16[128,2048]{1,0:T(8,128)(2,1)}, bf16[128,2048]{1,0:T(8,128)(2,1)S(1)}, u32[]{:S(2)}, u32[]{:S(2)}) %collective-permute-start.30) | collective-permute-done | bytes 524320 | tf_op jit(solution)/shard_map/cond/branch_1_fun/ppermute | solution.py:51
  481.8 7.2 collective-permute-done.32
  503.5 13.8 %attention_backward.1 = (bf16[1024,512]{1,0:T(8,128)(2,1)S(1)}, bf16[1024,256]{1,0:T(8,128)(2,1)S(1)}, bf16[1024,256]{1,0:T(8,128)(2,1)S(1)}, f32[2,1,128]{2,1,0:T(1,128)S(1)}, f32[2,1,128]{2,1,0:T(1,128)S(1)}) custom-call(s32[1]{0:T(128)} %bitcast.13.me_ref, f32[1024,1024]{1,0:T(8,128)S(1)} %copy-done.17, f32[1024,1024]{1,0:T(8,128)S(1)} %copy-done.17, ...), custom_call_target="tpu_custom_call" | custom-call | flops 5368709120 | bytes 10485760 | tf_op jit(solution)/shard_map/cond/branch_1_fun/attention_backward/pallas_call | solution.py:512
  520.4 4.9 convolution_convert_fusion.3
  536.5 14.9 %collective-permute-done.46 = bf16[768,512]{1,0:T(8,128)(2,1)S(1)} collective-permute-done((bf16[768,512]{1,0:T(8,128)(2,1)S(1)}, bf16[768,512]{1,0:T(8,128)(2,1)S(1)}, u32[]{:S(2)}, u32[]{:S(2)}) %collective-permute-start.46) | collective-permute-done | bytes 786464 | tf_op jit(solution)/shard_map/cond/branch_1_fun/ppermute | solution.py:51
  551.4 13.5 %collective-permute-done.45 = bf16[768,512]{1,0:T(8,128)(2,1)S(1)} collective-permute-done((bf16[768,512]{1,0:T(8,128)(2,1)S(1)}, bf16[768,512]{1,0:T(8,128)(2,1)S(1)}, u32[]{:S(2)}, u32[]{:S(2)}) %collective-permute-start.45) | collective-permute-done | bytes 786464 | tf_op jit(solution)/shard_map/cond/branch_1_fun/ppermute | solution.py:51
  579.2 5.1 collective-permute-done.38
  585.9 6.1 convolution_convert_fusion.4
  595.7 10.6 %collective-permute-done.42 = bf16[256,1024]{1,0:T(8,128)(2,1)} collective-permute-done((bf16[256,1024]{1,0:T(8,128)(2,1)}, bf16[256,1024]{1,0:T(8,128)(2,1)}, u32[]{:S(2)}, u32[]{:S(2)}) %collective-permute-start.42) | collective-permute-done | bytes 524320 | tf_op jit(solution)/shard_map/cond/branch_1_fun/ppermute | solution.py:51
  609.4 8.7 %place.5 = f32[6144,512]{1,0:T(8,128)} custom-call(s32[2]{0:T(128)S(1)} %pad_add_fusion.place, bf16[4,768,512]{2,1,0:T(8,128)(2,1)S(1)} %pad_maximum_fusion.1.mine, bf16[4,768,512]{2,1,0:T(8,128)(2,1)} %collective-permute-done.47.other), custom_call_target="tpu_custom_call" | custom-call | bytes 18874368 | tf_op jit(solution)/shard_map/cond/branch_1_fun/place/pallas_call | solution.py:313
  618.4 12.9 %all-reduce.10.cloned.1.call-done = (bf16[4,256,1536]{2,1,0:T(8,128)(2,1)}, bf16[4,256,1536]{2,1,0:T(8,128)(2,1)}) async-done(((bf16[4,256,1536]{2,1,0:T(8,128)(2,1)}, bf16[4,256,1536]{2,1,0:T(8,128)(2,1)}), (bf16[4,256,1536]{2,1,0:T(8,128)(2,1)}, bf16[4,256,1536]{2,1,0:T(8,128)(2,1)})) %all-reduce.10.cloned.1.call-update) | async-done | bytes 6291472 | tf_op jit(solution)/shard_map/psum | solution.py:860
  633.2 121.8 %conditional.5 = (f32[512]{0:T(512)S(1)}, f32[512]{0:T(512)S(1)}, f32[32]{0:T(128)S(1)}, f32[32]{0:T(128)S(1)}, f32[256,2048]{1,0:T(8,128)}, /*index=5*/f32[512,6144]{1,0:T(8,128)}, f32[512,6144]{1,0:T(8,128)}) conditional(s32[]{:T(128)} %convert_element_type.395, () %tuple.68, (bf16[1024,2048]{1,0:T(8,128)(2,1)}, ...), branch_computations={%region_19.20_spmd, %region_20.24_spmd} | conditional | flops 18921000 | bytes 147506976 | solution.py:69
  641.3 9.9 %collective-permute-done.1 = bf16[128,2048]{1,0:T(8,128)(2,1)} collective-permute-done((bf16[128,2048]{1,0:T(8,128)(2,1)}, bf16[128,2048]{1,0:T(8,128)(2,1)}, u32[]{:S(2)}, u32[]{:S(2)}) %collective-permute-start.1) | collective-permute-done | bytes 524320 | tf_op jit(solution)/shard_map/cond/branch_1_fun/ppermute | solution.py:51
  654.0 14.9 %collective-permute-done.14 = bf16[256,1536]{1,0:T(8,128)(2,1)S(1)} collective-permute-done((bf16[256,1536]{1,0:T(8,128)(2,1)S(1)}, bf16[256,1536]{1,0:T(8,128)(2,1)S(1)}, u32[]{:S(2)}, u32[]{:S(2)}) %collective-permute-start.14) | collective-permute-done | bytes 786464 | tf_op jit(solution)/shard_map/cond/branch_1_fun/ppermute | solution.py:51
  669.4 7.2 collective-permute-done.13
  677.2 7.7 collective-permute-done.12
  686.7 8.2 %collective-permute-done = bf16[128,2048]{1,0:T(8,128)(2,1)S(1)} collective-permute-done((bf16[128,2048]{1,0:T(8,128)(2,1)S(1)}, bf16[128,2048]{1,0:T(8,128)(2,1)S(1)}, u32[]{:S(2)}, u32[]{:S(2)}) %collective-permute-start) | collective-permute-done | bytes 524320 | tf_op jit(solution)/shard_map/cond/branch_1_fun/ppermute | solution.py:51
  714.4 10.5 %place.6 = f32[512,6144]{1,0:T(8,128)} custom-call(s32[2]{0:T(128)S(1)} %pad_add_fusion.1.place, bf16[4,256,1536]{2,1,0:T(8,128)(2,1)} %get-tuple-element.131.mine, bf16[4,256,1536]{2,1,0:T(8,128)(2,1)} %collective-permute-done.6.other), custom_call_target="tpu_custom_call" | custom-call | bytes 18874368 | tf_op jit(solution)/shard_map/cond/branch_1_fun/place/pallas_call | solution.py:313
  734.4 4.8 collective-permute-done.10
  739.9 4.4 fusion.13
  746.2 8.7 %place.7 = f32[512,6144]{1,0:T(8,128)} custom-call(s32[2]{0:T(128)S(1)} %pad_add_fusion.1.place, bf16[4,256,1536]{2,1,0:T(8,128)(2,1)S(1)} %pad_maximum_fusion.6.mine, bf16[4,256,1536]{2,1,0:T(8,128)(2,1)} %collective-permute-done.15.other), custom_call_target="tpu_custom_call" | custom-call | bytes 18874368 | tf_op jit(solution)/shard_map/cond/branch_1_fun/place/pallas_call | solution.py:313
  756.1 5.3 collective-permute-done.95.other
  766.8 5.0 place.8
  (561 shorter events, 345.4 us)
Async XLA Ops:
  7.2 399.7 %all-reduce.6.cloned.1.call-start = ((), (), s32[]{:S(2)}) async-start(), calls=%async_computation | async-start | bytes 6291456 | tf_op jit(solution)/shard_map/psum | solution.py:813
  16.9 48.5 %collective-permute-start.50 = (bf16[128,2048]{1,0:T(8,128)(2,1)}, bf16[128,2048]{1,0:T(8,128)(2,1)}, u32[]{:S(2)}, u32[]{:S(2)}) collective-permute-start(bf16[128,2048]{1,0:T(8,128)(2,1)} %get-tuple-element.466), channel_id=1, source_target_pairs={{0,8},{8,0},{16,24},{24,16},{1,9},{9,1},{17,25},{25,17},{2,10},{10... | collective-permute-start | bytes 1572872 | tf_op jit(solution)/shard_map/ppermute | solution.py:51
  18.8 27.7 %collective-permute-start.49 = (bf16[128,2048]{1,0:T(8,128)(2,1)}, bf16[128,2048]{1,0:T(8,128)(2,1)}, u32[]{:S(2)}, u32[]{:S(2)}) collective-permute-start(bf16[128,2048]{1,0:T(8,128)(2,1)} %get-tuple-element.466), channel_id=1, source_target_pairs={{0,16},{8,24},{16,0},{24,8},{1,17},{9,25},{17,1},{25,9},{2,18},{10... | collective-permute-start | bytes 1572872 | tf_op jit(solution)/shard_map/ppermute | solution.py:51
  46.5 22.2 %collective-permute-start.51 = (bf16[128,2048]{1,0:T(8,128)(2,1)}, bf16[128,2048]{1,0:T(8,128)(2,1)}, u32[]{:S(2)}, u32[]{:S(2)}) collective-permute-start(bf16[128,2048]{1,0:T(8,128)(2,1)} %get-tuple-element.465), channel_id=1, source_target_pairs={{0,16},{8,24},{16,0},{24,8},{1,17},{9,25},{17,1},{25,9},{2,18},{10... | collective-permute-start | bytes 1572872 | tf_op jit(solution)/shard_map/ppermute | solution.py:51
  63.7 22.8 %collective-permute-start.60 = (bf16[3,128,1536]{2,1,0:T(8,128)(2,1)S(1)}, bf16[3,128,1536]{2,1,0:T(8,128)(2,1)S(1)}, u32[]{:S(2)}, u32[]{:S(2)}) collective-permute-start(bf16[3,128,1536]{2,1,0:T(8,128)(2,1)S(1)} %pad_maximum_fusion.14.refs_0_), channel_id=1, source_target_pairs={{0,2},{2,0},{4,6},{6,4},{1,3},{3,1},{5,7},{7,5},{8,10},{10,8},{12,... | collective-permute-start | bytes 3538952 | tf_op jit(solution)/shard_map/ppermute | solution.py:51
  65.4 22.8 %collective-permute-start.61 = (bf16[3,128,1536]{2,1,0:T(8,128)(2,1)S(1)}, bf16[3,128,1536]{2,1,0:T(8,128)(2,1)S(1)}, u32[]{:S(2)}, u32[]{:S(2)}) collective-permute-start(bf16[3,128,1536]{2,1,0:T(8,128)(2,1)S(1)} %pad_maximum_fusion.14.refs_0_), channel_id=1, source_target_pairs={{0,1},{1,0},{2,3},{3,2},{4,5},{5,4},{6,7},{7,6},{8,9},{9,8},{10,11... | collective-permute-start | bytes 3538952 | tf_op jit(solution)/shard_map/ppermute | solution.py:51
  80.0 26.2 %collective-permute-start.63 = (bf16[128,3072]{1,0:T(8,128)(2,1)}, bf16[128,3072]{1,0:T(8,128)(2,1)}, u32[]{:S(2)}, u32[]{:S(2)}) collective-permute-start(bf16[128,3072]{1,0:T(8,128)(2,1)} %pad_maximum_fusion.22), channel_id=1, source_target_pairs={{0,8},{8,0},{16,24},{24,16},{1,9},{9,1},{17,25},{25,17},{2,10},{10... | collective-permute-start | bytes 2359304 | tf_op jit(solution)/shard_map/ppermute | solution.py:51
  81.6 34.2 %collective-permute-start.64 = (bf16[128,3072]{1,0:T(8,128)(2,1)}, bf16[128,3072]{1,0:T(8,128)(2,1)}, u32[]{:S(2)}, u32[]{:S(2)}) collective-permute-start(bf16[128,3072]{1,0:T(8,128)(2,1)} %pad_maximum_fusion.23), channel_id=1, source_target_pairs={{0,16},{8,24},{16,0},{24,8},{1,17},{9,25},{17,1},{25,9},{2,18},{10... | collective-permute-start | bytes 2359304 | tf_op jit(solution)/shard_map/ppermute | solution.py:51
  84.0 31.7 %collective-permute-start.65 = (bf16[128,3072]{1,0:T(8,128)(2,1)}, bf16[128,3072]{1,0:T(8,128)(2,1)}, u32[]{:S(2)}, u32[]{:S(2)}) collective-permute-start(bf16[128,3072]{1,0:T(8,128)(2,1)} %pad_maximum_fusion.24), channel_id=1, source_target_pairs={{0,24},{8,16},{16,8},{24,0},{1,25},{9,17},{17,9},{25,1},{2,26},{10... | collective-permute-start | bytes 2359304 | tf_op jit(solution)/shard_map/ppermute | solution.py:51
  116.6 30.2 %collective-permute-start.71 = (bf16[128,2048]{1,0:T(8,128)(2,1)S(1)}, bf16[128,2048]{1,0:T(8,128)(2,1)S(1)}, u32[]{:S(2)}, u32[]{:S(2)}) collective-permute-start(bf16[128,2048]{1,0:T(8,128)(2,1)S(1)} %convolution_convert_fusion.10), channel_id=1, source_target_pairs={{0,16},{8,24},{16,0},{24,8},{1,17},{9,25},{17,1},{25,9},{2,18},{10... | collective-permute-start | bytes 1572872 | tf_op jit(solution)/shard_map/ppermute | solution.py:51
  121.8 29.3 %collective-permute-start.66 = (bf16[128,2048]{1,0:T(8,128)(2,1)S(1)}, bf16[128,2048]{1,0:T(8,128)(2,1)S(1)}, u32[]{:S(2)}, u32[]{:S(2)}) collective-permute-start(bf16[128,2048]{1,0:T(8,128)(2,1)S(1)} %convolution_convert_fusion.16), channel_id=1, source_target_pairs={{0,8},{8,0},{16,24},{24,16},{1,9},{9,1},{17,25},{25,17},{2,10},{10... | collective-permute-start | bytes 1572872 | tf_op jit(solution)/shard_map/ppermute | solution.py:51
  145.2 62.8 %collective-permute-start.78 = (bf16[3,128,3072]{2,1,0:T(8,128)(2,1)S(1)}, bf16[3,128,3072]{2,1,0:T(8,128)(2,1)}, u32[]{:S(2)}, u32[]{:S(2)}) collective-permute-start(bf16[3,128,3072]{2,1,0:T(8,128)(2,1)S(1)} %pad_maximum_fusion.13.refs_0_), channel_id=1, source_target_pairs={{0,2},{2,0},{4,6},{6,4},{1,3},{3,1},{5,7},{7,5},{8,10},{10,8},{12,... | collective-permute-start | bytes 7077896 | tf_op jit(solution)/shard_map/ppermute | solution.py:51
  146.9 61.2 %collective-permute-start.79 = (bf16[3,128,3072]{2,1,0:T(8,128)(2,1)S(1)}, bf16[3,128,3072]{2,1,0:T(8,128)(2,1)S(1)}, u32[]{:S(2)}, u32[]{:S(2)}) collective-permute-start(bf16[3,128,3072]{2,1,0:T(8,128)(2,1)S(1)} %pad_maximum_fusion.13.refs_0_), channel_id=1, source_target_pairs={{0,1},{1,0},{2,3},{3,2},{4,5},{5,4},{6,7},{7,6},{8,9},{9,8},{10,11... | collective-permute-start | bytes 7077896 | tf_op jit(solution)/shard_map/ppermute | solution.py:51
  212.2 25.8 %collective-permute-start.84 = (bf16[128,2048]{1,0:T(8,128)(2,1)}, bf16[128,2048]{1,0:T(8,128)(2,1)S(1)}, u32[]{:S(2)}, u32[]{:S(2)}) collective-permute-start(bf16[128,2048]{1,0:T(8,128)(2,1)} %get-tuple-element.461), channel_id=1, source_target_pairs={{0,16},{8,24},{16,0},{24,8},{1,17},{9,25},{17,1},{25,9},{2,18},{10... | collective-permute-start | bytes 1572872 | tf_op jit(solution)/shard_map/ppermute | solution.py:51
  212.5 41.3 %collective-permute-start.86 = (bf16[128,2048]{1,0:T(8,128)(2,1)}, bf16[128,2048]{1,0:T(8,128)(2,1)S(1)}, u32[]{:S(2)}, u32[]{:S(2)}) collective-permute-start(bf16[128,2048]{1,0:T(8,128)(2,1)} %get-tuple-element.461), channel_id=1, source_target_pairs={{0,8},{8,0},{16,24},{24,16},{1,9},{9,1},{17,25},{25,17},{2,10},{10... | collective-permute-start | bytes 1572872 | tf_op jit(solution)/shard_map/ppermute | solution.py:51
  213.3 24.6 %collective-permute-start.83 = (bf16[128,2048]{1,0:T(8,128)(2,1)}, bf16[128,2048]{1,0:T(8,128)(2,1)S(1)}, u32[]{:S(2)}, u32[]{:S(2)}) collective-permute-start(bf16[128,2048]{1,0:T(8,128)(2,1)} %get-tuple-element.462), channel_id=1, source_target_pairs={{0,8},{8,0},{16,24},{24,16},{1,9},{9,1},{17,25},{25,17},{2,10},{10... | collective-permute-start | bytes 1572872 | tf_op jit(solution)/shard_map/ppermute | solution.py:51
  214.5 39.4 %collective-permute-start.87 = (bf16[128,2048]{1,0:T(8,128)(2,1)}, bf16[128,2048]{1,0:T(8,128)(2,1)S(1)}, u32[]{:S(2)}, u32[]{:S(2)}) collective-permute-start(bf16[128,2048]{1,0:T(8,128)(2,1)} %get-tuple-element.462), channel_id=1, source_target_pairs={{0,16},{8,24},{16,0},{24,8},{1,17},{9,25},{17,1},{25,9},{2,18},{10... | collective-permute-start | bytes 1572872 | tf_op jit(solution)/shard_map/ppermute | solution.py:51
  222.5 29.5 %collective-permute-start.90 = (bf16[3,384,512]{2,1,0:T(8,128)(2,1)S(1)}, bf16[3,384,512]{2,1,0:T(8,128)(2,1)S(1)}, u32[]{:S(2)}, u32[]{:S(2)}) collective-permute-start(bf16[3,384,512]{2,1,0:T(8,128)(2,1)S(1)} %pad_maximum_fusion.15.refs_0_), channel_id=1, source_target_pairs={{0,2},{2,0},{4,6},{6,4},{1,3},{3,1},{5,7},{7,5},{8,10},{10,8},{12,... | collective-permute-start | bytes 3538952 | tf_op jit(solution)/shard_map/ppermute | solution.py:51
  286.9 344.4 %all-reduce.10.cloned.1.call-start = ((), (), s32[]{:S(2)}) async-start(), calls=%async_computation.2 | async-start | bytes 12582912 | tf_op jit(solution)/shard_map/psum | solution.py:860
  300.6 45.6 %collective-permute-start.16 = (bf16[256,2048]{1,0:T(8,128)(2,1)}, bf16[256,2048]{1,0:T(8,128)(2,1)}, u32[]{:S(2)}, u32[]{:S(2)}) collective-permute-start(bf16[256,2048]{1,0:T(8,128)(2,1)} %get-tuple-element.404), channel_id=1, source_target_pairs={{0,8},{8,0},{16,24},{24,16},{1,9},{9,1},{17,25},{25,17},{2,10},{10... | collective-permute-start | bytes 3145736 | tf_op jit(solution)/shard_map/cond/branch_1_fun/ppermute | solution.py:51
  300.9 46.9 %collective-permute-start.17 = (bf16[256,2048]{1,0:T(8,128)(2,1)}, bf16[256,2048]{1,0:T(8,128)(2,1)}, u32[]{:S(2)}, u32[]{:S(2)}) collective-permute-start(bf16[256,2048]{1,0:T(8,128)(2,1)} %get-tuple-element.403), channel_id=1, source_target_pairs={{0,16},{8,24},{16,0},{24,8},{1,17},{9,25},{17,1},{25,9},{2,18},{10... | collective-permute-start | bytes 3145736 | tf_op jit(solution)/shard_map/cond/branch_1_fun/ppermute | solution.py:51
  301.6 46.3 %collective-permute-start.18 = (bf16[256,2048]{1,0:T(8,128)(2,1)}, bf16[256,2048]{1,0:T(8,128)(2,1)}, u32[]{:S(2)}, u32[]{:S(2)}) collective-permute-start(bf16[256,2048]{1,0:T(8,128)(2,1)} %get-tuple-element.402), channel_id=1, source_target_pairs={{0,24},{8,16},{16,8},{24,0},{1,25},{9,17},{17,9},{25,1},{2,26},{10... | collective-permute-start | bytes 3145736 | tf_op jit(solution)/shard_map/cond/branch_1_fun/ppermute | solution.py:51
  366.8 21.3 %collective-permute-start.22 = (bf16[256,1536]{1,0:T(8,128)(2,1)S(1)}, bf16[256,1536]{1,0:T(8,128)(2,1)S(1)}, u32[]{:S(2)}, u32[]{:S(2)}) collective-permute-start(bf16[256,1536]{1,0:T(8,128)(2,1)S(1)} %get-tuple-element.407), channel_id=1, source_target_pairs={{0,24},{8,16},{16,8},{24,0},{1,25},{9,17},{17,9},{25,1},{2,26},{10... | collective-permute-start | bytes 2359304 | tf_op jit(solution)/shard_map/cond/branch_1_fun/ppermute | solution.py:51
  367.9 36.5 %collective-permute-start.21 = (bf16[256,1536]{1,0:T(8,128)(2,1)S(1)}, bf16[256,1536]{1,0:T(8,128)(2,1)S(1)}, u32[]{:S(2)}, u32[]{:S(2)}) collective-permute-start(bf16[256,1536]{1,0:T(8,128)(2,1)S(1)} %get-tuple-element.408), channel_id=1, source_target_pairs={{0,16},{8,24},{16,0},{24,8},{1,17},{9,25},{17,1},{25,9},{2,18},{10... | collective-permute-start | bytes 2359304 | tf_op jit(solution)/shard_map/cond/branch_1_fun/ppermute | solution.py:51
  369.1 35.3 %collective-permute-start.20 = (bf16[256,1536]{1,0:T(8,128)(2,1)S(1)}, bf16[256,1536]{1,0:T(8,128)(2,1)S(1)}, u32[]{:S(2)}, u32[]{:S(2)}) collective-permute-start(bf16[256,1536]{1,0:T(8,128)(2,1)S(1)} %get-tuple-element.409), channel_id=1, source_target_pairs={{0,8},{8,0},{16,24},{24,16},{1,9},{9,1},{17,25},{25,17},{2,10},{10... | collective-permute-start | bytes 2359304 | tf_op jit(solution)/shard_map/cond/branch_1_fun/ppermute | solution.py:51
  407.0 348.6 %all-reduce.8.cloned.1.call-start = ((), (), s32[]{:S(2)}) async-start(), calls=%async_computation.1 | async-start | bytes 6291456 | tf_op jit(solution)/shard_map/psum | solution.py:887
  416.7 23.9 %collective-permute-start.24 = (bf16[128,2048]{1,0:T(8,128)(2,1)S(1)}, bf16[128,2048]{1,0:T(8,128)(2,1)S(1)}, u32[]{:S(2)}, u32[]{:S(2)}) collective-permute-start(bf16[128,2048]{1,0:T(8,128)(2,1)S(1)} %get-tuple-element.428), channel_id=1, source_target_pairs={{0,8},{8,0},{16,24},{24,16},{1,9},{9,1},{17,25},{25,17},{2,10},{10... | collective-permute-start | bytes 1572872 | tf_op jit(solution)/shard_map/cond/branch_1_fun/ppermute | solution.py:51
  417.5 23.1 %collective-permute-start.27 = (bf16[128,2048]{1,0:T(8,128)(2,1)S(1)}, bf16[128,2048]{1,0:T(8,128)(2,1)S(1)}, u32[]{:S(2)}, u32[]{:S(2)}) collective-permute-start(bf16[128,2048]{1,0:T(8,128)(2,1)S(1)} %get-tuple-element.430), channel_id=1, source_target_pairs={{0,16},{8,24},{16,0},{24,8},{1,17},{9,25},{17,1},{25,9},{2,18},{10... | collective-permute-start | bytes 1572872 | tf_op jit(solution)/shard_map/cond/branch_1_fun/ppermute | solution.py:51
  432.8 22.2 %collective-permute-start.29 = (bf16[128,2048]{1,0:T(8,128)(2,1)S(1)}, bf16[128,2048]{1,0:T(8,128)(2,1)S(1)}, u32[]{:S(2)}, u32[]{:S(2)}) collective-permute-start(bf16[128,2048]{1,0:T(8,128)(2,1)S(1)} %get-tuple-element.429), channel_id=1, source_target_pairs={{0,16},{8,24},{16,0},{24,8},{1,17},{9,25},{17,1},{25,9},{2,18},{10... | collective-permute-start | bytes 1572872 | tf_op jit(solution)/shard_map/cond/branch_1_fun/ppermute | solution.py:51
  465.3 23.6 %collective-permute-start.32 = (bf16[128,2048]{1,0:T(8,128)(2,1)}, bf16[128,2048]{1,0:T(8,128)(2,1)}, u32[]{:S(2)}, u32[]{:S(2)}) collective-permute-start(bf16[128,2048]{1,0:T(8,128)(2,1)} %get-tuple-element.444), channel_id=1, source_target_pairs={{0,8},{8,0},{16,24},{24,16},{1,9},{9,1},{17,25},{25,17},{2,10},{10... | collective-permute-start | bytes 1572872 | tf_op jit(solution)/shard_map/cond/branch_1_fun/ppermute | solution.py:51
  465.9 25.0 %collective-permute-start.33 = (bf16[128,2048]{1,0:T(8,128)(2,1)}, bf16[128,2048]{1,0:T(8,128)(2,1)}, u32[]{:S(2)}, u32[]{:S(2)}) collective-permute-start(bf16[128,2048]{1,0:T(8,128)(2,1)} %get-tuple-element.445), channel_id=1, source_target_pairs={{0,16},{8,24},{16,0},{24,8},{1,17},{9,25},{17,1},{25,9},{2,18},{10... | collective-permute-start | bytes 1572872 | tf_op jit(solution)/shard_map/cond/branch_1_fun/ppermute | solution.py:51
  526.9 45.2 %collective-permute-start.40 = (bf16[4,256,1024]{2,1,0:T(8,128)(2,1)}, bf16[4,256,1024]{2,1,0:T(8,128)(2,1)}, u32[]{:S(2)}, u32[]{:S(2)}) collective-permute-start(bf16[4,256,1024]{2,1,0:T(8,128)(2,1)} %constant_dynamic-slice_fusion.5), channel_id=1, source_target_pairs={{0,1},{1,0},{2,3},{3,2},{4,5},{5,4},{6,7},{7,6},{8,9},{9,8},{10,11... | collective-permute-start | bytes 6291464 | tf_op jit(solution)/shard_map/cond/branch_1_fun/ppermute | solution.py:51
  530.0 21.4 %collective-permute-start.46 = (bf16[768,512]{1,0:T(8,128)(2,1)S(1)}, bf16[768,512]{1,0:T(8,128)(2,1)S(1)}, u32[]{:S(2)}, u32[]{:S(2)}) collective-permute-start(bf16[768,512]{1,0:T(8,128)(2,1)S(1)} %get-tuple-element.433), channel_id=1, source_target_pairs={{0,24},{8,16},{16,8},{24,0},{1,25},{9,17},{17,9},{25,1},{2,26},{10... | collective-permute-start | bytes 2359304 | tf_op jit(solution)/shard_map/cond/branch_1_fun/ppermute | solution.py:51
  531.4 33.5 %collective-permute-start.45 = (bf16[768,512]{1,0:T(8,128)(2,1)S(1)}, bf16[768,512]{1,0:T(8,128)(2,1)S(1)}, u32[]{:S(2)}, u32[]{:S(2)}) collective-permute-start(bf16[768,512]{1,0:T(8,128)(2,1)S(1)} %get-tuple-element.434), channel_id=1, source_target_pairs={{0,16},{8,24},{16,0},{24,8},{1,17},{9,25},{17,1},{25,9},{2,18},{10... | collective-permute-start | bytes 2359304 | tf_op jit(solution)/shard_map/cond/branch_1_fun/ppermute | solution.py:51
  533.3 31.6 %collective-permute-start.44 = (bf16[768,512]{1,0:T(8,128)(2,1)S(1)}, bf16[768,512]{1,0:T(8,128)(2,1)S(1)}, u32[]{:S(2)}, u32[]{:S(2)}) collective-permute-start(bf16[768,512]{1,0:T(8,128)(2,1)S(1)} %get-tuple-element.435), channel_id=1, source_target_pairs={{0,8},{8,0},{16,24},{24,16},{1,9},{9,1},{17,25},{25,17},{2,10},{10... | collective-permute-start | bytes 2359304 | tf_op jit(solution)/shard_map/cond/branch_1_fun/ppermute | solution.py:51
  536.5 29.3 %collective-permute-start.36 = (bf16[4,256,512]{2,1,0:T(8,128)(2,1)}, bf16[4,256,512]{2,1,0:T(8,128)(2,1)}, u32[]{:S(2)}, u32[]{:S(2)}) collective-permute-start(bf16[4,256,512]{2,1,0:T(8,128)(2,1)} %constant_dynamic-slice_fusion.7), channel_id=1, source_target_pairs={{0,1},{1,0},{2,3},{3,2},{4,5},{5,4},{6,7},{7,6},{8,9},{9,8},{10,11... | collective-permute-start | bytes 3145736 | tf_op jit(solution)/shard_map/cond/branch_1_fun/ppermute | solution.py:51
  565.6 43.8 %collective-permute-start.47 = (bf16[4,768,512]{2,1,0:T(8,128)(2,1)S(1)}, bf16[4,768,512]{2,1,0:T(8,128)(2,1)}, u32[]{:S(2)}, u32[]{:S(2)}) collective-permute-start(bf16[4,768,512]{2,1,0:T(8,128)(2,1)S(1)} %pad_maximum_fusion.1.mine), channel_id=1, source_target_pairs={{0,1},{1,0},{2,3},{3,2},{4,5},{5,4},{6,7},{7,6},{8,9},{9,8},{10,11... | collective-permute-start | bytes 9437192 | tf_op jit(solution)/shard_map/cond/branch_1_fun/ppermute | solution.py:51
  578.7 27.6 %collective-permute-start.42 = (bf16[256,1024]{1,0:T(8,128)(2,1)}, bf16[256,1024]{1,0:T(8,128)(2,1)}, u32[]{:S(2)}, u32[]{:S(2)}) collective-permute-start(bf16[256,1024]{1,0:T(8,128)(2,1)} %get-tuple-element.438), channel_id=1, source_target_pairs={{0,16},{8,24},{16,0},{24,8},{1,17},{9,25},{17,1},{25,9},{2,18},{10... | collective-permute-start | bytes 1572872 | tf_op jit(solution)/shard_map/cond/branch_1_fun/ppermute | solution.py:51
  585.0 21.2 %collective-permute-start.41 = (bf16[256,1024]{1,0:T(8,128)(2,1)}, bf16[256,1024]{1,0:T(8,128)(2,1)}, u32[]{:S(2)}, u32[]{:S(2)}) collective-permute-start(bf16[256,1024]{1,0:T(8,128)(2,1)} %get-tuple-element.439), channel_id=1, source_target_pairs={{0,8},{8,0},{16,24},{24,16},{1,9},{9,1},{17,25},{25,17},{2,10},{10... | collective-permute-start | bytes 1572872 | tf_op jit(solution)/shard_map/cond/branch_1_fun/ppermute | solution.py:51
  637.7 31.1 %collective-permute-start.14 = (bf16[256,1536]{1,0:T(8,128)(2,1)S(1)}, bf16[256,1536]{1,0:T(8,128)(2,1)S(1)}, u32[]{:S(2)}, u32[]{:S(2)}) collective-permute-start(bf16[256,1536]{1,0:T(8,128)(2,1)S(1)} %get-tuple-element.417), channel_id=1, source_target_pairs={{0,24},{8,16},{16,8},{24,0},{1,25},{9,17},{17,9},{25,1},{2,26},{10... | collective-permute-start | bytes 2359304 | tf_op jit(solution)/shard_map/cond/branch_1_fun/ppermute | solution.py:51
  639.3 37.3 %collective-permute-start.13 = (bf16[256,1536]{1,0:T(8,128)(2,1)S(1)}, bf16[256,1536]{1,0:T(8,128)(2,1)S(1)}, u32[]{:S(2)}, u32[]{:S(2)}) collective-permute-start(bf16[256,1536]{1,0:T(8,128)(2,1)S(1)} %get-tuple-element.418), channel_id=1, source_target_pairs={{0,16},{8,24},{16,0},{24,8},{1,17},{9,25},{17,1},{25,9},{2,18},{10... | collective-permute-start | bytes 2359304 | tf_op jit(solution)/shard_map/cond/branch_1_fun/ppermute | solution.py:51
  639.8 74.5 %collective-permute-start.6 = (bf16[4,256,1536]{2,1,0:T(8,128)(2,1)}, bf16[4,256,1536]{2,1,0:T(8,128)(2,1)}, u32[]{:S(2)}, u32[]{:S(2)}) collective-permute-start(bf16[4,256,1536]{2,1,0:T(8,128)(2,1)} %get-tuple-element.131.mine), channel_id=1, source_target_pairs={{0,1},{1,0},{2,3},{3,2},{4,5},{5,4},{6,7},{7,6},{8,9},{9,8},{10,11... | collective-permute-start | bytes 9437192 | tf_op jit(solution)/shard_map/cond/branch_1_fun/ppermute | solution.py:51
  639.8 45.0 %collective-permute-start.12 = (bf16[256,1536]{1,0:T(8,128)(2,1)S(1)}, bf16[256,1536]{1,0:T(8,128)(2,1)S(1)}, u32[]{:S(2)}, u32[]{:S(2)}) collective-permute-start(bf16[256,1536]{1,0:T(8,128)(2,1)S(1)} %get-tuple-element.419), channel_id=1, source_target_pairs={{0,8},{8,0},{16,24},{24,16},{1,9},{9,1},{17,25},{25,17},{2,10},{10... | collective-permute-start | bytes 2359304 | tf_op jit(solution)/shard_map/cond/branch_1_fun/ppermute | solution.py:51
  651.2 43.7 %collective-permute-start = (bf16[128,2048]{1,0:T(8,128)(2,1)S(1)}, bf16[128,2048]{1,0:T(8,128)(2,1)S(1)}, u32[]{:S(2)}, u32[]{:S(2)}) collective-permute-start(bf16[128,2048]{1,0:T(8,128)(2,1)S(1)} %copy-done.59), channel_id=1, source_target_pairs={{0,8},{8,0},{16,24},{24,16},{1,9},{9,1},{17,25},{25,17},{2,10},{10... | collective-permute-start | bytes 1572872 | tf_op jit(solution)/shard_map/cond/branch_1_fun/ppermute | solution.py:51
  668.9 26.0 %collective-permute-start.3 = (bf16[128,2048]{1,0:T(8,128)(2,1)S(1)}, bf16[128,2048]{1,0:T(8,128)(2,1)S(1)}, u32[]{:S(2)}, u32[]{:S(2)}) collective-permute-start(bf16[128,2048]{1,0:T(8,128)(2,1)S(1)} %copy-done.58), channel_id=1, source_target_pairs={{0,16},{8,24},{16,0},{24,8},{1,17},{9,25},{17,1},{25,9},{2,18},{10... | collective-permute-start | bytes 1572872 | tf_op jit(solution)/shard_map/cond/branch_1_fun/ppermute | solution.py:51
  676.6 22.5 %collective-permute-start.2 = (bf16[128,2048]{1,0:T(8,128)(2,1)S(1)}, bf16[128,2048]{1,0:T(8,128)(2,1)S(1)}, u32[]{:S(2)}, u32[]{:S(2)}) collective-permute-start(bf16[128,2048]{1,0:T(8,128)(2,1)S(1)} %add_convert_fusion.8), channel_id=1, source_target_pairs={{0,16},{8,24},{16,0},{24,8},{1,17},{9,25},{17,1},{25,9},{2,18},{10... | collective-permute-start | bytes 1572872 | tf_op jit(solution)/shard_map/cond/branch_1_fun/ppermute | solution.py:51
  684.8 23.8 %collective-permute-start.5 = (bf16[128,2048]{1,0:T(8,128)(2,1)}, bf16[128,2048]{1,0:T(8,128)(2,1)}, u32[]{:S(2)}, u32[]{:S(2)}) collective-permute-start(bf16[128,2048]{1,0:T(8,128)(2,1)} %get-tuple-element.413), channel_id=1, source_target_pairs={{0,16},{8,24},{16,0},{24,8},{1,17},{9,25},{17,1},{25,9},{2,18},{10... | collective-permute-start | bytes 1572872 | tf_op jit(solution)/shard_map/cond/branch_1_fun/ppermute | solution.py:51
  694.9 51.3 %collective-permute-start.15 = (bf16[4,256,1536]{2,1,0:T(8,128)(2,1)S(1)}, bf16[4,256,1536]{2,1,0:T(8,128)(2,1)}, u32[]{:S(2)}, u32[]{:S(2)}) collective-permute-start(bf16[4,256,1536]{2,1,0:T(8,128)(2,1)S(1)} %pad_maximum_fusion.6.mine), channel_id=1, source_target_pairs={{0,1},{1,0},{2,3},{3,2},{4,5},{5,4},{6,7},{7,6},{8,9},{9,8},{10,11... | collective-permute-start | bytes 9437192 | tf_op jit(solution)/shard_map/cond/branch_1_fun/ppermute | solution.py:51
  (158 other events, 1748.7 us)
Sparse Core Ops, SparseCore 0:
  287.0 119.5 all-reduce.5
  409.0 222.2 all-reduce.9
  634.3 121.1 all-reduce.7

commit v5 on v4

--- a/solution.py
+++ b/solution.py
@@ -73,23 +73,25 @@
     )
 
 
-def gather(shard, beside=None):
+def gather(shard, beside=None, last=None):
     n = lax.axis_size("fsdp")
     if n != 4:
-        return fence([shard] + [swap(shard, "fsdp", k) for k in range(1, n)], beside)
+        return fence([shard] + [swap(shard, "fsdp", k) for k in range(1, n)], beside, last)
     half = shard.shape[0] // 2
     top, low = shard[:half], shard[half:]
     x_top, y_low = swap(top, "fsdp", 1), swap(low, "fsdp", 2)
     x_low, y_top = swap(low, "fsdp", 1), swap(top, "fsdp", 2)
     x_top, y_low, beside = fence(x_top, y_low, beside)
     far = [swap(x_top, "fsdp", 2), swap(y_low, "fsdp", 1)]
+    if last is not None:
+        far, last = fence(far, last)
     blocks = [
         shard,
         jnp.concatenate([x_top, x_low], axis=0),
         jnp.concatenate([y_top, y_low], axis=0),
         jnp.concatenate(far, axis=0),
     ]
-    return blocks, beside
+    return blocks, beside, last
 
 
 def scatter(part_of):
@@ -262,78 +264,117 @@
 
     def begin(self):
         core = lax.axis_index("core")
-        rows = self.grad.shape[1] // 2
+        axis = self.grad.ndim - 2
+        rows = self.grad.shape[axis] // 2
 
         def take(c):
-            return lax.dynamic_slice_in_dim(self.grad, c * rows, rows, axis=1)
+            return lax.dynamic_slice_in_dim(self.grad, c * rows, rows, axis=axis)
 
         both = take(core).astype(f32) + core_swap(take(1 - core)).astype(f32)
         self.half = both.astype(bf16)
 
     def exchange(self):
         n, me = lax.axis_size("fsdp"), lax.axis_index("fsdp")
-        parts = [
-            lax.dynamic_index_in_dim(self.half, me ^ k, 0, keepdims=False) for k in range(n)
-        ]
-        self.half = jnp.stack([parts[0]] + [swap(parts[k], "fsdp", k) for k in range(1, n)])
-
-    def finish(self, by_rows, sizes=None):
+
+        def part(j):
+            if self.half.ndim == 2:
+                width = self.half.shape[1] // n
+                return lax.dynamic_slice_in_dim(self.half, j * width, width, axis=1)
+            return lax.dynamic_index_in_dim(self.half, j, 0, keepdims=False)
+
+        self.half = jnp.stack(
+            [part(me)] + [swap(part(me ^ k), "fsdp", k) for k in range(1, n)]
+        )
+
+    def finish(self, by_rows, sizes=None, split=False):
         n, me = lax.axis_size("fsdp"), lax.axis_index("fsdp")
         core = lax.axis_index("core")
         other = core_swap(self.half)
         rows, width = self.half.shape[1:]
         sizes = [width] if sizes is None else sizes
-
-        def kernel(place, mine, other, *outs):
-            def write(ref):
-                start = 0
-                for out, size in zip(outs, sizes):
-                    out[...] = ref[0, :, start : start + size].astype(f32)
-                    start += size
-
-            @pl.when(pl.program_id(0) == 0)
-            def _():
-                write(mine)
-
-            @pl.when(pl.program_id(0) == 1)
-            def _():
-                write(other)
-
-        def mine_at(w, k, place):
-            return (jnp.where(w == 0, k, n - 1), 0, 0)
-
-        def other_at(w, k, place):
-            return (jnp.where(w == 0, 0, k), 0, 0)
+        count = len(sizes)
+        place = jnp.stack([me, core]).astype(jnp.int32)
+
+        def write(ref, outs):
+            start = 0
+            for out, size in zip(outs, sizes):
+                out[...] = ref[0, :, start : start + size].astype(f32)
+                start += size
 
         def out_at(w, k, place):
             source = place[0] ^ k
             side = jnp.where(w == 0, place[1], 1 - place[1])
             return (side, source) if by_rows else (source * 2 + side, 0)
 
-        result = pl.pallas_call(
-            kernel,
-            out_shape=[
-                jax.ShapeDtypeStruct(
-                    (2 * rows, n * size) if by_rows else (2 * n * rows, size), f32
-                )
-                for size in sizes
-            ],
-            grid_spec=pltpu.PrefetchScalarGridSpec(
-                num_scalar_prefetch=1,
-                grid=(2, n),
-                in_specs=[
-                    pl.BlockSpec((1, rows, width), mine_at),
-                    pl.BlockSpec((1, rows, width), other_at),
+        def call(kernel, grid, in_specs, out_index, aliases, operands):
+            return pl.pallas_call(
+                kernel,
+                out_shape=[
+                    jax.ShapeDtypeStruct(
+                        (2 * rows, n * size) if by_rows else (2 * n * rows, size), f32
+                    )
+                    for size in sizes
                 ],
-                out_specs=[pl.BlockSpec((rows, size), out_at) for size in sizes],
-            ),
-            compiler_params=pltpu.CompilerParams(vmem_limit_bytes=32 << 20),
-            cost_estimate=pl.CostEstimate(
-                flops=0, bytes_accessed=2 * n * rows * width * 6, transcendentals=0
-            ),
-            name="place",
-        )(jnp.stack([me, core]).astype(jnp.int32), self.half, other)
-        return result if len(sizes) > 1 else result[0]
+                grid_spec=pltpu.PrefetchScalarGridSpec(
+                    num_scalar_prefetch=1,
+                    grid=grid,
+                    in_specs=in_specs,
+                    out_specs=[pl.BlockSpec((rows, size), out_index) for size in sizes],
+                ),
+                input_output_aliases=aliases,
+                compiler_params=pltpu.CompilerParams(vmem_limit_bytes=32 << 20),
+                cost_estimate=pl.CostEstimate(
+                    flops=0, bytes_accessed=math.prod(grid) * rows * width * 6, transcendentals=0
+                ),
+                name="place",
+            )(place, *operands)
+
+        if split:
+            one = pl.BlockSpec((1, rows, width), lambda k, place: (k, 0, 0))
+
+            def own(place, mine, *outs):
+                write(mine, outs)
+
+            def rest(place, other, *refs):
+                write(other, refs[count:])
+
+            result = call(own, (n,), [one], lambda k, place: out_at(0, k, place), {}, [self.half])
+            result = call(
+                rest,
+                (n,),
+                [one] + [pl.BlockSpec(memory_space=pl.ANY)] * count,
+                lambda k, place: out_at(1, k, place),
+                {2 + i: i for i in range(count)},
+                [other, *result],
+            )
+        else:
+
+            def both(place, mine, other, *outs):
+                @pl.when(pl.program_id(0) == 0)
+                def _():
+                    write(mine, outs)
+
+                @pl.when(pl.program_id(0) == 1)
+                def _():
+                    write(other, outs)
+
+            result = call(
+                both,
+                (2, n),
+                [
+                    pl.BlockSpec(
+                        (1, rows, width),
+                        lambda w, k, place: (jnp.where(w == 0, k, n - 1), 0, 0),
+                    ),
+                    pl.BlockSpec(
+                        (1, rows, width), lambda w, k, place: (jnp.where(w == 0, 0, k), 0, 0)
+                    ),
+                ],
+                out_at,
+                {},
+                [self.half, other],
+            )
+        return result if count > 1 else result[0]
 
 
 def roll_half(value):
@@ -674,14 +715,9 @@
         return value[start : start + tok_rows // 2]
 
     def by_columns(first, second):
-        columns = second.shape[1] // n
-        grad = jnp.stack(
-            [
-                matmul_tn(first, second[:, j * columns : (j + 1) * columns]).astype(bf16)
-                for j in range(n)
-            ]
+        return with_layout_constraint(
+            matmul_tn(first, second).astype(bf16), Layout(major_to_minor=(0, 1))
         )
-        return with_layout_constraint(grad, Layout(major_to_minor=(0, 1, 2)))
 
     def by_rows(first, second):
         grad = with_layout_constraint(
@@ -691,11 +727,8 @@
 
     sizes = [attn_gain.shape[0], mlp_gain.shape[0], query_gain.shape[0], key_gain.shape[0]]
     packed = jnp.concatenate([attn_gain, mlp_gain, query_gain, key_gain])[None]
-    tok, _ = gather(tokens[0])
+    tok, _, _ = gather(tokens[0])
     gains = [packed] + [swap(packed, "fsdp", k) for k in range(1, n)]
-    gains, w_query, w_key, w_value, w_out = fence(gains, w_query, w_key, w_value, w_out)
-    attn_spread = Spread([w_query, w_key, w_value], [w_out])
-    attn_got = attn_spread.begin()
     index = jnp.concatenate(
         [(me ^ k) * tok_rows + jnp.arange(tok_rows, dtype=jnp.int32) for k in range(n)]
     )
@@ -710,6 +743,11 @@
     cos_table = jnp.concatenate([cosine, cosine], axis=1)
     sin_table = jnp.concatenate([-sine, sine], axis=1)
     first = earlier.reshape(n, 1, tok_rows)
+    cos_table, sin_table, w_query, w_key, w_value, w_out = fence(
+        cos_table, sin_table, w_query, w_key, w_value, w_out
+    )
+    attn_spread = Spread([w_query, w_key, w_value], [w_out])
+    attn_got = attn_spread.begin()
     gains = jnp.concatenate(gains, axis=0)
     gains = jnp.concatenate(
         [lax.dynamic_slice_in_dim(gains, me ^ j, 1, axis=0) for j in range(n)], axis=0
@@ -753,9 +791,11 @@
     middle = stream + scatter(out_part)
     mlp_scale = rms_scale(middle)
     normed_mine = (middle * mlp_scale * gain_mlp).astype(bf16)
-    middle, mlp_scale, normed_mine, w_down = fence(middle, mlp_scale, normed_mine, w_down)
-
-    normed_parts, _ = gather(normed_mine)
+    middle, mlp_scale, normed_mine, w_down, normed = fence(
+        middle, mlp_scale, normed_mine, w_down, normed
+    )
+
+    normed_parts, _, _ = gather(normed_mine)
     down_spread = Spread([], [w_down])
     down_got = jnp.stack(down_spread.begin())
     normed_parts, gu_along, gu_across, cot, down_got = fence(
@@ -771,8 +811,10 @@
 
     down_along, down_across = swap(down_got, "z", 1), core_swap(down_got)
     own_act = gate_and_up(normed_parts[0])
-    cot_parts, (own_act, full_gu) = gather(cot, beside=(own_act, full_gu))
-    acts = [own_act] + [gate_and_up(part) for part in normed_parts[1:]]
+    cot_parts, (own_act, full_gu, normed_parts), last = gather(
+        cot, beside=(own_act, full_gu, normed_parts), last=normed_parts[n - 1]
+    )
+    acts = [own_act] + [gate_and_up(part) for part in [*normed_parts[1 : n - 1], last]]
     acts, down_along, down_across = fence(acts, down_along, down_across)
     normed_mlp = jnp.concatenate(normed_parts, axis=0)
     hidden = jnp.concatenate([act[1] for act in acts], axis=0)
@@ -791,8 +833,8 @@
         return by_columns(part, cot_all)
 
     down = Reduction(None)
-    other = core_swap(down_grad(1 - core))
-    down.half = (down_grad(core).astype(f32) + other.astype(f32)).astype(bf16)
+    other, own = fence(core_swap(down_grad(1 - core)), down_grad(core))
+    down.half = (own.astype(f32) + other.astype(f32)).astype(bf16)
     down.half, cot_all, full_down = fence(down.half, cot_all, full_down)
 
     def feed_forward_part():
@@ -889,7 +931,9 @@
         qkv_sum.half, out_sum.half, block_of_work(whole, input_part)
     )
     shares, input_grad, gate_full, up_full = done
-    query_full, key_full, value_full = qkv_sum.finish(True, [q_width, kv_width, kv_width])
+    query_full, key_full, value_full = qkv_sum.finish(
+        True, [q_width, kv_width, kv_width], split=True
+    )
     return (
         output[None],
         input_grad[None],
@@ -899,7 +943,7 @@
         value_full,
         shares[2],
         shares[3],
-        out_sum.finish(False),
+        out_sum.finish(False, split=True),
         shares[1],
         gate_full,
         up_full,

time: 789 us -> 781 us (0.990)
  other arithmetic: 84.9 us -> 76.3 us
    ppermute x96, waiting for transfers between devices: 319 us -> 306 us  [swap(): lax.ppermute(value, axis, [(j, j ^ k) for j in range(lax.axis_size(axis))])]
    unnamed x162 -> x124, local copies, waits for them, and re-layouts: 19.9 us -> 25.8 us
    pallas_call x5 -> x7, Pallas kernels: 37.1 us -> 38.6 us  [call(): pl.pallas_call(kernel, out_shape=[jax.ShapeDtypeStruct((2 * rows, n * siz...]
    dot_general x15 -> x6, matrix products: 37.5 us -> 38.3 us  [matmul_tn(): lax.dot_general(first, second, (((0,), (0,)), ((), ())), preferred_elemen...]
  transfers between devices with their start and end apart: 99 -> 99, of which waited for: 56 -> 51; matrix products, arithmetic and copies ran while one was open for 25% -> 25% of each run, Pallas kernels for 12% -> 13%
where the time goes in v5:
time: 781 us; the launch traced here: 773 us
  waiting for transfers between devices  325 us (42%)
  Pallas kernels  105 us (13%)
  starting transfers between devices  91.7 us (12%)
  matrix products  82.2 us (11%)
  local copies, waits for them, and re-layouts  76.5 us (10%)
  other arithmetic  76.3 us (10%)
  between operations  15.8 us (2%)
    ppermute x96, waiting for transfers between devices, swap(): lax.ppermute(value, axis, [(j, j ^ k) for j in range(lax.axis_size(axis))])  306 us
    ppermute x96, starting transfers between devices, swap(): lax.ppermute(value, axis, [(j, j ^ k) for j in range(lax.axis_size(axis))])  91.6 us
    pallas_call x7, Pallas kernels, call(): pl.pallas_call(kernel, out_shape=[jax.ShapeDtypeStruct((2 * rows, n * siz...  38.6 us
    dot_general x6, matrix products, matmul_tn(): lax.dot_general(first, second, (((0,), (0,)), ((), ())), preferred_elemen...  38.3 us
    dot_general x14, matrix products, matmul(): return jnp.dot(first, second, preferred_element_type=f32)  33 us
    pallas_call x1, Pallas kernels, feed_forward_backward(): pl.pallas_call(kernel, out_shape=[jax.ShapeDtypeStruct((length, ff), bf16...  32.1 us
    unnamed x124, local copies, waits for them, and re-layouts  25.8 us
    psum x1, waiting for transfers between devices, on_device(): gate_half, up_half = lax.psum((gate_half, up_half), 'z')  17.6 us
  transfers between devices with their start and end apart: 99, of which 51 were waited for; matrix products, arithmetic and copies ran while one was open for 25% of the time, Pallas kernels for 13%

profile of v5, /device:TPU:0, one launch (start us, length us, event | category | flops | bytes accessed | tf_op | source)
XLA Modules:
  0.0 772.8 jit_solution(6166849772476811961)
XLA Ops:
  36.0 17.2 %collective-permute-done.48 = bf16[128,2048]{1,0:T(8,128)(2,1)S(1)} collective-permute-done((bf16[128,2048]{1,0:T(8,128)(2,1)}, bf16[128,2048]{1,0:T(8,128)(2,1)S(1)}, u32[]{:S(2)}, u32[]{:S(2)}) %collective-permute-start.48) | collective-permute-done | bytes 524320 | tf_op jit(solution)/shard_map/ppermute | solution.py:51
  58.4 7.3 collective-permute-done.57
  95.5 4.5 fusion.51.q_ref.k_ref.v_ref
  100.1 8.7 %attention_forward.1 = (bf16[1024,512]{1,0:T(8,128)(2,1)}, bf16[1024,256]{1,0:T(8,128)(2,1)}, bf16[1024,256]{1,0:T(8,128)(2,1)}, bf16[1024,512]{1,0:T(8,128)(2,1)S(1)}, f32[2,2,4,1,256]{4,3,2,1,0:T(1,128)}) custom-call(s32[1]{0:T(128)} %bitcast.44.me_ref, f32[1024,1024]{1,0:T(8,128)S(1)} %fusion.51.q_ref.k_ref.v_ref, ...), custom_call_target="tpu_custom_call" | custom-call | flops 2147483648 | bytes 6291456 | tf_op jit(solution)/shard_map/attention_forward/pallas_call | solution.py:445
  108.8 7.4 collective-permute-done.64
  122.2 16.1 %collective-permute-done.69 = bf16[128,2048]{1,0:T(8,128)(2,1)S(1)} collective-permute-done((bf16[128,2048]{1,0:T(8,128)(2,1)S(1)}, bf16[128,2048]{1,0:T(8,128)(2,1)S(1)}, u32[]{:S(2)}, u32[]{:S(2)}) %collective-permute-start.69) | collective-permute-done | bytes 524320 | tf_op jit(solution)/shard_map/ppermute | solution.py:51
  157.3 9.3 %collective-permute-done.82 = bf16[384,512]{1,0:T(8,128)(2,1)S(1)} collective-permute-done((bf16[384,512]{1,0:T(8,128)(2,1)S(1)}, bf16[384,512]{1,0:T(8,128)(2,1)S(1)}, u32[]{:S(2)}, u32[]{:S(2)}) %collective-permute-start.82) | collective-permute-done | bytes 393248 | tf_op jit(solution)/shard_map/ppermute | solution.py:51
  173.6 7.6 collective-permute-done.73
  182.4 9.8 %collective-permute-done.80 = bf16[384,512]{1,0:T(8,128)(2,1)S(1)} collective-permute-done((bf16[384,512]{1,0:T(8,128)(2,1)S(1)}, bf16[384,512]{1,0:T(8,128)(2,1)S(1)}, u32[]{:S(2)}, u32[]{:S(2)}) %collective-permute-start.80) | collective-permute-done | bytes 393248 | tf_op jit(solution)/shard_map/ppermute | solution.py:51
  197.2 6.3 collective-permute-done.77
  229.6 6.3 collective-permute-done.83
  266.9 7.1 convolution_convert_fusion.8
  274.1 6.1 convolution_convert_fusion.7
  284.9 119.2 %conditional.3 = (bf16[256,2048]{1,0:T(8,128)(2,1)}, bf16[1024,2048]{1,0:T(8,128)(2,1)}, bf16[4,256,1536]{2,1,0:T(8,128)(2,1)}, bf16[4,256,1536]{2,1,0:T(8,128)(2,1)}) conditional(s32[]{:T(128)} %convert_element_type.353, () %tuple.66, (bf16[1024,1536]{1,0:T(8,128)(2,1)}, bf16[1536,2048]{1,0:T(8,128)(2,1)}, bf16[1024,2048]{1,0:T(8,128)(2,1)}, ...), branch_computations={%region_7.8_spmd, %region_8.9_spmd} | conditional | flops 38685114368 | bytes 265290592 | solution.py:69
  284.9 10.7 %convolution_convert_fusion.2 = bf16[1024,2048]{1,0:T(8,128)(2,1)S(1)} fusion(bf16[1024,1536]{1,0:T(8,128)(2,1)} %get-tuple-element.81, bf16[1536,2048]{1,0:T(8,128)(2,1)} %get-tuple-element.82.refs_8_), kind=kOutput, calls=%fused_computation.4 | convolution fusion | flops 6444548096 | bytes 13631488 | tf_op jit(solution)/shard_map/cond/branch_1_fun/dot_general | solution.py:27
  300.8 32.1 %feed_forward_backward.1 = (bf16[1024,1536]{1,0:T(8,128)(2,1)}, bf16[1024,1536]{1,0:T(8,128)(2,1)}, bf16[1024,2048]{1,0:T(8,128)(2,1)}) custom-call(bf16[1024,2048]{1,0:T(8,128)(2,1)} %get-tuple-element.84.cot_ref, f32[256,3072]{1,0:T(8,128)} %get-tuple-element.85.refs_0_.refs_4_, f32[256,3072]{1,0:T(8,128)} %get-tuple-element.86.refs_1_.refs_5_, ...), custom_call_target="tpu_custom_call" | custom-call | flops 19327352832 | bytes 18874368 | tf_op jit(solution)/shard_map/cond/branch_1_fun/feed_forward_backward/pallas_call | solution.py:655
  332.9 9.9 %convolution_convert_fusion.1 = bf16[1536,2048]{0,1:T(8,128)(2,1)S(1)} fusion(bf16[1024,1536]{1,0:T(8,128)(2,1)} %get-tuple-element.90, bf16[1024,2048]{1,0:T(8,128)(2,1)} %get-tuple-element.91), kind=kOutput, calls=%fused_computation.1 | convolution fusion | flops 6445596672 | bytes 13631488 | tf_op jit(solution)/shard_map/cond/branch_1_fun/dot_general | solution.py:31
  349.0 7.3 convolution_convert_fusion
  371.5 4.5 add_convert_fusion
  376.0 9.6 %collective-permute-done.22 = bf16[256,1536]{1,0:T(8,128)(2,1)S(1)} collective-permute-done((bf16[256,1536]{1,0:T(8,128)(2,1)S(1)}, bf16[256,1536]{1,0:T(8,128)(2,1)S(1)}, u32[]{:S(2)}, u32[]{:S(2)}) %collective-permute-start.22) | collective-permute-done | bytes 786464 | tf_op jit(solution)/shard_map/cond/branch_1_fun/ppermute | solution.py:51
  385.7 16.4 %collective-permute-done.21 = bf16[256,1536]{1,0:T(8,128)(2,1)S(1)} collective-permute-done((bf16[256,1536]{1,0:T(8,128)(2,1)S(1)}, bf16[256,1536]{1,0:T(8,128)(2,1)S(1)}, u32[]{:S(2)}, u32[]{:S(2)}) %collective-permute-start.21) | collective-permute-done | bytes 786464 | tf_op jit(solution)/shard_map/cond/branch_1_fun/ppermute | solution.py:51
  406.0 204.1 %conditional.4 = (f32[256,2048]{1,0:T(8,128)}, f32[2048]{0:T(1024)S(1)}, bf16[1024,2048]{1,0:T(8,128)(2,1)}, f32[128]{0:T(128)S(1)}, f32[128]{0:T(128)S(1)}, /*i...) conditional(s32[]{:T(128)} %convert_element_type.353, () %tuple.69, ...), branch_computations={%region_11.12_spmd, %region_12.17_spmd} | conditional | flops 18288211968 | bytes 379641984 | solution.py:69
  411.3 11.3 %collective-permute-done.25 = bf16[128,2048]{1,0:T(8,128)(2,1)S(1)} collective-permute-done((bf16[128,2048]{1,0:T(8,128)(2,1)S(1)}, bf16[128,2048]{1,0:T(8,128)(2,1)S(1)}, u32[]{:S(2)}, u32[]{:S(2)}) %collective-permute-start.25) | collective-permute-done | bytes 524320 | tf_op jit(solution)/shard_map/cond/branch_1_fun/ppermute | solution.py:51
  425.9 7.2 collective-permute-done.24
  433.1 5.7 collective-permute-done.26
  442.1 5.4 collective-permute-done.29
  459.2 10.9 %collective-permute-done.30 = bf16[128,2048]{1,0:T(8,128)(2,1)S(1)} collective-permute-done((bf16[128,2048]{1,0:T(8,128)(2,1)}, bf16[128,2048]{1,0:T(8,128)(2,1)S(1)}, u32[]{:S(2)}, u32[]{:S(2)}) %collective-permute-start.30) | collective-permute-done | bytes 524320 | tf_op jit(solution)/shard_map/cond/branch_1_fun/ppermute | solution.py:51
  474.3 7.1 collective-permute-done.32
  489.9 4.8 convolution_convert_fusion.6.da_ref
  494.8 13.9 %attention_backward.1 = (bf16[1024,512]{1,0:T(8,128)(2,1)S(1)}, bf16[1024,256]{1,0:T(8,128)(2,1)S(1)}, bf16[1024,256]{1,0:T(8,128)(2,1)S(1)}, f32[2,1,128]{2,1,0:T(1,128)S(1)}, f32[2,1,128]{2,1,0:T(1,128)S(1)}) custom-call(s32[1]{0:T(128)} %bitcast.13.me_ref, f32[1024,1024]{1,0:T(8,128)S(1)} %copy-done.18, f32[1024,1024]{1,0:T(8,128)S(1)} %copy-done.18, ...), custom_call_target="tpu_custom_call" | custom-call | flops 5368709120 | bytes 10485760 | tf_op jit(solution)/shard_map/cond/branch_1_fun/attention_backward/pallas_call | solution.py:553
  511.7 5.4 convolution_convert_fusion.3
  528.8 14.2 %collective-permute-done.46 = bf16[768,512]{1,0:T(8,128)(2,1)S(1)} collective-permute-done((bf16[768,512]{1,0:T(8,128)(2,1)S(1)}, bf16[768,512]{1,0:T(8,128)(2,1)S(1)}, u32[]{:S(2)}, u32[]{:S(2)}) %collective-permute-start.46) | collective-permute-done | bytes 786464 | tf_op jit(solution)/shard_map/cond/branch_1_fun/ppermute | solution.py:51
  543.1 13.8 %collective-permute-done.45 = bf16[768,512]{1,0:T(8,128)(2,1)S(1)} collective-permute-done((bf16[768,512]{1,0:T(8,128)(2,1)S(1)}, bf16[768,512]{1,0:T(8,128)(2,1)S(1)}, u32[]{:S(2)}, u32[]{:S(2)}) %collective-permute-start.45) | collective-permute-done | bytes 786464 | tf_op jit(solution)/shard_map/cond/branch_1_fun/ppermute | solution.py:51
  571.1 5.1 collective-permute-done.38
  577.5 6.1 convolution_convert_fusion.4
  587.6 10.6 %collective-permute-done.42 = bf16[256,1024]{1,0:T(8,128)(2,1)} collective-permute-done((bf16[256,1024]{1,0:T(8,128)(2,1)}, bf16[256,1024]{1,0:T(8,128)(2,1)}, u32[]{:S(2)}, u32[]{:S(2)}) %collective-permute-start.42) | collective-permute-done | bytes 524320 | tf_op jit(solution)/shard_map/cond/branch_1_fun/ppermute | solution.py:51
  601.3 8.7 %place.7 = f32[6144,512]{1,0:T(8,128)} custom-call(s32[2]{0:T(128)S(1)} %pad_add_fusion.place, bf16[4,768,512]{2,1,0:T(8,128)(2,1)S(1)} %pad_maximum_fusion.1.mine, bf16[4,768,512]{2,1,0:T(8,128)(2,1)} %collective-permute-done.47.other), custom_call_target="tpu_custom_call" | custom-call | bytes 18874368 | tf_op jit(solution)/shard_map/cond/branch_1_fun/place/pallas_call | solution.py:310
  610.2 17.6 %all-reduce.10.cloned.1.call-done = (bf16[4,256,1536]{2,1,0:T(8,128)(2,1)}, bf16[4,256,1536]{2,1,0:T(8,128)(2,1)}) async-done(((bf16[4,256,1536]{2,1,0:T(8,128)(2,1)}, bf16[4,256,1536]{2,1,0:T(8,128)(2,1)}), (bf16[4,256,1536]{2,1,0:T(8,128)(2,1)}, bf16[4,256,1536]{2,1,0:T(8,128)(2,1)})) %all-reduce.10.cloned.1.call-update) | async-done | bytes 6291472 | tf_op jit(solution)/shard_map/psum | solution.py:902
  629.6 121.8 %conditional.5 = (f32[512]{0:T(512)S(1)}, f32[512]{0:T(512)S(1)}, f32[32]{0:T(128)S(1)}, f32[32]{0:T(128)S(1)}, f32[256,2048]{1,0:T(8,128)}, /*index=5*/f32[512,6144]{1,0:T(8,128)}, f32[512,6144]{1,0:T(8,128)}) conditional(s32[]{:T(128)} %convert_element_type.353, () %tuple.72, (bf16[1024,2048]{1,0:T(8,128)(2,1)}, ...), branch_computations={%region_19.20_spmd, %region_20.24_spmd} | conditional | flops 18921000 | bytes 147506976 | solution.py:69
  637.8 9.9 %collective-permute-done.1 = bf16[128,2048]{1,0:T(8,128)(2,1)} collective-permute-done((bf16[128,2048]{1,0:T(8,128)(2,1)}, bf16[128,2048]{1,0:T(8,128)(2,1)}, u32[]{:S(2)}, u32[]{:S(2)}) %collective-permute-start.1) | collective-permute-done | bytes 524320 | tf_op jit(solution)/shard_map/cond/branch_1_fun/ppermute | solution.py:51
  650.5 14.9 %collective-permute-done.14 = bf16[256,1536]{1,0:T(8,128)(2,1)S(1)} collective-permute-done((bf16[256,1536]{1,0:T(8,128)(2,1)S(1)}, bf16[256,1536]{1,0:T(8,128)(2,1)S(1)}, u32[]{:S(2)}, u32[]{:S(2)}) %collective-permute-start.14) | collective-permute-done | bytes 786464 | tf_op jit(solution)/shard_map/cond/branch_1_fun/ppermute | solution.py:51
  665.9 7.2 collective-permute-done.13
  673.6 7.7 collective-permute-done.12
  683.2 8.2 %collective-permute-done = bf16[128,2048]{1,0:T(8,128)(2,1)S(1)} collective-permute-done((bf16[128,2048]{1,0:T(8,128)(2,1)S(1)}, bf16[128,2048]{1,0:T(8,128)(2,1)S(1)}, u32[]{:S(2)}, u32[]{:S(2)}) %collective-permute-start) | collective-permute-done | bytes 524320 | tf_op jit(solution)/shard_map/cond/branch_1_fun/ppermute | solution.py:51
  710.8 10.5 %place.8 = f32[512,6144]{1,0:T(8,128)} custom-call(s32[2]{0:T(128)S(1)} %pad_add_fusion.1.place, bf16[4,256,1536]{2,1,0:T(8,128)(2,1)} %get-tuple-element.131.mine, bf16[4,256,1536]{2,1,0:T(8,128)(2,1)} %collective-permute-done.6.other), custom_call_target="tpu_custom_call" | custom-call | bytes 18874368 | tf_op jit(solution)/shard_map/cond/branch_1_fun/place/pallas_call | solution.py:310
  730.9 4.8 collective-permute-done.10
  736.3 4.4 fusion.6
  742.7 8.7 %place.9 = f32[512,6144]{1,0:T(8,128)} custom-call(s32[2]{0:T(128)S(1)} %pad_add_fusion.1.place, bf16[4,256,1536]{2,1,0:T(8,128)(2,1)S(1)} %pad_maximum_fusion.5.mine, bf16[4,256,1536]{2,1,0:T(8,128)(2,1)} %collective-permute-done.15.other), custom_call_target="tpu_custom_call" | custom-call | bytes 18874368 | tf_op jit(solution)/shard_map/cond/branch_1_fun/place/pallas_call | solution.py:310
  (513 shorter events, 327.8 us)
Async XLA Ops:
  7.2 396.9 %all-reduce.6.cloned.1.call-start = ((), (), s32[]{:S(2)}) async-start(), calls=%async_computation | async-start | bytes 6291456 | tf_op jit(solution)/shard_map/psum | solution.py:855
  9.6 59.1 %collective-permute-start.50 = (bf16[128,2048]{1,0:T(8,128)(2,1)}, bf16[128,2048]{1,0:T(8,128)(2,1)}, u32[]{:S(2)}, u32[]{:S(2)}) collective-permute-start(bf16[128,2048]{1,0:T(8,128)(2,1)} %get-tuple-element.488), channel_id=1, source_target_pairs={{0,8},{8,0},{16,24},{24,16},{1,9},{9,1},{17,25},{25,17},{2,10},{10... | collective-permute-start | bytes 1572872 | tf_op jit(solution)/shard_map/ppermute | solution.py:51
  12.5 41.8 %collective-permute-start.49 = (bf16[128,2048]{1,0:T(8,128)(2,1)}, bf16[128,2048]{1,0:T(8,128)(2,1)}, u32[]{:S(2)}, u32[]{:S(2)}) collective-permute-start(bf16[128,2048]{1,0:T(8,128)(2,1)} %get-tuple-element.488), channel_id=1, source_target_pairs={{0,16},{8,24},{16,0},{24,8},{1,17},{9,25},{17,1},{25,9},{2,18},{10... | collective-permute-start | bytes 1572872 | tf_op jit(solution)/shard_map/ppermute | solution.py:51
  32.3 24.0 %collective-permute-start.59 = (bf16[128,1536]{1,0:T(8,128)(2,1)}, bf16[128,1536]{1,0:T(8,128)(2,1)}, u32[]{:S(2)}, u32[]{:S(2)}) collective-permute-start(bf16[128,1536]{1,0:T(8,128)(2,1)} %pad_maximum_fusion.27), channel_id=1, source_target_pairs={{0,24},{8,16},{16,8},{24,0},{1,25},{9,17},{17,9},{25,1},{2,26},{10... | collective-permute-start | bytes 1179656 | tf_op jit(solution)/shard_map/ppermute | solution.py:51
  32.5 25.4 %collective-permute-start.58 = (bf16[128,1536]{1,0:T(8,128)(2,1)}, bf16[128,1536]{1,0:T(8,128)(2,1)}, u32[]{:S(2)}, u32[]{:S(2)}) collective-permute-start(bf16[128,1536]{1,0:T(8,128)(2,1)} %pad_maximum_fusion.26), channel_id=1, source_target_pairs={{0,16},{8,24},{16,0},{24,8},{1,17},{9,25},{17,1},{25,9},{2,18},{10... | collective-permute-start | bytes 1179656 | tf_op jit(solution)/shard_map/ppermute | solution.py:51
  68.6 23.1 %collective-permute-start.61 = (bf16[3,128,1536]{2,1,0:T(8,128)(2,1)S(1)}, bf16[3,128,1536]{2,1,0:T(8,128)(2,1)S(1)}, u32[]{:S(2)}, u32[]{:S(2)}) collective-permute-start(bf16[3,128,1536]{2,1,0:T(8,128)(2,1)S(1)} %pad_maximum_fusion.12.refs_0_), channel_id=1, source_target_pairs={{0,1},{1,0},{2,3},{3,2},{4,5},{5,4},{6,7},{7,6},{8,9},{9,8},{10,11... | collective-permute-start | bytes 3538952 | tf_op jit(solution)/shard_map/ppermute | solution.py:51
  80.3 28.5 %collective-permute-start.63 = (bf16[128,3072]{1,0:T(8,128)(2,1)}, bf16[128,3072]{1,0:T(8,128)(2,1)}, u32[]{:S(2)}, u32[]{:S(2)}) collective-permute-start(bf16[128,3072]{1,0:T(8,128)(2,1)} %pad_maximum_fusion.20), channel_id=1, source_target_pairs={{0,8},{8,0},{16,24},{24,16},{1,9},{9,1},{17,25},{25,17},{2,10},{10... | collective-permute-start | bytes 2359304 | tf_op jit(solution)/shard_map/ppermute | solution.py:51
  82.4 33.7 %collective-permute-start.64 = (bf16[128,3072]{1,0:T(8,128)(2,1)}, bf16[128,3072]{1,0:T(8,128)(2,1)}, u32[]{:S(2)}, u32[]{:S(2)}) collective-permute-start(bf16[128,3072]{1,0:T(8,128)(2,1)} %pad_maximum_fusion.21), channel_id=1, source_target_pairs={{0,16},{8,24},{16,0},{24,8},{1,17},{9,25},{17,1},{25,9},{2,18},{10... | collective-permute-start | bytes 2359304 | tf_op jit(solution)/shard_map/ppermute | solution.py:51
  84.9 31.3 %collective-permute-start.65 = (bf16[128,3072]{1,0:T(8,128)(2,1)}, bf16[128,3072]{1,0:T(8,128)(2,1)}, u32[]{:S(2)}, u32[]{:S(2)}) collective-permute-start(bf16[128,3072]{1,0:T(8,128)(2,1)} %pad_maximum_fusion.22), channel_id=1, source_target_pairs={{0,24},{8,16},{16,8},{24,0},{1,25},{9,17},{17,9},{25,1},{2,26},{10... | collective-permute-start | bytes 2359304 | tf_op jit(solution)/shard_map/ppermute | solution.py:51
  117.1 28.2 %collective-permute-start.71 = (bf16[128,2048]{1,0:T(8,128)(2,1)S(1)}, bf16[128,2048]{1,0:T(8,128)(2,1)S(1)}, u32[]{:S(2)}, u32[]{:S(2)}) collective-permute-start(bf16[128,2048]{1,0:T(8,128)(2,1)S(1)} %convolution_convert_fusion.9), channel_id=1, source_target_pairs={{0,16},{8,24},{16,0},{24,8},{1,17},{9,25},{17,1},{25,9},{2,18},{10... | collective-permute-start | bytes 1572872 | tf_op jit(solution)/shard_map/ppermute | solution.py:51
  121.0 28.1 %collective-permute-start.66 = (bf16[128,2048]{1,0:T(8,128)(2,1)S(1)}, bf16[128,2048]{1,0:T(8,128)(2,1)S(1)}, u32[]{:S(2)}, u32[]{:S(2)}) collective-permute-start(bf16[128,2048]{1,0:T(8,128)(2,1)S(1)} %convolution_convert_fusion.15), channel_id=1, source_target_pairs={{0,8},{8,0},{16,24},{24,16},{1,9},{9,1},{17,25},{25,17},{2,10},{10... | collective-permute-start | bytes 1572872 | tf_op jit(solution)/shard_map/ppermute | solution.py:51
  143.7 62.2 %collective-permute-start.78 = (bf16[3,128,3072]{2,1,0:T(8,128)(2,1)S(1)}, bf16[3,128,3072]{2,1,0:T(8,128)(2,1)}, u32[]{:S(2)}, u32[]{:S(2)}) collective-permute-start(bf16[3,128,3072]{2,1,0:T(8,128)(2,1)S(1)} %pad_maximum_fusion.11.refs_0_), channel_id=1, source_target_pairs={{0,2},{2,0},{4,6},{6,4},{1,3},{3,1},{5,7},{7,5},{8,10},{10,8},{12,... | collective-permute-start | bytes 7077896 | tf_op jit(solution)/shard_map/ppermute | solution.py:51
  145.3 60.7 %collective-permute-start.79 = (bf16[3,128,3072]{2,1,0:T(8,128)(2,1)S(1)}, bf16[3,128,3072]{2,1,0:T(8,128)(2,1)S(1)}, u32[]{:S(2)}, u32[]{:S(2)}) collective-permute-start(bf16[3,128,3072]{2,1,0:T(8,128)(2,1)S(1)} %pad_maximum_fusion.11.refs_0_), channel_id=1, source_target_pairs={{0,1},{1,0},{2,3},{3,2},{4,5},{5,4},{6,7},{7,6},{8,9},{9,8},{10,11... | collective-permute-start | bytes 7077896 | tf_op jit(solution)/shard_map/ppermute | solution.py:51
  171.6 21.8 %collective-permute-start.74 = (bf16[128,2048]{1,0:T(8,128)(2,1)S(1)}, bf16[128,2048]{1,0:T(8,128)(2,1)S(1)}, u32[]{:S(2)}, u32[]{:S(2)}) collective-permute-start(bf16[128,2048]{1,0:T(8,128)(2,1)S(1)} %get-tuple-element.486), channel_id=1, source_target_pairs={{0,8},{8,0},{16,24},{24,16},{1,9},{9,1},{17,25},{25,17},{2,10},{10... | collective-permute-start | bytes 1572872 | tf_op jit(solution)/shard_map/ppermute | solution.py:51
  209.1 26.8 %collective-permute-start.84 = (bf16[128,2048]{1,0:T(8,128)(2,1)S(1)}, bf16[128,2048]{1,0:T(8,128)(2,1)S(1)}, u32[]{:S(2)}, u32[]{:S(2)}) collective-permute-start(bf16[128,2048]{1,0:T(8,128)(2,1)S(1)} %get-tuple-element.483), channel_id=1, source_target_pairs={{0,16},{8,24},{16,0},{24,8},{1,17},{9,25},{17,1},{25,9},{2,18},{10... | collective-permute-start | bytes 1572872 | tf_op jit(solution)/shard_map/ppermute | solution.py:51
  210.5 27.4 %collective-permute-start.86 = (bf16[128,2048]{1,0:T(8,128)(2,1)S(1)}, bf16[128,2048]{1,0:T(8,128)(2,1)S(1)}, u32[]{:S(2)}, u32[]{:S(2)}) collective-permute-start(bf16[128,2048]{1,0:T(8,128)(2,1)S(1)} %get-tuple-element.483), channel_id=1, source_target_pairs={{0,8},{8,0},{16,24},{24,16},{1,9},{9,1},{17,25},{25,17},{2,10},{10... | collective-permute-start | bytes 1572872 | tf_op jit(solution)/shard_map/ppermute | solution.py:51
  211.8 24.0 %collective-permute-start.83 = (bf16[128,2048]{1,0:T(8,128)(2,1)S(1)}, bf16[128,2048]{1,0:T(8,128)(2,1)S(1)}, u32[]{:S(2)}, u32[]{:S(2)}) collective-permute-start(bf16[128,2048]{1,0:T(8,128)(2,1)S(1)} %get-tuple-element.484), channel_id=1, source_target_pairs={{0,8},{8,0},{16,24},{24,16},{1,9},{9,1},{17,25},{25,17},{2,10},{10... | collective-permute-start | bytes 1572872 | tf_op jit(solution)/shard_map/ppermute | solution.py:51
  212.6 28.0 %collective-permute-start.87 = (bf16[128,2048]{1,0:T(8,128)(2,1)S(1)}, bf16[128,2048]{1,0:T(8,128)(2,1)S(1)}, u32[]{:S(2)}, u32[]{:S(2)}) collective-permute-start(bf16[128,2048]{1,0:T(8,128)(2,1)S(1)} %get-tuple-element.484), channel_id=1, source_target_pairs={{0,16},{8,24},{16,0},{24,8},{1,17},{9,25},{17,1},{25,9},{2,18},{10... | collective-permute-start | bytes 1572872 | tf_op jit(solution)/shard_map/ppermute | solution.py:51
  216.0 41.5 %collective-permute-start.90 = (bf16[3,384,512]{2,1,0:T(8,128)(2,1)S(1)}, bf16[3,384,512]{2,1,0:T(8,128)(2,1)S(1)}, u32[]{:S(2)}, u32[]{:S(2)}) collective-permute-start(bf16[3,384,512]{2,1,0:T(8,128)(2,1)S(1)} %pad_maximum_fusion.13.refs_0_), channel_id=1, source_target_pairs={{0,2},{2,0},{4,6},{6,4},{1,3},{3,1},{5,7},{7,5},{8,10},{10,8},{12,... | collective-permute-start | bytes 3538952 | tf_op jit(solution)/shard_map/ppermute | solution.py:51
  235.8 21.7 %collective-permute-start.91 = (bf16[3,384,512]{2,1,0:T(8,128)(2,1)S(1)}, bf16[3,384,512]{2,1,0:T(8,128)(2,1)S(1)}, u32[]{:S(2)}, u32[]{:S(2)}) collective-permute-start(bf16[3,384,512]{2,1,0:T(8,128)(2,1)S(1)} %pad_maximum_fusion.13.refs_0_), channel_id=1, source_target_pairs={{0,1},{1,0},{2,3},{3,2},{4,5},{5,4},{6,7},{7,6},{8,9},{9,8},{10,11... | collective-permute-start | bytes 3538952 | tf_op jit(solution)/shard_map/ppermute | solution.py:51
  283.3 344.5 %all-reduce.10.cloned.1.call-start = ((), (), s32[]{:S(2)}) async-start(), calls=%async_computation.2 | async-start | bytes 12582912 | tf_op jit(solution)/shard_map/psum | solution.py:902
  297.3 45.6 %collective-permute-start.16 = (bf16[256,2048]{1,0:T(8,128)(2,1)}, bf16[256,2048]{1,0:T(8,128)(2,1)}, u32[]{:S(2)}, u32[]{:S(2)}) collective-permute-start(bf16[256,2048]{1,0:T(8,128)(2,1)} %get-tuple-element.426), channel_id=1, source_target_pairs={{0,8},{8,0},{16,24},{24,16},{1,9},{9,1},{17,25},{25,17},{2,10},{10... | collective-permute-start | bytes 3145736 | tf_op jit(solution)/shard_map/cond/branch_1_fun/ppermute | solution.py:51
  297.3 48.2 %collective-permute-start.17 = (bf16[256,2048]{1,0:T(8,128)(2,1)}, bf16[256,2048]{1,0:T(8,128)(2,1)}, u32[]{:S(2)}, u32[]{:S(2)}) collective-permute-start(bf16[256,2048]{1,0:T(8,128)(2,1)} %get-tuple-element.425), channel_id=1, source_target_pairs={{0,16},{8,24},{16,0},{24,8},{1,17},{9,25},{17,1},{25,9},{2,18},{10... | collective-permute-start | bytes 3145736 | tf_op jit(solution)/shard_map/cond/branch_1_fun/ppermute | solution.py:51
  297.8 47.7 %collective-permute-start.18 = (bf16[256,2048]{1,0:T(8,128)(2,1)}, bf16[256,2048]{1,0:T(8,128)(2,1)}, u32[]{:S(2)}, u32[]{:S(2)}) collective-permute-start(bf16[256,2048]{1,0:T(8,128)(2,1)} %get-tuple-element.424), channel_id=1, source_target_pairs={{0,24},{8,16},{16,8},{24,0},{1,25},{9,17},{17,9},{25,1},{2,26},{10... | collective-permute-start | bytes 3145736 | tf_op jit(solution)/shard_map/cond/branch_1_fun/ppermute | solution.py:51
  365.7 36.4 %collective-permute-start.21 = (bf16[256,1536]{1,0:T(8,128)(2,1)S(1)}, bf16[256,1536]{1,0:T(8,128)(2,1)S(1)}, u32[]{:S(2)}, u32[]{:S(2)}) collective-permute-start(bf16[256,1536]{1,0:T(8,128)(2,1)S(1)} %get-tuple-element.430), channel_id=1, source_target_pairs={{0,16},{8,24},{16,0},{24,8},{1,17},{9,25},{17,1},{25,9},{2,18},{10... | collective-permute-start | bytes 2359304 | tf_op jit(solution)/shard_map/cond/branch_1_fun/ppermute | solution.py:51
  367.6 34.5 %collective-permute-start.20 = (bf16[256,1536]{1,0:T(8,128)(2,1)S(1)}, bf16[256,1536]{1,0:T(8,128)(2,1)S(1)}, u32[]{:S(2)}, u32[]{:S(2)}) collective-permute-start(bf16[256,1536]{1,0:T(8,128)(2,1)S(1)} %get-tuple-element.431), channel_id=1, source_target_pairs={{0,8},{8,0},{16,24},{24,16},{1,9},{9,1},{17,25},{25,17},{2,10},{10... | collective-permute-start | bytes 2359304 | tf_op jit(solution)/shard_map/cond/branch_1_fun/ppermute | solution.py:51
  404.2 347.8 %all-reduce.8.cloned.1.call-start = ((), (), s32[]{:S(2)}) async-start(), calls=%async_computation.1 | async-start | bytes 6291456 | tf_op jit(solution)/shard_map/psum | solution.py:929
  409.5 23.5 %collective-permute-start.24 = (bf16[128,2048]{1,0:T(8,128)(2,1)S(1)}, bf16[128,2048]{1,0:T(8,128)(2,1)S(1)}, u32[]{:S(2)}, u32[]{:S(2)}) collective-permute-start(bf16[128,2048]{1,0:T(8,128)(2,1)S(1)} %get-tuple-element.450), channel_id=1, source_target_pairs={{0,8},{8,0},{16,24},{24,16},{1,9},{9,1},{17,25},{25,17},{2,10},{10... | collective-permute-start | bytes 1572872 | tf_op jit(solution)/shard_map/cond/branch_1_fun/ppermute | solution.py:51
  409.9 23.2 %collective-permute-start.27 = (bf16[128,2048]{1,0:T(8,128)(2,1)S(1)}, bf16[128,2048]{1,0:T(8,128)(2,1)S(1)}, u32[]{:S(2)}, u32[]{:S(2)}) collective-permute-start(bf16[128,2048]{1,0:T(8,128)(2,1)S(1)} %get-tuple-element.452), channel_id=1, source_target_pairs={{0,16},{8,24},{16,0},{24,8},{1,17},{9,25},{17,1},{25,9},{2,18},{10... | collective-permute-start | bytes 1572872 | tf_op jit(solution)/shard_map/cond/branch_1_fun/ppermute | solution.py:51
  425.3 22.3 %collective-permute-start.29 = (bf16[128,2048]{1,0:T(8,128)(2,1)S(1)}, bf16[128,2048]{1,0:T(8,128)(2,1)S(1)}, u32[]{:S(2)}, u32[]{:S(2)}) collective-permute-start(bf16[128,2048]{1,0:T(8,128)(2,1)S(1)} %get-tuple-element.451), channel_id=1, source_target_pairs={{0,16},{8,24},{16,0},{24,8},{1,17},{9,25},{17,1},{25,9},{2,18},{10... | collective-permute-start | bytes 1572872 | tf_op jit(solution)/shard_map/cond/branch_1_fun/ppermute | solution.py:51
  457.3 24.1 %collective-permute-start.32 = (bf16[128,2048]{1,0:T(8,128)(2,1)}, bf16[128,2048]{1,0:T(8,128)(2,1)}, u32[]{:S(2)}, u32[]{:S(2)}) collective-permute-start(bf16[128,2048]{1,0:T(8,128)(2,1)} %get-tuple-element.466), channel_id=1, source_target_pairs={{0,8},{8,0},{16,24},{24,16},{1,9},{9,1},{17,25},{25,17},{2,10},{10... | collective-permute-start | bytes 1572872 | tf_op jit(solution)/shard_map/cond/branch_1_fun/ppermute | solution.py:51
  458.4 24.9 %collective-permute-start.33 = (bf16[128,2048]{1,0:T(8,128)(2,1)}, bf16[128,2048]{1,0:T(8,128)(2,1)}, u32[]{:S(2)}, u32[]{:S(2)}) collective-permute-start(bf16[128,2048]{1,0:T(8,128)(2,1)} %get-tuple-element.467), channel_id=1, source_target_pairs={{0,16},{8,24},{16,0},{24,8},{1,17},{9,25},{17,1},{25,9},{2,18},{10... | collective-permute-start | bytes 1572872 | tf_op jit(solution)/shard_map/cond/branch_1_fun/ppermute | solution.py:51
  518.7 45.3 %collective-permute-start.40 = (bf16[4,256,1024]{2,1,0:T(8,128)(2,1)}, bf16[4,256,1024]{2,1,0:T(8,128)(2,1)}, u32[]{:S(2)}, u32[]{:S(2)}) collective-permute-start(bf16[4,256,1024]{2,1,0:T(8,128)(2,1)} %constant_dynamic-slice_fusion.7), channel_id=1, source_target_pairs={{0,1},{1,0},{2,3},{3,2},{4,5},{5,4},{6,7},{7,6},{8,9},{9,8},{10,11... | collective-permute-start | bytes 6291464 | tf_op jit(solution)/shard_map/cond/branch_1_fun/ppermute | solution.py:51
  521.6 21.4 %collective-permute-start.46 = (bf16[768,512]{1,0:T(8,128)(2,1)S(1)}, bf16[768,512]{1,0:T(8,128)(2,1)S(1)}, u32[]{:S(2)}, u32[]{:S(2)}) collective-permute-start(bf16[768,512]{1,0:T(8,128)(2,1)S(1)} %get-tuple-element.455), channel_id=1, source_target_pairs={{0,24},{8,16},{16,8},{24,0},{1,25},{9,17},{17,9},{25,1},{2,26},{10... | collective-permute-start | bytes 2359304 | tf_op jit(solution)/shard_map/cond/branch_1_fun/ppermute | solution.py:51
  523.2 33.7 %collective-permute-start.45 = (bf16[768,512]{1,0:T(8,128)(2,1)S(1)}, bf16[768,512]{1,0:T(8,128)(2,1)S(1)}, u32[]{:S(2)}, u32[]{:S(2)}) collective-permute-start(bf16[768,512]{1,0:T(8,128)(2,1)S(1)} %get-tuple-element.456), channel_id=1, source_target_pairs={{0,16},{8,24},{16,0},{24,8},{1,17},{9,25},{17,1},{25,9},{2,18},{10... | collective-permute-start | bytes 2359304 | tf_op jit(solution)/shard_map/cond/branch_1_fun/ppermute | solution.py:51
  523.8 33.0 %collective-permute-start.44 = (bf16[768,512]{1,0:T(8,128)(2,1)S(1)}, bf16[768,512]{1,0:T(8,128)(2,1)S(1)}, u32[]{:S(2)}, u32[]{:S(2)}) collective-permute-start(bf16[768,512]{1,0:T(8,128)(2,1)S(1)} %get-tuple-element.457), channel_id=1, source_target_pairs={{0,8},{8,0},{16,24},{24,16},{1,9},{9,1},{17,25},{25,17},{2,10},{10... | collective-permute-start | bytes 2359304 | tf_op jit(solution)/shard_map/cond/branch_1_fun/ppermute | solution.py:51
  528.8 28.7 %collective-permute-start.36 = (bf16[256,2048]{1,0:T(8,128)(2,1)}, bf16[256,2048]{1,0:T(8,128)(2,1)}, u32[]{:S(2)}, u32[]{:S(2)}) collective-permute-start(bf16[256,2048]{1,0:T(8,128)(2,1)} %constant_dynamic-slice_fusion.11), channel_id=1, source_target_pairs={{0,1},{1,0},{2,3},{3,2},{4,5},{5,4},{6,7},{7,6},{8,9},{9,8},{10,11... | collective-permute-start | bytes 3145736 | tf_op jit(solution)/shard_map/cond/branch_1_fun/ppermute | solution.py:51
  557.3 44.0 %collective-permute-start.47 = (bf16[4,768,512]{2,1,0:T(8,128)(2,1)S(1)}, bf16[4,768,512]{2,1,0:T(8,128)(2,1)}, u32[]{:S(2)}, u32[]{:S(2)}) collective-permute-start(bf16[4,768,512]{2,1,0:T(8,128)(2,1)S(1)} %pad_maximum_fusion.1.mine), channel_id=1, source_target_pairs={{0,1},{1,0},{2,3},{3,2},{4,5},{5,4},{6,7},{7,6},{8,9},{9,8},{10,11... | collective-permute-start | bytes 9437192 | tf_op jit(solution)/shard_map/cond/branch_1_fun/ppermute | solution.py:51
  570.6 27.6 %collective-permute-start.42 = (bf16[256,1024]{1,0:T(8,128)(2,1)}, bf16[256,1024]{1,0:T(8,128)(2,1)}, u32[]{:S(2)}, u32[]{:S(2)}) collective-permute-start(bf16[256,1024]{1,0:T(8,128)(2,1)} %get-tuple-element.460), channel_id=1, source_target_pairs={{0,16},{8,24},{16,0},{24,8},{1,17},{9,25},{17,1},{25,9},{2,18},{10... | collective-permute-start | bytes 1572872 | tf_op jit(solution)/shard_map/cond/branch_1_fun/ppermute | solution.py:51
  634.2 31.1 %collective-permute-start.14 = (bf16[256,1536]{1,0:T(8,128)(2,1)S(1)}, bf16[256,1536]{1,0:T(8,128)(2,1)S(1)}, u32[]{:S(2)}, u32[]{:S(2)}) collective-permute-start(bf16[256,1536]{1,0:T(8,128)(2,1)S(1)} %get-tuple-element.439), channel_id=1, source_target_pairs={{0,24},{8,16},{16,8},{24,0},{1,25},{9,17},{17,9},{25,1},{2,26},{10... | collective-permute-start | bytes 2359304 | tf_op jit(solution)/shard_map/cond/branch_1_fun/ppermute | solution.py:51
  635.7 37.3 %collective-permute-start.13 = (bf16[256,1536]{1,0:T(8,128)(2,1)S(1)}, bf16[256,1536]{1,0:T(8,128)(2,1)S(1)}, u32[]{:S(2)}, u32[]{:S(2)}) collective-permute-start(bf16[256,1536]{1,0:T(8,128)(2,1)S(1)} %get-tuple-element.440), channel_id=1, source_target_pairs={{0,16},{8,24},{16,0},{24,8},{1,17},{9,25},{17,1},{25,9},{2,18},{10... | collective-permute-start | bytes 2359304 | tf_op jit(solution)/shard_map/cond/branch_1_fun/ppermute | solution.py:51
  636.3 74.5 %collective-permute-start.6 = (bf16[4,256,1536]{2,1,0:T(8,128)(2,1)}, bf16[4,256,1536]{2,1,0:T(8,128)(2,1)}, u32[]{:S(2)}, u32[]{:S(2)}) collective-permute-start(bf16[4,256,1536]{2,1,0:T(8,128)(2,1)} %get-tuple-element.131.mine), channel_id=1, source_target_pairs={{0,1},{1,0},{2,3},{3,2},{4,5},{5,4},{6,7},{7,6},{8,9},{9,8},{10,11... | collective-permute-start | bytes 9437192 | tf_op jit(solution)/shard_map/cond/branch_1_fun/ppermute | solution.py:51
  636.3 45.0 %collective-permute-start.12 = (bf16[256,1536]{1,0:T(8,128)(2,1)S(1)}, bf16[256,1536]{1,0:T(8,128)(2,1)S(1)}, u32[]{:S(2)}, u32[]{:S(2)}) collective-permute-start(bf16[256,1536]{1,0:T(8,128)(2,1)S(1)} %get-tuple-element.441), channel_id=1, source_target_pairs={{0,8},{8,0},{16,24},{24,16},{1,9},{9,1},{17,25},{25,17},{2,10},{10... | collective-permute-start | bytes 2359304 | tf_op jit(solution)/shard_map/cond/branch_1_fun/ppermute | solution.py:51
  647.7 43.7 %collective-permute-start = (bf16[128,2048]{1,0:T(8,128)(2,1)S(1)}, bf16[128,2048]{1,0:T(8,128)(2,1)S(1)}, u32[]{:S(2)}, u32[]{:S(2)}) collective-permute-start(bf16[128,2048]{1,0:T(8,128)(2,1)S(1)} %copy-done.54), channel_id=1, source_target_pairs={{0,8},{8,0},{16,24},{24,16},{1,9},{9,1},{17,25},{25,17},{2,10},{10... | collective-permute-start | bytes 1572872 | tf_op jit(solution)/shard_map/cond/branch_1_fun/ppermute | solution.py:51
  665.4 26.0 %collective-permute-start.3 = (bf16[128,2048]{1,0:T(8,128)(2,1)S(1)}, bf16[128,2048]{1,0:T(8,128)(2,1)S(1)}, u32[]{:S(2)}, u32[]{:S(2)}) collective-permute-start(bf16[128,2048]{1,0:T(8,128)(2,1)S(1)} %copy-done.53), channel_id=1, source_target_pairs={{0,16},{8,24},{16,0},{24,8},{1,17},{9,25},{17,1},{25,9},{2,18},{10... | collective-permute-start | bytes 1572872 | tf_op jit(solution)/shard_map/cond/branch_1_fun/ppermute | solution.py:51
  673.1 22.5 %collective-permute-start.2 = (bf16[128,2048]{1,0:T(8,128)(2,1)S(1)}, bf16[128,2048]{1,0:T(8,128)(2,1)S(1)}, u32[]{:S(2)}, u32[]{:S(2)}) collective-permute-start(bf16[128,2048]{1,0:T(8,128)(2,1)S(1)} %add_convert_fusion.8), channel_id=1, source_target_pairs={{0,16},{8,24},{16,0},{24,8},{1,17},{9,25},{17,1},{25,9},{2,18},{10... | collective-permute-start | bytes 1572872 | tf_op jit(solution)/shard_map/cond/branch_1_fun/ppermute | solution.py:51
  681.3 23.8 %collective-permute-start.5 = (bf16[128,2048]{1,0:T(8,128)(2,1)}, bf16[128,2048]{1,0:T(8,128)(2,1)}, u32[]{:S(2)}, u32[]{:S(2)}) collective-permute-start(bf16[128,2048]{1,0:T(8,128)(2,1)} %get-tuple-element.435), channel_id=1, source_target_pairs={{0,16},{8,24},{16,0},{24,8},{1,17},{9,25},{17,1},{25,9},{2,18},{10... | collective-permute-start | bytes 1572872 | tf_op jit(solution)/shard_map/cond/branch_1_fun/ppermute | solution.py:51
  691.4 51.3 %collective-permute-start.15 = (bf16[4,256,1536]{2,1,0:T(8,128)(2,1)S(1)}, bf16[4,256,1536]{2,1,0:T(8,128)(2,1)}, u32[]{:S(2)}, u32[]{:S(2)}) collective-permute-start(bf16[4,256,1536]{2,1,0:T(8,128)(2,1)S(1)} %pad_maximum_fusion.5.mine), channel_id=1, source_target_pairs={{0,1},{1,0},{2,3},{3,2},{4,5},{5,4},{6,7},{7,6},{8,9},{9,8},{10,11... | collective-permute-start | bytes 9437192 | tf_op jit(solution)/shard_map/cond/branch_1_fun/ppermute | solution.py:51
  (139 other events, 1598.4 us)
Sparse Core Ops, SparseCore 0:
  283.4 119.6 all-reduce.5
  405.5 222.2 all-reduce.9
  630.8 121.1 all-reduce.7

commit v6 on v5

--- a/solution.py
+++ b/solution.py
@@ -819,11 +819,9 @@
     normed_mlp = jnp.concatenate(normed_parts, axis=0)
     hidden = jnp.concatenate([act[1] for act in acts], axis=0)
     cot_all = jnp.concatenate(cot_parts, axis=0)
-    full_down = down_spread.join_columns(
-        [down_got, down_along, down_across, core_swap(down_along)]
-    )
-    cot_all, full_down, hidden, normed_mlp, acts = fence(
-        cot_all, full_down, hidden, normed_mlp, acts
+    down_last = core_swap(down_along)
+    cot_all, down_across, down_last, hidden, normed_mlp, acts = fence(
+        cot_all, down_across, down_last, hidden, normed_mlp, acts
     )
 
     core = lax.axis_index("core")
@@ -835,27 +833,27 @@
     down = Reduction(None)
     other, own = fence(core_swap(down_grad(1 - core)), down_grad(core))
     down.half = (own.astype(f32) + other.astype(f32)).astype(bf16)
-    down.half, cot_all, full_down = fence(down.half, cot_all, full_down)
+    down.half, cot_all = fence(down.half, cot_all)
 
     def feed_forward_part():
+        full_down = down_spread.join_columns([down_got, down_along, down_across, down_last])
         out_partial, cots = fence(matmul(hidden, full_down).astype(bf16), cot_all)
         out_got = scatter_direct(lambda k: block(out_partial, k))
         d_gate, d_up, d_normed_mlp = feed_forward_backward(
             cots, [act[0] for act in acts], full_down, full_gu
         )
         grad_gate, d_up, out_got = fence(by_rows(normed_mlp, d_gate), d_up, out_got)
-        output = (middle + add_up(out_got)).astype(bf16)
         gate = Reduction(grad_gate)
         gate.begin()
         gate.exchange()
         up = Reduction(by_rows(normed_mlp, d_up))
         up.begin()
-        return output, d_normed_mlp, gate.half, up.half
+        return out_got, d_normed_mlp, gate.half, up.half
 
     down.half = lax.psum(down.half, "z")
-    output, d_normed_mlp, gate_half, up_half = block_of_work(whole, feed_forward_part)
-    down.half, output, d_normed_mlp, gate_half, up_half = fence(
-        down.half, output, d_normed_mlp, gate_half, up_half
+    out_got, d_normed_mlp, gate_half, up_half = block_of_work(whole, feed_forward_part)
+    down.half, out_got, d_normed_mlp, gate_half, up_half = fence(
+        down.half, out_got, d_normed_mlp, gate_half, up_half
     )
 
     def attention_part():
@@ -890,6 +888,7 @@
         down_sum.half = down_half
         down_sum.exchange()
         return (
+            (middle + add_up(out_got)).astype(bf16),
             d_middle,
             mlp_gain_grad,
             matmul_nt(d_qkv, full_qkv).astype(bf16),
@@ -901,7 +900,7 @@
 
     gate_half, up_half = lax.psum((gate_half, up_half), "z")
     gate_half, up_half, done = fence(gate_half, up_half, block_of_work(whole, attention_part))
-    d_middle, mlp_gain_grad, partial, head_gain_grads, out_half, qkv_half, down_full = done
+    output, d_middle, mlp_gain_grad, partial, head_gain_grads, out_half, qkv_half, down_full = done
 
     def input_part():
         d_normed = scatter(lambda k, h: half_block(partial, k, h))

time: 781 us -> 778 us (level)
  waiting for transfers between devices: 325 us -> 310 us
  local copies, waits for them, and re-layouts: 76.5 us -> 85.5 us
    another operation x1 -> x6, local copies, waits for them, and re-layouts: 0.01 us -> 9.05 us
    cond x69 -> x77, local copies, waits for them, and re-layouts: 15.7 us -> 18.7 us
    unnamed x124 -> x128, local copies, waits for them, and re-layouts: 25.8 us -> 24.6 us
  transfers between devices with their start and end apart: 99 -> 99, of which waited for: 51 -> 50; matrix products, arithmetic and copies ran while one was open for 25% -> 26% of each run, Pallas kernels for 13% -> 13%
where the time goes in v6:
time: 778 us; the launch traced here: 770 us
  waiting for transfers between devices  310 us (40%)
  Pallas kernels  104 us (13%)
  starting transfers between devices  94.4 us (12%)
  local copies, waits for them, and re-layouts  85.5 us (11%)
  other arithmetic  80.7 us (10%)
  matrix products  78.3 us (10%)
  between operations  15.8 us (2%)
    ppermute x96, waiting for transfers between devices, swap(): lax.ppermute(value, axis, [(j, j ^ k) for j in range(lax.axis_size(axis))])  299 us
    ppermute x96, starting transfers between devices, swap(): lax.ppermute(value, axis, [(j, j ^ k) for j in range(lax.axis_size(axis))])  94.3 us
    pallas_call x7, Pallas kernels, call(): pl.pallas_call(kernel, out_shape=[jax.ShapeDtypeStruct((2 * rows, n * siz...  38.6 us
    dot_general x6, matrix products, matmul_tn(): lax.dot_general(first, second, (((0,), (0,)), ((), ())), preferred_elemen...  38.2 us
    pallas_call x1, Pallas kernels, feed_forward_backward(): pl.pallas_call(kernel, out_shape=[jax.ShapeDtypeStruct((length, ff), bf16...  30.9 us
    dot_general x14, matrix products, matmul(): return jnp.dot(first, second, preferred_element_type=f32)  29.4 us
    unnamed x128, local copies, waits for them, and re-layouts  24.6 us
    cond x77, local copies, waits for them, and re-layouts  18.7 us
  transfers between devices with their start and end apart: 99, of which 50 were waited for; matrix products, arithmetic and copies ran while one was open for 26% of the time, Pallas kernels for 13%

profile of v6, /device:TPU:0, one launch (start us, length us, event | category | flops | bytes accessed | tf_op | source)
XLA Modules:
  0.0 769.9 jit_solution(14351174103882758370)
XLA Ops:
  36.0 17.2 %collective-permute-done.48 = bf16[128,2048]{1,0:T(8,128)(2,1)S(1)} collective-permute-done((bf16[128,2048]{1,0:T(8,128)(2,1)}, bf16[128,2048]{1,0:T(8,128)(2,1)S(1)}, u32[]{:S(2)}, u32[]{:S(2)}) %collective-permute-start.48) | collective-permute-done | bytes 524320 | tf_op jit(solution)/shard_map/ppermute | solution.py:51
  58.8 6.8 collective-permute-done.57
  95.9 4.5 fusion.51.q_ref.k_ref.v_ref
  100.5 8.3 %attention_forward.1 = (bf16[1024,512]{1,0:T(8,128)(2,1)}, bf16[1024,256]{1,0:T(8,128)(2,1)}, bf16[1024,256]{1,0:T(8,128)(2,1)}, bf16[1024,512]{1,0:T(8,128)(2,1)S(1)}, f32[2,2,4,1,256]{4,3,2,1,0:T(1,128)}) custom-call(s32[1]{0:T(128)} %bitcast.54.me_ref, f32[1024,1024]{1,0:T(8,128)S(1)} %fusion.51.q_ref.k_ref.v_ref, ...), custom_call_target="tpu_custom_call" | custom-call | flops 2147483648 | bytes 6291456 | tf_op jit(solution)/shard_map/attention_forward/pallas_call | solution.py:445
  108.8 7.4 collective-permute-done.64
  122.2 16.1 %collective-permute-done.69 = bf16[128,2048]{1,0:T(8,128)(2,1)S(1)} collective-permute-done((bf16[128,2048]{1,0:T(8,128)(2,1)S(1)}, bf16[128,2048]{1,0:T(8,128)(2,1)S(1)}, u32[]{:S(2)}, u32[]{:S(2)}) %collective-permute-start.69) | collective-permute-done | bytes 524320 | tf_op jit(solution)/shard_map/ppermute | solution.py:51
  157.3 9.3 %collective-permute-done.82 = bf16[384,512]{1,0:T(8,128)(2,1)S(1)} collective-permute-done((bf16[384,512]{1,0:T(8,128)(2,1)S(1)}, bf16[384,512]{1,0:T(8,128)(2,1)S(1)}, u32[]{:S(2)}, u32[]{:S(2)}) %collective-permute-start.82) | collective-permute-done | bytes 393248 | tf_op jit(solution)/shard_map/ppermute | solution.py:51
  173.6 7.6 collective-permute-done.73
  182.4 9.8 %collective-permute-done.80 = bf16[384,512]{1,0:T(8,128)(2,1)S(1)} collective-permute-done((bf16[384,512]{1,0:T(8,128)(2,1)S(1)}, bf16[384,512]{1,0:T(8,128)(2,1)S(1)}, u32[]{:S(2)}, u32[]{:S(2)}) %collective-permute-start.80) | collective-permute-done | bytes 393248 | tf_op jit(solution)/shard_map/ppermute | solution.py:51
  198.3 5.2 collective-permute-done.77
  226.7 7.7 collective-permute-done.83
  261.1 7.5 convolution_convert_fusion.7
  268.6 5.9 convolution_convert_fusion.6
  274.6 4.9 add_convert_fusion.9
  279.6 120.4 %conditional.3 = (bf16[256,2048]{0,1:T(8,128)(2,1)}, bf16[256,2048]{0,1:T(8,128)(2,1)}, bf16[256,2048]{0,1:T(8,128)(2,1)}, bf16[256,2048]{0,1:T(8,128)(2,1)}, bf...) conditional(s32[]{:T(128)} %convert_element_type.356, () %tuple.66, ...), branch_computations={%region_7.8_spmd, %region_8.9_spmd} | conditional | flops 38680395776 | bytes 339740512 | solution.py:69
  281.4 4.7 assemble.4.refs_8_
  286.2 7.3 convert_bitcast_fusion
  299.3 30.9 %feed_forward_backward.1 = (bf16[1024,1536]{1,0:T(8,128)(2,1)}, bf16[1024,1536]{1,0:T(8,128)(2,1)}, bf16[1024,2048]{1,0:T(8,128)(2,1)}) custom-call(bf16[1024,2048]{1,0:T(8,128)(2,1)} %get-tuple-element.101.cot_ref, f32[256,3072]{1,0:T(8,128)S(1)} %copy-done.46, f32[256,3072]{1,0:T(8,128)} %get-tuple-element.103.refs_1_.refs_5_, ...), custom_call_target="tpu_custom_call" | custom-call | flops 19327352832 | bytes 18874368 | tf_op jit(solution)/shard_map/cond/branch_1_fun/feed_forward_backward/pallas_call | solution.py:655
  330.2 10.0 %convolution_convert_fusion.1 = bf16[1536,2048]{0,1:T(8,128)(2,1)S(1)} fusion(bf16[1024,1536]{1,0:T(8,128)(2,1)} %get-tuple-element.107, bf16[1024,2048]{1,0:T(8,128)(2,1)} %get-tuple-element.108), kind=kOutput, calls=%fused_computation.1 | convolution fusion | flops 6445596672 | bytes 13631488 | tf_op jit(solution)/shard_map/cond/branch_1_fun/dot_general | solution.py:31
  347.7 7.2 convolution_convert_fusion
  365.1 4.4 add_convert_fusion
  369.6 13.3 %collective-permute-done.22 = bf16[256,1536]{1,0:T(8,128)(2,1)S(1)} collective-permute-done((bf16[256,1536]{1,0:T(8,128)(2,1)S(1)}, bf16[256,1536]{1,0:T(8,128)(2,1)S(1)}, u32[]{:S(2)}, u32[]{:S(2)}) %collective-permute-start.22) | collective-permute-done | bytes 786464 | tf_op jit(solution)/shard_map/cond/branch_1_fun/ppermute | solution.py:51
  382.9 16.4 %collective-permute-done.21 = bf16[256,1536]{1,0:T(8,128)(2,1)S(1)} collective-permute-done((bf16[256,1536]{1,0:T(8,128)(2,1)S(1)}, bf16[256,1536]{1,0:T(8,128)(2,1)S(1)}, u32[]{:S(2)}, u32[]{:S(2)}) %collective-permute-start.21) | collective-permute-done | bytes 786464 | tf_op jit(solution)/shard_map/cond/branch_1_fun/ppermute | solution.py:51
  403.6 210.4 %conditional.4 = (bf16[256,2048]{1,0:T(8,128)(2,1)}, f32[256,2048]{1,0:T(8,128)}, f32[2048]{0:T(1024)S(1)}, bf16[1024,2048]{1,0:T(8,128)(2,1)}, f32[128]{0:T(128...) conditional(s32[]{:T(128)} %convert_element_type.356, () %tuple.69, ...), branch_computations={%region_11.12_spmd, %region_12.17_spmd} | conditional | flops 18292930560 | bytes 397467776 | solution.py:69
  409.6 11.3 %collective-permute-done.25 = bf16[128,2048]{1,0:T(8,128)(2,1)S(1)} collective-permute-done((bf16[128,2048]{1,0:T(8,128)(2,1)S(1)}, bf16[128,2048]{1,0:T(8,128)(2,1)S(1)}, u32[]{:S(2)}, u32[]{:S(2)}) %collective-permute-start.25) | collective-permute-done | bytes 524320 | tf_op jit(solution)/shard_map/cond/branch_1_fun/ppermute | solution.py:51
  424.2 7.1 collective-permute-done.24
  431.2 5.8 collective-permute-done.26
  452.6 5.0 multiply_reduce_fusion
  465.2 10.9 %collective-permute-done.30 = bf16[128,2048]{1,0:T(8,128)(2,1)S(1)} collective-permute-done((bf16[128,2048]{1,0:T(8,128)(2,1)}, bf16[128,2048]{1,0:T(8,128)(2,1)S(1)}, u32[]{:S(2)}, u32[]{:S(2)}) %collective-permute-start.30) | collective-permute-done | bytes 524320 | tf_op jit(solution)/shard_map/cond/branch_1_fun/ppermute | solution.py:51
  479.7 7.0 collective-permute-done.32
  493.9 4.7 convolution_convert_fusion.5.da_ref
  498.7 14.1 %attention_backward.1 = (bf16[1024,512]{1,0:T(8,128)(2,1)S(1)}, bf16[1024,256]{1,0:T(8,128)(2,1)S(1)}, bf16[1024,256]{1,0:T(8,128)(2,1)S(1)}, f32[2,1,128]{2,1,0:T(1,128)S(1)}, f32[2,1,128]{2,1,0:T(1,128)S(1)}) custom-call(s32[1]{0:T(128)} %bitcast.23.me_ref, f32[1024,1024]{1,0:T(8,128)S(1)} %copy-done.16, f32[1024,1024]{1,0:T(8,128)S(1)} %copy-done.16, ...), custom_call_target="tpu_custom_call" | custom-call | flops 5368709120 | bytes 10485760 | tf_op jit(solution)/shard_map/cond/branch_1_fun/attention_backward/pallas_call | solution.py:553
  515.8 5.1 convolution_convert_fusion.2
  532.8 14.2 %collective-permute-done.46 = bf16[768,512]{1,0:T(8,128)(2,1)S(1)} collective-permute-done((bf16[768,512]{1,0:T(8,128)(2,1)S(1)}, bf16[768,512]{1,0:T(8,128)(2,1)S(1)}, u32[]{:S(2)}, u32[]{:S(2)}) %collective-permute-start.46) | collective-permute-done | bytes 786464 | tf_op jit(solution)/shard_map/cond/branch_1_fun/ppermute | solution.py:51
  546.9 13.7 %collective-permute-done.45 = bf16[768,512]{1,0:T(8,128)(2,1)S(1)} collective-permute-done((bf16[768,512]{1,0:T(8,128)(2,1)S(1)}, bf16[768,512]{1,0:T(8,128)(2,1)S(1)}, u32[]{:S(2)}, u32[]{:S(2)}) %collective-permute-start.45) | collective-permute-done | bytes 786464 | tf_op jit(solution)/shard_map/cond/branch_1_fun/ppermute | solution.py:51
  582.4 6.1 convolution_convert_fusion.3
  591.4 10.6 %collective-permute-done.42 = bf16[256,1024]{1,0:T(8,128)(2,1)} collective-permute-done((bf16[256,1024]{1,0:T(8,128)(2,1)}, bf16[256,1024]{1,0:T(8,128)(2,1)}, u32[]{:S(2)}, u32[]{:S(2)}) %collective-permute-start.42) | collective-permute-done | bytes 524320 | tf_op jit(solution)/shard_map/cond/branch_1_fun/ppermute | solution.py:51
  605.1 8.7 %place.7 = f32[6144,512]{1,0:T(8,128)} custom-call(s32[2]{0:T(128)S(1)} %pad_add_fusion.place, bf16[4,768,512]{2,1,0:T(8,128)(2,1)S(1)} %pad_maximum_fusion.1.mine, bf16[4,768,512]{2,1,0:T(8,128)(2,1)} %collective-permute-done.47.other), custom_call_target="tpu_custom_call" | custom-call | bytes 18874368 | tf_op jit(solution)/shard_map/cond/branch_1_fun/place/pallas_call | solution.py:310
  614.0 10.8 %all-reduce.10.cloned.1.call-done = (bf16[4,256,1536]{2,1,0:T(8,128)(2,1)}, bf16[4,256,1536]{2,1,0:T(8,128)(2,1)}) async-done(((bf16[4,256,1536]{2,1,0:T(8,128)(2,1)}, bf16[4,256,1536]{2,1,0:T(8,128)(2,1)}), (bf16[4,256,1536]{2,1,0:T(8,128)(2,1)}, bf16[4,256,1536]{2,1,0:T(8,128)(2,1)})) %all-reduce.10.cloned.1.call-update) | async-done | bytes 6291472 | tf_op jit(solution)/shard_map/psum | solution.py:901
  626.7 121.8 %conditional.5 = (f32[512]{0:T(512)S(1)}, f32[512]{0:T(512)S(1)}, f32[32]{0:T(128)S(1)}, f32[32]{0:T(128)S(1)}, f32[256,2048]{1,0:T(8,128)}, /*index=5*/f32[512,6144]{1,0:T(8,128)}, f32[512,6144]{1,0:T(8,128)}) conditional(s32[]{:T(128)} %convert_element_type.356, () %tuple.72, (bf16[1024,2048]{1,0:T(8,128)(2,1)}, ...), branch_computations={%region_19.20_spmd, %region_20.24_spmd} | conditional | flops 18921000 | bytes 147506976 | solution.py:69
  634.8 9.9 %collective-permute-done.1 = bf16[128,2048]{1,0:T(8,128)(2,1)} collective-permute-done((bf16[128,2048]{1,0:T(8,128)(2,1)}, bf16[128,2048]{1,0:T(8,128)(2,1)}, u32[]{:S(2)}, u32[]{:S(2)}) %collective-permute-start.1) | collective-permute-done | bytes 524320 | tf_op jit(solution)/shard_map/cond/branch_1_fun/ppermute | solution.py:51
  647.5 14.9 %collective-permute-done.14 = bf16[256,1536]{1,0:T(8,128)(2,1)S(1)} collective-permute-done((bf16[256,1536]{1,0:T(8,128)(2,1)S(1)}, bf16[256,1536]{1,0:T(8,128)(2,1)S(1)}, u32[]{:S(2)}, u32[]{:S(2)}) %collective-permute-start.14) | collective-permute-done | bytes 786464 | tf_op jit(solution)/shard_map/cond/branch_1_fun/ppermute | solution.py:51
  663.0 7.2 collective-permute-done.13
  670.7 7.7 collective-permute-done.12
  680.3 8.2 %collective-permute-done = bf16[128,2048]{1,0:T(8,128)(2,1)S(1)} collective-permute-done((bf16[128,2048]{1,0:T(8,128)(2,1)S(1)}, bf16[128,2048]{1,0:T(8,128)(2,1)S(1)}, u32[]{:S(2)}, u32[]{:S(2)}) %collective-permute-start) | collective-permute-done | bytes 524320 | tf_op jit(solution)/shard_map/cond/branch_1_fun/ppermute | solution.py:51
  707.9 10.5 %place.8 = f32[512,6144]{1,0:T(8,128)} custom-call(s32[2]{0:T(128)S(1)} %pad_add_fusion.1.place, bf16[4,256,1536]{2,1,0:T(8,128)(2,1)} %get-tuple-element.152.mine, bf16[4,256,1536]{2,1,0:T(8,128)(2,1)} %collective-permute-done.6.other), custom_call_target="tpu_custom_call" | custom-call | bytes 18874368 | tf_op jit(solution)/shard_map/cond/branch_1_fun/place/pallas_call | solution.py:310
  727.9 4.8 collective-permute-done.10
  739.7 8.7 %place.9 = f32[512,6144]{1,0:T(8,128)} custom-call(s32[2]{0:T(128)S(1)} %pad_add_fusion.1.place, bf16[4,256,1536]{2,1,0:T(8,128)(2,1)S(1)} %pad_maximum_fusion.5.mine, bf16[4,256,1536]{2,1,0:T(8,128)(2,1)} %collective-permute-done.15.other), custom_call_target="tpu_custom_call" | custom-call | bytes 18874368 | tf_op jit(solution)/shard_map/cond/branch_1_fun/place/pallas_call | solution.py:310
  (527 shorter events, 333.8 us)
Async XLA Ops:
  7.2 392.9 %all-reduce.6.cloned.1.call-start = ((), (), s32[]{:S(2)}) async-start(), calls=%async_computation | async-start | bytes 6291456 | tf_op jit(solution)/shard_map/psum | solution.py:853
  9.6 59.1 %collective-permute-start.50 = (bf16[128,2048]{1,0:T(8,128)(2,1)}, bf16[128,2048]{1,0:T(8,128)(2,1)}, u32[]{:S(2)}, u32[]{:S(2)}) collective-permute-start(bf16[128,2048]{1,0:T(8,128)(2,1)} %get-tuple-element.574), channel_id=1, source_target_pairs={{0,8},{8,0},{16,24},{24,16},{1,9},{9,1},{17,25},{25,17},{2,10},{10... | collective-permute-start | bytes 1572872 | tf_op jit(solution)/shard_map/ppermute | solution.py:51
  12.5 41.8 %collective-permute-start.49 = (bf16[128,2048]{1,0:T(8,128)(2,1)}, bf16[128,2048]{1,0:T(8,128)(2,1)}, u32[]{:S(2)}, u32[]{:S(2)}) collective-permute-start(bf16[128,2048]{1,0:T(8,128)(2,1)} %get-tuple-element.574), channel_id=1, source_target_pairs={{0,16},{8,24},{16,0},{24,8},{1,17},{9,25},{17,1},{25,9},{2,18},{10... | collective-permute-start | bytes 1572872 | tf_op jit(solution)/shard_map/ppermute | solution.py:51
  32.3 24.4 %collective-permute-start.59 = (bf16[128,1536]{1,0:T(8,128)(2,1)}, bf16[128,1536]{1,0:T(8,128)(2,1)}, u32[]{:S(2)}, u32[]{:S(2)}) collective-permute-start(bf16[128,1536]{1,0:T(8,128)(2,1)} %pad_maximum_fusion.27), channel_id=1, source_target_pairs={{0,24},{8,16},{16,8},{24,0},{1,25},{9,17},{17,9},{25,1},{2,26},{10... | collective-permute-start | bytes 1179656 | tf_op jit(solution)/shard_map/ppermute | solution.py:51
  32.5 25.9 %collective-permute-start.58 = (bf16[128,1536]{1,0:T(8,128)(2,1)}, bf16[128,1536]{1,0:T(8,128)(2,1)}, u32[]{:S(2)}, u32[]{:S(2)}) collective-permute-start(bf16[128,1536]{1,0:T(8,128)(2,1)} %pad_maximum_fusion.26), channel_id=1, source_target_pairs={{0,16},{8,24},{16,0},{24,8},{1,17},{9,25},{17,1},{25,9},{2,18},{10... | collective-permute-start | bytes 1179656 | tf_op jit(solution)/shard_map/ppermute | solution.py:51
  68.6 23.4 %collective-permute-start.61 = (bf16[3,128,1536]{2,1,0:T(8,128)(2,1)S(1)}, bf16[3,128,1536]{2,1,0:T(8,128)(2,1)S(1)}, u32[]{:S(2)}, u32[]{:S(2)}) collective-permute-start(bf16[3,128,1536]{2,1,0:T(8,128)(2,1)S(1)} %pad_maximum_fusion.12.refs_0_), channel_id=1, source_target_pairs={{0,1},{1,0},{2,3},{3,2},{4,5},{5,4},{6,7},{7,6},{8,9},{9,8},{10,11... | collective-permute-start | bytes 3538952 | tf_op jit(solution)/shard_map/ppermute | solution.py:51
  80.2 28.6 %collective-permute-start.63 = (bf16[128,3072]{1,0:T(8,128)(2,1)}, bf16[128,3072]{1,0:T(8,128)(2,1)}, u32[]{:S(2)}, u32[]{:S(2)}) collective-permute-start(bf16[128,3072]{1,0:T(8,128)(2,1)} %pad_maximum_fusion.20), channel_id=1, source_target_pairs={{0,8},{8,0},{16,24},{24,16},{1,9},{9,1},{17,25},{25,17},{2,10},{10... | collective-permute-start | bytes 2359304 | tf_op jit(solution)/shard_map/ppermute | solution.py:51
  82.4 33.7 %collective-permute-start.64 = (bf16[128,3072]{1,0:T(8,128)(2,1)}, bf16[128,3072]{1,0:T(8,128)(2,1)}, u32[]{:S(2)}, u32[]{:S(2)}) collective-permute-start(bf16[128,3072]{1,0:T(8,128)(2,1)} %pad_maximum_fusion.21), channel_id=1, source_target_pairs={{0,16},{8,24},{16,0},{24,8},{1,17},{9,25},{17,1},{25,9},{2,18},{10... | collective-permute-start | bytes 2359304 | tf_op jit(solution)/shard_map/ppermute | solution.py:51
  84.9 31.3 %collective-permute-start.65 = (bf16[128,3072]{1,0:T(8,128)(2,1)}, bf16[128,3072]{1,0:T(8,128)(2,1)}, u32[]{:S(2)}, u32[]{:S(2)}) collective-permute-start(bf16[128,3072]{1,0:T(8,128)(2,1)} %pad_maximum_fusion.22), channel_id=1, source_target_pairs={{0,24},{8,16},{16,8},{24,0},{1,25},{9,17},{17,9},{25,1},{2,26},{10... | collective-permute-start | bytes 2359304 | tf_op jit(solution)/shard_map/ppermute | solution.py:51
  117.1 28.2 %collective-permute-start.71 = (bf16[128,2048]{1,0:T(8,128)(2,1)S(1)}, bf16[128,2048]{1,0:T(8,128)(2,1)S(1)}, u32[]{:S(2)}, u32[]{:S(2)}) collective-permute-start(bf16[128,2048]{1,0:T(8,128)(2,1)S(1)} %convolution_convert_fusion.8), channel_id=1, source_target_pairs={{0,16},{8,24},{16,0},{24,8},{1,17},{9,25},{17,1},{25,9},{2,18},{10... | collective-permute-start | bytes 1572872 | tf_op jit(solution)/shard_map/ppermute | solution.py:51
  121.0 28.1 %collective-permute-start.66 = (bf16[128,2048]{1,0:T(8,128)(2,1)S(1)}, bf16[128,2048]{1,0:T(8,128)(2,1)S(1)}, u32[]{:S(2)}, u32[]{:S(2)}) collective-permute-start(bf16[128,2048]{1,0:T(8,128)(2,1)S(1)} %convolution_convert_fusion.14), channel_id=1, source_target_pairs={{0,8},{8,0},{16,24},{24,16},{1,9},{9,1},{17,25},{25,17},{2,10},{10... | collective-permute-start | bytes 1572872 | tf_op jit(solution)/shard_map/ppermute | solution.py:51
  143.7 62.3 %collective-permute-start.78 = (bf16[3,128,3072]{2,1,0:T(8,128)(2,1)S(1)}, bf16[3,128,3072]{2,1,0:T(8,128)(2,1)}, u32[]{:S(2)}, u32[]{:S(2)}) collective-permute-start(bf16[3,128,3072]{2,1,0:T(8,128)(2,1)S(1)} %pad_maximum_fusion.11.refs_0_), channel_id=1, source_target_pairs={{0,2},{2,0},{4,6},{6,4},{1,3},{3,1},{5,7},{7,5},{8,10},{10,8},{12,... | collective-permute-start | bytes 7077896 | tf_op jit(solution)/shard_map/ppermute | solution.py:51
  145.3 60.7 %collective-permute-start.79 = (bf16[3,128,3072]{2,1,0:T(8,128)(2,1)S(1)}, bf16[3,128,3072]{2,1,0:T(8,128)(2,1)S(1)}, u32[]{:S(2)}, u32[]{:S(2)}) collective-permute-start(bf16[3,128,3072]{2,1,0:T(8,128)(2,1)S(1)} %pad_maximum_fusion.11.refs_0_), channel_id=1, source_target_pairs={{0,1},{1,0},{2,3},{3,2},{4,5},{5,4},{6,7},{7,6},{8,9},{9,8},{10,11... | collective-permute-start | bytes 7077896 | tf_op jit(solution)/shard_map/ppermute | solution.py:51
  171.6 21.8 %collective-permute-start.74 = (bf16[128,2048]{1,0:T(8,128)(2,1)S(1)}, bf16[128,2048]{1,0:T(8,128)(2,1)S(1)}, u32[]{:S(2)}, u32[]{:S(2)}) collective-permute-start(bf16[128,2048]{1,0:T(8,128)(2,1)S(1)} %get-tuple-element.572), channel_id=1, source_target_pairs={{0,8},{8,0},{16,24},{24,16},{1,9},{9,1},{17,25},{25,17},{2,10},{10... | collective-permute-start | bytes 1572872 | tf_op jit(solution)/shard_map/ppermute | solution.py:51
  207.6 26.8 %collective-permute-start.84 = (bf16[128,2048]{1,0:T(8,128)(2,1)S(1)}, bf16[128,2048]{1,0:T(8,128)(2,1)S(1)}, u32[]{:S(2)}, u32[]{:S(2)}) collective-permute-start(bf16[128,2048]{1,0:T(8,128)(2,1)S(1)} %get-tuple-element.569), channel_id=1, source_target_pairs={{0,16},{8,24},{16,0},{24,8},{1,17},{9,25},{17,1},{25,9},{2,18},{10... | collective-permute-start | bytes 1572872 | tf_op jit(solution)/shard_map/ppermute | solution.py:51
  209.1 27.5 %collective-permute-start.86 = (bf16[128,2048]{1,0:T(8,128)(2,1)S(1)}, bf16[128,2048]{1,0:T(8,128)(2,1)S(1)}, u32[]{:S(2)}, u32[]{:S(2)}) collective-permute-start(bf16[128,2048]{1,0:T(8,128)(2,1)S(1)} %get-tuple-element.569), channel_id=1, source_target_pairs={{0,8},{8,0},{16,24},{24,16},{1,9},{9,1},{17,25},{25,17},{2,10},{10... | collective-permute-start | bytes 1572872 | tf_op jit(solution)/shard_map/ppermute | solution.py:51
  210.4 24.0 %collective-permute-start.83 = (bf16[128,2048]{1,0:T(8,128)(2,1)S(1)}, bf16[128,2048]{1,0:T(8,128)(2,1)S(1)}, u32[]{:S(2)}, u32[]{:S(2)}) collective-permute-start(bf16[128,2048]{1,0:T(8,128)(2,1)S(1)} %get-tuple-element.570), channel_id=1, source_target_pairs={{0,8},{8,0},{16,24},{24,16},{1,9},{9,1},{17,25},{25,17},{2,10},{10... | collective-permute-start | bytes 1572872 | tf_op jit(solution)/shard_map/ppermute | solution.py:51
  211.1 28.1 %collective-permute-start.87 = (bf16[128,2048]{1,0:T(8,128)(2,1)S(1)}, bf16[128,2048]{1,0:T(8,128)(2,1)S(1)}, u32[]{:S(2)}, u32[]{:S(2)}) collective-permute-start(bf16[128,2048]{1,0:T(8,128)(2,1)S(1)} %get-tuple-element.570), channel_id=1, source_target_pairs={{0,16},{8,24},{16,0},{24,8},{1,17},{9,25},{17,1},{25,9},{2,18},{10... | collective-permute-start | bytes 1572872 | tf_op jit(solution)/shard_map/ppermute | solution.py:51
  213.2 42.8 %collective-permute-start.90 = (bf16[3,384,512]{2,1,0:T(8,128)(2,1)}, bf16[3,384,512]{2,1,0:T(8,128)(2,1)S(1)}, u32[]{:S(2)}, u32[]{:S(2)}) collective-permute-start(bf16[3,384,512]{2,1,0:T(8,128)(2,1)} %pad_maximum_fusion.13), channel_id=1, source_target_pairs={{0,2},{2,0},{4,6},{6,4},{1,3},{3,1},{5,7},{7,5},{8,10},{10,8},{12,... | collective-permute-start | bytes 3538952 | tf_op jit(solution)/shard_map/ppermute | solution.py:51
  234.4 21.6 %collective-permute-start.91 = (bf16[3,384,512]{2,1,0:T(8,128)(2,1)S(1)}, bf16[3,384,512]{2,1,0:T(8,128)(2,1)S(1)}, u32[]{:S(2)}, u32[]{:S(2)}) collective-permute-start(bf16[3,384,512]{2,1,0:T(8,128)(2,1)S(1)} %copy-done.30), channel_id=1, source_target_pairs={{0,1},{1,0},{2,3},{3,2},{4,5},{5,4},{6,7},{7,6},{8,9},{9,8},{10,11... | collective-permute-start | bytes 3538952 | tf_op jit(solution)/shard_map/ppermute | solution.py:51
  279.6 345.2 %all-reduce.10.cloned.1.call-start = ((), (), s32[]{:S(2)}) async-start(), calls=%async_computation.2 | async-start | bytes 12582912 | tf_op jit(solution)/shard_map/psum | solution.py:901
  295.8 44.5 %collective-permute-start.16 = (bf16[256,2048]{0,1:T(8,128)(2,1)}, bf16[256,2048]{0,1:T(8,128)(2,1)}, u32[]{:S(2)}, u32[]{:S(2)}) collective-permute-start(bf16[256,2048]{0,1:T(8,128)(2,1)} %get-tuple-element.511), channel_id=1, source_target_pairs={{0,8},{8,0},{16,24},{24,16},{1,9},{9,1},{17,25},{25,17},{2,10},{10... | collective-permute-start | bytes 3145736 | tf_op jit(solution)/shard_map/cond/branch_1_fun/ppermute | solution.py:51
  295.8 48.3 %collective-permute-start.17 = (bf16[256,2048]{0,1:T(8,128)(2,1)}, bf16[256,2048]{0,1:T(8,128)(2,1)}, u32[]{:S(2)}, u32[]{:S(2)}) collective-permute-start(bf16[256,2048]{0,1:T(8,128)(2,1)} %get-tuple-element.510), channel_id=1, source_target_pairs={{0,16},{8,24},{16,0},{24,8},{1,17},{9,25},{17,1},{25,9},{2,18},{10... | collective-permute-start | bytes 3145736 | tf_op jit(solution)/shard_map/cond/branch_1_fun/ppermute | solution.py:51
  296.2 47.9 %collective-permute-start.18 = (bf16[256,2048]{0,1:T(8,128)(2,1)}, bf16[256,2048]{0,1:T(8,128)(2,1)}, u32[]{:S(2)}, u32[]{:S(2)}) collective-permute-start(bf16[256,2048]{0,1:T(8,128)(2,1)} %get-tuple-element.509), channel_id=1, source_target_pairs={{0,24},{8,16},{16,8},{24,0},{1,25},{9,17},{17,9},{25,1},{2,26},{10... | collective-permute-start | bytes 3145736 | tf_op jit(solution)/shard_map/cond/branch_1_fun/ppermute | solution.py:51
  363.1 36.2 %collective-permute-start.21 = (bf16[256,1536]{1,0:T(8,128)(2,1)S(1)}, bf16[256,1536]{1,0:T(8,128)(2,1)S(1)}, u32[]{:S(2)}, u32[]{:S(2)}) collective-permute-start(bf16[256,1536]{1,0:T(8,128)(2,1)S(1)} %get-tuple-element.515), channel_id=1, source_target_pairs={{0,16},{8,24},{16,0},{24,8},{1,17},{9,25},{17,1},{25,9},{2,18},{10... | collective-permute-start | bytes 2359304 | tf_op jit(solution)/shard_map/cond/branch_1_fun/ppermute | solution.py:51
  364.8 34.5 %collective-permute-start.20 = (bf16[256,1536]{1,0:T(8,128)(2,1)S(1)}, bf16[256,1536]{1,0:T(8,128)(2,1)S(1)}, u32[]{:S(2)}, u32[]{:S(2)}) collective-permute-start(bf16[256,1536]{1,0:T(8,128)(2,1)S(1)} %get-tuple-element.516), channel_id=1, source_target_pairs={{0,8},{8,0},{16,24},{24,16},{1,9},{9,1},{17,25},{25,17},{2,10},{10... | collective-permute-start | bytes 2359304 | tf_op jit(solution)/shard_map/cond/branch_1_fun/ppermute | solution.py:51
  401.8 347.3 %all-reduce.8.cloned.1.call-start = ((), (), s32[]{:S(2)}) async-start(), calls=%async_computation.1 | async-start | bytes 6291456 | tf_op jit(solution)/shard_map/psum | solution.py:928
  407.8 23.4 %collective-permute-start.24 = (bf16[128,2048]{1,0:T(8,128)(2,1)S(1)}, bf16[128,2048]{1,0:T(8,128)(2,1)S(1)}, u32[]{:S(2)}, u32[]{:S(2)}) collective-permute-start(bf16[128,2048]{1,0:T(8,128)(2,1)S(1)} %get-tuple-element.535), channel_id=1, source_target_pairs={{0,8},{8,0},{16,24},{24,16},{1,9},{9,1},{17,25},{25,17},{2,10},{10... | collective-permute-start | bytes 1572872 | tf_op jit(solution)/shard_map/cond/branch_1_fun/ppermute | solution.py:51
  408.1 23.1 %collective-permute-start.27 = (bf16[128,2048]{1,0:T(8,128)(2,1)S(1)}, bf16[128,2048]{1,0:T(8,128)(2,1)S(1)}, u32[]{:S(2)}, u32[]{:S(2)}) collective-permute-start(bf16[128,2048]{1,0:T(8,128)(2,1)S(1)} %get-tuple-element.536), channel_id=1, source_target_pairs={{0,16},{8,24},{16,0},{24,8},{1,17},{9,25},{17,1},{25,9},{2,18},{10... | collective-permute-start | bytes 1572872 | tf_op jit(solution)/shard_map/cond/branch_1_fun/ppermute | solution.py:51
  423.6 27.0 %collective-permute-start.29 = (bf16[128,2048]{1,0:T(8,128)(2,1)}, bf16[128,2048]{1,0:T(8,128)(2,1)}, u32[]{:S(2)}, u32[]{:S(2)}) collective-permute-start(bf16[128,2048]{1,0:T(8,128)(2,1)} %get-tuple-element.538), channel_id=1, source_target_pairs={{0,16},{8,24},{16,0},{24,8},{1,17},{9,25},{17,1},{25,9},{2,18},{10... | collective-permute-start | bytes 1572872 | tf_op jit(solution)/shard_map/cond/branch_1_fun/ppermute | solution.py:51
  462.9 23.8 %collective-permute-start.32 = (bf16[128,2048]{1,0:T(8,128)(2,1)}, bf16[128,2048]{1,0:T(8,128)(2,1)}, u32[]{:S(2)}, u32[]{:S(2)}) collective-permute-start(bf16[128,2048]{1,0:T(8,128)(2,1)} %get-tuple-element.552), channel_id=1, source_target_pairs={{0,8},{8,0},{16,24},{24,16},{1,9},{9,1},{17,25},{25,17},{2,10},{10... | collective-permute-start | bytes 1572872 | tf_op jit(solution)/shard_map/cond/branch_1_fun/ppermute | solution.py:51
  463.8 24.8 %collective-permute-start.33 = (bf16[128,2048]{1,0:T(8,128)(2,1)}, bf16[128,2048]{1,0:T(8,128)(2,1)}, u32[]{:S(2)}, u32[]{:S(2)}) collective-permute-start(bf16[128,2048]{1,0:T(8,128)(2,1)} %get-tuple-element.553), channel_id=1, source_target_pairs={{0,16},{8,24},{16,0},{24,8},{1,17},{9,25},{17,1},{25,9},{2,18},{10... | collective-permute-start | bytes 1572872 | tf_op jit(solution)/shard_map/cond/branch_1_fun/ppermute | solution.py:51
  522.5 45.3 %collective-permute-start.40 = (bf16[4,256,1024]{2,1,0:T(8,128)(2,1)}, bf16[4,256,1024]{2,1,0:T(8,128)(2,1)}, u32[]{:S(2)}, u32[]{:S(2)}) collective-permute-start(bf16[4,256,1024]{2,1,0:T(8,128)(2,1)} %constant_dynamic-slice_fusion.7), channel_id=1, source_target_pairs={{0,1},{1,0},{2,3},{3,2},{4,5},{5,4},{6,7},{7,6},{8,9},{9,8},{10,11... | collective-permute-start | bytes 6291464 | tf_op jit(solution)/shard_map/cond/branch_1_fun/ppermute | solution.py:51
  525.5 21.4 %collective-permute-start.46 = (bf16[768,512]{1,0:T(8,128)(2,1)S(1)}, bf16[768,512]{1,0:T(8,128)(2,1)S(1)}, u32[]{:S(2)}, u32[]{:S(2)}) collective-permute-start(bf16[768,512]{1,0:T(8,128)(2,1)S(1)} %get-tuple-element.540), channel_id=1, source_target_pairs={{0,24},{8,16},{16,8},{24,0},{1,25},{9,17},{17,9},{25,1},{2,26},{10... | collective-permute-start | bytes 2359304 | tf_op jit(solution)/shard_map/cond/branch_1_fun/ppermute | solution.py:51
  527.1 33.5 %collective-permute-start.45 = (bf16[768,512]{1,0:T(8,128)(2,1)S(1)}, bf16[768,512]{1,0:T(8,128)(2,1)S(1)}, u32[]{:S(2)}, u32[]{:S(2)}) collective-permute-start(bf16[768,512]{1,0:T(8,128)(2,1)S(1)} %get-tuple-element.541), channel_id=1, source_target_pairs={{0,16},{8,24},{16,0},{24,8},{1,17},{9,25},{17,1},{25,9},{2,18},{10... | collective-permute-start | bytes 2359304 | tf_op jit(solution)/shard_map/cond/branch_1_fun/ppermute | solution.py:51
  528.8 31.9 %collective-permute-start.44 = (bf16[768,512]{1,0:T(8,128)(2,1)S(1)}, bf16[768,512]{1,0:T(8,128)(2,1)S(1)}, u32[]{:S(2)}, u32[]{:S(2)}) collective-permute-start(bf16[768,512]{1,0:T(8,128)(2,1)S(1)} %get-tuple-element.542), channel_id=1, source_target_pairs={{0,8},{8,0},{16,24},{24,16},{1,9},{9,1},{17,25},{25,17},{2,10},{10... | collective-permute-start | bytes 2359304 | tf_op jit(solution)/shard_map/cond/branch_1_fun/ppermute | solution.py:51
  532.8 28.6 %collective-permute-start.36 = (bf16[256,2048]{1,0:T(8,128)(2,1)}, bf16[256,2048]{1,0:T(8,128)(2,1)}, u32[]{:S(2)}, u32[]{:S(2)}) collective-permute-start(bf16[256,2048]{1,0:T(8,128)(2,1)} %constant_dynamic-slice_fusion.11), channel_id=1, source_target_pairs={{0,1},{1,0},{2,3},{3,2},{4,5},{5,4},{6,7},{7,6},{8,9},{9,8},{10,11... | collective-permute-start | bytes 3145736 | tf_op jit(solution)/shard_map/cond/branch_1_fun/ppermute | solution.py:51
  561.1 44.0 %collective-permute-start.47 = (bf16[4,768,512]{2,1,0:T(8,128)(2,1)S(1)}, bf16[4,768,512]{2,1,0:T(8,128)(2,1)}, u32[]{:S(2)}, u32[]{:S(2)}) collective-permute-start(bf16[4,768,512]{2,1,0:T(8,128)(2,1)S(1)} %pad_maximum_fusion.1.mine), channel_id=1, source_target_pairs={{0,1},{1,0},{2,3},{3,2},{4,5},{5,4},{6,7},{7,6},{8,9},{9,8},{10,11... | collective-permute-start | bytes 9437192 | tf_op jit(solution)/shard_map/cond/branch_1_fun/ppermute | solution.py:51
  574.4 27.6 %collective-permute-start.42 = (bf16[256,1024]{1,0:T(8,128)(2,1)}, bf16[256,1024]{1,0:T(8,128)(2,1)}, u32[]{:S(2)}, u32[]{:S(2)}) collective-permute-start(bf16[256,1024]{1,0:T(8,128)(2,1)} %get-tuple-element.545), channel_id=1, source_target_pairs={{0,16},{8,24},{16,0},{24,8},{1,17},{9,25},{17,1},{25,9},{2,18},{10... | collective-permute-start | bytes 1572872 | tf_op jit(solution)/shard_map/cond/branch_1_fun/ppermute | solution.py:51
  631.3 31.1 %collective-permute-start.14 = (bf16[256,1536]{1,0:T(8,128)(2,1)S(1)}, bf16[256,1536]{1,0:T(8,128)(2,1)S(1)}, u32[]{:S(2)}, u32[]{:S(2)}) collective-permute-start(bf16[256,1536]{1,0:T(8,128)(2,1)S(1)} %get-tuple-element.524), channel_id=1, source_target_pairs={{0,24},{8,16},{16,8},{24,0},{1,25},{9,17},{17,9},{25,1},{2,26},{10... | collective-permute-start | bytes 2359304 | tf_op jit(solution)/shard_map/cond/branch_1_fun/ppermute | solution.py:51
  632.8 37.3 %collective-permute-start.13 = (bf16[256,1536]{1,0:T(8,128)(2,1)S(1)}, bf16[256,1536]{1,0:T(8,128)(2,1)S(1)}, u32[]{:S(2)}, u32[]{:S(2)}) collective-permute-start(bf16[256,1536]{1,0:T(8,128)(2,1)S(1)} %get-tuple-element.525), channel_id=1, source_target_pairs={{0,16},{8,24},{16,0},{24,8},{1,17},{9,25},{17,1},{25,9},{2,18},{10... | collective-permute-start | bytes 2359304 | tf_op jit(solution)/shard_map/cond/branch_1_fun/ppermute | solution.py:51
  633.4 74.5 %collective-permute-start.6 = (bf16[4,256,1536]{2,1,0:T(8,128)(2,1)}, bf16[4,256,1536]{2,1,0:T(8,128)(2,1)}, u32[]{:S(2)}, u32[]{:S(2)}) collective-permute-start(bf16[4,256,1536]{2,1,0:T(8,128)(2,1)} %get-tuple-element.152.mine), channel_id=1, source_target_pairs={{0,1},{1,0},{2,3},{3,2},{4,5},{5,4},{6,7},{7,6},{8,9},{9,8},{10,11... | collective-permute-start | bytes 9437192 | tf_op jit(solution)/shard_map/cond/branch_1_fun/ppermute | solution.py:51
  633.4 45.0 %collective-permute-start.12 = (bf16[256,1536]{1,0:T(8,128)(2,1)S(1)}, bf16[256,1536]{1,0:T(8,128)(2,1)S(1)}, u32[]{:S(2)}, u32[]{:S(2)}) collective-permute-start(bf16[256,1536]{1,0:T(8,128)(2,1)S(1)} %get-tuple-element.526), channel_id=1, source_target_pairs={{0,8},{8,0},{16,24},{24,16},{1,9},{9,1},{17,25},{25,17},{2,10},{10... | collective-permute-start | bytes 2359304 | tf_op jit(solution)/shard_map/cond/branch_1_fun/ppermute | solution.py:51
  644.7 43.7 %collective-permute-start = (bf16[128,2048]{1,0:T(8,128)(2,1)S(1)}, bf16[128,2048]{1,0:T(8,128)(2,1)S(1)}, u32[]{:S(2)}, u32[]{:S(2)}) collective-permute-start(bf16[128,2048]{1,0:T(8,128)(2,1)S(1)} %copy-done.64), channel_id=1, source_target_pairs={{0,8},{8,0},{16,24},{24,16},{1,9},{9,1},{17,25},{25,17},{2,10},{10... | collective-permute-start | bytes 1572872 | tf_op jit(solution)/shard_map/cond/branch_1_fun/ppermute | solution.py:51
  662.4 26.0 %collective-permute-start.3 = (bf16[128,2048]{1,0:T(8,128)(2,1)S(1)}, bf16[128,2048]{1,0:T(8,128)(2,1)S(1)}, u32[]{:S(2)}, u32[]{:S(2)}) collective-permute-start(bf16[128,2048]{1,0:T(8,128)(2,1)S(1)} %copy-done.63), channel_id=1, source_target_pairs={{0,16},{8,24},{16,0},{24,8},{1,17},{9,25},{17,1},{25,9},{2,18},{10... | collective-permute-start | bytes 1572872 | tf_op jit(solution)/shard_map/cond/branch_1_fun/ppermute | solution.py:51
  670.1 22.5 %collective-permute-start.2 = (bf16[128,2048]{1,0:T(8,128)(2,1)S(1)}, bf16[128,2048]{1,0:T(8,128)(2,1)S(1)}, u32[]{:S(2)}, u32[]{:S(2)}) collective-permute-start(bf16[128,2048]{1,0:T(8,128)(2,1)S(1)} %add_convert_fusion.8), channel_id=1, source_target_pairs={{0,16},{8,24},{16,0},{24,8},{1,17},{9,25},{17,1},{25,9},{2,18},{10... | collective-permute-start | bytes 1572872 | tf_op jit(solution)/shard_map/cond/branch_1_fun/ppermute | solution.py:51
  678.4 23.8 %collective-permute-start.5 = (bf16[128,2048]{1,0:T(8,128)(2,1)}, bf16[128,2048]{1,0:T(8,128)(2,1)}, u32[]{:S(2)}, u32[]{:S(2)}) collective-permute-start(bf16[128,2048]{1,0:T(8,128)(2,1)} %get-tuple-element.520), channel_id=1, source_target_pairs={{0,16},{8,24},{16,0},{24,8},{1,17},{9,25},{17,1},{25,9},{2,18},{10... | collective-permute-start | bytes 1572872 | tf_op jit(solution)/shard_map/cond/branch_1_fun/ppermute | solution.py:51
  688.5 51.3 %collective-permute-start.15 = (bf16[4,256,1536]{2,1,0:T(8,128)(2,1)S(1)}, bf16[4,256,1536]{2,1,0:T(8,128)(2,1)}, u32[]{:S(2)}, u32[]{:S(2)}) collective-permute-start(bf16[4,256,1536]{2,1,0:T(8,128)(2,1)S(1)} %pad_maximum_fusion.5.mine), channel_id=1, source_target_pairs={{0,1},{1,0},{2,3},{3,2},{4,5},{5,4},{6,7},{7,6},{8,9},{9,8},{10,11... | collective-permute-start | bytes 9437192 | tf_op jit(solution)/shard_map/cond/branch_1_fun/ppermute | solution.py:51
  (145 other events, 1580.0 us)
Sparse Core Ops, SparseCore 0:
  279.7 119.6 all-reduce.5
  402.4 222.3 all-reduce.9
  627.8 121.1 all-reduce.7
